TPU v7x, 32 devices: a whole 2x2x4 slice. The times are simulated.
32 devices in a mesh: dp: 4 (over y, x), enc: 4 (over z), seq: 2 (over core).
Axes of the slice: x: 2, y: 2, z: 4, core: 2. Of those that a mesh axis runs over, the one named last changes fastest.
Arguments:
- queries: bfloat16 [4096, 1280], P(('dp', 'enc', 'seq')), may hold values from -6 to 6
- key_vectors: bfloat16 [4096, 1280], P(('dp', 'enc', 'seq')), may hold values from -6 to 6
- value_vectors: bfloat16 [4096, 1280], P(('dp', 'enc', 'seq')), may hold values from -6 to 6
- residual: bfloat16 [4096, 1280], P(('dp', 'enc', 'seq')), may hold values from -6 to 6
- out_weight: bfloat16 [1280, 1280], replicated, may hold values from -0.15625 to 0.15625
- cotangent: bfloat16 [4096, 1280], P(('dp', 'enc', 'seq')), may hold values from -0.09375 to 0.09375
- send_row: int32 [8192], P(('dp', 'enc', 'seq')), may hold values from 0 to 128, as said below
- image_id: int32 [4096], P(('dp', 'enc', 'seq')), may hold values from 0 to 127, as said below
Outputs:
- layer_out: bfloat16 [4096, 1280], P(('dp', 'enc', 'seq'))
- grad_weight: float32 [1280, 1280], P(('dp', 'seq'), 'enc')
Inputs may be any that keep to these rules, and one draw needn't show every extreme that they name: `send_row`: in each device's block of 256 entries every local row 0 .. 127 appears exactly once and every other entry is 128; at most 64 rows go to one encoder device, and in every device's block some encoder device gets exactly 64. Rows with equal image_id lie in one encoder group (equal dp and seq indices) and are all sent to the same encoder device.
All inputs are finite; a program needn't handle non-finite values.
Results may differ from a plain program's by a relative error of at most 0.017.
Values may be sent and summed in bfloat16 or wider, within the bound.
No kernel may reach another device: no remote copies, remote signals or barrier semaphores. Data moves between devices by JAX's collectives and lax.ppermute only.
A program may use at most 64 MiB of HBM per device.

v0:
```python
import math

import jax
import jax.numpy as jnp
from jax import lax
from jax.sharding import PartitionSpec as P

HEADS = 16


def attend_groups(query_group, key_group, value_group, image_ids):
    items, slot_count, group_width = query_group.shape
    group_heads = HEADS // 2
    head_width = group_width // group_heads
    scale = 1.0 / math.sqrt(head_width)
    position = jnp.arange(slot_count)
    image_ids = jnp.where(image_ids < 0, -1 - position[None, :], image_ids)
    shaped_query = query_group.reshape(items, slot_count, group_heads, head_width)
    shaped_key = key_group.reshape(items, slot_count, group_heads, head_width)
    shaped_value = value_group.reshape(items, slot_count, group_heads, head_width)
    scores = (
        jnp.einsum("gqhd,gkhd->ghqk", shaped_query, shaped_key, preferred_element_type=jnp.float32)
        * scale
    )
    same_image = image_ids[:, None, :, None] == image_ids[:, None, None, :]
    scores = jnp.where(same_image, scores, -1e30)
    highest = jnp.max(scores, axis=-1, keepdims=True)
    weights = jnp.exp(scores - highest)
    probs = (weights / jnp.sum(weights, axis=-1, keepdims=True)).astype(jnp.bfloat16)
    mixed = jnp.einsum("ghqk,gkhd->gqhd", probs, shaped_value, preferred_element_type=jnp.float32)
    return mixed.reshape(items, slot_count, group_width).astype(jnp.bfloat16)


def body(queries, key_vectors, value_vectors, residual, out_weight, cotangent, send_row, image_id):
    row_count, full_width = queries.shape
    half_width = full_width // 2
    is_live = send_row < row_count
    source_row = jnp.minimum(send_row, row_count - 1)

    def arrange(data):
        grouped = data.reshape(row_count, 2, half_width).transpose(1, 0, 2)
        return jnp.where(is_live[None, :, None], grouped[:, source_row], jnp.zeros((), data.dtype))

    send_query = arrange(queries)
    send_key = arrange(key_vectors)
    send_value = arrange(value_vectors)
    send_image = jnp.where(is_live, image_id[source_row], -1)
    send_image = jnp.broadcast_to(send_image[None, :], (2, send_row.shape[0]))
    received = (
        lax.all_to_all(send_query, "enc", split_axis=1, concat_axis=1, tiled=True),
        lax.all_to_all(send_key, "enc", split_axis=1, concat_axis=1, tiled=True),
        lax.all_to_all(send_value, "enc", split_axis=1, concat_axis=1, tiled=True),
        lax.all_to_all(send_image, "enc", split_axis=1, concat_axis=1, tiled=True),
    )
    output = attend_groups(received[0], received[1], received[2], received[3])
    returned = lax.all_to_all(output, "enc", split_axis=1, concat_axis=1, tiled=True)
    holder = jnp.zeros((2, row_count + 1, half_width), jnp.bfloat16).at[:, send_row].set(returned)
    attended = holder[:, :row_count].transpose(1, 0, 2).reshape(row_count, full_width)
    projected = jnp.dot(attended, out_weight, preferred_element_type=jnp.float32)
    layer_out = (residual.astype(jnp.float32) + projected).astype(jnp.bfloat16)
    first_sum = lax.psum_scatter(
        lax.dot_general(
            attended, cotangent, (((0,), (0,)), ((), ())), preferred_element_type=jnp.float32
        ).astype(jnp.bfloat16),
        "dp",
        scatter_dimension=0,
        tiled=True,
    )
    second_sum = lax.psum_scatter(first_sum, "seq", scatter_dimension=0, tiled=True).astype(
        jnp.float32
    )
    grad_weight = lax.psum_scatter(second_sum, "enc", scatter_dimension=1, tiled=True)
    return (layer_out, grad_weight)


def solution(mesh):
    placed = (
        P(("dp", "enc", "seq"), None),
        P(("dp", "enc", "seq"), None),
        P(("dp", "enc", "seq"), None),
        P(("dp", "enc", "seq"), None),
        P(),
        P(("dp", "enc", "seq"), None),
        P(("dp", "enc", "seq")),
        P(("dp", "enc", "seq")),
    )
    return jax.shard_map(
        body,
        mesh=mesh,
        in_specs=placed,
        out_specs=(P(("dp", "enc", "seq"), None), P(("dp", "seq"), "enc")),
        check_vma=False,
    )
```

profile of v0, /device:TPU:0, one launch (start us, length us, event | category | flops | bytes accessed | tf_op | source)
XLA Modules:
  0.0 269.2 jit_solution(1657478024315463821)
XLA Ops:
  7.2 0.8 compare_select_fusion.1
  8.0 2.0 gather_fusion.1
  11.5 6.3 %all-to-all-start.1 = ((s32[4,1,128]{2,1,0:T(1,128)}), s32[4,1,128]{2,1,0:T(1,128)S(1)}, u32[]{:S(2)}, u32[]{:S(2)}) async-start(s32[4,1,128]{2,1,0:T(1,128)} %reshape.143), calls=%async_computation.1 | async-start | bytes 4096 | tf_op jit(solution)/shard_map/all_to_all | solution.py:53
  17.8 1.8 reshape.89
  19.6 3.8 %gather_fusion = bf16[256,2,640]{2,1,0:T(2,128)(2,1)} fusion(bf16[2,128,640]{2,0,1:T(2,128)(2,1)} %bitcast.37, s32[1024]{0:T(1024)S(1)} %pad_clamp_fusion), kind=kCustom, calls=%fused_computation | custom fusion | bytes 1311744 | tf_op jit(solution)/shard_map/gather | solution.py:42
  23.4 1.8 reshape.91
  25.2 3.8 %gather_fusion.2 = bf16[256,2,640]{2,1,0:T(2,128)(2,1)} fusion(bf16[2,128,640]{2,0,1:T(2,128)(2,1)} %bitcast.38, s32[1024]{0:T(1024)S(1)} %pad_clamp_fusion), kind=kCustom, calls=%fused_computation.2 | custom fusion | bytes 1311744 | tf_op jit(solution)/shard_map/gather | solution.py:42
  29.0 1.8 reshape.93
  30.7 3.8 %gather_fusion.3 = bf16[256,2,640]{2,1,0:T(2,128)(2,1)} fusion(bf16[2,128,640]{2,0,1:T(2,128)(2,1)} %bitcast.36, s32[1024]{0:T(1024)S(1)} %pad_clamp_fusion), kind=kCustom, calls=%fused_computation.3 | custom fusion | bytes 1311744 | tf_op jit(solution)/shard_map/gather | solution.py:42
  34.5 4.3 %fusion.10 = (bf16[2,256,640]{2,0,1:T(2,128)(2,1)}, bf16[2,256,640]{2,0,1:T(2,128)(2,1)}, bf16[2,256,640]{2,0,1:T(2,128)(2,1)}) fusion(bf16[256,2,640]{2,1,0:T(2,128)(2,1)} %gather_fusion.3, pred[256]{0:T(512)(128)(4,1)S(1)} %get-tuple-element.3, bf16[256,2,640]{2,1,0:T(2,128)(2,1)} %gather_fusion.2, bf16[256,2,640]{2,1,0:T(2,128)(2,1)} %gather_fusion), kind=kLoop, calls=%fused_computation.23 | loop fusion | flops 983040 | bytes 3932416 | tf_op jit(solution)/shard_map/jit(_where)/select_n | solution.py:42
  38.8 21.9 %all_to_all.29 = bf16[2,256,640]{2,0,1:T(2,128)(2,1)} all-to-all(bf16[2,256,640]{2,0,1:T(2,128)(2,1)} %get-tuple-element.6), channel_id=1, replica_groups=mesh['dp'=4,'enc'=4,'seq'=2] {'enc'}, dimensions={1} | all-to-all | bytes 1310720 | tf_op jit(solution)/shard_map/all_to_all | solution.py:50
  60.8 20.6 %all_to_all.30 = bf16[2,256,640]{2,0,1:T(2,128)(2,1)} all-to-all(bf16[2,256,640]{2,0,1:T(2,128)(2,1)} %get-tuple-element.5), channel_id=1, replica_groups=mesh['dp'=4,'enc'=4,'seq'=2] {'enc'}, dimensions={1} | all-to-all | bytes 1310720 | tf_op jit(solution)/shard_map/all_to_all | solution.py:51
  81.4 4.2 %all-to-all-start = ((bf16[2,256,640]{2,0,1:T(2,128)(2,1)}), bf16[2,256,640]{2,0,1:T(2,128)(2,1)}, u32[]{:S(2)}, u32[]{:S(2)}) async-start(bf16[2,256,640]{2,0,1:T(2,128)(2,1)} %get-tuple-element.7), calls=%async_computation | async-start | bytes 1310720 | tf_op jit(solution)/shard_map/all_to_all | solution.py:52
  87.1 2.9 %copy.24 = bf16[2,256,640]{1,2,0:T(8,128)(2,1)} copy(bf16[2,256,640]{2,0,1:T(2,128)(2,1)} %all_to_all.29) | data formatting | bytes 1310720 | tf_op jit(solution)/shard_map/all_to_all | solution.py:50
  90.0 2.9 %copy.25 = bf16[2,256,640]{1,2,0:T(8,128)(2,1)} copy(bf16[2,256,640]{2,0,1:T(2,128)(2,1)} %all_to_all.30) | data formatting | bytes 1310720 | tf_op jit(solution)/shard_map/all_to_all | solution.py:51
  93.0 4.7 %fusion.15 = (f32[2,8,256]{2,1,0:T(8,128)S(1)}, f32[2,8,256,256]{2,3,1,0:T(8,128)}) fusion(pred[2,256,256]{1,2,0:T(8,128)(4,1)S(1)} %broadcast_compare_fusion, bf16[2,256,8,80]{1,3,2,0:T(8,128)(2,1)} %bitcast.41, bf16[2,256,8,80]{1,3,2,0:T(8,128)(2,1)} %bitcast.42), kind=kOutput, calls=%fused_computation.35 | convolution fusion | flops 171966720 | bytes 5652480 | tf_op jit(solution)/shard_map/sub | solution.py:28
  97.7 4.3 %all-to-all-done = bf16[2,256,640]{2,0,1:T(2,128)(2,1)} async-done(((bf16[2,256,640]{2,0,1:T(2,128)(2,1)}), bf16[2,256,640]{2,0,1:T(2,128)(2,1)}, u32[]{:S(2)}, u32[]{:S(2)}) %all-to-all-start) | async-done | bytes 655392 | tf_op jit(solution)/shard_map/all_to_all | solution.py:52
  102.0 2.9 %copy.22 = bf16[2,256,640]{1,2,0:T(8,128)(2,1)} copy(bf16[2,256,640]{2,0,1:T(2,128)(2,1)} %all-to-all-done) | data formatting | bytes 1310720 | tf_op jit(solution)/shard_map/all_to_all | solution.py:52
  104.9 3.7 %fusion.7 = bf16[2,8,80,256]{3,2,1,0:T(8,128)(2,1)} fusion(bf16[2,256,8,80]{1,3,2,0:T(8,128)(2,1)} %bitcast.43, f32[2,8,256,256]{2,3,1,0:T(8,128)} %get-tuple-element.9, f32[2,8,256]{2,1,0:T(8,128)S(1)} %get-tuple-element.8), kind=kOutput, calls=%fused_computation.17 | convolution fusion | flops 170196992 | bytes 5521408 | tf_op jit(solution)/shard_map/ghqk,gkhd->gqhd/dot_general | solution.py:30
  108.7 3.0 %copy.27 = bf16[2,256,640]{2,0,1:T(2,128)(2,1)} copy(bf16[2,256,640]{1,2,0:T(8,128)(2,1)} %bitcast.44) | data formatting | bytes 1310720 | tf_op jit(solution)/shard_map/convert_element_type | solution.py:31
  111.6 21.0 %all_to_all.31 = bf16[2,256,640]{2,0,1:T(2,128)(2,1)} all-to-all(bf16[2,256,640]{2,0,1:T(2,128)(2,1)} %copy.27), channel_id=1, replica_groups=mesh['dp'=4,'enc'=4,'seq'=2] {'enc'}, dimensions={1} | all-to-all | bytes 1310720 | tf_op jit(solution)/shard_map/all_to_all | solution.py:56
  132.6 0.9 broadcast_in_dim.72
  133.5 31.9 %scatter_fusion = bf16[2,129,640]{2,0,1:T(2,128)(2,1)} fusion(bf16[2,129,640]{2,0,1:T(2,128)(2,1)} %broadcast_in_dim.72, s32[256]{0:T(256)S(1)} %get-tuple-element.4, bf16[256,2,640]{2,1,0:T(2,128)(2,1)} %bitcast.39), kind=kCustom, calls=%fused_computation.4 | custom fusion | bytes 1967104 | tf_op jit(solution)/shard_map/scatter | solution.py:57
  165.4 1.2 slice.12
  166.7 0.7 copy-done.1
  167.4 3.7 %convolution_convert_fusion = bf16[1280,1280]{1,0:T(8,128)(2,1)} fusion(bf16[128,1280]{1,0:T(8,128)(2,1)S(1)} %bitcast.34, bf16[128,1280]{1,0:T(8,128)(2,1)} %param.13), kind=kOutput, calls=%fused_computation.6 | convolution fusion | flops 421068800 | bytes 3932160 | tf_op jit(solution)/shard_map/dot_general | solution.py:62
  171.1 44.3 %reduce-scatter.6.cloned.1.call-done = bf16[320,1280]{1,0:T(8,128)(2,1)} async-done(((bf16[1280,1280]{1,0:T(8,128)(2,1)}), bf16[320,1280]{1,0:T(8,128)(2,1)}) %reduce-scatter.6.cloned.1.call-update) | async-done | bytes 819216 | tf_op jit(solution)/shard_map/reduce_scatter | solution.py:61
  215.5 10.5 %reduce-scatter.8.cloned.1.call-done = bf16[160,1280]{1,0:T(8,128)(2,1)} async-done(((bf16[320,1280]{1,0:T(8,128)(2,1)}), bf16[160,1280]{1,0:T(8,128)(2,1)}) %reduce-scatter.8.cloned.1.call-update) | async-done | bytes 409616 | tf_op jit(solution)/shard_map/reduce_scatter | solution.py:69
  226.0 2.3 copy.29
  228.3 2.4 fusion.2
  230.7 30.1 %reduce-scatter.10.cloned.1.call-done = f32[320,160]{1,0:T(8,128)} async-done(((f32[1280,160]{1,0:T(8,128)}), f32[320,160]{1,0:T(8,128)}) %reduce-scatter.10.cloned.1.call-update) | async-done | bytes 204816
  260.9 1.8 copy.30
  (24 shorter events, 3.2 us)
Async XLA Ops:
  7.2 221.1 %copy-start = (bf16[1280,1280]{1,0:T(8,128)(2,1)S(1)}, bf16[1280,1280]{1,0:T(8,128)(2,1)}, u32[]{:S(2)}) copy-start(bf16[1280,1280]{1,0:T(8,128)(2,1)} %param.12) | copy-start | bytes 9830404
  11.5 27.3 %all-to-all-start.1 = ((s32[4,1,128]{2,1,0:T(1,128)}), s32[4,1,128]{2,1,0:T(1,128)S(1)}, u32[]{:S(2)}, u32[]{:S(2)}) async-start(s32[4,1,128]{2,1,0:T(1,128)} %reshape.143), calls=%async_computation.1 | async-start | bytes 4096 | tf_op jit(solution)/shard_map/all_to_all | solution.py:53
  81.4 20.6 %all-to-all-start = ((bf16[2,256,640]{2,0,1:T(2,128)(2,1)}), bf16[2,256,640]{2,0,1:T(2,128)(2,1)}, u32[]{:S(2)}, u32[]{:S(2)}) async-start(bf16[2,256,640]{2,0,1:T(2,128)(2,1)} %get-tuple-element.7), calls=%async_computation | async-start | bytes 1310720 | tf_op jit(solution)/shard_map/all_to_all | solution.py:52
  85.5 129.9 %reduce-scatter.6.cloned.1.call-start = ((), (), s32[]{:S(2)}) async-start(), calls=%async_computation.8 | async-start | bytes 4096000 | tf_op jit(solution)/shard_map/reduce_scatter | solution.py:61
  166.7 0.7 copy-start.1
  171.1 54.9 %reduce-scatter.8.cloned.1.call-start = ((), (), s32[]{:S(2)}) async-start(), calls=%async_computation.9 | async-start | bytes 1228800 | tf_op jit(solution)/shard_map/reduce_scatter | solution.py:69
  215.5 45.4 %reduce-scatter.10.cloned.1.call-start = ((), (), s32[]{:S(2)}) async-start(), calls=%async_computation.10 | async-start | bytes 1638400
Sparse Core Ops, SparseCore 0:
  171.2 44.1 reduce-scatter.5
  217.7 8.2 reduce-scatter.7
  228.4 32.3 reduce-scatter.9
where the time goes:
time: 272 us; the launch traced here: 269 us
  waiting for transfers between devices  89.2 us (33%)
  local copies, waits for them, and re-layouts  70.7 us (26%)
  blocking collectives  63.5 us (23%)
  matrix products  14.6 us (5%)
  between operations  13.8 us (5%)
  starting transfers between devices  10.6 us (4%)
  other arithmetic  6.67 us (2%)
    reduce_scatter x1, waiting for transfers between devices, body(): lax.psum_scatter(lax.dot_general(attended, cotangent, (((0,), (0,)), ((),...  44.3 us
    scatter x1, local copies, waits for them, and re-layouts, body(): jnp.zeros((2, row_count + 1, half_width), jnp.bfloat16).at[:, send_row]  31.9 us
    unnamed x4, waiting for transfers between devices  30.2 us
    all_to_all x1, blocking collectives, body(): lax.all_to_all(send_query, 'enc', split_axis=1, concat_axis=1, tiled=True)  21.9 us
    all_to_all x1, blocking collectives, body(): lax.all_to_all(output, 'enc', split_axis=1, concat_axis=1, tiled=True)  21 us
    all_to_all x1, blocking collectives, body(): lax.all_to_all(send_key, 'enc', split_axis=1, concat_axis=1, tiled=True)  20.6 us
    gather x3, local copies, waits for them, and re-layouts, arrange(): grouped[:, source_row]  11.4 us
    reduce_scatter x1, waiting for transfers between devices, body(): lax.psum_scatter(first_sum, 'seq', scatter_dimension=0, tiled=True)  10.5 us
  transfers between devices with their start and end apart: 5, of which 4 were waited for; matrix products, arithmetic and copies ran while one was open for 13% of the time, Pallas kernels for 0%

commit v1 on v0

--- a/solution.py
+++ b/solution.py
@@ -1,11 +1,360 @@
+import functools
 import math
 
 import jax
 import jax.numpy as jnp
 from jax import lax
+from jax.experimental import pallas as pl
+from jax.experimental.pallas import tpu as pltpu
 from jax.sharding import PartitionSpec as P
 
 HEADS = 16
+AXES = ("dp", "enc", "seq")
+ID_ROWS = 16
+ID_BASE = 64
+
+
+def call(
+    kernel,
+    out_shape,
+    *args,
+    spaces=None,
+    out_spaces=None,
+    aliases=None,
+    scratch=(),
+    limit=16,
+    flops=0,
+    bytes_accessed=0,
+):
+    def placed(space):
+        return pl.BlockSpec(memory_space=space)
+
+    many = isinstance(out_shape, (list, tuple))
+    spaces = spaces or [pltpu.VMEM] * len(args)
+    args = [
+        pltpu.with_memory_space_constraint(arg, pltpu.HBM) if space == pltpu.HBM else arg
+        for arg, space in zip(args, spaces)
+    ]
+    return pl.pallas_call(
+        kernel,
+        out_shape=out_shape,
+        in_specs=[placed(space) for space in spaces],
+        out_specs=[placed(space) for space in out_spaces or [pltpu.VMEM] * len(out_shape)]
+        if many
+        else placed(pltpu.VMEM),
+        input_output_aliases=aliases or {},
+        scratch_shapes=list(scratch),
+        compiler_params=pltpu.CompilerParams(vmem_limit_bytes=limit * 1024 * 1024),
+        cost_estimate=pl.CostEstimate(
+            flops=flops, bytes_accessed=bytes_accessed, transcendentals=0
+        ),
+    )(*args)
+
+
+def pack_kernel(count, half, *refs):
+    sources, own, cross = refs[:5], refs[5 : 5 + count], refs[5 + count : 5 + 2 * count]
+    ready, held, arrived, ids_held, sems = refs[5 + 2 * count :]
+    targets = [ids_held] + [arrived.at[which] for which in range(3)] + [ready]
+    copies = [
+        pltpu.make_async_copy(source, target, sems.at[which])
+        for which, (source, target) in enumerate(zip(sources, targets))
+    ]
+    for copy in copies:
+        copy.start()
+    e, s = lax.axis_index("enc"), lax.axis_index("seq")
+    copies[0].wait()
+    ids = ids_held[...]
+    row = lax.broadcasted_iota(jnp.int32, (ID_ROWS, ids.shape[1]), 0)
+    digits = jnp.where(row == 0, ids // ID_BASE, jnp.where(row == 1, ids % ID_BASE, 0))
+    digits = digits.astype(jnp.float32).astype(jnp.bfloat16)
+    for out in own + cross:
+        out[3 * half :] = digits
+    for which in range(3):
+        copies[1 + which].wait()
+        held[...] = arrived[which].T
+        span = slice(which * half, (which + 1) * half)
+        for step in range(count):
+            block = (e ^ step) * 2
+            own[step][span] = held[pl.ds(pl.multiple_of((block + s) * half, 16), half)]
+            cross[step][span] = held[pl.ds(pl.multiple_of((block + 1 - s) * half, 16), half)]
+    copies[4].wait()
+
+
+def attend(slabs, outs, bias, half, head_width, base=0):
+    count, rows = len(slabs), slabs[0].shape[1]
+    numbers = []
+    for slab in slabs:
+        digits = slab[3 * half : 3 * half + ID_ROWS].astype(jnp.float32)
+        numbers.append(digits[0:1] * ID_BASE + digits[1:2])
+    query_ids = jnp.concatenate(numbers, axis=1)
+    for index in range(count):
+        column = jnp.broadcast_to(numbers[index], (rows, rows)).T
+        column = jnp.concatenate([column] * count, axis=1)
+        bias[index * rows : (index + 1) * rows] = jnp.where(column == query_ids, 0.0, -1e30)
+    factor = math.log2(math.e) / math.sqrt(head_width)
+    span = 2 * rows
+
+    def part(which, head):
+        begin = which * half + head * head_width
+        return jnp.concatenate([slab[begin : begin + head_width] for slab in slabs], axis=1)
+
+    for head in range(half // head_width):
+        query, key, value = part(0, head), part(1, head), part(2, head)
+        for first in range(0, count * rows, span):
+            scores = lax.dot_general(
+                key,
+                query[:, first : first + span],
+                (((0,), (0,)), ((), ())),
+                preferred_element_type=jnp.float32,
+            )
+            scores = scores + bias[:, first : first + span]
+            highest = jnp.max(scores, axis=0, keepdims=True)
+            weights = jnp.exp2((scores - highest) * factor)
+            total = jnp.sum(weights, axis=0, keepdims=True)
+            mixed = jnp.dot(
+                value, weights.astype(jnp.bfloat16), preferred_element_type=jnp.float32
+            )
+            mixed = (mixed / total).astype(jnp.bfloat16)
+            for index in range(first // rows, (first + span) // rows):
+                at = index * rows - first
+                outs[index][head * head_width : (head + 1) * head_width, base : base + rows] = mixed[
+                    :, at : at + rows
+                ]
+
+
+def attend_own_kernel(count, half, head_width, *refs):
+    slabs, beside, outs = refs[:count], refs[count], refs[-3 - count : -3]
+    late, bias, sem = refs[-3:]
+    copy = pltpu.make_async_copy(beside, late, sem)
+    copy.start()
+    attend(slabs, outs, bias, half, head_width)
+    copy.wait()
+
+
+def attend_cross_kernel(count, half, head_width, *refs):
+    slabs, own, sources = refs[:count], refs[count : 2 * count], refs[2 * count : 3 * count - 1]
+    outs, (stacked, bias, sems) = refs[3 * count - 1 : -3], refs[-3:]
+    copies = [
+        pltpu.make_async_copy(source, stacked.at[index], sems.at[index])
+        for index, source in enumerate(sources)
+    ]
+    for copy in copies:
+        copy.start()
+    rows = slabs[0].shape[1]
+    for mine, out in zip(own, outs):
+        out[:, :rows] = mine[...]
+    attend(slabs, outs, bias, half, head_width, rows)
+    for copy in copies:
+        copy.wait()
+
+
+def order_kernel(count, *refs):
+    pieces, outs, (given, held) = refs[:count], refs[count + 2 : 2 * count + 2], refs[-2:]
+    d, e = lax.axis_index("dp"), lax.axis_index("enc")
+    rows = given.shape[2]
+    for step, piece in enumerate(pieces):
+        held[step] = piece[...]
+        given[step] = piece[:, rows:]
+    for step, out in enumerate(outs):
+        out[...] = held[d ^ e ^ step]
+
+
+def project_kernel(count, *refs):
+    pieces, (given, residual, weight, out, attended) = refs[:count], refs[count:]
+    e, s = lax.axis_index("enc"), lax.axis_index("seq")
+    half, rows = given.shape[1:]
+    for step, piece in enumerate(pieces):
+        for which, source in ((s, piece[:, :rows]), (1 - s, given[step])):
+            begin = pl.multiple_of((2 * (e ^ step) + which) * half, 16)
+            attended[pl.ds(begin, half)] = source
+    projected = lax.dot_general(
+        attended[...], weight[...], (((0,), (0,)), ((), ())), preferred_element_type=jnp.float32
+    )
+    out[...] = (residual[...].astype(jnp.float32) + projected).astype(jnp.bfloat16)
+
+
+def gradient_kernel(count, *refs):
+    pieces, (same, last, others, last_other) = refs[:count], refs[count : count + 4]
+    own, *outs = refs[count + 4 :]
+    e = lax.axis_index("enc")
+    rows = []
+    for step in range(count - 1):
+        rows += [same[step], others[step]]
+    rows += [last[...], last_other[...]]
+    total = jnp.dot(
+        jnp.concatenate([piece[...] for piece in pieces], axis=1),
+        jnp.concatenate(rows, axis=0),
+        preferred_element_type=jnp.float32,
+    )
+    width, short = total.shape[1] // count, total.shape[0] // 2
+    for target in range(count):
+        block = total[:, target * width : (target + 1) * width]
+        folded = jnp.concatenate([block[:short], block[short:]], axis=1).astype(jnp.bfloat16)
+
+        @pl.when(e == target)
+        def _():
+            own[...] = block
+
+        for index, out in enumerate(outs):
+
+            @pl.when(e ^ target == index + 1)
+            def _():
+                out[...] = folded
+
+
+def add_kernel(own, *refs):
+    out, width = refs[-1], own.shape[1]
+    total = refs[0][...].astype(jnp.float32)
+    for ref in refs[1:-1]:
+        total = total + ref[...].astype(jnp.float32)
+    short = total.shape[0]
+    out[:short] = own[:short] + total[:, :width]
+    out[short:] = own[short:] + total[:, width:]
+
+
+def exchange_body(
+    sizes, queries, key_vectors, value_vectors, residual, out_weight, cotangent, send_row, image_id
+):
+    n_dp, n_enc, n_seq = sizes
+    rows, width = queries.shape
+    block = width // n_enc
+    half = block // n_seq
+    head_width = width // HEADS
+    group = n_enc * rows
+    tall = 3 * half + ID_ROWS
+    bf16 = functools.partial(jax.ShapeDtypeStruct, dtype=jnp.bfloat16)
+    hbm = pltpu.HBM
+
+    hops = range(n_enc - 1, 0, -1)
+
+    def move(data, partner):
+        pairs = []
+        for d in range(n_dp):
+            for e in range(n_enc):
+                for s in range(n_seq):
+                    to_d, to_e, to_s = partner(d, e, s)
+                    pairs.append(
+                        ((d * n_enc + e) * n_seq + s, (to_d * n_enc + to_e) * n_seq + to_s)
+                    )
+        return lax.ppermute(data, AXES, pairs)
+
+    def along_enc(pieces, flip=0):
+        moved = {k: move(pieces[k], lambda d, e, s: (d, e ^ k, s ^ flip)) for k in hops}
+        if 0 in pieces:
+            moved[0] = move(pieces[0], lambda d, e, s: (d, e, s ^ flip)) if flip else pieces[0]
+        return [moved[k] for k in sorted(moved)]
+
+    def along_seq(data):
+        return move(data, lambda d, e, s: (d, e, s ^ 1))
+
+    with jax.named_scope("pack"):
+        outs = call(
+            functools.partial(pack_kernel, n_enc, half),
+            [bf16((tall, rows))] * (2 * n_enc) + [bf16((rows, width))],
+            image_id.reshape(1, rows),
+            queries,
+            key_vectors,
+            value_vectors,
+            cotangent,
+            spaces=[hbm] * 5,
+            scratch=[
+                pltpu.VMEM((width, rows), jnp.bfloat16),
+                pltpu.VMEM((3, rows, width), jnp.bfloat16),
+                pltpu.VMEM((1, rows), jnp.int32),
+                pltpu.SemaphoreType.DMA((5,)),
+            ],
+            bytes_accessed=8 * rows * width * 2,
+        )
+        own, cross = dict(enumerate(outs[:n_enc])), dict(enumerate(outs[n_enc:-1]))
+        cotangent = outs[-1]
+    with jax.named_scope("exchange_own"):
+        own = along_enc(own)
+    with jax.named_scope("exchange_cross"):
+        cross = along_enc(cross, 1)
+    with jax.named_scope("gather_cotangent"):
+        beside = move(cotangent, lambda d, e, s: (d ^ 1, e, s))
+        above = move(cotangent, lambda d, e, s: (d ^ 2, e, s))
+    cost = dict(flops=4 * group * group * half, bytes_accessed=4 * group * half * 2)
+    bias = pltpu.VMEM((group, group), jnp.float32)
+    with jax.named_scope("attend_own"):
+        *own, late = call(
+            functools.partial(attend_own_kernel, n_enc, half, head_width),
+            [bf16((half, rows))] * n_enc + [bf16((rows, width))],
+            *own,
+            beside,
+            *cross,
+            spaces=[pltpu.VMEM] * (n_enc + 1) + [pl.ANY] * n_enc,
+            scratch=[bias, pltpu.SemaphoreType.DMA],
+            **cost,
+        )
+    with jax.named_scope("gather_cotangent"):
+        last = move(late, lambda d, e, s: (d ^ 2, e, s))
+    with jax.named_scope("attend_cross"):
+        *pieces, stacked = call(
+            functools.partial(attend_cross_kernel, n_enc, half, head_width),
+            [bf16((half, 2 * rows))] * n_enc + [bf16((n_dp - 1, rows, width))],
+            *cross,
+            *own,
+            cotangent,
+            beside,
+            above,
+            scratch=[bias, pltpu.SemaphoreType.DMA((n_dp - 1,))],
+            **cost,
+        )
+    with jax.named_scope("return_heads"):
+        pieces = along_enc(dict(enumerate(pieces)))
+    with jax.named_scope("exchange_features"):
+        *features, stacked, last, given = call(
+            functools.partial(order_kernel, n_enc),
+            [bf16((half, 2 * rows))] * n_dp
+            + [bf16((n_dp - 1, rows, width)), bf16((rows, width)), bf16((n_enc, half, rows))],
+            *pieces,
+            stacked,
+            last,
+            spaces=[pltpu.VMEM] * n_enc + [pl.ANY] * 2,
+            out_spaces=[pltpu.VMEM] * n_dp + [pl.ANY] * 2 + [pltpu.VMEM],
+            aliases={n_enc: n_dp, n_enc + 1: n_dp + 1},
+            scratch=[pltpu.VMEM((n_enc, half, 2 * rows), jnp.bfloat16)],
+        )
+        features = [features[0]] + [
+            move(features[k], lambda d, e, s, k=k: (d ^ k, e, s)) for k in range(1, n_dp)
+        ]
+    with jax.named_scope("gradient"):
+        mine, *partial = call(
+            functools.partial(gradient_kernel, n_enc),
+            [jax.ShapeDtypeStruct((half, block), jnp.float32)]
+            + [bf16((half // 2, 2 * block))] * (n_enc - 1),
+            *features,
+            stacked,
+            last,
+            along_seq(stacked),
+            along_seq(last),
+            flops=2 * half * width * rows * n_dp * n_seq,
+            bytes_accessed=2 * n_dp * n_seq * rows * width,
+        )
+    with jax.named_scope("sum_gradient"):
+        partial = along_enc({k + 1: part for k, part in enumerate(partial)})
+    with jax.named_scope("project"):
+        layer_out = call(
+            functools.partial(project_kernel, n_enc),
+            bf16((rows, width)),
+            *pieces,
+            along_seq(given),
+            residual,
+            out_weight,
+            scratch=[pltpu.VMEM((width, rows), jnp.bfloat16)],
+            flops=2 * rows * width * width,
+            bytes_accessed=2 * width * width,
+        )
+    with jax.named_scope("add_gradient"):
+        grad_weight = call(
+            add_kernel,
+            jax.ShapeDtypeStruct((half, block), jnp.float32),
+            mine,
+            *partial,
+            bytes_accessed=4 * half * block * 4,
+        )
+    return (layer_out, grad_weight)
 
 
 def attend_groups(query_group, key_group, value_group, image_ids):
@@ -31,7 +380,9 @@
     return mixed.reshape(items, slot_count, group_width).astype(jnp.bfloat16)
 
 
-def body(queries, key_vectors, value_vectors, residual, out_weight, cotangent, send_row, image_id):
+def routed_body(
+    queries, key_vectors, value_vectors, residual, out_weight, cotangent, send_row, image_id
+):
     row_count, full_width = queries.shape
     half_width = full_width // 2
     is_live = send_row < row_count
@@ -74,6 +425,10 @@
 
 
 def solution(mesh):
+    sizes = tuple(mesh.shape[name] for name in AXES)
+    n_dp, n_enc, n_seq = sizes
+    fits = n_seq == 2 and n_dp == n_enc == 4 and HEADS % (2 * n_enc) == 0
+    body = functools.partial(exchange_body, sizes) if fits else routed_body
     placed = (
         P(("dp", "enc", "seq"), None),
         P(("dp", "enc", "seq"), None),

time: 272 us -> 69.6 us (0.26)
  local copies, waits for them, and re-layouts: 70.7 us -> 0.01 us
  blocking collectives: 63.5 us -> 0 us
  waiting for transfers between devices: 89.2 us -> 27.9 us
  starting transfers between devices: 10.6 us -> 32.1 us
  matrix products: 14.6 us -> 0 us
  between operations: 13.8 us -> 0.72 us
  Pallas kernels: 0 us -> 8.7 us
  other arithmetic: 6.67 us -> 0 us
    all_to_all x3 -> x0, blocking collectives: 63.5 us -> none  [the longest x1 21.9 us: body(): lax.all_to_all(send_query, 'enc', split_axis=1, concat_axis=1, tiled=True)]
    reduce_scatter x2 -> x0, waiting for transfers between devices: 54.8 us -> none  [the longest x1 44.3 us: body(): lax.psum_scatter(lax.dot_general(attended, cotangent, (((0,), (0,)), ((),...]
    ppermute x0 -> x22, starting transfers between devices: none -> 32.1 us  [move(): return lax.ppermute(data, AXES, pairs)]
    scatter x1 -> x0, local copies, waits for them, and re-layouts: 31.9 us -> none  [body(): jnp.zeros((2, row_count + 1, half_width), jnp.bfloat16).at[:, send_row]]
    unnamed x4 -> x0, waiting for transfers between devices: 30.2 us -> none
    ppermute x0 -> x22, waiting for transfers between devices: none -> 27.9 us  [move(): return lax.ppermute(data, AXES, pairs)]
    gather x4 -> x0, local copies, waits for them, and re-layouts: 13.4 us -> none  [the longest x3 11.4 us: arrange(): grouped[:, source_row]]
    all_to_all x2 -> x0, starting transfers between devices: 10.5 us -> none  [the longest x1 6.32 us: body(): lax.all_to_all(send_image, 'enc', split_axis=1, concat_axis=1, tiled=True)]
  transfers between devices with their start and end apart: 5 -> 22, of which waited for: 4 -> 9; matrix products, arithmetic and copies ran while one was open for 13% -> 0% of each run, Pallas kernels for 0% -> 9%
where the time goes in v1:
time: 69.6 us; the launch traced here: 69.4 us
  starting transfers between devices  32.1 us (46%)
  waiting for transfers between devices  27.9 us (40%)
  Pallas kernels  8.7 us (12%)
  between operations  0.72 us (1%)
    ppermute x22, starting transfers between devices, move(): return lax.ppermute(data, AXES, pairs)  32.1 us
    ppermute x22, waiting for transfers between devices, move(): return lax.ppermute(data, AXES, pairs)  27.9 us
    pallas_call x7, Pallas kernels, call(): pl.pallas_call(kernel, out_shape=out_shape, in_specs=[placed(space) for s...  8.7 us
  transfers between devices with their start and end apart: 22, of which 9 were waited for; matrix products, arithmetic and copies ran while one was open for 0% of the time, Pallas kernels for 9%

profile of v1, /device:TPU:0, one launch (start us, length us, event | category | flops | bytes accessed | tf_op | source)
XLA Modules:
  0.0 69.4 jit_solution(6656260672438552618)
XLA Ops:
  0.6 1.5 %pack.1 = (bf16[496,128]{1,0:T(8,128)(2,1)S(1)}, bf16[496,128]{1,0:T(8,128)(2,1)S(1)}, bf16[496,128]{1,0:T(8,128)(2,1)S(1)}, bf16[496,128]{1,0:T(8,128)(2,1)S(1)...) custom-call(s32[1,128]{1,0:T(1,128)} %bitcast.1, ...), custom_call_target="tpu_custom_call" | custom-call | bytes 2621440 | tf_op jit(solution)/shard_map/pack/pallas_call | solution.py:38
  2.2 3.0 %collective-permute-start.7 = (bf16[128,1280]{1,0:T(8,128)(2,1)S(1)}, bf16[128,1280]{1,0:T(8,128)(2,1)S(1)}, u32[]{:S(2)}, u32[]{:S(2)}) collective-permute-start(bf16[128,1280]{1,0:T(8,128)(2,1)S(1)} %get-tuple-element.40.refs_8_), channel_id=1, source_target_pairs={{0,8},{1,9},{2,10},{3,11},{4,12},{5,13},{6,14},{7,15},{8,0},{9,1},... | collective-permute-start | bytes 983048 | tf_op jit(solution)/shard_map/gather_cotangent/ppermute | solution.py:239
  5.2 1.7 %collective-permute-start.1 = (bf16[496,128]{1,0:T(8,128)(2,1)S(1)}, bf16[496,128]{1,0:T(8,128)(2,1)S(1)}, u32[]{:S(2)}, u32[]{:S(2)}) collective-permute-start(bf16[496,128]{1,0:T(8,128)(2,1)S(1)} %get-tuple-element.33), channel_id=1, source_target_pairs={{0,3},{1,2},{2,1},{3,0},{4,7},{5,6},{6,5},{7,4},{8,11},{9,10},{10,... | collective-permute-start | bytes 380936 | tf_op jit(solution)/shard_map/exchange_cross/ppermute | solution.py:239
  6.9 2.2 %collective-permute-start.2 = (bf16[496,128]{1,0:T(8,128)(2,1)S(1)}, bf16[496,128]{1,0:T(8,128)(2,1)S(1)}, u32[]{:S(2)}, u32[]{:S(2)}) collective-permute-start(bf16[496,128]{1,0:T(8,128)(2,1)S(1)} %get-tuple-element.34), channel_id=1, source_target_pairs={{0,5},{1,4},{2,7},{3,6},{4,1},{5,0},{6,3},{7,2},{8,13},{9,12},{10,... | collective-permute-start | bytes 380936 | tf_op jit(solution)/shard_map/exchange_cross/ppermute | solution.py:239
  9.4 0.7 collective-permute-start.4
  10.2 3.4 %collective-permute-start.5 = (bf16[496,128]{1,0:T(8,128)(2,1)S(1)}, bf16[496,128]{1,0:T(8,128)(2,1)S(1)}, u32[]{:S(2)}, u32[]{:S(2)}) collective-permute-start(bf16[496,128]{1,0:T(8,128)(2,1)S(1)} %get-tuple-element.38), channel_id=1, source_target_pairs={{0,4},{1,5},{2,6},{3,7},{4,0},{5,1},{6,2},{7,3},{8,12},{9,13},{10,... | collective-permute-start | bytes 380936 | tf_op jit(solution)/shard_map/exchange_own/ppermute | solution.py:239
  13.7 4.8 %collective-permute-done.2.refs_7_.refs_2_ = bf16[496,128]{1,0:T(8,128)(2,1)S(1)} collective-permute-done((bf16[496,128]{1,0:T(8,128)(2,1)S(1)}, bf16[496,128]{1,0:T(8,128)(2,1)S(1)}, u32[]{:S(2)}, u32[]{:S(2)}) %collective-permute-start.2) | collective-permute-done | bytes 127008 | tf_op jit(solution)/shard_map/exchange_cross/ppermute | solution.py:239
  18.5 2.9 %collective-permute-start.6 = (bf16[496,128]{1,0:T(8,128)(2,1)S(1)}, bf16[496,128]{1,0:T(8,128)(2,1)S(1)}, u32[]{:S(2)}, u32[]{:S(2)}) collective-permute-start(bf16[496,128]{1,0:T(8,128)(2,1)S(1)} %get-tuple-element.39), channel_id=1, source_target_pairs={{0,6},{1,7},{2,4},{3,5},{4,2},{5,3},{6,0},{7,1},{8,14},{9,15},{10,... | collective-permute-start | bytes 380936 | tf_op jit(solution)/shard_map/exchange_own/ppermute | solution.py:239
  21.3 1.5 %collective-permute-start.8 = (bf16[128,1280]{1,0:T(8,128)(2,1)S(1)}, bf16[128,1280]{1,0:T(8,128)(2,1)S(1)}, u32[]{:S(2)}, u32[]{:S(2)}) collective-permute-start(bf16[128,1280]{1,0:T(8,128)(2,1)S(1)} %get-tuple-element.40.refs_8_), channel_id=1, source_target_pairs={{0,16},{1,17},{2,18},{3,19},{4,20},{5,21},{6,22},{7,23},{8,24},{9,... | collective-permute-start | bytes 983048 | tf_op jit(solution)/shard_map/gather_cotangent/ppermute | solution.py:239
  22.9 7.2 %collective-permute-done.5.refs_2_ = bf16[496,128]{1,0:T(8,128)(2,1)S(1)} collective-permute-done((bf16[496,128]{1,0:T(8,128)(2,1)S(1)}, bf16[496,128]{1,0:T(8,128)(2,1)S(1)}, u32[]{:S(2)}, u32[]{:S(2)}) %collective-permute-start.5) | collective-permute-done | bytes 127008 | tf_op jit(solution)/shard_map/exchange_own/ppermute | solution.py:239
  30.1 1.9 %attend_own.1 = (bf16[160,128]{1,0:T(8,128)(2,1)S(1)}, bf16[160,128]{1,0:T(8,128)(2,1)S(1)}, bf16[160,128]{1,0:T(8,128)(2,1)S(1)}, bf16[160,128]{1,0:T(8,128)(2,1)S(1)}, bf16[128,1280]{1,0:T(8,128)(2,1)S(1)}) custom-call(bf16[496,128]{1,0:T(8,128)(2,1)S(1)} %get-tuple-element.36.refs_0_, bf16[496,128]{1,0:T(8,128)(2,1)S(1)} %collective-permute-done.4.refs_1_, ...), custom_call_target="tpu_custom_call" | custom-call | flops 167772160 | bytes 655360 | tf_op jit(solution)/shard_map/attend_own/pallas_call | solution.py:38
  32.0 1.6 %collective-permute-start.12 = (bf16[128,1280]{1,0:T(8,128)(2,1)S(1)}, bf16[128,1280]{1,0:T(8,128)(2,1)S(1)}, u32[]{:S(2)}, u32[]{:S(2)}) collective-permute-start(bf16[128,1280]{1,0:T(8,128)(2,1)S(1)} %get-tuple-element.50), channel_id=1, source_target_pairs={{0,16},{1,17},{2,18},{3,19},{4,20},{5,21},{6,22},{7,23},{8,24},{9,... | collective-permute-start | bytes 983048 | tf_op jit(solution)/shard_map/gather_cotangent/ppermute | solution.py:239
  33.6 2.1 %attend_cross.1 = (bf16[160,256]{1,0:T(8,128)(2,1)S(1)}, bf16[160,256]{1,0:T(8,128)(2,1)S(1)}, bf16[160,256]{1,0:T(8,128)(2,1)S(1)}, bf16[160,256]{1,0:T(8,128)(2,1)S(1)}, bf16[3,128,1280]{2,1,0:T(8,128)(2,1)S(1)}) custom-call(bf16[496,128]{1,0:T(8,128)(2,1)S(1)} %collective-permute-done.refs_5_.refs_0_, ...), custom_call_target="tpu_custom_call" | custom-call | flops 167772160 | bytes 655360 | tf_op jit(solution)/shard_map/attend_cross/pallas_call | solution.py:38
  35.7 3.9 %collective-permute-start.9 = (bf16[160,256]{1,0:T(8,128)(2,1)S(1)}, bf16[160,256]{1,0:T(8,128)(2,1)S(1)}, u32[]{:S(2)}, u32[]{:S(2)}) collective-permute-start(bf16[160,256]{1,0:T(8,128)(2,1)S(1)} %get-tuple-element.46), channel_id=1, source_target_pairs={{0,2},{1,3},{2,0},{3,1},{4,6},{5,7},{6,4},{7,5},{8,10},{9,11},{10,... | collective-permute-start | bytes 245768 | tf_op jit(solution)/shard_map/return_heads/ppermute | solution.py:239
  39.6 1.0 %collective-permute-start.10 = (bf16[160,256]{1,0:T(8,128)(2,1)S(1)}, bf16[160,256]{1,0:T(8,128)(2,1)S(1)}, u32[]{:S(2)}, u32[]{:S(2)}) collective-permute-start(bf16[160,256]{1,0:T(8,128)(2,1)S(1)} %get-tuple-element.47), channel_id=1, source_target_pairs={{0,4},{1,5},{2,6},{3,7},{4,0},{5,1},{6,2},{7,3},{8,12},{9,13},{10,... | collective-permute-start | bytes 245768 | tf_op jit(solution)/shard_map/return_heads/ppermute | solution.py:239
  40.6 1.4 %collective-permute-start.11 = (bf16[160,256]{1,0:T(8,128)(2,1)S(1)}, bf16[160,256]{1,0:T(8,128)(2,1)S(1)}, u32[]{:S(2)}, u32[]{:S(2)}) collective-permute-start(bf16[160,256]{1,0:T(8,128)(2,1)S(1)} %get-tuple-element.48), channel_id=1, source_target_pairs={{0,6},{1,7},{2,4},{3,5},{4,2},{5,3},{6,0},{7,1},{8,14},{9,15},{10,... | collective-permute-start | bytes 245768 | tf_op jit(solution)/shard_map/return_heads/ppermute | solution.py:239
  42.0 0.4 collective-permute-done.9.refs_1_
  42.4 6.1 %collective-permute-done.10.refs_2_ = bf16[160,256]{1,0:T(8,128)(2,1)S(1)} collective-permute-done((bf16[160,256]{1,0:T(8,128)(2,1)S(1)}, bf16[160,256]{1,0:T(8,128)(2,1)S(1)}, u32[]{:S(2)}, u32[]{:S(2)}) %collective-permute-start.10) | collective-permute-done | bytes 81952 | tf_op jit(solution)/shard_map/return_heads/ppermute | solution.py:239
  48.6 0.5 collective-permute-start.18
  49.1 0.5 collective-permute-start.14
  49.6 1.6 %collective-permute-start.15 = (bf16[160,256]{1,0:T(8,128)(2,1)S(1)}, bf16[160,256]{1,0:T(8,128)(2,1)S(1)}, u32[]{:S(2)}, u32[]{:S(2)}) collective-permute-start(bf16[160,256]{1,0:T(8,128)(2,1)S(1)} %get-tuple-element.54), channel_id=1, source_target_pairs={{0,16},{1,17},{2,18},{3,19},{4,20},{5,21},{6,22},{7,23},{8,24},{9,... | collective-permute-start | bytes 245768 | tf_op jit(solution)/shard_map/exchange_features/ppermute | solution.py:239
  51.1 1.4 %collective-permute-start.16 = (bf16[160,256]{1,0:T(8,128)(2,1)S(1)}, bf16[160,256]{1,0:T(8,128)(2,1)S(1)}, u32[]{:S(2)}, u32[]{:S(2)}) collective-permute-start(bf16[160,256]{1,0:T(8,128)(2,1)S(1)} %get-tuple-element.55), channel_id=1, source_target_pairs={{0,24},{1,25},{2,26},{3,27},{4,28},{5,29},{6,30},{7,31},{8,16},{9,... | collective-permute-start | bytes 245768 | tf_op jit(solution)/shard_map/exchange_features/ppermute | solution.py:239
  52.6 1.4 %collective-permute-done.14.refs_1_ = bf16[160,256]{1,0:T(8,128)(2,1)S(1)} collective-permute-done((bf16[160,256]{1,0:T(8,128)(2,1)S(1)}, bf16[160,256]{1,0:T(8,128)(2,1)S(1)}, u32[]{:S(2)}, u32[]{:S(2)}) %collective-permute-start.14) | collective-permute-done | bytes 81952 | tf_op jit(solution)/shard_map/exchange_features/ppermute | solution.py:239
  54.0 0.8 %collective-permute-done.15.refs_2_ = bf16[160,256]{1,0:T(8,128)(2,1)S(1)} collective-permute-done((bf16[160,256]{1,0:T(8,128)(2,1)S(1)}, bf16[160,256]{1,0:T(8,128)(2,1)S(1)}, u32[]{:S(2)}, u32[]{:S(2)}) %collective-permute-start.15) | collective-permute-done | bytes 81952 | tf_op jit(solution)/shard_map/exchange_features/ppermute | solution.py:239
  54.8 1.7 %collective-permute-done.16.refs_3_ = bf16[160,256]{1,0:T(8,128)(2,1)S(1)} collective-permute-done((bf16[160,256]{1,0:T(8,128)(2,1)S(1)}, bf16[160,256]{1,0:T(8,128)(2,1)S(1)}, u32[]{:S(2)}, u32[]{:S(2)}) %collective-permute-start.16) | collective-permute-done | bytes 81952 | tf_op jit(solution)/shard_map/exchange_features/ppermute | solution.py:239
  56.5 0.9 %gradient.1 = (f32[160,320]{1,0:T(8,128)S(1)}, bf16[80,640]{1,0:T(8,128)(2,1)S(1)}, bf16[80,640]{1,0:T(8,128)(2,1)S(1)}, bf16[80,640]{1,0:T(8,128)(2,1)S(1)}) custom-call(bf16[160,256]{1,0:T(8,128)(2,1)S(1)} %get-tuple-element.52.refs_0_, bf16[160,256]{1,0:T(8,128)(2,1)S(1)} %collective-permute-done.14.refs_1_, ...), custom_call_target="tpu_custom_call" | custom-call | flops 419430400 | bytes 2621440 | tf_op jit(solution)/shard_map/gradient/pallas_call | solution.py:38
  57.4 1.6 %collective-permute-start.19 = (bf16[80,640]{1,0:T(8,128)(2,1)S(1)}, bf16[80,640]{1,0:T(8,128)(2,1)S(1)}, u32[]{:S(2)}, u32[]{:S(2)}) collective-permute-start(bf16[80,640]{1,0:T(8,128)(2,1)S(1)} %get-tuple-element.59), channel_id=1, source_target_pairs={{0,2},{1,3},{2,0},{3,1},{4,6},{5,7},{6,4},{7,5},{8,10},{9,11},{10,... | collective-permute-start | bytes 307208 | tf_op jit(solution)/shard_map/sum_gradient/ppermute | solution.py:239
  59.0 1.2 %collective-permute-start.20 = (bf16[80,640]{1,0:T(8,128)(2,1)S(1)}, bf16[80,640]{1,0:T(8,128)(2,1)S(1)}, u32[]{:S(2)}, u32[]{:S(2)}) collective-permute-start(bf16[80,640]{1,0:T(8,128)(2,1)S(1)} %get-tuple-element.60), channel_id=1, source_target_pairs={{0,4},{1,5},{2,6},{3,7},{4,0},{5,1},{6,2},{7,3},{8,12},{9,13},{10,... | collective-permute-start | bytes 307208 | tf_op jit(solution)/shard_map/sum_gradient/ppermute | solution.py:239
  60.2 1.7 %collective-permute-start.21 = (bf16[80,640]{1,0:T(8,128)(2,1)S(1)}, bf16[80,640]{1,0:T(8,128)(2,1)S(1)}, u32[]{:S(2)}, u32[]{:S(2)}) collective-permute-start(bf16[80,640]{1,0:T(8,128)(2,1)S(1)} %get-tuple-element.61), channel_id=1, source_target_pairs={{0,6},{1,7},{2,4},{3,5},{4,2},{5,3},{6,0},{7,1},{8,14},{9,15},{10,... | collective-permute-start | bytes 307208 | tf_op jit(solution)/shard_map/sum_gradient/ppermute | solution.py:239
  61.9 1.4 %project.1 = bf16[128,1280]{1,0:T(8,128)(2,1)} custom-call(bf16[160,256]{1,0:T(8,128)(2,1)S(1)} %get-tuple-element.45.refs_0_, bf16[160,256]{1,0:T(8,128)(2,1)S(1)} %collective-permute-done.9.refs_1_, bf16[160,256]{1,0:T(8,128)(2,1)S(1)} %collective-permute-done.10.refs_2_, bf16[160,256]{1,0:T(8,128)(2,1)S(1)} %collective-permute-done.11.refs_3_, ...), custom_call_target="tpu_custom_call" | custom-call | flops 419430400 | bytes 3276800 | tf_op jit(solution)/shard_map/project/pallas_call | solution.py:38
  63.3 5.3 %collective-permute-done.20.refs_1_ = bf16[80,640]{1,0:T(8,128)(2,1)S(1)} collective-permute-done((bf16[80,640]{1,0:T(8,128)(2,1)S(1)}, bf16[80,640]{1,0:T(8,128)(2,1)S(1)}, u32[]{:S(2)}, u32[]{:S(2)}) %collective-permute-start.20) | collective-permute-done | bytes 102432 | tf_op jit(solution)/shard_map/sum_gradient/ppermute | solution.py:239
  68.6 0.8 %add_gradient.1 = f32[160,320]{1,0:T(8,128)} custom-call(f32[160,320]{1,0:T(8,128)S(1)} %get-tuple-element.58.own, bf16[80,640]{1,0:T(8,128)(2,1)S(1)} %collective-permute-done.19.refs_0_, bf16[80,640]{1,0:T(8,128)(2,1)S(1)} %collective-permute-done.20.refs_1_, bf16[80,640]{1,0:T(8,128)(2,1)S(1)} %collective-permute-done.21.refs_2_), custom_call_target="tpu_custom_call" | custom-call | bytes 819200 | tf_op jit(solution)/shard_map/add_gradient/pallas_call | solution.py:38
  (23 shorter events, 0.7 us)
Async XLA Ops:
  2.2 28.0 %collective-permute-start.7 = (bf16[128,1280]{1,0:T(8,128)(2,1)S(1)}, bf16[128,1280]{1,0:T(8,128)(2,1)S(1)}, u32[]{:S(2)}, u32[]{:S(2)}) collective-permute-start(bf16[128,1280]{1,0:T(8,128)(2,1)S(1)} %get-tuple-element.40.refs_8_), channel_id=1, source_target_pairs={{0,8},{1,9},{2,10},{3,11},{4,12},{5,13},{6,14},{7,15},{8,0},{9,1},... | collective-permute-start | bytes 983048 | tf_op jit(solution)/shard_map/gather_cotangent/ppermute | solution.py:239
  5.2 4.2 %collective-permute-start = (bf16[496,128]{1,0:T(8,128)(2,1)S(1)}, bf16[496,128]{1,0:T(8,128)(2,1)S(1)}, u32[]{:S(2)}, u32[]{:S(2)}) collective-permute-start(bf16[496,128]{1,0:T(8,128)(2,1)S(1)} %get-tuple-element.32), channel_id=1, source_target_pairs={{0,1},{1,0},{2,3},{3,2},{4,5},{5,4},{6,7},{7,6},{8,9},{9,8},{10,11... | collective-permute-start | bytes 380936 | tf_op jit(solution)/shard_map/exchange_cross/ppermute | solution.py:239
  5.2 5.1 %collective-permute-start.1 = (bf16[496,128]{1,0:T(8,128)(2,1)S(1)}, bf16[496,128]{1,0:T(8,128)(2,1)S(1)}, u32[]{:S(2)}, u32[]{:S(2)}) collective-permute-start(bf16[496,128]{1,0:T(8,128)(2,1)S(1)} %get-tuple-element.33), channel_id=1, source_target_pairs={{0,3},{1,2},{2,1},{3,0},{4,7},{5,6},{6,5},{7,4},{8,11},{9,10},{10,... | collective-permute-start | bytes 380936 | tf_op jit(solution)/shard_map/exchange_cross/ppermute | solution.py:239
  6.9 11.6 %collective-permute-start.2 = (bf16[496,128]{1,0:T(8,128)(2,1)S(1)}, bf16[496,128]{1,0:T(8,128)(2,1)S(1)}, u32[]{:S(2)}, u32[]{:S(2)}) collective-permute-start(bf16[496,128]{1,0:T(8,128)(2,1)S(1)} %get-tuple-element.34), channel_id=1, source_target_pairs={{0,5},{1,4},{2,7},{3,6},{4,1},{5,0},{6,3},{7,2},{8,13},{9,12},{10,... | collective-permute-start | bytes 380936 | tf_op jit(solution)/shard_map/exchange_cross/ppermute | solution.py:239
  9.1 12.3 %collective-permute-start.3 = (bf16[496,128]{1,0:T(8,128)(2,1)S(1)}, bf16[496,128]{1,0:T(8,128)(2,1)S(1)}, u32[]{:S(2)}, u32[]{:S(2)}) collective-permute-start(bf16[496,128]{1,0:T(8,128)(2,1)S(1)} %get-tuple-element.35), channel_id=1, source_target_pairs={{0,7},{1,6},{2,5},{3,4},{4,3},{5,2},{6,1},{7,0},{8,15},{9,14},{10,... | collective-permute-start | bytes 380936 | tf_op jit(solution)/shard_map/exchange_cross/ppermute | solution.py:239
  9.4 13.5 %collective-permute-start.4 = (bf16[496,128]{1,0:T(8,128)(2,1)S(1)}, bf16[496,128]{1,0:T(8,128)(2,1)S(1)}, u32[]{:S(2)}, u32[]{:S(2)}) collective-permute-start(bf16[496,128]{1,0:T(8,128)(2,1)S(1)} %get-tuple-element.37), channel_id=1, source_target_pairs={{0,2},{1,3},{2,0},{3,1},{4,6},{5,7},{6,4},{7,5},{8,10},{9,11},{10,... | collective-permute-start | bytes 380936 | tf_op jit(solution)/shard_map/exchange_own/ppermute | solution.py:239
  10.2 19.9 %collective-permute-start.5 = (bf16[496,128]{1,0:T(8,128)(2,1)S(1)}, bf16[496,128]{1,0:T(8,128)(2,1)S(1)}, u32[]{:S(2)}, u32[]{:S(2)}) collective-permute-start(bf16[496,128]{1,0:T(8,128)(2,1)S(1)} %get-tuple-element.38), channel_id=1, source_target_pairs={{0,4},{1,5},{2,6},{3,7},{4,0},{5,1},{6,2},{7,3},{8,12},{9,13},{10,... | collective-permute-start | bytes 380936 | tf_op jit(solution)/shard_map/exchange_own/ppermute | solution.py:239
  18.5 11.6 %collective-permute-start.6 = (bf16[496,128]{1,0:T(8,128)(2,1)S(1)}, bf16[496,128]{1,0:T(8,128)(2,1)S(1)}, u32[]{:S(2)}, u32[]{:S(2)}) collective-permute-start(bf16[496,128]{1,0:T(8,128)(2,1)S(1)} %get-tuple-element.39), channel_id=1, source_target_pairs={{0,6},{1,7},{2,4},{3,5},{4,2},{5,3},{6,0},{7,1},{8,14},{9,15},{10,... | collective-permute-start | bytes 380936 | tf_op jit(solution)/shard_map/exchange_own/ppermute | solution.py:239
  21.3 12.3 %collective-permute-start.8 = (bf16[128,1280]{1,0:T(8,128)(2,1)S(1)}, bf16[128,1280]{1,0:T(8,128)(2,1)S(1)}, u32[]{:S(2)}, u32[]{:S(2)}) collective-permute-start(bf16[128,1280]{1,0:T(8,128)(2,1)S(1)} %get-tuple-element.40.refs_8_), channel_id=1, source_target_pairs={{0,16},{1,17},{2,18},{3,19},{4,20},{5,21},{6,22},{7,23},{8,24},{9,... | collective-permute-start | bytes 983048 | tf_op jit(solution)/shard_map/gather_cotangent/ppermute | solution.py:239
  32.0 29.9 %copy-start = (bf16[1280,1280]{1,0:T(8,128)(2,1)S(1)}, bf16[1280,1280]{1,0:T(8,128)(2,1)}, u32[]{:S(2)}) copy-start(bf16[1280,1280]{1,0:T(8,128)(2,1)} %refs_6_.1) | copy-start | bytes 9830404
  32.0 29.9 %copy-start.1 = (bf16[128,1280]{1,0:T(8,128)(2,1)S(1)}, bf16[128,1280]{1,0:T(8,128)(2,1)}, u32[]{:S(2)}) copy-start(bf16[128,1280]{1,0:T(8,128)(2,1)} %refs_5_.1) | copy-start | bytes 983044
  32.0 16.4 %collective-permute-start.12 = (bf16[128,1280]{1,0:T(8,128)(2,1)S(1)}, bf16[128,1280]{1,0:T(8,128)(2,1)S(1)}, u32[]{:S(2)}, u32[]{:S(2)}) collective-permute-start(bf16[128,1280]{1,0:T(8,128)(2,1)S(1)} %get-tuple-element.50), channel_id=1, source_target_pairs={{0,16},{1,17},{2,18},{3,19},{4,20},{5,21},{6,22},{7,23},{8,24},{9,... | collective-permute-start | bytes 983048 | tf_op jit(solution)/shard_map/gather_cotangent/ppermute | solution.py:239
  35.7 6.6 %collective-permute-start.9 = (bf16[160,256]{1,0:T(8,128)(2,1)S(1)}, bf16[160,256]{1,0:T(8,128)(2,1)S(1)}, u32[]{:S(2)}, u32[]{:S(2)}) collective-permute-start(bf16[160,256]{1,0:T(8,128)(2,1)S(1)} %get-tuple-element.46), channel_id=1, source_target_pairs={{0,2},{1,3},{2,0},{3,1},{4,6},{5,7},{6,4},{7,5},{8,10},{9,11},{10,... | collective-permute-start | bytes 245768 | tf_op jit(solution)/shard_map/return_heads/ppermute | solution.py:239
  39.6 8.9 %collective-permute-start.10 = (bf16[160,256]{1,0:T(8,128)(2,1)S(1)}, bf16[160,256]{1,0:T(8,128)(2,1)S(1)}, u32[]{:S(2)}, u32[]{:S(2)}) collective-permute-start(bf16[160,256]{1,0:T(8,128)(2,1)S(1)} %get-tuple-element.47), channel_id=1, source_target_pairs={{0,4},{1,5},{2,6},{3,7},{4,0},{5,1},{6,2},{7,3},{8,12},{9,13},{10,... | collective-permute-start | bytes 245768 | tf_op jit(solution)/shard_map/return_heads/ppermute | solution.py:239
  40.6 7.8 %collective-permute-start.11 = (bf16[160,256]{1,0:T(8,128)(2,1)S(1)}, bf16[160,256]{1,0:T(8,128)(2,1)S(1)}, u32[]{:S(2)}, u32[]{:S(2)}) collective-permute-start(bf16[160,256]{1,0:T(8,128)(2,1)S(1)} %get-tuple-element.48), channel_id=1, source_target_pairs={{0,6},{1,7},{2,4},{3,5},{4,2},{5,3},{6,0},{7,1},{8,14},{9,15},{10,... | collective-permute-start | bytes 245768 | tf_op jit(solution)/shard_map/return_heads/ppermute | solution.py:239
  48.5 8.0 %collective-permute-start.17 = (bf16[3,128,1280]{2,1,0:T(8,128)(2,1)S(1)}, bf16[3,128,1280]{2,1,0:T(8,128)(2,1)S(1)}, u32[]{:S(2)}, u32[]{:S(2)}) collective-permute-start(bf16[3,128,1280]{2,1,0:T(8,128)(2,1)S(1)} %get-tuple-element.56.refs_4_), channel_id=1, source_target_pairs={{0,1},{1,0},{2,3},{3,2},{4,5},{5,4},{6,7},{7,6},{8,9},{9,8},{10,11... | collective-permute-start | bytes 2949128 | tf_op jit(solution)/shard_map/gradient/ppermute | solution.py:239
  48.6 7.9 %collective-permute-start.18 = (bf16[128,1280]{1,0:T(8,128)(2,1)S(1)}, bf16[128,1280]{1,0:T(8,128)(2,1)S(1)}, u32[]{:S(2)}, u32[]{:S(2)}) collective-permute-start(bf16[128,1280]{1,0:T(8,128)(2,1)S(1)} %get-tuple-element.57.refs_5_), channel_id=1, source_target_pairs={{0,1},{1,0},{2,3},{3,2},{4,5},{5,4},{6,7},{7,6},{8,9},{9,8},{10,11... | collective-permute-start | bytes 983048 | tf_op jit(solution)/shard_map/gradient/ppermute | solution.py:239
  49.1 4.9 %collective-permute-start.14 = (bf16[160,256]{1,0:T(8,128)(2,1)S(1)}, bf16[160,256]{1,0:T(8,128)(2,1)S(1)}, u32[]{:S(2)}, u32[]{:S(2)}) collective-permute-start(bf16[160,256]{1,0:T(8,128)(2,1)S(1)} %get-tuple-element.53), channel_id=1, source_target_pairs={{0,8},{1,9},{2,10},{3,11},{4,12},{5,13},{6,14},{7,15},{8,0},{9,1},... | collective-permute-start | bytes 245768 | tf_op jit(solution)/shard_map/exchange_features/ppermute | solution.py:239
  49.6 5.2 %collective-permute-start.15 = (bf16[160,256]{1,0:T(8,128)(2,1)S(1)}, bf16[160,256]{1,0:T(8,128)(2,1)S(1)}, u32[]{:S(2)}, u32[]{:S(2)}) collective-permute-start(bf16[160,256]{1,0:T(8,128)(2,1)S(1)} %get-tuple-element.54), channel_id=1, source_target_pairs={{0,16},{1,17},{2,18},{3,19},{4,20},{5,21},{6,22},{7,23},{8,24},{9,... | collective-permute-start | bytes 245768 | tf_op jit(solution)/shard_map/exchange_features/ppermute | solution.py:239
  51.1 5.3 %collective-permute-start.16 = (bf16[160,256]{1,0:T(8,128)(2,1)S(1)}, bf16[160,256]{1,0:T(8,128)(2,1)S(1)}, u32[]{:S(2)}, u32[]{:S(2)}) collective-permute-start(bf16[160,256]{1,0:T(8,128)(2,1)S(1)} %get-tuple-element.55), channel_id=1, source_target_pairs={{0,24},{1,25},{2,26},{3,27},{4,28},{5,29},{6,30},{7,31},{8,16},{9,... | collective-permute-start | bytes 245768 | tf_op jit(solution)/shard_map/exchange_features/ppermute | solution.py:239
  54.0 7.9 %collective-permute-start.13 = (bf16[4,160,128]{2,1,0:T(8,128)(2,1)S(1)}, bf16[4,160,128]{2,1,0:T(8,128)(2,1)S(1)}, u32[]{:S(2)}, u32[]{:S(2)}) collective-permute-start(bf16[4,160,128]{2,1,0:T(8,128)(2,1)S(1)} %get-tuple-element.51), channel_id=1, source_target_pairs={{0,1},{1,0},{2,3},{3,2},{4,5},{5,4},{6,7},{7,6},{8,9},{9,8},{10,11... | collective-permute-start | bytes 491528 | tf_op jit(solution)/shard_map/project/ppermute | solution.py:239
  57.4 5.9 %collective-permute-start.19 = (bf16[80,640]{1,0:T(8,128)(2,1)S(1)}, bf16[80,640]{1,0:T(8,128)(2,1)S(1)}, u32[]{:S(2)}, u32[]{:S(2)}) collective-permute-start(bf16[80,640]{1,0:T(8,128)(2,1)S(1)} %get-tuple-element.59), channel_id=1, source_target_pairs={{0,2},{1,3},{2,0},{3,1},{4,6},{5,7},{6,4},{7,5},{8,10},{9,11},{10,... | collective-permute-start | bytes 307208 | tf_op jit(solution)/shard_map/sum_gradient/ppermute | solution.py:239
  59.0 9.6 %collective-permute-start.20 = (bf16[80,640]{1,0:T(8,128)(2,1)S(1)}, bf16[80,640]{1,0:T(8,128)(2,1)S(1)}, u32[]{:S(2)}, u32[]{:S(2)}) collective-permute-start(bf16[80,640]{1,0:T(8,128)(2,1)S(1)} %get-tuple-element.60), channel_id=1, source_target_pairs={{0,4},{1,5},{2,6},{3,7},{4,0},{5,1},{6,2},{7,3},{8,12},{9,13},{10,... | collective-permute-start | bytes 307208 | tf_op jit(solution)/shard_map/sum_gradient/ppermute | solution.py:239
  60.2 8.4 %collective-permute-start.21 = (bf16[80,640]{1,0:T(8,128)(2,1)S(1)}, bf16[80,640]{1,0:T(8,128)(2,1)S(1)}, u32[]{:S(2)}, u32[]{:S(2)}) collective-permute-start(bf16[80,640]{1,0:T(8,128)(2,1)S(1)} %get-tuple-element.61), channel_id=1, source_target_pairs={{0,6},{1,7},{2,4},{3,5},{4,2},{5,3},{6,0},{7,1},{8,14},{9,15},{10,... | collective-permute-start | bytes 307208 | tf_op jit(solution)/shard_map/sum_gradient/ppermute | solution.py:239

commit v2 on v1

v2 whole, which is shorter than its diff:
```python
import functools
import math

import jax
import jax.numpy as jnp
from jax import lax
from jax.experimental import pallas as pl
from jax.experimental.pallas import tpu as pltpu
from jax.sharding import PartitionSpec as P

HEADS = 16
AXES = ("dp", "enc", "seq")
ID_ROWS = 16
ID_BASE = 64
SENDS = (3, 2, 1, 0)
RETURNS = (3, 2, 1, 0)
SUMS = (3, 2, 1, 0)


def call(
    kernel,
    out_shape,
    *args,
    spaces=None,
    scratch=(),
    limit=16,
    flops=0,
    bytes_accessed=0,
):
    def placed(space):
        return pl.BlockSpec(memory_space=space)

    many = isinstance(out_shape, (list, tuple))
    spaces = spaces or [pltpu.VMEM] * len(args)
    args = [
        pltpu.with_memory_space_constraint(arg, pltpu.HBM) if space == pltpu.HBM else arg
        for arg, space in zip(args, spaces)
    ]
    return pl.pallas_call(
        kernel,
        out_shape=out_shape,
        in_specs=[placed(space) for space in spaces],
        out_specs=[placed(pltpu.VMEM)] * len(out_shape) if many else placed(pltpu.VMEM),
        scratch_shapes=list(scratch),
        compiler_params=pltpu.CompilerParams(vmem_limit_bytes=limit * 1024 * 1024),
        cost_estimate=pl.CostEstimate(
            flops=flops, bytes_accessed=bytes_accessed, transcendentals=0
        ),
    )(*args)


def pack_kernel(block, *refs):
    sources, outs, (ready, held, arrived, ids_held, sems) = refs[:5], refs[5:-5], refs[-5:]
    targets = [ids_held] + [arrived.at[which] for which in range(3)] + [ready]
    copies = [
        pltpu.make_async_copy(source, target, sems.at[which])
        for which, (source, target) in enumerate(zip(sources, targets))
    ]
    for copy in copies:
        copy.start()
    first = lax.axis_index("dp") ^ lax.axis_index("enc")
    copies[0].wait()
    ids = ids_held[...]
    row = lax.broadcasted_iota(jnp.int32, (ID_ROWS, ids.shape[1]), 0)
    digits = jnp.where(row == 0, ids // ID_BASE, jnp.where(row == 1, ids % ID_BASE, 0))
    digits = digits.astype(jnp.float32).astype(jnp.bfloat16)
    for out in outs:
        out[3 * block :] = digits
    for which in range(3):
        copies[1 + which].wait()
        held[...] = arrived[which].T
        for hop, out in zip(SENDS, outs):
            begin = pl.multiple_of((first ^ hop) * block, 16)
            out[which * block : (which + 1) * block] = held[pl.ds(begin, block)]
    copies[4].wait()


def attend_kernel(count, block, head_width, *refs):
    slabs, outs, bias = refs[:count], refs[count : 2 * count], refs[2 * count]
    rows = slabs[0].shape[1]
    numbers = []
    for slab in slabs:
        digits = slab[3 * block : 3 * block + ID_ROWS].astype(jnp.float32)
        numbers.append(digits[0:1] * ID_BASE + digits[1:2])
    query_ids = jnp.concatenate(numbers, axis=1)
    for index in range(count):
        column = jnp.broadcast_to(numbers[index], (rows, rows)).T
        column = jnp.concatenate([column] * count, axis=1)
        bias[index * rows : (index + 1) * rows] = jnp.where(column == query_ids, 0.0, -1e30)
    factor = math.log2(math.e) / math.sqrt(head_width)
    span = 2 * rows

    def part(which, head):
        begin = which * block + head * head_width
        return jnp.concatenate([slab[begin : begin + head_width] for slab in slabs], axis=1)

    for head in range(block // head_width):
        query, key, value = part(0, head), part(1, head), part(2, head)
        for first in range(0, count * rows, span):
            scores = lax.dot_general(
                key,
                query[:, first : first + span],
                (((0,), (0,)), ((), ())),
                preferred_element_type=jnp.float32,
            )
            scores = scores + bias[:, first : first + span]
            highest = jnp.max(scores, axis=0, keepdims=True)
            weights = jnp.exp2((scores - highest) * factor)
            total = jnp.sum(weights, axis=0, keepdims=True)
            mixed = jnp.dot(
                value, weights.astype(jnp.bfloat16), preferred_element_type=jnp.float32
            )
            mixed = (mixed / total).astype(jnp.bfloat16)
            for index in range(first // rows, (first + span) // rows):
                at = index * rows - first
                out = outs[RETURNS.index(SENDS[index])]
                out[head * head_width : (head + 1) * head_width] = mixed[:, at : at + rows]


def stack_kernel(count, *refs):
    sources, out, sems = refs[:count], refs[-2], refs[-1]
    copies = [
        pltpu.make_async_copy(source, out.at[index], sems.at[index])
        for index, source in enumerate(sources)
    ]
    for copy in copies:
        copy.start()
    for copy in copies:
        copy.wait()


def halve_kernel(*refs):
    pieces, (kept, given) = refs[:-2], refs[-2:]
    s = lax.axis_index("seq")
    half = kept.shape[1]
    for hop, piece in zip(RETURNS, pieces):
        kept[hop] = piece[pl.ds(pl.multiple_of(s * half, 16), half)]
        given[hop] = piece[pl.ds(pl.multiple_of((1 - s) * half, 16), half)]


def gradient_kernel(count, *refs):
    kept, given, same, others, *outs = refs
    e = lax.axis_index("enc")
    features, rows = [], []
    for step in range(count):
        features += [kept[step], given[step]]
        rows += [same[step], others[step]]
    total = jnp.dot(
        jnp.concatenate(features, axis=1),
        jnp.concatenate(rows, axis=0),
        preferred_element_type=jnp.float32,
    )
    width, short = total.shape[1] // count, total.shape[0] // 2
    for target in range(count):
        block = total[:, target * width : (target + 1) * width]
        folded = jnp.concatenate([block[:short], block[short:]], axis=1).astype(jnp.bfloat16)

        for index, out in enumerate(outs):

            @pl.when(e ^ target == SUMS[index])
            def _():
                out[...] = folded


def project(pieces, steps, weight, attended):
    first = lax.axis_index("dp") ^ lax.axis_index("enc")
    block = pieces[0].shape[0]
    rows = []
    for index, (step, piece) in enumerate(zip(steps, pieces)):
        attended[index * block : (index + 1) * block] = piece[...]
        rows.append(weight[pl.ds(pl.multiple_of((first ^ step) * block, 16), block)])
    return lax.dot_general(
        attended[...],
        jnp.concatenate(rows, axis=0),
        (((0,), (0,)), ((), ())),
        preferred_element_type=jnp.float32,
    )


def project_kernel(residual, weight, *refs):
    pieces, (out, attended) = refs[:-2], refs[-2:]
    out[...] = residual[...].astype(jnp.float32) + project(
        pieces, range(len(pieces)), weight, attended
    )


def finish_kernel(count, early, *refs):
    partial, pieces = refs[:count], refs[count : 2 * count - early]
    projected, weight, out, grad, attended = refs[2 * count - early :]
    total = partial[0][...].astype(jnp.float32)
    for ref in partial[1:]:
        total = total + ref[...].astype(jnp.float32)
    short, width = total.shape[0], grad.shape[1]
    grad[:short] = total[:, :width]
    grad[short:] = total[:, width:]
    projected = projected[...] + project(pieces, range(early, count), weight, attended)
    out[...] = projected.astype(jnp.bfloat16)


def exchange_body(
    sizes, queries, key_vectors, value_vectors, residual, out_weight, cotangent, send_row, image_id
):
    n_dp, n_enc, n_seq = sizes
    rows, width = queries.shape
    block = width // n_enc
    half = block // n_seq
    head_width = width // HEADS
    group = n_enc * rows
    tall = 3 * block + ID_ROWS
    bf16 = functools.partial(jax.ShapeDtypeStruct, dtype=jnp.bfloat16)
    hbm = pltpu.HBM

    def move(data, partner):
        pairs = []
        for d in range(n_dp):
            for e in range(n_enc):
                for s in range(n_seq):
                    to_d, to_e, to_s = partner(d, e, s)
                    pairs.append(
                        ((d * n_enc + e) * n_seq + s, (to_d * n_enc + to_e) * n_seq + to_s)
                    )
        return lax.ppermute(data, AXES, pairs)

    def along_enc(pieces, hops):
        return [
            move(piece, lambda d, e, s, hop=hop: (d, e ^ hop, s)) if hop else piece
            for hop, piece in zip(hops, pieces)
        ]

    def along_seq(data):
        return move(data, lambda d, e, s: (d, e, s ^ 1))

    with jax.named_scope("pack"):
        outs = call(
            functools.partial(pack_kernel, block),
            [bf16((tall, rows))] * n_enc + [bf16((rows, width))],
            image_id.reshape(1, rows),
            queries,
            key_vectors,
            value_vectors,
            cotangent,
            spaces=[hbm] * 5,
            scratch=[
                pltpu.VMEM((width, rows), jnp.bfloat16),
                pltpu.VMEM((3, rows, width), jnp.bfloat16),
                pltpu.VMEM((1, rows), jnp.int32),
                pltpu.SemaphoreType.DMA((5,)),
            ],
            bytes_accessed=8 * rows * width * 2,
        )
        slabs, cotangent = outs[:-1], outs[-1]
    with jax.named_scope("exchange_heads"):
        slabs = along_enc(slabs, SENDS)
    with jax.named_scope("gather_cotangent"):
        same = [cotangent] + [
            move(cotangent, lambda d, e, s, k=k: (d ^ k, e, s)) for k in range(1, n_dp)
        ]
    with jax.named_scope("attention"):
        pieces = call(
            functools.partial(attend_kernel, n_enc, block, head_width),
            [bf16((block, rows))] * n_enc,
            *slabs,
            scratch=[pltpu.VMEM((group, group), jnp.float32)],
            flops=55 * group * group * block,
            bytes_accessed=8 * group * block,
        )
    with jax.named_scope("send_to_owner"):
        pieces = [
            move(piece, lambda d, e, s, hop=hop: (d ^ hop, e ^ hop, s)) if hop else piece
            for hop, piece in zip(RETURNS, pieces)
        ]
        kept, given = call(
            halve_kernel,
            [bf16((n_dp, half, rows))] * 2,
            *pieces,
            flops=400 * group * group * half,
        )
        given = along_seq(given)
    with jax.named_scope("swap_cotangent"):
        stacked = call(
            functools.partial(stack_kernel, n_dp),
            bf16((n_dp, rows, width)),
            *same,
            spaces=[pltpu.VMEM] * n_dp + [pl.ANY] * 0,
            scratch=[pltpu.SemaphoreType.DMA((n_dp,))],
            bytes_accessed=4 * n_dp * rows * width,
        )
    with jax.named_scope("gradient"):
        partial = call(
            functools.partial(gradient_kernel, n_enc),
            [bf16((half // 2, 2 * block))] * n_enc,
            kept,
            given,
            stacked,
            along_seq(stacked),
            flops=2 * half * width * rows * n_dp * n_seq,
            bytes_accessed=2 * n_dp * n_seq * rows * width,
        )
    with jax.named_scope("sum_gradient"):
        partial = [
            move(part, lambda d, e, s, hop=hop: (d ^ e, e ^ hop, s))
            for hop, part in zip(SUMS, partial)
        ]
    with jax.named_scope("send_home"):
        homes = [pieces[RETURNS.index(k)] for k in range(n_dp)]
        homes[1:] = [
            move(homes[k], lambda d, e, s, k=k: (d ^ k, e, s)) for k in range(1, n_dp)
        ]
    early = 3
    with jax.named_scope("project"):
        projected = call(
            project_kernel,
            jax.ShapeDtypeStruct((rows, width), jnp.float32),
            residual,
            out_weight,
            *homes[:early],
            scratch=[pltpu.VMEM((early * block, rows), jnp.bfloat16)],
            flops=2 * rows * early * block * width,
            bytes_accessed=2 * early * block * width,
        )
    with jax.named_scope("finish"):
        layer_out, grad_weight = call(
            functools.partial(finish_kernel, n_dp, early),
            [bf16((rows, width)), jax.ShapeDtypeStruct((half, block), jnp.float32)],
            *partial,
            *homes[early:],
            projected,
            out_weight,
            scratch=[pltpu.VMEM(((n_dp - early) * block, rows), jnp.bfloat16)],
            flops=2 * rows * (n_dp - early) * block * width,
            bytes_accessed=2 * (n_dp - early) * block * width,
        )
    return (layer_out, grad_weight)


def attend_groups(query_group, key_group, value_group, image_ids):
    items, slot_count, group_width = query_group.shape
    group_heads = HEADS // 2
    head_width = group_width // group_heads
    scale = 1.0 / math.sqrt(head_width)
    position = jnp.arange(slot_count)
    image_ids = jnp.where(image_ids < 0, -1 - position[None, :], image_ids)
    shaped_query = query_group.reshape(items, slot_count, group_heads, head_width)
    shaped_key = key_group.reshape(items, slot_count, group_heads, head_width)
    shaped_value = value_group.reshape(items, slot_count, group_heads, head_width)
    scores = (
        jnp.einsum("gqhd,gkhd->ghqk", shaped_query, shaped_key, preferred_element_type=jnp.float32)
        * scale
    )
    same_image = image_ids[:, None, :, None] == image_ids[:, None, None, :]
    scores = jnp.where(same_image, scores, -1e30)
    highest = jnp.max(scores, axis=-1, keepdims=True)
    weights = jnp.exp(scores - highest)
    probs = (weights / jnp.sum(weights, axis=-1, keepdims=True)).astype(jnp.bfloat16)
    mixed = jnp.einsum("ghqk,gkhd->gqhd", probs, shaped_value, preferred_element_type=jnp.float32)
    return mixed.reshape(items, slot_count, group_width).astype(jnp.bfloat16)


def routed_body(
    queries, key_vectors, value_vectors, residual, out_weight, cotangent, send_row, image_id
):
    row_count, full_width = queries.shape
    half_width = full_width // 2
    is_live = send_row < row_count
    source_row = jnp.minimum(send_row, row_count - 1)

    def arrange(data):
        grouped = data.reshape(row_count, 2, half_width).transpose(1, 0, 2)
        return jnp.where(is_live[None, :, None], grouped[:, source_row], jnp.zeros((), data.dtype))

    send_query = arrange(queries)
    send_key = arrange(key_vectors)
    send_value = arrange(value_vectors)
    send_image = jnp.where(is_live, image_id[source_row], -1)
    send_image = jnp.broadcast_to(send_image[None, :], (2, send_row.shape[0]))
    received = (
        lax.all_to_all(send_query, "enc", split_axis=1, concat_axis=1, tiled=True),
        lax.all_to_all(send_key, "enc", split_axis=1, concat_axis=1, tiled=True),
        lax.all_to_all(send_value, "enc", split_axis=1, concat_axis=1, tiled=True),
        lax.all_to_all(send_image, "enc", split_axis=1, concat_axis=1, tiled=True),
    )
    output = attend_groups(received[0], received[1], received[2], received[3])
    returned = lax.all_to_all(output, "enc", split_axis=1, concat_axis=1, tiled=True)
    holder = jnp.zeros((2, row_count + 1, half_width), jnp.bfloat16).at[:, send_row].set(returned)
    attended = holder[:, :row_count].transpose(1, 0, 2).reshape(row_count, full_width)
    projected = jnp.dot(attended, out_weight, preferred_element_type=jnp.float32)
    layer_out = (residual.astype(jnp.float32) + projected).astype(jnp.bfloat16)
    first_sum = lax.psum_scatter(
        lax.dot_general(
            attended, cotangent, (((0,), (0,)), ((), ())), preferred_element_type=jnp.float32
        ).astype(jnp.bfloat16),
        "dp",
        scatter_dimension=0,
        tiled=True,
    )
    second_sum = lax.psum_scatter(first_sum, "seq", scatter_dimension=0, tiled=True).astype(
        jnp.float32
    )
    grad_weight = lax.psum_scatter(second_sum, "enc", scatter_dimension=1, tiled=True)
    return (layer_out, grad_weight)


def solution(mesh):
    sizes = tuple(mesh.shape[name] for name in AXES)
    n_dp, n_enc, n_seq = sizes
    fits = n_seq == 2 and n_dp == n_enc == 4 and HEADS % (2 * n_enc) == 0
    body = functools.partial(exchange_body, sizes) if fits else routed_body
    placed = (
        P(("dp", "enc", "seq"), None),
        P(("dp", "enc", "seq"), None),
        P(("dp", "enc", "seq"), None),
        P(("dp", "enc", "seq"), None),
        P(),
        P(("dp", "enc", "seq"), None),
        P(("dp", "enc", "seq")),
        P(("dp", "enc", "seq")),
    )
    return jax.shard_map(
        body,
        mesh=mesh,
        in_specs=placed,
        out_specs=(P(("dp", "enc", "seq"), None), P(("dp", "seq"), "enc")),
        check_vma=False,
    )
```

time: 69.6 us -> 60.9 us (0.88)
  starting transfers between devices: 32.1 us -> 27.9 us
  waiting for transfers between devices: 27.9 us -> 24.2 us
  Pallas kernels: 8.7 us -> 7.95 us
    ppermute x22 -> x18, starting transfers between devices: 32.1 us -> 27.9 us  [move(): return lax.ppermute(data, AXES, pairs)]
    ppermute x22 -> x18, waiting for transfers between devices: 27.9 us -> 24.2 us  [move(): return lax.ppermute(data, AXES, pairs)]
    pallas_call x7, Pallas kernels: 8.7 us -> 7.95 us  [call(): pl.pallas_call(kernel, out_shape=out_shape, in_specs=[placed(space) for s...]
  transfers between devices with their start and end apart: 22 -> 18, of which waited for: 9 -> 6; matrix products, arithmetic and copies ran while one was open for 0% -> 0% of each run, Pallas kernels for 9% -> 9%
where the time goes in v2:
time: 60.9 us; the launch traced here: 60.7 us
  starting transfers between devices  27.9 us (46%)
  waiting for transfers between devices  24.2 us (40%)
  Pallas kernels  7.95 us (13%)
  between operations  0.74 us (1%)
    ppermute x18, starting transfers between devices, move(): return lax.ppermute(data, AXES, pairs)  27.9 us
    ppermute x18, waiting for transfers between devices, move(): return lax.ppermute(data, AXES, pairs)  24.2 us
    pallas_call x7, Pallas kernels, call(): pl.pallas_call(kernel, out_shape=out_shape, in_specs=[placed(space) for s...  7.95 us
  transfers between devices with their start and end apart: 18, of which 6 were waited for; matrix products, arithmetic and copies ran while one was open for 0% of the time, Pallas kernels for 9%

profile of v2, /device:TPU:0, one launch (start us, length us, event | category | flops | bytes accessed | tf_op | source)
XLA Modules:
  0.0 60.7 jit_solution(6247446632725590140)
XLA Ops:
  0.6 1.5 %pack.1 = (bf16[976,128]{1,0:T(8,128)(2,1)S(1)}, bf16[976,128]{1,0:T(8,128)(2,1)S(1)}, bf16[976,128]{1,0:T(8,128)(2,1)S(1)}, bf16[976,128]{1,0:T(8,128)(2,1)S(1)}, bf16[128,1280]{1,0:T(8,128)(2,1)S(1)}) custom-call(s32[1,128]{1,0:T(1,128)} %bitcast.1, bf16[128,1280]{1,0:T(8,128)(2,1)} %refs_1_.1, bf16[128,1280]{1,0:T(8,128)(2,1)} %refs_2_.1, ...), custom_call_target="tpu_custom_call" | custom-call | bytes 2621440 | tf_op jit(solution)/shard_map/pack/pallas_call | solution.py:39
  2.2 5.1 %collective-permute-start = (bf16[976,128]{1,0:T(8,128)(2,1)S(1)}, bf16[976,128]{1,0:T(8,128)(2,1)S(1)}, u32[]{:S(2)}, u32[]{:S(2)}) collective-permute-start(bf16[976,128]{1,0:T(8,128)(2,1)S(1)} %get-tuple-element.17), channel_id=1, source_target_pairs={{0,6},{1,7},{2,4},{3,5},{4,2},{5,3},{6,0},{7,1},{8,14},{9,15},{10,... | collective-permute-start | bytes 749576 | tf_op jit(solution)/shard_map/exchange_heads/ppermute | solution.py:222
  7.3 0.0 collective-permute-start.1
  7.3 0.6 %collective-permute-start.2 = (bf16[976,128]{1,0:T(8,128)(2,1)S(1)}, bf16[976,128]{1,0:T(8,128)(2,1)S(1)}, u32[]{:S(2)}, u32[]{:S(2)}) collective-permute-start(bf16[976,128]{1,0:T(8,128)(2,1)S(1)} %get-tuple-element.19), channel_id=1, source_target_pairs={{0,2},{1,3},{2,0},{3,1},{4,6},{5,7},{6,4},{7,5},{8,10},{9,11},{10,... | collective-permute-start | bytes 749576 | tf_op jit(solution)/shard_map/exchange_heads/ppermute | solution.py:222
  7.9 1.6 %collective-permute-start.7 = (bf16[128,1280]{1,0:T(8,128)(2,1)S(1)}, bf16[128,1280]{1,0:T(8,128)(2,1)S(1)}, u32[]{:S(2)}, u32[]{:S(2)}) collective-permute-start(bf16[128,1280]{1,0:T(8,128)(2,1)S(1)} %get-tuple-element.27.refs_0_), channel_id=1, source_target_pairs={{0,8},{1,9},{2,10},{3,11},{4,12},{5,13},{6,14},{7,15},{8,0},{9,1},... | collective-permute-start | bytes 983048 | tf_op jit(solution)/shard_map/gather_cotangent/ppermute | solution.py:222
  9.6 1.5 %collective-permute-start.8 = (bf16[128,1280]{1,0:T(8,128)(2,1)S(1)}, bf16[128,1280]{1,0:T(8,128)(2,1)S(1)}, u32[]{:S(2)}, u32[]{:S(2)}) collective-permute-start(bf16[128,1280]{1,0:T(8,128)(2,1)S(1)} %get-tuple-element.27.refs_0_), channel_id=1, source_target_pairs={{0,16},{1,17},{2,18},{3,19},{4,20},{5,21},{6,22},{7,23},{8,24},{9,... | collective-permute-start | bytes 983048 | tf_op jit(solution)/shard_map/gather_cotangent/ppermute | solution.py:222
  11.1 3.2 %collective-permute-done.refs_0_ = bf16[976,128]{1,0:T(8,128)(2,1)S(1)} collective-permute-done((bf16[976,128]{1,0:T(8,128)(2,1)S(1)}, bf16[976,128]{1,0:T(8,128)(2,1)S(1)}, u32[]{:S(2)}, u32[]{:S(2)}) %collective-permute-start) | collective-permute-done | bytes 249888 | tf_op jit(solution)/shard_map/exchange_heads/ppermute | solution.py:222
  14.3 2.6 %collective-permute-start.9 = (bf16[128,1280]{1,0:T(8,128)(2,1)S(1)}, bf16[128,1280]{1,0:T(8,128)(2,1)S(1)}, u32[]{:S(2)}, u32[]{:S(2)}) collective-permute-start(bf16[128,1280]{1,0:T(8,128)(2,1)S(1)} %get-tuple-element.27.refs_0_), channel_id=1, source_target_pairs={{0,24},{1,25},{2,26},{3,27},{4,28},{5,29},{6,30},{7,31},{8,16},{9,... | collective-permute-start | bytes 983048 | tf_op jit(solution)/shard_map/gather_cotangent/ppermute | solution.py:222
  16.9 11.6 %collective-permute-done.1.refs_1_ = bf16[976,128]{1,0:T(8,128)(2,1)S(1)} collective-permute-done((bf16[976,128]{1,0:T(8,128)(2,1)S(1)}, bf16[976,128]{1,0:T(8,128)(2,1)S(1)}, u32[]{:S(2)}, u32[]{:S(2)}) %collective-permute-start.1) | collective-permute-done | bytes 249888 | tf_op jit(solution)/shard_map/exchange_heads/ppermute | solution.py:222
  28.5 3.3 %attention.1 = (bf16[320,128]{1,0:T(8,128)(2,1)S(1)}, bf16[320,128]{1,0:T(8,128)(2,1)S(1)}, bf16[320,128]{1,0:T(8,128)(2,1)S(1)}, bf16[320,128]{1,0:T(8,128)(2,1)S(1)}) custom-call(bf16[976,128]{1,0:T(8,128)(2,1)S(1)} %collective-permute-done.refs_0_, bf16[976,128]{1,0:T(8,128)(2,1)S(1)} %collective-permute-done.1.refs_1_, ...), custom_call_target="tpu_custom_call" | custom-call | flops 4613734400 | bytes 1310720 | tf_op jit(solution)/shard_map/attention/pallas_call | solution.py:39
  31.9 4.4 %collective-permute-start.3 = (bf16[320,128]{1,0:T(8,128)(2,1)S(1)}, bf16[320,128]{1,0:T(8,128)(2,1)S(1)}, u32[]{:S(2)}, u32[]{:S(2)}) collective-permute-start(bf16[320,128]{1,0:T(8,128)(2,1)S(1)} %get-tuple-element.21), channel_id=1, source_target_pairs={{0,30},{1,31},{2,28},{3,29},{4,26},{5,27},{6,24},{7,25},{8,22},{9,... | collective-permute-start | bytes 245768 | tf_op jit(solution)/shard_map/send_to_owner/ppermute | solution.py:222
  36.3 0.0 collective-permute-start.4
  36.3 0.0 collective-permute-done.7.refs_1_
  36.3 1.8 %collective-permute-start.5 = (bf16[320,128]{1,0:T(8,128)(2,1)S(1)}, bf16[320,128]{1,0:T(8,128)(2,1)S(1)}, u32[]{:S(2)}, u32[]{:S(2)}) collective-permute-start(bf16[320,128]{1,0:T(8,128)(2,1)S(1)} %get-tuple-element.23), channel_id=1, source_target_pairs={{0,10},{1,11},{2,8},{3,9},{4,14},{5,15},{6,12},{7,13},{8,2},{9,3},... | collective-permute-start | bytes 245768 | tf_op jit(solution)/shard_map/send_to_owner/ppermute | solution.py:222
  38.1 0.0 collective-permute-done.9.refs_3_
  38.1 0.4 swap_cotangent.1.refs_2_
  38.6 0.1 collective-permute-start.10
  38.7 1.5 %collective-permute-done.3.refs_0_ = bf16[320,128]{1,0:T(8,128)(2,1)S(1)} collective-permute-done((bf16[320,128]{1,0:T(8,128)(2,1)S(1)}, bf16[320,128]{1,0:T(8,128)(2,1)S(1)}, u32[]{:S(2)}, u32[]{:S(2)}) %collective-permute-start.3) | collective-permute-done | bytes 81952 | tf_op jit(solution)/shard_map/send_to_owner/ppermute | solution.py:222
  40.1 2.5 %collective-permute-done.4.refs_1_ = bf16[320,128]{1,0:T(8,128)(2,1)S(1)} collective-permute-done((bf16[320,128]{1,0:T(8,128)(2,1)S(1)}, bf16[320,128]{1,0:T(8,128)(2,1)S(1)}, u32[]{:S(2)}, u32[]{:S(2)}) %collective-permute-start.4) | collective-permute-done | bytes 81952 | tf_op jit(solution)/shard_map/send_to_owner/ppermute | solution.py:222
  42.6 0.6 collective-permute-done.5.refs_2_
  43.2 0.1 collective-permute-start.6
  43.3 0.1 collective-permute-start.16
  43.5 1.9 %collective-permute-start.17 = (bf16[320,128]{1,0:T(8,128)(2,1)S(1)}, bf16[320,128]{1,0:T(8,128)(2,1)S(1)}, u32[]{:S(2)}, u32[]{:S(2)}) collective-permute-start(bf16[320,128]{1,0:T(8,128)(2,1)S(1)} %collective-permute-done.4.refs_1_), channel_id=1, source_target_pairs={{0,16},{1,17},{2,18},{3,19},{4,20},{5,21},{6,22},{7,23},{8,24},{9,... | collective-permute-start | bytes 245768 | tf_op jit(solution)/shard_map/send_home/ppermute | solution.py:222
  45.4 0.9 %gradient.1 = (bf16[80,640]{1,0:T(8,128)(2,1)S(1)}, bf16[80,640]{1,0:T(8,128)(2,1)S(1)}, bf16[80,640]{1,0:T(8,128)(2,1)S(1)}, bf16[80,640]{1,0:T(8,128)(2,1)S(1)}) custom-call(bf16[4,160,128]{2,1,0:T(8,128)(2,1)S(1)} %get-tuple-element.25.refs_0_, bf16[4,160,128]{2,1,0:T(8,128)(2,1)S(1)} %collective-permute-done.6.refs_1_, ...), custom_call_target="tpu_custom_call" | custom-call | flops 419430400 | bytes 2621440 | tf_op jit(solution)/shard_map/gradient/pallas_call | solution.py:39
  46.3 2.1 %collective-permute-start.11 = (bf16[80,640]{1,0:T(8,128)(2,1)S(1)}, bf16[80,640]{1,0:T(8,128)(2,1)S(1)}, u32[]{:S(2)}, u32[]{:S(2)}) collective-permute-start(bf16[80,640]{1,0:T(8,128)(2,1)S(1)} %get-tuple-element.28), channel_id=1, source_target_pairs={{0,6},{1,7},{2,12},{3,13},{4,18},{5,19},{6,24},{7,25},{8,14},{9,15... | collective-permute-start | bytes 307208 | tf_op jit(solution)/shard_map/sum_gradient/ppermute | solution.py:222
  48.4 0.2 collective-permute-start.12
  48.7 2.6 %collective-permute-start.13 = (bf16[80,640]{1,0:T(8,128)(2,1)S(1)}, bf16[80,640]{1,0:T(8,128)(2,1)S(1)}, u32[]{:S(2)}, u32[]{:S(2)}) collective-permute-start(bf16[80,640]{1,0:T(8,128)(2,1)S(1)} %get-tuple-element.30), channel_id=1, source_target_pairs={{0,2},{1,3},{2,8},{3,9},{4,22},{5,23},{6,28},{7,29},{8,10},{9,11},... | collective-permute-start | bytes 307208 | tf_op jit(solution)/shard_map/sum_gradient/ppermute | solution.py:222
  51.3 0.7 %collective-permute-start.14 = (bf16[80,640]{1,0:T(8,128)(2,1)S(1)}, bf16[80,640]{1,0:T(8,128)(2,1)S(1)}, u32[]{:S(2)}, u32[]{:S(2)}) collective-permute-start(bf16[80,640]{1,0:T(8,128)(2,1)S(1)} %get-tuple-element.31), channel_id=1, source_target_pairs={{0,0},{1,1},{2,10},{3,11},{4,20},{5,21},{6,30},{7,31},{8,8},{9,9},... | collective-permute-start | bytes 307208 | tf_op jit(solution)/shard_map/sum_gradient/ppermute | solution.py:222
  52.0 2.2 %collective-permute-start.15 = (bf16[320,128]{1,0:T(8,128)(2,1)S(1)}, bf16[320,128]{1,0:T(8,128)(2,1)S(1)}, u32[]{:S(2)}, u32[]{:S(2)}) collective-permute-start(bf16[320,128]{1,0:T(8,128)(2,1)S(1)} %collective-permute-done.3.refs_0_), channel_id=1, source_target_pairs={{0,24},{1,25},{2,26},{3,27},{4,28},{5,29},{6,30},{7,31},{8,16},{9,... | collective-permute-start | bytes 245768 | tf_op jit(solution)/shard_map/send_home/ppermute | solution.py:222
  54.2 0.6 project.1.refs_5_
  54.8 4.8 %collective-permute-done.15.refs_4_ = bf16[320,128]{1,0:T(8,128)(2,1)S(1)} collective-permute-done((bf16[320,128]{1,0:T(8,128)(2,1)S(1)}, bf16[320,128]{1,0:T(8,128)(2,1)S(1)}, u32[]{:S(2)}, u32[]{:S(2)}) %collective-permute-start.15) | collective-permute-done | bytes 81952 | tf_op jit(solution)/shard_map/send_home/ppermute | solution.py:222
  59.6 1.1 %finish.1 = (bf16[128,1280]{1,0:T(8,128)(2,1)}, f32[160,320]{1,0:T(8,128)}) custom-call(bf16[80,640]{1,0:T(8,128)(2,1)S(1)} %collective-permute-done.11.refs_0_, bf16[80,640]{1,0:T(8,128)(2,1)S(1)} %collective-permute-done.12.refs_1_, bf16[80,640]{1,0:T(8,128)(2,1)S(1)} %collective-permute-done.13.refs_2_, ...), custom_call_target="tpu_custom_call" | custom-call | flops 104857600 | bytes 819200 | tf_op jit(solution)/shard_map/finish/pallas_call | solution.py:39
  (15 shorter events, 0.1 us)
Async XLA Ops:
  2.2 12.1 %collective-permute-start = (bf16[976,128]{1,0:T(8,128)(2,1)S(1)}, bf16[976,128]{1,0:T(8,128)(2,1)S(1)}, u32[]{:S(2)}, u32[]{:S(2)}) collective-permute-start(bf16[976,128]{1,0:T(8,128)(2,1)S(1)} %get-tuple-element.17), channel_id=1, source_target_pairs={{0,6},{1,7},{2,4},{3,5},{4,2},{5,3},{6,0},{7,1},{8,14},{9,15},{10,... | collective-permute-start | bytes 749576 | tf_op jit(solution)/shard_map/exchange_heads/ppermute | solution.py:222
  7.3 21.3 %collective-permute-start.1 = (bf16[976,128]{1,0:T(8,128)(2,1)S(1)}, bf16[976,128]{1,0:T(8,128)(2,1)S(1)}, u32[]{:S(2)}, u32[]{:S(2)}) collective-permute-start(bf16[976,128]{1,0:T(8,128)(2,1)S(1)} %get-tuple-element.18), channel_id=1, source_target_pairs={{0,4},{1,5},{2,6},{3,7},{4,0},{5,1},{6,2},{7,3},{8,12},{9,13},{10,... | collective-permute-start | bytes 749576 | tf_op jit(solution)/shard_map/exchange_heads/ppermute | solution.py:222
  7.3 21.3 %collective-permute-start.2 = (bf16[976,128]{1,0:T(8,128)(2,1)S(1)}, bf16[976,128]{1,0:T(8,128)(2,1)S(1)}, u32[]{:S(2)}, u32[]{:S(2)}) collective-permute-start(bf16[976,128]{1,0:T(8,128)(2,1)S(1)} %get-tuple-element.19), channel_id=1, source_target_pairs={{0,2},{1,3},{2,0},{3,1},{4,6},{5,7},{6,4},{7,5},{8,10},{9,11},{10,... | collective-permute-start | bytes 749576 | tf_op jit(solution)/shard_map/exchange_heads/ppermute | solution.py:222
  7.9 28.4 %collective-permute-start.7 = (bf16[128,1280]{1,0:T(8,128)(2,1)S(1)}, bf16[128,1280]{1,0:T(8,128)(2,1)S(1)}, u32[]{:S(2)}, u32[]{:S(2)}) collective-permute-start(bf16[128,1280]{1,0:T(8,128)(2,1)S(1)} %get-tuple-element.27.refs_0_), channel_id=1, source_target_pairs={{0,8},{1,9},{2,10},{3,11},{4,12},{5,13},{6,14},{7,15},{8,0},{9,1},... | collective-permute-start | bytes 983048 | tf_op jit(solution)/shard_map/gather_cotangent/ppermute | solution.py:222
  9.6 28.6 %collective-permute-start.8 = (bf16[128,1280]{1,0:T(8,128)(2,1)S(1)}, bf16[128,1280]{1,0:T(8,128)(2,1)S(1)}, u32[]{:S(2)}, u32[]{:S(2)}) collective-permute-start(bf16[128,1280]{1,0:T(8,128)(2,1)S(1)} %get-tuple-element.27.refs_0_), channel_id=1, source_target_pairs={{0,16},{1,17},{2,18},{3,19},{4,20},{5,21},{6,22},{7,23},{8,24},{9,... | collective-permute-start | bytes 983048 | tf_op jit(solution)/shard_map/gather_cotangent/ppermute | solution.py:222
  14.3 23.8 %collective-permute-start.9 = (bf16[128,1280]{1,0:T(8,128)(2,1)S(1)}, bf16[128,1280]{1,0:T(8,128)(2,1)S(1)}, u32[]{:S(2)}, u32[]{:S(2)}) collective-permute-start(bf16[128,1280]{1,0:T(8,128)(2,1)S(1)} %get-tuple-element.27.refs_0_), channel_id=1, source_target_pairs={{0,24},{1,25},{2,26},{3,27},{4,28},{5,29},{6,30},{7,31},{8,16},{9,... | collective-permute-start | bytes 983048 | tf_op jit(solution)/shard_map/gather_cotangent/ppermute | solution.py:222
  31.9 8.3 %collective-permute-start.3 = (bf16[320,128]{1,0:T(8,128)(2,1)S(1)}, bf16[320,128]{1,0:T(8,128)(2,1)S(1)}, u32[]{:S(2)}, u32[]{:S(2)}) collective-permute-start(bf16[320,128]{1,0:T(8,128)(2,1)S(1)} %get-tuple-element.21), channel_id=1, source_target_pairs={{0,30},{1,31},{2,28},{3,29},{4,26},{5,27},{6,24},{7,25},{8,22},{9,... | collective-permute-start | bytes 245768 | tf_op jit(solution)/shard_map/send_to_owner/ppermute | solution.py:222
  36.3 6.3 %collective-permute-start.4 = (bf16[320,128]{1,0:T(8,128)(2,1)S(1)}, bf16[320,128]{1,0:T(8,128)(2,1)S(1)}, u32[]{:S(2)}, u32[]{:S(2)}) collective-permute-start(bf16[320,128]{1,0:T(8,128)(2,1)S(1)} %get-tuple-element.22), channel_id=1, source_target_pairs={{0,20},{1,21},{2,22},{3,23},{4,16},{5,17},{6,18},{7,19},{8,28},{9,... | collective-permute-start | bytes 245768 | tf_op jit(solution)/shard_map/send_to_owner/ppermute | solution.py:222
  36.3 6.9 %collective-permute-start.5 = (bf16[320,128]{1,0:T(8,128)(2,1)S(1)}, bf16[320,128]{1,0:T(8,128)(2,1)S(1)}, u32[]{:S(2)}, u32[]{:S(2)}) collective-permute-start(bf16[320,128]{1,0:T(8,128)(2,1)S(1)} %get-tuple-element.23), channel_id=1, source_target_pairs={{0,10},{1,11},{2,8},{3,9},{4,14},{5,15},{6,12},{7,13},{8,2},{9,3},... | collective-permute-start | bytes 245768 | tf_op jit(solution)/shard_map/send_to_owner/ppermute | solution.py:222
  38.6 6.8 %collective-permute-start.10 = (bf16[4,128,1280]{2,1,0:T(8,128)(2,1)S(1)}, bf16[4,128,1280]{2,1,0:T(8,128)(2,1)S(1)}, u32[]{:S(2)}, u32[]{:S(2)}) collective-permute-start(bf16[4,128,1280]{2,1,0:T(8,128)(2,1)S(1)} %swap_cotangent.1.refs_2_), channel_id=1, source_target_pairs={{0,1},{1,0},{2,3},{3,2},{4,5},{5,4},{6,7},{7,6},{8,9},{9,8},{10,11... | collective-permute-start | bytes 3932168 | tf_op jit(solution)/shard_map/gradient/ppermute | solution.py:222
  43.2 11.0 %copy-start = (bf16[1280,1280]{1,0:T(8,128)(2,1)S(1)}, bf16[1280,1280]{1,0:T(8,128)(2,1)}, u32[]{:S(2)}) copy-start(bf16[1280,1280]{1,0:T(8,128)(2,1)} %refs_6_.1) | copy-start | bytes 9830404
  43.2 2.1 %collective-permute-start.6 = (bf16[4,160,128]{2,1,0:T(8,128)(2,1)S(1)}, bf16[4,160,128]{2,1,0:T(8,128)(2,1)S(1)}, u32[]{:S(2)}, u32[]{:S(2)}) collective-permute-start(bf16[4,160,128]{2,1,0:T(8,128)(2,1)S(1)} %get-tuple-element.26), channel_id=1, source_target_pairs={{0,1},{1,0},{2,3},{3,2},{4,5},{5,4},{6,7},{7,6},{8,9},{9,8},{10,11... | collective-permute-start | bytes 491528 | tf_op jit(solution)/shard_map/send_to_owner/ppermute | solution.py:222
  43.3 8.0 %collective-permute-start.16 = (bf16[320,128]{1,0:T(8,128)(2,1)S(1)}, bf16[320,128]{1,0:T(8,128)(2,1)S(1)}, u32[]{:S(2)}, u32[]{:S(2)}) collective-permute-start(bf16[320,128]{1,0:T(8,128)(2,1)S(1)} %collective-permute-done.5.refs_2_), channel_id=1, source_target_pairs={{0,8},{1,9},{2,10},{3,11},{4,12},{5,13},{6,14},{7,15},{8,0},{9,1},... | collective-permute-start | bytes 245768 | tf_op jit(solution)/shard_map/send_home/ppermute | solution.py:222
  43.5 8.5 %collective-permute-start.17 = (bf16[320,128]{1,0:T(8,128)(2,1)S(1)}, bf16[320,128]{1,0:T(8,128)(2,1)S(1)}, u32[]{:S(2)}, u32[]{:S(2)}) collective-permute-start(bf16[320,128]{1,0:T(8,128)(2,1)S(1)} %collective-permute-done.4.refs_1_), channel_id=1, source_target_pairs={{0,16},{1,17},{2,18},{3,19},{4,20},{5,21},{6,22},{7,23},{8,24},{9,... | collective-permute-start | bytes 245768 | tf_op jit(solution)/shard_map/send_home/ppermute | solution.py:222
  45.4 8.8 %copy-start.1 = (bf16[128,1280]{1,0:T(8,128)(2,1)S(1)}, bf16[128,1280]{1,0:T(8,128)(2,1)}, u32[]{:S(2)}) copy-start(bf16[128,1280]{1,0:T(8,128)(2,1)} %residual.1) | copy-start | bytes 983044
  46.3 13.3 %collective-permute-start.11 = (bf16[80,640]{1,0:T(8,128)(2,1)S(1)}, bf16[80,640]{1,0:T(8,128)(2,1)S(1)}, u32[]{:S(2)}, u32[]{:S(2)}) collective-permute-start(bf16[80,640]{1,0:T(8,128)(2,1)S(1)} %get-tuple-element.28), channel_id=1, source_target_pairs={{0,6},{1,7},{2,12},{3,13},{4,18},{5,19},{6,24},{7,25},{8,14},{9,15... | collective-permute-start | bytes 307208 | tf_op jit(solution)/shard_map/sum_gradient/ppermute | solution.py:222
  48.4 11.2 %collective-permute-start.12 = (bf16[80,640]{1,0:T(8,128)(2,1)S(1)}, bf16[80,640]{1,0:T(8,128)(2,1)S(1)}, u32[]{:S(2)}, u32[]{:S(2)}) collective-permute-start(bf16[80,640]{1,0:T(8,128)(2,1)S(1)} %get-tuple-element.29), channel_id=1, source_target_pairs={{0,4},{1,5},{2,14},{3,15},{4,16},{5,17},{6,26},{7,27},{8,12},{9,13... | collective-permute-start | bytes 307208 | tf_op jit(solution)/shard_map/sum_gradient/ppermute | solution.py:222
  48.7 10.9 %collective-permute-start.13 = (bf16[80,640]{1,0:T(8,128)(2,1)S(1)}, bf16[80,640]{1,0:T(8,128)(2,1)S(1)}, u32[]{:S(2)}, u32[]{:S(2)}) collective-permute-start(bf16[80,640]{1,0:T(8,128)(2,1)S(1)} %get-tuple-element.30), channel_id=1, source_target_pairs={{0,2},{1,3},{2,8},{3,9},{4,22},{5,23},{6,28},{7,29},{8,10},{9,11},... | collective-permute-start | bytes 307208 | tf_op jit(solution)/shard_map/sum_gradient/ppermute | solution.py:222
  51.3 8.3 %collective-permute-start.14 = (bf16[80,640]{1,0:T(8,128)(2,1)S(1)}, bf16[80,640]{1,0:T(8,128)(2,1)S(1)}, u32[]{:S(2)}, u32[]{:S(2)}) collective-permute-start(bf16[80,640]{1,0:T(8,128)(2,1)S(1)} %get-tuple-element.31), channel_id=1, source_target_pairs={{0,0},{1,1},{2,10},{3,11},{4,20},{5,21},{6,30},{7,31},{8,8},{9,9},... | collective-permute-start | bytes 307208 | tf_op jit(solution)/shard_map/sum_gradient/ppermute | solution.py:222
  52.0 7.6 %collective-permute-start.15 = (bf16[320,128]{1,0:T(8,128)(2,1)S(1)}, bf16[320,128]{1,0:T(8,128)(2,1)S(1)}, u32[]{:S(2)}, u32[]{:S(2)}) collective-permute-start(bf16[320,128]{1,0:T(8,128)(2,1)S(1)} %collective-permute-done.3.refs_0_), channel_id=1, source_target_pairs={{0,24},{1,25},{2,26},{3,27},{4,28},{5,29},{6,30},{7,31},{8,16},{9,... | collective-permute-start | bytes 245768 | tf_op jit(solution)/shard_map/send_home/ppermute | solution.py:222

commit v3 on v2

--- a/solution.py
+++ b/solution.py
@@ -12,7 +12,7 @@
 AXES = ("dp", "enc", "seq")
 ID_ROWS = 16
 ID_BASE = 64
-SENDS = (3, 2, 1, 0)
+SENDS = (0, 3, 1, 2)
 RETURNS = (3, 2, 1, 0)
 SUMS = (3, 2, 1, 0)
 
@@ -75,46 +75,92 @@
     copies[4].wait()
 
 
-def attend_kernel(count, block, head_width, *refs):
-    slabs, outs, bias = refs[:count], refs[count : 2 * count], refs[2 * count]
-    rows = slabs[0].shape[1]
+def identifiers(slabs, block):
     numbers = []
     for slab in slabs:
         digits = slab[3 * block : 3 * block + ID_ROWS].astype(jnp.float32)
         numbers.append(digits[0:1] * ID_BASE + digits[1:2])
-    query_ids = jnp.concatenate(numbers, axis=1)
-    for index in range(count):
-        column = jnp.broadcast_to(numbers[index], (rows, rows)).T
-        column = jnp.concatenate([column] * count, axis=1)
-        bias[index * rows : (index + 1) * rows] = jnp.where(column == query_ids, 0.0, -1e30)
+    return numbers
+
+
+def set_bias(bias, key_ids, query_ids):
+    queries = jnp.concatenate(query_ids, axis=1)
+    for index, ids in enumerate(key_ids):
+        rows = ids.shape[1]
+        column = jnp.broadcast_to(ids, (rows, rows)).T
+        column = jnp.concatenate([column] * len(query_ids), axis=1)
+        bias[index * rows : (index + 1) * rows] = jnp.where(column == queries, 0.0, -1e30)
+
+
+def gather(slabs, which, block, head, head_width):
+    begin = which * block + head * head_width
+    return jnp.concatenate([slab[begin : begin + head_width] for slab in slabs], axis=1)
+
+
+def weigh(key, query, bias):
+    scores = lax.dot_general(
+        key, query, (((0,), (0,)), ((), ())), preferred_element_type=jnp.float32
+    )
+    scores = scores + bias
+    return scores, jnp.max(scores, axis=0, keepdims=True)
+
+
+def attend_first_kernel(block, head_width, *refs):
+    slabs, (mixed, highest, total, bias) = refs[:-4], refs[-4:]
+    ids = identifiers(slabs, block)
+    set_bias(bias, ids, ids)
     factor = math.log2(math.e) / math.sqrt(head_width)
-    span = 2 * rows
-
-    def part(which, head):
-        begin = which * block + head * head_width
-        return jnp.concatenate([slab[begin : begin + head_width] for slab in slabs], axis=1)
-
     for head in range(block // head_width):
-        query, key, value = part(0, head), part(1, head), part(2, head)
-        for first in range(0, count * rows, span):
-            scores = lax.dot_general(
-                key,
-                query[:, first : first + span],
-                (((0,), (0,)), ((), ())),
-                preferred_element_type=jnp.float32,
-            )
-            scores = scores + bias[:, first : first + span]
-            highest = jnp.max(scores, axis=0, keepdims=True)
-            weights = jnp.exp2((scores - highest) * factor)
-            total = jnp.sum(weights, axis=0, keepdims=True)
-            mixed = jnp.dot(
-                value, weights.astype(jnp.bfloat16), preferred_element_type=jnp.float32
-            )
-            mixed = (mixed / total).astype(jnp.bfloat16)
-            for index in range(first // rows, (first + span) // rows):
-                at = index * rows - first
-                out = outs[RETURNS.index(SENDS[index])]
-                out[head * head_width : (head + 1) * head_width] = mixed[:, at : at + rows]
+        query, key, value = (gather(slabs, which, block, head, head_width) for which in range(3))
+        scores, top = weigh(key, query, bias[...])
+        weights = jnp.exp2((scores - top) * factor)
+        highest[head : head + 1] = top
+        total[head : head + 1] = jnp.sum(weights, axis=0, keepdims=True)
+        mixed[head * head_width : (head + 1) * head_width] = jnp.dot(
+            value, weights.astype(jnp.bfloat16), preferred_element_type=jnp.float32
+        )
+
+
+def attend_last_kernel(block, head_width, *refs):
+    count = len(SENDS)
+    slabs, (mixed, highest, total), outs = refs[:count], refs[count : count + 3], refs[count + 3 : -2]
+    old_bias, new_bias = refs[-2:]
+    *early, late = slabs
+    rows = late.shape[1]
+    *early_ids, late_id = identifiers(slabs, block)
+    set_bias(old_bias, [late_id], early_ids)
+    set_bias(new_bias, early_ids + [late_id], [late_id])
+    factor = math.log2(math.e) / math.sqrt(head_width)
+    for head in range(block // head_width):
+        span = slice(head * head_width, (head + 1) * head_width)
+        query, key, value = (gather(early, which, block, head, head_width) for which in range(3))
+        new_query, new_key, new_value = (
+            gather([late], which, block, head, head_width) for which in range(3)
+        )
+        scores, top = weigh(new_key, query, old_bias[...])
+        before = highest[head : head + 1]
+        top = jnp.maximum(top, before)
+        weights = jnp.exp2((scores - top) * factor)
+        shrink = jnp.exp2((before - top) * factor)
+        sums = total[head : head + 1] * shrink + jnp.sum(weights, axis=0, keepdims=True)
+        result = mixed[span] * shrink + jnp.dot(
+            new_value, weights.astype(jnp.bfloat16), preferred_element_type=jnp.float32
+        )
+        result = (result / sums).astype(jnp.bfloat16)
+        for index in range(count - 1):
+            out = outs[RETURNS.index(SENDS[index])]
+            out[span] = result[:, index * rows : (index + 1) * rows]
+        scores, top = weigh(
+            jnp.concatenate([key, new_key], axis=1), new_query, new_bias[...]
+        )
+        weights = jnp.exp2((scores - top) * factor)
+        sums = jnp.sum(weights, axis=0, keepdims=True)
+        result = jnp.dot(
+            jnp.concatenate([value, new_value], axis=1),
+            weights.astype(jnp.bfloat16),
+            preferred_element_type=jnp.float32,
+        )
+        outs[RETURNS.index(SENDS[-1])][span] = (result / sums).astype(jnp.bfloat16)
 
 
 def stack_kernel(count, *refs):
@@ -162,39 +208,26 @@
                 out[...] = folded
 
 
-def project(pieces, steps, weight, attended):
+def project_kernel(*refs):
+    pieces, (residual, weight, out, attended) = refs[:-4], refs[-4:]
     first = lax.axis_index("dp") ^ lax.axis_index("enc")
     block = pieces[0].shape[0]
-    rows = []
-    for index, (step, piece) in enumerate(zip(steps, pieces)):
-        attended[index * block : (index + 1) * block] = piece[...]
-        rows.append(weight[pl.ds(pl.multiple_of((first ^ step) * block, 16), block)])
-    return lax.dot_general(
-        attended[...],
-        jnp.concatenate(rows, axis=0),
-        (((0,), (0,)), ((), ())),
-        preferred_element_type=jnp.float32,
-    )
-
-
-def project_kernel(residual, weight, *refs):
-    pieces, (out, attended) = refs[:-2], refs[-2:]
-    out[...] = residual[...].astype(jnp.float32) + project(
-        pieces, range(len(pieces)), weight, attended
-    )
-
-
-def finish_kernel(count, early, *refs):
-    partial, pieces = refs[:count], refs[count : 2 * count - early]
-    projected, weight, out, grad, attended = refs[2 * count - early :]
+    for hop, piece in zip(RETURNS, pieces):
+        attended[pl.ds(pl.multiple_of((first ^ hop) * block, 16), block)] = piece[...]
+    projected = lax.dot_general(
+        attended[...], weight[...], (((0,), (0,)), ((), ())), preferred_element_type=jnp.float32
+    )
+    out[...] = (residual[...].astype(jnp.float32) + projected).astype(jnp.bfloat16)
+
+
+def add_kernel(*refs):
+    partial, out = refs[:-1], refs[-1]
     total = partial[0][...].astype(jnp.float32)
     for ref in partial[1:]:
         total = total + ref[...].astype(jnp.float32)
-    short, width = total.shape[0], grad.shape[1]
-    grad[:short] = total[:, :width]
-    grad[short:] = total[:, width:]
-    projected = projected[...] + project(pieces, range(early, count), weight, attended)
-    out[...] = projected.astype(jnp.bfloat16)
+    short, width = total.shape[0], out.shape[1]
+    out[:short] = total[:, :width]
+    out[short:] = total[:, width:]
 
 
 def exchange_body(
@@ -256,12 +289,23 @@
             move(cotangent, lambda d, e, s, k=k: (d ^ k, e, s)) for k in range(1, n_dp)
         ]
     with jax.named_scope("attention"):
+        known = group - rows
+        f32 = functools.partial(jax.ShapeDtypeStruct, dtype=jnp.float32)
+        state = call(
+            functools.partial(attend_first_kernel, block, head_width),
+            [f32((block, known)), f32((8, known)), f32((8, known))],
+            *slabs[:-1],
+            scratch=[pltpu.VMEM((known, known), jnp.float32)],
+            flops=55 * known * known * block,
+            bytes_accessed=8 * group * block,
+        )
         pieces = call(
-            functools.partial(attend_kernel, n_enc, block, head_width),
+            functools.partial(attend_last_kernel, block, head_width),
             [bf16((block, rows))] * n_enc,
             *slabs,
-            scratch=[pltpu.VMEM((group, group), jnp.float32)],
-            flops=55 * group * group * block,
+            *state,
+            scratch=[pltpu.VMEM((rows, known), jnp.float32), pltpu.VMEM((group, rows), jnp.float32)],
+            flops=55 * (group * group - known * known) * block,
             bytes_accessed=8 * group * block,
         )
     with jax.named_scope("send_to_owner"):
@@ -302,33 +346,27 @@
             for hop, part in zip(SUMS, partial)
         ]
     with jax.named_scope("send_home"):
-        homes = [pieces[RETURNS.index(k)] for k in range(n_dp)]
-        homes[1:] = [
-            move(homes[k], lambda d, e, s, k=k: (d ^ k, e, s)) for k in range(1, n_dp)
+        homes = [
+            move(piece, lambda d, e, s, hop=hop: (d ^ hop, e, s)) if hop else piece
+            for hop, piece in zip(RETURNS, pieces)
         ]
-    early = 3
     with jax.named_scope("project"):
-        projected = call(
+        layer_out = call(
             project_kernel,
-            jax.ShapeDtypeStruct((rows, width), jnp.float32),
+            bf16((rows, width)),
+            *homes,
             residual,
             out_weight,
-            *homes[:early],
-            scratch=[pltpu.VMEM((early * block, rows), jnp.bfloat16)],
-            flops=2 * rows * early * block * width,
-            bytes_accessed=2 * early * block * width,
-        )
-    with jax.named_scope("finish"):
-        layer_out, grad_weight = call(
-            functools.partial(finish_kernel, n_dp, early),
-            [bf16((rows, width)), jax.ShapeDtypeStruct((half, block), jnp.float32)],
+            scratch=[pltpu.VMEM((width, rows), jnp.bfloat16)],
+            flops=rows * width * width,
+            bytes_accessed=2 * width * width,
+        )
+    with jax.named_scope("add_gradient"):
+        grad_weight = call(
+            add_kernel,
+            jax.ShapeDtypeStruct((half, block), jnp.float32),
             *partial,
-            *homes[early:],
-            projected,
-            out_weight,
-            scratch=[pltpu.VMEM(((n_dp - early) * block, rows), jnp.bfloat16)],
-            flops=2 * rows * (n_dp - early) * block * width,
-            bytes_accessed=2 * (n_dp - early) * block * width,
+            bytes_accessed=4 * half * block * 4,
         )
     return (layer_out, grad_weight)
 

time: 60.9 us -> 60.6 us (level); the launches traced: 60.7 us -> 59.7 us
  starting transfers between devices: 27.9 us -> 26.8 us
  waiting for transfers between devices: 24.2 us -> 23.2 us
  Pallas kernels: 7.95 us -> 8.9 us
    ppermute x18, starting transfers between devices: 27.9 us -> 26.8 us  [move(): return lax.ppermute(data, AXES, pairs)]
    ppermute x18, waiting for transfers between devices: 24.2 us -> 23.2 us  [move(): return lax.ppermute(data, AXES, pairs)]
    pallas_call x7 -> x8, Pallas kernels: 7.95 us -> 8.9 us  [call(): pl.pallas_call(kernel, out_shape=out_shape, in_specs=[placed(space) for s...]
  transfers between devices with their start and end apart: 18 -> 18, of which waited for: 6 -> 7; matrix products, arithmetic and copies ran while one was open for 0% -> 0% of each run, Pallas kernels for 9% -> 11%
where the time goes in v3:
time: 60.6 us; the launch traced here: 59.7 us
  starting transfers between devices  26.8 us (44%)
  waiting for transfers between devices  23.2 us (38%)
  Pallas kernels  8.9 us (15%)
  between operations  0.74 us (1%)
    ppermute x18, starting transfers between devices, move(): return lax.ppermute(data, AXES, pairs)  26.8 us
    ppermute x18, waiting for transfers between devices, move(): return lax.ppermute(data, AXES, pairs)  23.2 us
    pallas_call x8, Pallas kernels, call(): pl.pallas_call(kernel, out_shape=out_shape, in_specs=[placed(space) for s...  8.9 us
  transfers between devices with their start and end apart: 18, of which 7 were waited for; matrix products, arithmetic and copies ran while one was open for 0% of the time, Pallas kernels for 11%

profile of v3, /device:TPU:0, one launch (start us, length us, event | category | flops | bytes accessed | tf_op | source)
XLA Modules:
  0.0 59.7 jit_solution(6902381191672673483)
XLA Ops:
  0.6 1.5 %pack.1 = (bf16[976,128]{1,0:T(8,128)(2,1)S(1)}, bf16[976,128]{1,0:T(8,128)(2,1)S(1)}, bf16[976,128]{1,0:T(8,128)(2,1)S(1)}, bf16[976,128]{1,0:T(8,128)(2,1)S(1)}, bf16[128,1280]{1,0:T(8,128)(2,1)S(1)}) custom-call(s32[1,128]{1,0:T(1,128)} %bitcast.1, bf16[128,1280]{1,0:T(8,128)(2,1)} %refs_1_.1, bf16[128,1280]{1,0:T(8,128)(2,1)} %refs_2_.1, ...), custom_call_target="tpu_custom_call" | custom-call | bytes 2621440 | tf_op jit(solution)/shard_map/pack/pallas_call | solution.py:39
  2.2 5.1 %collective-permute-start = (bf16[976,128]{1,0:T(8,128)(2,1)S(1)}, bf16[976,128]{1,0:T(8,128)(2,1)S(1)}, u32[]{:S(2)}, u32[]{:S(2)}) collective-permute-start(bf16[976,128]{1,0:T(8,128)(2,1)S(1)} %get-tuple-element.21), channel_id=1, source_target_pairs={{0,6},{1,7},{2,4},{3,5},{4,2},{5,3},{6,0},{7,1},{8,14},{9,15},{10,... | collective-permute-start | bytes 749576 | tf_op jit(solution)/shard_map/exchange_heads/ppermute | solution.py:255
  7.3 0.6 %collective-permute-start.2 = (bf16[976,128]{1,0:T(8,128)(2,1)S(1)}, bf16[976,128]{1,0:T(8,128)(2,1)S(1)}, u32[]{:S(2)}, u32[]{:S(2)}) collective-permute-start(bf16[976,128]{1,0:T(8,128)(2,1)S(1)} %get-tuple-element.23), channel_id=1, source_target_pairs={{0,4},{1,5},{2,6},{3,7},{4,0},{5,1},{6,2},{7,3},{8,12},{9,13},{10,... | collective-permute-start | bytes 749576 | tf_op jit(solution)/shard_map/exchange_heads/ppermute | solution.py:255
  7.9 2.6 %collective-permute-start.12 = (bf16[128,1280]{1,0:T(8,128)(2,1)S(1)}, bf16[128,1280]{1,0:T(8,128)(2,1)S(1)}, u32[]{:S(2)}, u32[]{:S(2)}) collective-permute-start(bf16[128,1280]{1,0:T(8,128)(2,1)S(1)} %get-tuple-element.33.refs_0_), channel_id=1, source_target_pairs={{0,24},{1,25},{2,26},{3,27},{4,28},{5,29},{6,30},{7,31},{8,16},{9,... | collective-permute-start | bytes 983048 | tf_op jit(solution)/shard_map/gather_cotangent/ppermute | solution.py:255
  10.5 0.5 collective-permute-start.11
  11.0 3.2 %collective-permute-done.refs_1_ = bf16[976,128]{1,0:T(8,128)(2,1)S(1)} collective-permute-done((bf16[976,128]{1,0:T(8,128)(2,1)S(1)}, bf16[976,128]{1,0:T(8,128)(2,1)S(1)}, u32[]{:S(2)}, u32[]{:S(2)}) %collective-permute-start) | collective-permute-done | bytes 249888 | tf_op jit(solution)/shard_map/exchange_heads/ppermute | solution.py:255
  14.2 1.7 %collective-permute-start.10 = (bf16[128,1280]{1,0:T(8,128)(2,1)S(1)}, bf16[128,1280]{1,0:T(8,128)(2,1)S(1)}, u32[]{:S(2)}, u32[]{:S(2)}) collective-permute-start(bf16[128,1280]{1,0:T(8,128)(2,1)S(1)} %get-tuple-element.33.refs_0_), channel_id=1, source_target_pairs={{0,8},{1,9},{2,10},{3,11},{4,12},{5,13},{6,14},{7,15},{8,0},{9,1},... | collective-permute-start | bytes 983048 | tf_op jit(solution)/shard_map/gather_cotangent/ppermute | solution.py:255
  15.9 3.9 %collective-permute-done.1.refs_2_ = bf16[976,128]{1,0:T(8,128)(2,1)S(1)} collective-permute-done((bf16[976,128]{1,0:T(8,128)(2,1)S(1)}, bf16[976,128]{1,0:T(8,128)(2,1)S(1)}, u32[]{:S(2)}, u32[]{:S(2)}) %collective-permute-start.1) | collective-permute-done | bytes 249888 | tf_op jit(solution)/shard_map/exchange_heads/ppermute | solution.py:255
  19.8 1.7 %attention.2 = (f32[320,384]{1,0:T(8,128)S(1)}, f32[8,384]{1,0:T(8,128)S(1)}, f32[8,384]{1,0:T(8,128)S(1)}) custom-call(bf16[976,128]{1,0:T(8,128)(2,1)S(1)} %get-tuple-element.20.refs_0_, bf16[976,128]{1,0:T(8,128)(2,1)S(1)} %collective-permute-done.refs_1_, bf16[976,128]{1,0:T(8,128)(2,1)S(1)} %collective-permute-done.1.refs_2_), custom_call_target="tpu_custom_call" | custom-call | flops 2595225600 | bytes 1310720 | tf_op jit(solution)/shard_map/attention/pallas_call | solution.py:39
  21.5 7.0 %collective-permute-done.2.refs_3_ = bf16[976,128]{1,0:T(8,128)(2,1)S(1)} collective-permute-done((bf16[976,128]{1,0:T(8,128)(2,1)S(1)}, bf16[976,128]{1,0:T(8,128)(2,1)S(1)}, u32[]{:S(2)}, u32[]{:S(2)}) %collective-permute-start.2) | collective-permute-done | bytes 249888 | tf_op jit(solution)/shard_map/exchange_heads/ppermute | solution.py:255
  28.5 2.1 %attention.3 = (bf16[320,128]{1,0:T(8,128)(2,1)S(1)}, bf16[320,128]{1,0:T(8,128)(2,1)S(1)}, bf16[320,128]{1,0:T(8,128)(2,1)S(1)}, bf16[320,128]{1,0:T(8,128)(2,1)S(1)}) custom-call(bf16[976,128]{1,0:T(8,128)(2,1)S(1)} %get-tuple-element.20.refs_0_, bf16[976,128]{1,0:T(8,128)(2,1)S(1)} %collective-permute-done.refs_1_, ...), custom_call_target="tpu_custom_call" | custom-call | flops 2018508800 | bytes 1310720 | tf_op jit(solution)/shard_map/attention/pallas_call | solution.py:39
  30.7 4.4 %collective-permute-start.3 = (bf16[320,128]{1,0:T(8,128)(2,1)S(1)}, bf16[320,128]{1,0:T(8,128)(2,1)S(1)}, u32[]{:S(2)}, u32[]{:S(2)}) collective-permute-start(bf16[320,128]{1,0:T(8,128)(2,1)S(1)} %get-tuple-element.27), channel_id=1, source_target_pairs={{0,30},{1,31},{2,28},{3,29},{4,26},{5,27},{6,24},{7,25},{8,22},{9,... | collective-permute-start | bytes 245768 | tf_op jit(solution)/shard_map/send_to_owner/ppermute | solution.py:255
  35.1 0.0 collective-permute-start.5
  35.1 0.0 collective-permute-done.12.refs_3_
  35.1 1.8 %collective-permute-start.7 = (bf16[320,128]{1,0:T(8,128)(2,1)S(1)}, bf16[320,128]{1,0:T(8,128)(2,1)S(1)}, u32[]{:S(2)}, u32[]{:S(2)}) collective-permute-start(bf16[320,128]{1,0:T(8,128)(2,1)S(1)} %get-tuple-element.29), channel_id=1, source_target_pairs={{0,10},{1,11},{2,8},{3,9},{4,14},{5,15},{6,12},{7,13},{8,2},{9,3},... | collective-permute-start | bytes 245768 | tf_op jit(solution)/shard_map/send_to_owner/ppermute | solution.py:255
  36.9 0.4 swap_cotangent.1.refs_2_
  37.4 0.1 collective-permute-start.13
  37.5 1.5 %collective-permute-done.3.refs_0_ = bf16[320,128]{1,0:T(8,128)(2,1)S(1)} collective-permute-done((bf16[320,128]{1,0:T(8,128)(2,1)S(1)}, bf16[320,128]{1,0:T(8,128)(2,1)S(1)}, u32[]{:S(2)}, u32[]{:S(2)}) %collective-permute-start.3) | collective-permute-done | bytes 81952 | tf_op jit(solution)/shard_map/send_to_owner/ppermute | solution.py:255
  38.9 2.5 %collective-permute-done.5.refs_1_ = bf16[320,128]{1,0:T(8,128)(2,1)S(1)} collective-permute-done((bf16[320,128]{1,0:T(8,128)(2,1)S(1)}, bf16[320,128]{1,0:T(8,128)(2,1)S(1)}, u32[]{:S(2)}, u32[]{:S(2)}) %collective-permute-start.5) | collective-permute-done | bytes 81952 | tf_op jit(solution)/shard_map/send_to_owner/ppermute | solution.py:255
  41.4 0.6 collective-permute-done.7.refs_2_
  42.1 0.1 collective-permute-start.9
  42.1 1.5 %collective-permute-start.4 = (bf16[320,128]{1,0:T(8,128)(2,1)S(1)}, bf16[320,128]{1,0:T(8,128)(2,1)S(1)}, u32[]{:S(2)}, u32[]{:S(2)}) collective-permute-start(bf16[320,128]{1,0:T(8,128)(2,1)S(1)} %collective-permute-done.3.refs_0_), channel_id=1, source_target_pairs={{0,24},{1,25},{2,26},{3,27},{4,28},{5,29},{6,30},{7,31},{8,16},{9,... | collective-permute-start | bytes 245768 | tf_op jit(solution)/shard_map/send_home/ppermute | solution.py:255
  43.6 0.1 collective-permute-start.6
  43.7 0.9 %gradient.1 = (bf16[80,640]{1,0:T(8,128)(2,1)S(1)}, bf16[80,640]{1,0:T(8,128)(2,1)S(1)}, bf16[80,640]{1,0:T(8,128)(2,1)S(1)}, bf16[80,640]{1,0:T(8,128)(2,1)S(1)}) custom-call(bf16[4,160,128]{2,1,0:T(8,128)(2,1)S(1)} %get-tuple-element.31.refs_0_, bf16[4,160,128]{2,1,0:T(8,128)(2,1)S(1)} %collective-permute-done.9.refs_1_, ...), custom_call_target="tpu_custom_call" | custom-call | flops 419430400 | bytes 2621440 | tf_op jit(solution)/shard_map/gradient/pallas_call | solution.py:39
  44.7 2.4 %collective-permute-start.14 = (bf16[80,640]{1,0:T(8,128)(2,1)S(1)}, bf16[80,640]{1,0:T(8,128)(2,1)S(1)}, u32[]{:S(2)}, u32[]{:S(2)}) collective-permute-start(bf16[80,640]{1,0:T(8,128)(2,1)S(1)} %get-tuple-element.34), channel_id=1, source_target_pairs={{0,6},{1,7},{2,12},{3,13},{4,18},{5,19},{6,24},{7,25},{8,14},{9,15... | collective-permute-start | bytes 307208 | tf_op jit(solution)/shard_map/sum_gradient/ppermute | solution.py:255
  47.1 0.8 %collective-permute-start.15 = (bf16[80,640]{1,0:T(8,128)(2,1)S(1)}, bf16[80,640]{1,0:T(8,128)(2,1)S(1)}, u32[]{:S(2)}, u32[]{:S(2)}) collective-permute-start(bf16[80,640]{1,0:T(8,128)(2,1)S(1)} %get-tuple-element.35), channel_id=1, source_target_pairs={{0,4},{1,5},{2,14},{3,15},{4,16},{5,17},{6,26},{7,27},{8,12},{9,13... | collective-permute-start | bytes 307208 | tf_op jit(solution)/shard_map/sum_gradient/ppermute | solution.py:255
  47.9 3.5 %collective-permute-start.16 = (bf16[80,640]{1,0:T(8,128)(2,1)S(1)}, bf16[80,640]{1,0:T(8,128)(2,1)S(1)}, u32[]{:S(2)}, u32[]{:S(2)}) collective-permute-start(bf16[80,640]{1,0:T(8,128)(2,1)S(1)} %get-tuple-element.36), channel_id=1, source_target_pairs={{0,2},{1,3},{2,8},{3,9},{4,22},{5,23},{6,28},{7,29},{8,10},{9,11},... | collective-permute-start | bytes 307208 | tf_op jit(solution)/shard_map/sum_gradient/ppermute | solution.py:255
  51.4 0.7 %collective-permute-start.17 = (bf16[80,640]{1,0:T(8,128)(2,1)S(1)}, bf16[80,640]{1,0:T(8,128)(2,1)S(1)}, u32[]{:S(2)}, u32[]{:S(2)}) collective-permute-start(bf16[80,640]{1,0:T(8,128)(2,1)S(1)} %get-tuple-element.37), channel_id=1, source_target_pairs={{0,0},{1,1},{2,10},{3,11},{4,20},{5,21},{6,30},{7,31},{8,8},{9,9},... | collective-permute-start | bytes 307208 | tf_op jit(solution)/shard_map/sum_gradient/ppermute | solution.py:255
  52.0 1.0 %collective-permute-start.8 = (bf16[320,128]{1,0:T(8,128)(2,1)S(1)}, bf16[320,128]{1,0:T(8,128)(2,1)S(1)}, u32[]{:S(2)}, u32[]{:S(2)}) collective-permute-start(bf16[320,128]{1,0:T(8,128)(2,1)S(1)} %collective-permute-done.7.refs_2_), channel_id=1, source_target_pairs={{0,8},{1,9},{2,10},{3,11},{4,12},{5,13},{6,14},{7,15},{8,0},{9,1},... | collective-permute-start | bytes 245768 | tf_op jit(solution)/shard_map/send_home/ppermute | solution.py:255
  53.0 4.5 %collective-permute-done.8.refs_2_ = bf16[320,128]{1,0:T(8,128)(2,1)S(1)} collective-permute-done((bf16[320,128]{1,0:T(8,128)(2,1)S(1)}, bf16[320,128]{1,0:T(8,128)(2,1)S(1)}, u32[]{:S(2)}, u32[]{:S(2)}) %collective-permute-start.8) | collective-permute-done | bytes 81952 | tf_op jit(solution)/shard_map/send_home/ppermute | solution.py:255
  57.5 1.4 %project.1 = bf16[128,1280]{1,0:T(8,128)(2,1)} custom-call(bf16[320,128]{1,0:T(8,128)(2,1)S(1)} %collective-permute-done.4.refs_0_, bf16[320,128]{1,0:T(8,128)(2,1)S(1)} %collective-permute-done.6.refs_1_, bf16[320,128]{1,0:T(8,128)(2,1)S(1)} %collective-permute-done.8.refs_2_, bf16[320,128]{1,0:T(8,128)(2,1)S(1)} %get-tuple-element.30.refs_3_, ...), custom_call_target="tpu_custom_call" | custom-call | flops 209715200 | bytes 3276800 | tf_op jit(solution)/shard_map/project/pallas_call | solution.py:39
  58.9 0.8 %add_gradient.1 = f32[160,320]{1,0:T(8,128)} custom-call(bf16[80,640]{1,0:T(8,128)(2,1)S(1)} %collective-permute-done.14.refs_0_, bf16[80,640]{1,0:T(8,128)(2,1)S(1)} %collective-permute-done.15.refs_1_, bf16[80,640]{1,0:T(8,128)(2,1)S(1)} %collective-permute-done.16.refs_2_, bf16[80,640]{1,0:T(8,128)(2,1)S(1)} %collective-permute-done.17.refs_3_), custom_call_target="tpu_custom_call" | custom-call | bytes 819200 | tf_op jit(solution)/shard_map/add_gradient/pallas_call | solution.py:39
  (16 shorter events, 0.1 us)
Async XLA Ops:
  2.2 12.1 %collective-permute-start = (bf16[976,128]{1,0:T(8,128)(2,1)S(1)}, bf16[976,128]{1,0:T(8,128)(2,1)S(1)}, u32[]{:S(2)}, u32[]{:S(2)}) collective-permute-start(bf16[976,128]{1,0:T(8,128)(2,1)S(1)} %get-tuple-element.21), channel_id=1, source_target_pairs={{0,6},{1,7},{2,4},{3,5},{4,2},{5,3},{6,0},{7,1},{8,14},{9,15},{10,... | collective-permute-start | bytes 749576 | tf_op jit(solution)/shard_map/exchange_heads/ppermute | solution.py:255
  7.3 12.5 %collective-permute-start.1 = (bf16[976,128]{1,0:T(8,128)(2,1)S(1)}, bf16[976,128]{1,0:T(8,128)(2,1)S(1)}, u32[]{:S(2)}, u32[]{:S(2)}) collective-permute-start(bf16[976,128]{1,0:T(8,128)(2,1)S(1)} %get-tuple-element.22), channel_id=1, source_target_pairs={{0,2},{1,3},{2,0},{3,1},{4,6},{5,7},{6,4},{7,5},{8,10},{9,11},{10,... | collective-permute-start | bytes 749576 | tf_op jit(solution)/shard_map/exchange_heads/ppermute | solution.py:255
  7.3 21.2 %collective-permute-start.2 = (bf16[976,128]{1,0:T(8,128)(2,1)S(1)}, bf16[976,128]{1,0:T(8,128)(2,1)S(1)}, u32[]{:S(2)}, u32[]{:S(2)}) collective-permute-start(bf16[976,128]{1,0:T(8,128)(2,1)S(1)} %get-tuple-element.23), channel_id=1, source_target_pairs={{0,4},{1,5},{2,6},{3,7},{4,0},{5,1},{6,2},{7,3},{8,12},{9,13},{10,... | collective-permute-start | bytes 749576 | tf_op jit(solution)/shard_map/exchange_heads/ppermute | solution.py:255
  7.9 27.2 %collective-permute-start.12 = (bf16[128,1280]{1,0:T(8,128)(2,1)S(1)}, bf16[128,1280]{1,0:T(8,128)(2,1)S(1)}, u32[]{:S(2)}, u32[]{:S(2)}) collective-permute-start(bf16[128,1280]{1,0:T(8,128)(2,1)S(1)} %get-tuple-element.33.refs_0_), channel_id=1, source_target_pairs={{0,24},{1,25},{2,26},{3,27},{4,28},{5,29},{6,30},{7,31},{8,16},{9,... | collective-permute-start | bytes 983048 | tf_op jit(solution)/shard_map/gather_cotangent/ppermute | solution.py:255
  10.5 26.4 %collective-permute-start.11 = (bf16[128,1280]{1,0:T(8,128)(2,1)S(1)}, bf16[128,1280]{1,0:T(8,128)(2,1)S(1)}, u32[]{:S(2)}, u32[]{:S(2)}) collective-permute-start(bf16[128,1280]{1,0:T(8,128)(2,1)S(1)} %get-tuple-element.33.refs_0_), channel_id=1, source_target_pairs={{0,16},{1,17},{2,18},{3,19},{4,20},{5,21},{6,22},{7,23},{8,24},{9,... | collective-permute-start | bytes 983048 | tf_op jit(solution)/shard_map/gather_cotangent/ppermute | solution.py:255
  14.2 22.7 %collective-permute-start.10 = (bf16[128,1280]{1,0:T(8,128)(2,1)S(1)}, bf16[128,1280]{1,0:T(8,128)(2,1)S(1)}, u32[]{:S(2)}, u32[]{:S(2)}) collective-permute-start(bf16[128,1280]{1,0:T(8,128)(2,1)S(1)} %get-tuple-element.33.refs_0_), channel_id=1, source_target_pairs={{0,8},{1,9},{2,10},{3,11},{4,12},{5,13},{6,14},{7,15},{8,0},{9,1},... | collective-permute-start | bytes 983048 | tf_op jit(solution)/shard_map/gather_cotangent/ppermute | solution.py:255
  30.7 8.3 %collective-permute-start.3 = (bf16[320,128]{1,0:T(8,128)(2,1)S(1)}, bf16[320,128]{1,0:T(8,128)(2,1)S(1)}, u32[]{:S(2)}, u32[]{:S(2)}) collective-permute-start(bf16[320,128]{1,0:T(8,128)(2,1)S(1)} %get-tuple-element.27), channel_id=1, source_target_pairs={{0,30},{1,31},{2,28},{3,29},{4,26},{5,27},{6,24},{7,25},{8,22},{9,... | collective-permute-start | bytes 245768 | tf_op jit(solution)/shard_map/send_to_owner/ppermute | solution.py:255
  35.1 6.3 %collective-permute-start.5 = (bf16[320,128]{1,0:T(8,128)(2,1)S(1)}, bf16[320,128]{1,0:T(8,128)(2,1)S(1)}, u32[]{:S(2)}, u32[]{:S(2)}) collective-permute-start(bf16[320,128]{1,0:T(8,128)(2,1)S(1)} %get-tuple-element.28), channel_id=1, source_target_pairs={{0,20},{1,21},{2,22},{3,23},{4,16},{5,17},{6,18},{7,19},{8,28},{9,... | collective-permute-start | bytes 245768 | tf_op jit(solution)/shard_map/send_to_owner/ppermute | solution.py:255
  35.1 6.9 %collective-permute-start.7 = (bf16[320,128]{1,0:T(8,128)(2,1)S(1)}, bf16[320,128]{1,0:T(8,128)(2,1)S(1)}, u32[]{:S(2)}, u32[]{:S(2)}) collective-permute-start(bf16[320,128]{1,0:T(8,128)(2,1)S(1)} %get-tuple-element.29), channel_id=1, source_target_pairs={{0,10},{1,11},{2,8},{3,9},{4,14},{5,15},{6,12},{7,13},{8,2},{9,3},... | collective-permute-start | bytes 245768 | tf_op jit(solution)/shard_map/send_to_owner/ppermute | solution.py:255
  37.4 6.3 %collective-permute-start.13 = (bf16[4,128,1280]{2,1,0:T(8,128)(2,1)S(1)}, bf16[4,128,1280]{2,1,0:T(8,128)(2,1)S(1)}, u32[]{:S(2)}, u32[]{:S(2)}) collective-permute-start(bf16[4,128,1280]{2,1,0:T(8,128)(2,1)S(1)} %swap_cotangent.1.refs_2_), channel_id=1, source_target_pairs={{0,1},{1,0},{2,3},{3,2},{4,5},{5,4},{6,7},{7,6},{8,9},{9,8},{10,11... | collective-permute-start | bytes 3932168 | tf_op jit(solution)/shard_map/gradient/ppermute | solution.py:255
  42.0 15.5 %copy-start = (bf16[1280,1280]{1,0:T(8,128)(2,1)S(1)}, bf16[1280,1280]{1,0:T(8,128)(2,1)}, u32[]{:S(2)}) copy-start(bf16[1280,1280]{1,0:T(8,128)(2,1)} %refs_5_.1) | copy-start | bytes 9830404
  42.1 1.7 %collective-permute-start.9 = (bf16[4,160,128]{2,1,0:T(8,128)(2,1)S(1)}, bf16[4,160,128]{2,1,0:T(8,128)(2,1)S(1)}, u32[]{:S(2)}, u32[]{:S(2)}) collective-permute-start(bf16[4,160,128]{2,1,0:T(8,128)(2,1)S(1)} %get-tuple-element.32), channel_id=1, source_target_pairs={{0,1},{1,0},{2,3},{3,2},{4,5},{5,4},{6,7},{7,6},{8,9},{9,8},{10,11... | collective-permute-start | bytes 491528 | tf_op jit(solution)/shard_map/send_to_owner/ppermute | solution.py:255
  42.1 9.2 %collective-permute-start.4 = (bf16[320,128]{1,0:T(8,128)(2,1)S(1)}, bf16[320,128]{1,0:T(8,128)(2,1)S(1)}, u32[]{:S(2)}, u32[]{:S(2)}) collective-permute-start(bf16[320,128]{1,0:T(8,128)(2,1)S(1)} %collective-permute-done.3.refs_0_), channel_id=1, source_target_pairs={{0,24},{1,25},{2,26},{3,27},{4,28},{5,29},{6,30},{7,31},{8,16},{9,... | collective-permute-start | bytes 245768 | tf_op jit(solution)/shard_map/send_home/ppermute | solution.py:255
  43.6 8.4 %collective-permute-start.6 = (bf16[320,128]{1,0:T(8,128)(2,1)S(1)}, bf16[320,128]{1,0:T(8,128)(2,1)S(1)}, u32[]{:S(2)}, u32[]{:S(2)}) collective-permute-start(bf16[320,128]{1,0:T(8,128)(2,1)S(1)} %collective-permute-done.5.refs_1_), channel_id=1, source_target_pairs={{0,16},{1,17},{2,18},{3,19},{4,20},{5,21},{6,22},{7,23},{8,24},{9,... | collective-permute-start | bytes 245768 | tf_op jit(solution)/shard_map/send_home/ppermute | solution.py:255
  43.7 13.8 %copy-start.1 = (bf16[128,1280]{1,0:T(8,128)(2,1)S(1)}, bf16[128,1280]{1,0:T(8,128)(2,1)}, u32[]{:S(2)}) copy-start(bf16[128,1280]{1,0:T(8,128)(2,1)} %refs_4_.3) | copy-start | bytes 983044
  44.7 14.2 %collective-permute-start.14 = (bf16[80,640]{1,0:T(8,128)(2,1)S(1)}, bf16[80,640]{1,0:T(8,128)(2,1)S(1)}, u32[]{:S(2)}, u32[]{:S(2)}) collective-permute-start(bf16[80,640]{1,0:T(8,128)(2,1)S(1)} %get-tuple-element.34), channel_id=1, source_target_pairs={{0,6},{1,7},{2,12},{3,13},{4,18},{5,19},{6,24},{7,25},{8,14},{9,15... | collective-permute-start | bytes 307208 | tf_op jit(solution)/shard_map/sum_gradient/ppermute | solution.py:255
  47.1 11.8 %collective-permute-start.15 = (bf16[80,640]{1,0:T(8,128)(2,1)S(1)}, bf16[80,640]{1,0:T(8,128)(2,1)S(1)}, u32[]{:S(2)}, u32[]{:S(2)}) collective-permute-start(bf16[80,640]{1,0:T(8,128)(2,1)S(1)} %get-tuple-element.35), channel_id=1, source_target_pairs={{0,4},{1,5},{2,14},{3,15},{4,16},{5,17},{6,26},{7,27},{8,12},{9,13... | collective-permute-start | bytes 307208 | tf_op jit(solution)/shard_map/sum_gradient/ppermute | solution.py:255
  47.9 11.0 %collective-permute-start.16 = (bf16[80,640]{1,0:T(8,128)(2,1)S(1)}, bf16[80,640]{1,0:T(8,128)(2,1)S(1)}, u32[]{:S(2)}, u32[]{:S(2)}) collective-permute-start(bf16[80,640]{1,0:T(8,128)(2,1)S(1)} %get-tuple-element.36), channel_id=1, source_target_pairs={{0,2},{1,3},{2,8},{3,9},{4,22},{5,23},{6,28},{7,29},{8,10},{9,11},... | collective-permute-start | bytes 307208 | tf_op jit(solution)/shard_map/sum_gradient/ppermute | solution.py:255
  51.4 7.5 %collective-permute-start.17 = (bf16[80,640]{1,0:T(8,128)(2,1)S(1)}, bf16[80,640]{1,0:T(8,128)(2,1)S(1)}, u32[]{:S(2)}, u32[]{:S(2)}) collective-permute-start(bf16[80,640]{1,0:T(8,128)(2,1)S(1)} %get-tuple-element.37), channel_id=1, source_target_pairs={{0,0},{1,1},{2,10},{3,11},{4,20},{5,21},{6,30},{7,31},{8,8},{9,9},... | collective-permute-start | bytes 307208 | tf_op jit(solution)/shard_map/sum_gradient/ppermute | solution.py:255
  52.0 5.5 %collective-permute-start.8 = (bf16[320,128]{1,0:T(8,128)(2,1)S(1)}, bf16[320,128]{1,0:T(8,128)(2,1)S(1)}, u32[]{:S(2)}, u32[]{:S(2)}) collective-permute-start(bf16[320,128]{1,0:T(8,128)(2,1)S(1)} %collective-permute-done.7.refs_2_), channel_id=1, source_target_pairs={{0,8},{1,9},{2,10},{3,11},{4,12},{5,13},{6,14},{7,15},{8,0},{9,1},... | collective-permute-start | bytes 245768 | tf_op jit(solution)/shard_map/send_home/ppermute | solution.py:255

commit v4 on v3

--- a/solution.py
+++ b/solution.py
@@ -13,8 +13,8 @@
 ID_ROWS = 16
 ID_BASE = 64
 SENDS = (0, 3, 1, 2)
-RETURNS = (3, 2, 1, 0)
-SUMS = (3, 2, 1, 0)
+RETURNS = (1, 3, 2, 0)
+SUMS = (1, 3, 2, 0)
 
 
 def call(
@@ -358,7 +358,7 @@
             residual,
             out_weight,
             scratch=[pltpu.VMEM((width, rows), jnp.bfloat16)],
-            flops=rows * width * width,
+            flops=2 * rows * width * width,
             bytes_accessed=2 * width * width,
         )
     with jax.named_scope("add_gradient"):

time: 60.6 us -> 62.2 us (1.026); the launches traced: 59.7 us -> 62 us
  waiting for transfers between devices: 23.2 us -> 27.2 us
  starting transfers between devices: 26.8 us -> 25.2 us
    ppermute x18, waiting for transfers between devices: 23.2 us -> 27.2 us  [move(): return lax.ppermute(data, AXES, pairs)]
    ppermute x18, starting transfers between devices: 26.8 us -> 25.2 us  [move(): return lax.ppermute(data, AXES, pairs)]
where the time goes in v4:
time: 62.2 us; the launch traced here: 62 us
  waiting for transfers between devices  27.2 us (44%)
  starting transfers between devices  25.2 us (41%)
  Pallas kernels  8.9 us (14%)
  between operations  0.75 us (1%)
    ppermute x18, waiting for transfers between devices, move(): return lax.ppermute(data, AXES, pairs)  27.2 us
    ppermute x18, starting transfers between devices, move(): return lax.ppermute(data, AXES, pairs)  25.2 us
    pallas_call x8, Pallas kernels, call(): pl.pallas_call(kernel, out_shape=out_shape, in_specs=[placed(space) for s...  8.9 us
  transfers between devices with their start and end apart: 18, of which 7 were waited for; matrix products, arithmetic and copies ran while one was open for 0% of the time, Pallas kernels for 11%

profile of v4, /device:TPU:0, one launch (start us, length us, event | category | flops | bytes accessed | tf_op | source)
XLA Modules:
  0.0 62.0 jit_solution(1467048909373683415)
XLA Ops:
  0.6 1.5 %pack.1 = (bf16[976,128]{1,0:T(8,128)(2,1)S(1)}, bf16[976,128]{1,0:T(8,128)(2,1)S(1)}, bf16[976,128]{1,0:T(8,128)(2,1)S(1)}, bf16[976,128]{1,0:T(8,128)(2,1)S(1)}, bf16[128,1280]{1,0:T(8,128)(2,1)S(1)}) custom-call(s32[1,128]{1,0:T(1,128)} %bitcast.1, bf16[128,1280]{1,0:T(8,128)(2,1)} %refs_1_.1, bf16[128,1280]{1,0:T(8,128)(2,1)} %refs_2_.1, ...), custom_call_target="tpu_custom_call" | custom-call | bytes 2621440 | tf_op jit(solution)/shard_map/pack/pallas_call | solution.py:39
  2.2 5.1 %collective-permute-start = (bf16[976,128]{1,0:T(8,128)(2,1)S(1)}, bf16[976,128]{1,0:T(8,128)(2,1)S(1)}, u32[]{:S(2)}, u32[]{:S(2)}) collective-permute-start(bf16[976,128]{1,0:T(8,128)(2,1)S(1)} %get-tuple-element.21), channel_id=1, source_target_pairs={{0,6},{1,7},{2,4},{3,5},{4,2},{5,3},{6,0},{7,1},{8,14},{9,15},{10,... | collective-permute-start | bytes 749576 | tf_op jit(solution)/shard_map/exchange_heads/ppermute | solution.py:255
  7.3 0.0 collective-permute-start.1
  7.3 0.6 %collective-permute-start.2 = (bf16[976,128]{1,0:T(8,128)(2,1)S(1)}, bf16[976,128]{1,0:T(8,128)(2,1)S(1)}, u32[]{:S(2)}, u32[]{:S(2)}) collective-permute-start(bf16[976,128]{1,0:T(8,128)(2,1)S(1)} %get-tuple-element.23), channel_id=1, source_target_pairs={{0,4},{1,5},{2,6},{3,7},{4,0},{5,1},{6,2},{7,3},{8,12},{9,13},{10,... | collective-permute-start | bytes 749576 | tf_op jit(solution)/shard_map/exchange_heads/ppermute | solution.py:255
  7.9 2.6 %collective-permute-start.12 = (bf16[128,1280]{1,0:T(8,128)(2,1)S(1)}, bf16[128,1280]{1,0:T(8,128)(2,1)S(1)}, u32[]{:S(2)}, u32[]{:S(2)}) collective-permute-start(bf16[128,1280]{1,0:T(8,128)(2,1)S(1)} %get-tuple-element.33.refs_0_), channel_id=1, source_target_pairs={{0,24},{1,25},{2,26},{3,27},{4,28},{5,29},{6,30},{7,31},{8,16},{9,... | collective-permute-start | bytes 983048 | tf_op jit(solution)/shard_map/gather_cotangent/ppermute | solution.py:255
  10.5 0.5 collective-permute-start.11
  11.0 3.2 %collective-permute-done.refs_1_ = bf16[976,128]{1,0:T(8,128)(2,1)S(1)} collective-permute-done((bf16[976,128]{1,0:T(8,128)(2,1)S(1)}, bf16[976,128]{1,0:T(8,128)(2,1)S(1)}, u32[]{:S(2)}, u32[]{:S(2)}) %collective-permute-start) | collective-permute-done | bytes 249888 | tf_op jit(solution)/shard_map/exchange_heads/ppermute | solution.py:255
  14.2 1.7 %collective-permute-start.10 = (bf16[128,1280]{1,0:T(8,128)(2,1)S(1)}, bf16[128,1280]{1,0:T(8,128)(2,1)S(1)}, u32[]{:S(2)}, u32[]{:S(2)}) collective-permute-start(bf16[128,1280]{1,0:T(8,128)(2,1)S(1)} %get-tuple-element.33.refs_0_), channel_id=1, source_target_pairs={{0,8},{1,9},{2,10},{3,11},{4,12},{5,13},{6,14},{7,15},{8,0},{9,1},... | collective-permute-start | bytes 983048 | tf_op jit(solution)/shard_map/gather_cotangent/ppermute | solution.py:255
  15.9 3.9 %collective-permute-done.1.refs_2_ = bf16[976,128]{1,0:T(8,128)(2,1)S(1)} collective-permute-done((bf16[976,128]{1,0:T(8,128)(2,1)S(1)}, bf16[976,128]{1,0:T(8,128)(2,1)S(1)}, u32[]{:S(2)}, u32[]{:S(2)}) %collective-permute-start.1) | collective-permute-done | bytes 249888 | tf_op jit(solution)/shard_map/exchange_heads/ppermute | solution.py:255
  19.8 1.7 %attention.2 = (f32[320,384]{1,0:T(8,128)S(1)}, f32[8,384]{1,0:T(8,128)S(1)}, f32[8,384]{1,0:T(8,128)S(1)}) custom-call(bf16[976,128]{1,0:T(8,128)(2,1)S(1)} %get-tuple-element.20.refs_0_, bf16[976,128]{1,0:T(8,128)(2,1)S(1)} %collective-permute-done.refs_1_, bf16[976,128]{1,0:T(8,128)(2,1)S(1)} %collective-permute-done.1.refs_2_), custom_call_target="tpu_custom_call" | custom-call | flops 2595225600 | bytes 1310720 | tf_op jit(solution)/shard_map/attention/pallas_call | solution.py:39
  21.5 7.0 %collective-permute-done.2.refs_3_ = bf16[976,128]{1,0:T(8,128)(2,1)S(1)} collective-permute-done((bf16[976,128]{1,0:T(8,128)(2,1)S(1)}, bf16[976,128]{1,0:T(8,128)(2,1)S(1)}, u32[]{:S(2)}, u32[]{:S(2)}) %collective-permute-start.2) | collective-permute-done | bytes 249888 | tf_op jit(solution)/shard_map/exchange_heads/ppermute | solution.py:255
  28.5 2.1 %attention.3 = (bf16[320,128]{1,0:T(8,128)(2,1)S(1)}, bf16[320,128]{1,0:T(8,128)(2,1)S(1)}, bf16[320,128]{1,0:T(8,128)(2,1)S(1)}, bf16[320,128]{1,0:T(8,128)(2,1)S(1)}) custom-call(bf16[976,128]{1,0:T(8,128)(2,1)S(1)} %get-tuple-element.20.refs_0_, bf16[976,128]{1,0:T(8,128)(2,1)S(1)} %collective-permute-done.refs_1_, ...), custom_call_target="tpu_custom_call" | custom-call | flops 2018508800 | bytes 1310720 | tf_op jit(solution)/shard_map/attention/pallas_call | solution.py:39
  30.7 0.7 %collective-permute-start.3 = (bf16[320,128]{1,0:T(8,128)(2,1)S(1)}, bf16[320,128]{1,0:T(8,128)(2,1)S(1)}, u32[]{:S(2)}, u32[]{:S(2)}) collective-permute-start(bf16[320,128]{1,0:T(8,128)(2,1)S(1)} %get-tuple-element.27), channel_id=1, source_target_pairs={{0,10},{1,11},{2,8},{3,9},{4,14},{5,15},{6,12},{7,13},{8,2},{9,3},... | collective-permute-start | bytes 245768 | tf_op jit(solution)/shard_map/send_to_owner/ppermute | solution.py:255
  31.3 3.8 %collective-permute-start.5 = (bf16[320,128]{1,0:T(8,128)(2,1)S(1)}, bf16[320,128]{1,0:T(8,128)(2,1)S(1)}, u32[]{:S(2)}, u32[]{:S(2)}) collective-permute-start(bf16[320,128]{1,0:T(8,128)(2,1)S(1)} %get-tuple-element.28), channel_id=1, source_target_pairs={{0,30},{1,31},{2,28},{3,29},{4,26},{5,27},{6,24},{7,25},{8,22},{9,... | collective-permute-start | bytes 245768 | tf_op jit(solution)/shard_map/send_to_owner/ppermute | solution.py:255
  35.2 0.8 %collective-permute-start.7 = (bf16[320,128]{1,0:T(8,128)(2,1)S(1)}, bf16[320,128]{1,0:T(8,128)(2,1)S(1)}, u32[]{:S(2)}, u32[]{:S(2)}) collective-permute-start(bf16[320,128]{1,0:T(8,128)(2,1)S(1)} %get-tuple-element.29), channel_id=1, source_target_pairs={{0,20},{1,21},{2,22},{3,23},{4,16},{5,17},{6,18},{7,19},{8,28},{9,... | collective-permute-start | bytes 245768 | tf_op jit(solution)/shard_map/send_to_owner/ppermute | solution.py:255
  36.0 0.4 swap_cotangent.1.refs_2_
  36.5 0.1 collective-permute-start.13
  36.6 2.9 %collective-permute-done.5.refs_1_ = bf16[320,128]{1,0:T(8,128)(2,1)S(1)} collective-permute-done((bf16[320,128]{1,0:T(8,128)(2,1)S(1)}, bf16[320,128]{1,0:T(8,128)(2,1)S(1)}, u32[]{:S(2)}, u32[]{:S(2)}) %collective-permute-start.5) | collective-permute-done | bytes 81952 | tf_op jit(solution)/shard_map/send_to_owner/ppermute | solution.py:255
  39.5 3.3 %collective-permute-done.7.refs_2_ = bf16[320,128]{1,0:T(8,128)(2,1)S(1)} collective-permute-done((bf16[320,128]{1,0:T(8,128)(2,1)S(1)}, bf16[320,128]{1,0:T(8,128)(2,1)S(1)}, u32[]{:S(2)}, u32[]{:S(2)}) %collective-permute-start.7) | collective-permute-done | bytes 81952 | tf_op jit(solution)/shard_map/send_to_owner/ppermute | solution.py:255
  42.9 0.1 collective-permute-start.9
  42.9 1.3 %collective-permute-start.4 = (bf16[320,128]{1,0:T(8,128)(2,1)S(1)}, bf16[320,128]{1,0:T(8,128)(2,1)S(1)}, u32[]{:S(2)}, u32[]{:S(2)}) collective-permute-start(bf16[320,128]{1,0:T(8,128)(2,1)S(1)} %collective-permute-done.3.refs_0_), channel_id=1, source_target_pairs={{0,8},{1,9},{2,10},{3,11},{4,12},{5,13},{6,14},{7,15},{8,0},{9,1},... | collective-permute-start | bytes 245768 | tf_op jit(solution)/shard_map/send_home/ppermute | solution.py:255
  44.2 1.4 %collective-permute-start.6 = (bf16[320,128]{1,0:T(8,128)(2,1)S(1)}, bf16[320,128]{1,0:T(8,128)(2,1)S(1)}, u32[]{:S(2)}, u32[]{:S(2)}) collective-permute-start(bf16[320,128]{1,0:T(8,128)(2,1)S(1)} %collective-permute-done.5.refs_1_), channel_id=1, source_target_pairs={{0,24},{1,25},{2,26},{3,27},{4,28},{5,29},{6,30},{7,31},{8,16},{9,... | collective-permute-start | bytes 245768 | tf_op jit(solution)/shard_map/send_home/ppermute | solution.py:255
  45.7 0.8 %collective-permute-start.8 = (bf16[320,128]{1,0:T(8,128)(2,1)S(1)}, bf16[320,128]{1,0:T(8,128)(2,1)S(1)}, u32[]{:S(2)}, u32[]{:S(2)}) collective-permute-start(bf16[320,128]{1,0:T(8,128)(2,1)S(1)} %collective-permute-done.7.refs_2_), channel_id=1, source_target_pairs={{0,16},{1,17},{2,18},{3,19},{4,20},{5,21},{6,22},{7,23},{8,24},{9,... | collective-permute-start | bytes 245768 | tf_op jit(solution)/shard_map/send_home/ppermute | solution.py:255
  46.5 0.9 %gradient.1 = (bf16[80,640]{1,0:T(8,128)(2,1)S(1)}, bf16[80,640]{1,0:T(8,128)(2,1)S(1)}, bf16[80,640]{1,0:T(8,128)(2,1)S(1)}, bf16[80,640]{1,0:T(8,128)(2,1)S(1)}) custom-call(bf16[4,160,128]{2,1,0:T(8,128)(2,1)S(1)} %get-tuple-element.31.refs_0_, bf16[4,160,128]{2,1,0:T(8,128)(2,1)S(1)} %collective-permute-done.9.refs_1_, ...), custom_call_target="tpu_custom_call" | custom-call | flops 419430400 | bytes 2621440 | tf_op jit(solution)/shard_map/gradient/pallas_call | solution.py:39
  47.4 0.2 collective-permute-start.14
  47.6 3.3 %collective-permute-start.15 = (bf16[80,640]{1,0:T(8,128)(2,1)S(1)}, bf16[80,640]{1,0:T(8,128)(2,1)S(1)}, u32[]{:S(2)}, u32[]{:S(2)}) collective-permute-start(bf16[80,640]{1,0:T(8,128)(2,1)S(1)} %get-tuple-element.35), channel_id=1, source_target_pairs={{0,6},{1,7},{2,12},{3,13},{4,18},{5,19},{6,24},{7,25},{8,14},{9,15... | collective-permute-start | bytes 307208 | tf_op jit(solution)/shard_map/sum_gradient/ppermute | solution.py:255
  51.0 1.4 %collective-permute-start.16 = (bf16[80,640]{1,0:T(8,128)(2,1)S(1)}, bf16[80,640]{1,0:T(8,128)(2,1)S(1)}, u32[]{:S(2)}, u32[]{:S(2)}) collective-permute-start(bf16[80,640]{1,0:T(8,128)(2,1)S(1)} %get-tuple-element.36), channel_id=1, source_target_pairs={{0,4},{1,5},{2,14},{3,15},{4,16},{5,17},{6,26},{7,27},{8,12},{9,13... | collective-permute-start | bytes 307208 | tf_op jit(solution)/shard_map/sum_gradient/ppermute | solution.py:255
  52.4 0.7 %collective-permute-start.17 = (bf16[80,640]{1,0:T(8,128)(2,1)S(1)}, bf16[80,640]{1,0:T(8,128)(2,1)S(1)}, u32[]{:S(2)}, u32[]{:S(2)}) collective-permute-start(bf16[80,640]{1,0:T(8,128)(2,1)S(1)} %get-tuple-element.37), channel_id=1, source_target_pairs={{0,0},{1,1},{2,10},{3,11},{4,20},{5,21},{6,30},{7,31},{8,8},{9,9},... | collective-permute-start | bytes 307208 | tf_op jit(solution)/shard_map/sum_gradient/ppermute | solution.py:255
  53.1 1.4 %project.1 = bf16[128,1280]{1,0:T(8,128)(2,1)} custom-call(bf16[320,128]{1,0:T(8,128)(2,1)S(1)} %collective-permute-done.4.refs_0_, bf16[320,128]{1,0:T(8,128)(2,1)S(1)} %collective-permute-done.6.refs_1_, bf16[320,128]{1,0:T(8,128)(2,1)S(1)} %collective-permute-done.8.refs_2_, bf16[320,128]{1,0:T(8,128)(2,1)S(1)} %get-tuple-element.30.refs_3_, ...), custom_call_target="tpu_custom_call" | custom-call | flops 419430400 | bytes 3276800 | tf_op jit(solution)/shard_map/project/pallas_call | solution.py:39
  54.5 2.6 %collective-permute-done.15.refs_1_ = bf16[80,640]{1,0:T(8,128)(2,1)S(1)} collective-permute-done((bf16[80,640]{1,0:T(8,128)(2,1)S(1)}, bf16[80,640]{1,0:T(8,128)(2,1)S(1)}, u32[]{:S(2)}, u32[]{:S(2)}) %collective-permute-start.15) | collective-permute-done | bytes 102432 | tf_op jit(solution)/shard_map/sum_gradient/ppermute | solution.py:255
  57.1 4.1 %collective-permute-done.16.refs_2_ = bf16[80,640]{1,0:T(8,128)(2,1)S(1)} collective-permute-done((bf16[80,640]{1,0:T(8,128)(2,1)S(1)}, bf16[80,640]{1,0:T(8,128)(2,1)S(1)}, u32[]{:S(2)}, u32[]{:S(2)}) %collective-permute-start.16) | collective-permute-done | bytes 102432 | tf_op jit(solution)/shard_map/sum_gradient/ppermute | solution.py:255
  61.2 0.8 %add_gradient.1 = f32[160,320]{1,0:T(8,128)} custom-call(bf16[80,640]{1,0:T(8,128)(2,1)S(1)} %collective-permute-done.14.refs_0_, bf16[80,640]{1,0:T(8,128)(2,1)S(1)} %collective-permute-done.15.refs_1_, bf16[80,640]{1,0:T(8,128)(2,1)S(1)} %collective-permute-done.16.refs_2_, bf16[80,640]{1,0:T(8,128)(2,1)S(1)} %collective-permute-done.17.refs_3_), custom_call_target="tpu_custom_call" | custom-call | bytes 819200 | tf_op jit(solution)/shard_map/add_gradient/pallas_call | solution.py:39
  (16 shorter events, 0.1 us)
Async XLA Ops:
  2.2 12.1 %collective-permute-start = (bf16[976,128]{1,0:T(8,128)(2,1)S(1)}, bf16[976,128]{1,0:T(8,128)(2,1)S(1)}, u32[]{:S(2)}, u32[]{:S(2)}) collective-permute-start(bf16[976,128]{1,0:T(8,128)(2,1)S(1)} %get-tuple-element.21), channel_id=1, source_target_pairs={{0,6},{1,7},{2,4},{3,5},{4,2},{5,3},{6,0},{7,1},{8,14},{9,15},{10,... | collective-permute-start | bytes 749576 | tf_op jit(solution)/shard_map/exchange_heads/ppermute | solution.py:255
  7.3 12.5 %collective-permute-start.1 = (bf16[976,128]{1,0:T(8,128)(2,1)S(1)}, bf16[976,128]{1,0:T(8,128)(2,1)S(1)}, u32[]{:S(2)}, u32[]{:S(2)}) collective-permute-start(bf16[976,128]{1,0:T(8,128)(2,1)S(1)} %get-tuple-element.22), channel_id=1, source_target_pairs={{0,2},{1,3},{2,0},{3,1},{4,6},{5,7},{6,4},{7,5},{8,10},{9,11},{10,... | collective-permute-start | bytes 749576 | tf_op jit(solution)/shard_map/exchange_heads/ppermute | solution.py:255
  7.3 21.2 %collective-permute-start.2 = (bf16[976,128]{1,0:T(8,128)(2,1)S(1)}, bf16[976,128]{1,0:T(8,128)(2,1)S(1)}, u32[]{:S(2)}, u32[]{:S(2)}) collective-permute-start(bf16[976,128]{1,0:T(8,128)(2,1)S(1)} %get-tuple-element.23), channel_id=1, source_target_pairs={{0,4},{1,5},{2,6},{3,7},{4,0},{5,1},{6,2},{7,3},{8,12},{9,13},{10,... | collective-permute-start | bytes 749576 | tf_op jit(solution)/shard_map/exchange_heads/ppermute | solution.py:255
  7.9 27.3 %collective-permute-start.12 = (bf16[128,1280]{1,0:T(8,128)(2,1)S(1)}, bf16[128,1280]{1,0:T(8,128)(2,1)S(1)}, u32[]{:S(2)}, u32[]{:S(2)}) collective-permute-start(bf16[128,1280]{1,0:T(8,128)(2,1)S(1)} %get-tuple-element.33.refs_0_), channel_id=1, source_target_pairs={{0,24},{1,25},{2,26},{3,27},{4,28},{5,29},{6,30},{7,31},{8,16},{9,... | collective-permute-start | bytes 983048 | tf_op jit(solution)/shard_map/gather_cotangent/ppermute | solution.py:255
  10.5 25.5 %collective-permute-start.11 = (bf16[128,1280]{1,0:T(8,128)(2,1)S(1)}, bf16[128,1280]{1,0:T(8,128)(2,1)S(1)}, u32[]{:S(2)}, u32[]{:S(2)}) collective-permute-start(bf16[128,1280]{1,0:T(8,128)(2,1)S(1)} %get-tuple-element.33.refs_0_), channel_id=1, source_target_pairs={{0,16},{1,17},{2,18},{3,19},{4,20},{5,21},{6,22},{7,23},{8,24},{9,... | collective-permute-start | bytes 983048 | tf_op jit(solution)/shard_map/gather_cotangent/ppermute | solution.py:255
  14.2 21.8 %collective-permute-start.10 = (bf16[128,1280]{1,0:T(8,128)(2,1)S(1)}, bf16[128,1280]{1,0:T(8,128)(2,1)S(1)}, u32[]{:S(2)}, u32[]{:S(2)}) collective-permute-start(bf16[128,1280]{1,0:T(8,128)(2,1)S(1)} %get-tuple-element.33.refs_0_), channel_id=1, source_target_pairs={{0,8},{1,9},{2,10},{3,11},{4,12},{5,13},{6,14},{7,15},{8,0},{9,1},... | collective-permute-start | bytes 983048 | tf_op jit(solution)/shard_map/gather_cotangent/ppermute | solution.py:255
  30.7 5.9 %collective-permute-start.3 = (bf16[320,128]{1,0:T(8,128)(2,1)S(1)}, bf16[320,128]{1,0:T(8,128)(2,1)S(1)}, u32[]{:S(2)}, u32[]{:S(2)}) collective-permute-start(bf16[320,128]{1,0:T(8,128)(2,1)S(1)} %get-tuple-element.27), channel_id=1, source_target_pairs={{0,10},{1,11},{2,8},{3,9},{4,14},{5,15},{6,12},{7,13},{8,2},{9,3},... | collective-permute-start | bytes 245768 | tf_op jit(solution)/shard_map/send_to_owner/ppermute | solution.py:255
  31.3 8.2 %collective-permute-start.5 = (bf16[320,128]{1,0:T(8,128)(2,1)S(1)}, bf16[320,128]{1,0:T(8,128)(2,1)S(1)}, u32[]{:S(2)}, u32[]{:S(2)}) collective-permute-start(bf16[320,128]{1,0:T(8,128)(2,1)S(1)} %get-tuple-element.28), channel_id=1, source_target_pairs={{0,30},{1,31},{2,28},{3,29},{4,26},{5,27},{6,24},{7,25},{8,22},{9,... | collective-permute-start | bytes 245768 | tf_op jit(solution)/shard_map/send_to_owner/ppermute | solution.py:255
  35.2 7.6 %collective-permute-start.7 = (bf16[320,128]{1,0:T(8,128)(2,1)S(1)}, bf16[320,128]{1,0:T(8,128)(2,1)S(1)}, u32[]{:S(2)}, u32[]{:S(2)}) collective-permute-start(bf16[320,128]{1,0:T(8,128)(2,1)S(1)} %get-tuple-element.29), channel_id=1, source_target_pairs={{0,20},{1,21},{2,22},{3,23},{4,16},{5,17},{6,18},{7,19},{8,28},{9,... | collective-permute-start | bytes 245768 | tf_op jit(solution)/shard_map/send_to_owner/ppermute | solution.py:255
  36.5 10.0 %collective-permute-start.13 = (bf16[4,128,1280]{2,1,0:T(8,128)(2,1)S(1)}, bf16[4,128,1280]{2,1,0:T(8,128)(2,1)S(1)}, u32[]{:S(2)}, u32[]{:S(2)}) collective-permute-start(bf16[4,128,1280]{2,1,0:T(8,128)(2,1)S(1)} %swap_cotangent.1.refs_2_), channel_id=1, source_target_pairs={{0,1},{1,0},{2,3},{3,2},{4,5},{5,4},{6,7},{7,6},{8,9},{9,8},{10,11... | collective-permute-start | bytes 3932168 | tf_op jit(solution)/shard_map/gradient/ppermute | solution.py:255
  42.8 10.2 %copy-start = (bf16[1280,1280]{1,0:T(8,128)(2,1)S(1)}, bf16[1280,1280]{1,0:T(8,128)(2,1)}, u32[]{:S(2)}) copy-start(bf16[1280,1280]{1,0:T(8,128)(2,1)} %refs_5_.1) | copy-start | bytes 9830404
  42.9 3.6 %collective-permute-start.9 = (bf16[4,160,128]{2,1,0:T(8,128)(2,1)S(1)}, bf16[4,160,128]{2,1,0:T(8,128)(2,1)S(1)}, u32[]{:S(2)}, u32[]{:S(2)}) collective-permute-start(bf16[4,160,128]{2,1,0:T(8,128)(2,1)S(1)} %get-tuple-element.32), channel_id=1, source_target_pairs={{0,1},{1,0},{2,3},{3,2},{4,5},{5,4},{6,7},{7,6},{8,9},{9,8},{10,11... | collective-permute-start | bytes 491528 | tf_op jit(solution)/shard_map/send_to_owner/ppermute | solution.py:255
  42.9 8.0 %collective-permute-start.4 = (bf16[320,128]{1,0:T(8,128)(2,1)S(1)}, bf16[320,128]{1,0:T(8,128)(2,1)S(1)}, u32[]{:S(2)}, u32[]{:S(2)}) collective-permute-start(bf16[320,128]{1,0:T(8,128)(2,1)S(1)} %collective-permute-done.3.refs_0_), channel_id=1, source_target_pairs={{0,8},{1,9},{2,10},{3,11},{4,12},{5,13},{6,14},{7,15},{8,0},{9,1},... | collective-permute-start | bytes 245768 | tf_op jit(solution)/shard_map/send_home/ppermute | solution.py:255
  44.2 8.2 %collective-permute-start.6 = (bf16[320,128]{1,0:T(8,128)(2,1)S(1)}, bf16[320,128]{1,0:T(8,128)(2,1)S(1)}, u32[]{:S(2)}, u32[]{:S(2)}) collective-permute-start(bf16[320,128]{1,0:T(8,128)(2,1)S(1)} %collective-permute-done.5.refs_1_), channel_id=1, source_target_pairs={{0,24},{1,25},{2,26},{3,27},{4,28},{5,29},{6,30},{7,31},{8,16},{9,... | collective-permute-start | bytes 245768 | tf_op jit(solution)/shard_map/send_home/ppermute | solution.py:255
  45.7 7.4 %collective-permute-start.8 = (bf16[320,128]{1,0:T(8,128)(2,1)S(1)}, bf16[320,128]{1,0:T(8,128)(2,1)S(1)}, u32[]{:S(2)}, u32[]{:S(2)}) collective-permute-start(bf16[320,128]{1,0:T(8,128)(2,1)S(1)} %collective-permute-done.7.refs_2_), channel_id=1, source_target_pairs={{0,16},{1,17},{2,18},{3,19},{4,20},{5,21},{6,22},{7,23},{8,24},{9,... | collective-permute-start | bytes 245768 | tf_op jit(solution)/shard_map/send_home/ppermute | solution.py:255
  46.5 6.6 %copy-start.1 = (bf16[128,1280]{1,0:T(8,128)(2,1)S(1)}, bf16[128,1280]{1,0:T(8,128)(2,1)}, u32[]{:S(2)}) copy-start(bf16[128,1280]{1,0:T(8,128)(2,1)} %refs_4_.3) | copy-start | bytes 983044
  47.4 7.1 %collective-permute-start.14 = (bf16[80,640]{1,0:T(8,128)(2,1)S(1)}, bf16[80,640]{1,0:T(8,128)(2,1)S(1)}, u32[]{:S(2)}, u32[]{:S(2)}) collective-permute-start(bf16[80,640]{1,0:T(8,128)(2,1)S(1)} %get-tuple-element.34), channel_id=1, source_target_pairs={{0,2},{1,3},{2,8},{3,9},{4,22},{5,23},{6,28},{7,29},{8,10},{9,11},... | collective-permute-start | bytes 307208 | tf_op jit(solution)/shard_map/sum_gradient/ppermute | solution.py:255
  47.6 9.4 %collective-permute-start.15 = (bf16[80,640]{1,0:T(8,128)(2,1)S(1)}, bf16[80,640]{1,0:T(8,128)(2,1)S(1)}, u32[]{:S(2)}, u32[]{:S(2)}) collective-permute-start(bf16[80,640]{1,0:T(8,128)(2,1)S(1)} %get-tuple-element.35), channel_id=1, source_target_pairs={{0,6},{1,7},{2,12},{3,13},{4,18},{5,19},{6,24},{7,25},{8,14},{9,15... | collective-permute-start | bytes 307208 | tf_op jit(solution)/shard_map/sum_gradient/ppermute | solution.py:255
  51.0 10.2 %collective-permute-start.16 = (bf16[80,640]{1,0:T(8,128)(2,1)S(1)}, bf16[80,640]{1,0:T(8,128)(2,1)S(1)}, u32[]{:S(2)}, u32[]{:S(2)}) collective-permute-start(bf16[80,640]{1,0:T(8,128)(2,1)S(1)} %get-tuple-element.36), channel_id=1, source_target_pairs={{0,4},{1,5},{2,14},{3,15},{4,16},{5,17},{6,26},{7,27},{8,12},{9,13... | collective-permute-start | bytes 307208 | tf_op jit(solution)/shard_map/sum_gradient/ppermute | solution.py:255
  52.4 8.8 %collective-permute-start.17 = (bf16[80,640]{1,0:T(8,128)(2,1)S(1)}, bf16[80,640]{1,0:T(8,128)(2,1)S(1)}, u32[]{:S(2)}, u32[]{:S(2)}) collective-permute-start(bf16[80,640]{1,0:T(8,128)(2,1)S(1)} %get-tuple-element.37), channel_id=1, source_target_pairs={{0,0},{1,1},{2,10},{3,11},{4,20},{5,21},{6,30},{7,31},{8,8},{9,9},... | collective-permute-start | bytes 307208 | tf_op jit(solution)/shard_map/sum_gradient/ppermute | solution.py:255

commit v5 on v4

--- a/solution.py
+++ b/solution.py
@@ -13,8 +13,8 @@
 ID_ROWS = 16
 ID_BASE = 64
 SENDS = (0, 3, 1, 2)
-RETURNS = (1, 3, 2, 0)
-SUMS = (1, 3, 2, 0)
+RETURNS = (2, 3, 1, 0)
+SUMS = (2, 3, 1, 0)
 
 
 def call(
@@ -98,20 +98,19 @@
 
 
 def weigh(key, query, bias):
-    scores = lax.dot_general(
-        key, query, (((0,), (0,)), ((), ())), preferred_element_type=jnp.float32
-    )
-    scores = scores + bias
+    scores = jnp.dot(key, query, preferred_element_type=jnp.float32) + bias
     return scores, jnp.max(scores, axis=0, keepdims=True)
 
 
 def attend_first_kernel(block, head_width, *refs):
-    slabs, (mixed, highest, total, bias) = refs[:-4], refs[-4:]
+    slabs, (mixed, highest, total, turned, bias) = refs[:-5], refs[-5:]
     ids = identifiers(slabs, block)
     set_bias(bias, ids, ids)
     factor = math.log2(math.e) / math.sqrt(head_width)
     for head in range(block // head_width):
         query, key, value = (gather(slabs, which, block, head, head_width) for which in range(3))
+        key = key.T
+        turned[head] = key
         scores, top = weigh(key, query, bias[...])
         weights = jnp.exp2((scores - top) * factor)
         highest[head : head + 1] = top
@@ -123,7 +122,8 @@
 
 def attend_last_kernel(block, head_width, *refs):
     count = len(SENDS)
-    slabs, (mixed, highest, total), outs = refs[:count], refs[count : count + 3], refs[count + 3 : -2]
+    slabs, (mixed, highest, total, turned) = refs[:count], refs[count : count + 4]
+    outs = refs[count + 4 : -2]
     old_bias, new_bias = refs[-2:]
     *early, late = slabs
     rows = late.shape[1]
@@ -133,10 +133,11 @@
     factor = math.log2(math.e) / math.sqrt(head_width)
     for head in range(block // head_width):
         span = slice(head * head_width, (head + 1) * head_width)
-        query, key, value = (gather(early, which, block, head, head_width) for which in range(3))
+        query, value = (gather(early, which, block, head, head_width) for which in (0, 2))
         new_query, new_key, new_value = (
             gather([late], which, block, head, head_width) for which in range(3)
         )
+        new_key = new_key.T
         scores, top = weigh(new_key, query, old_bias[...])
         before = highest[head : head + 1]
         top = jnp.maximum(top, before)
@@ -151,7 +152,7 @@
             out = outs[RETURNS.index(SENDS[index])]
             out[span] = result[:, index * rows : (index + 1) * rows]
         scores, top = weigh(
-            jnp.concatenate([key, new_key], axis=1), new_query, new_bias[...]
+            jnp.concatenate([turned[head], new_key], axis=0), new_query, new_bias[...]
         )
         weights = jnp.exp2((scores - top) * factor)
         sums = jnp.sum(weights, axis=0, keepdims=True)
@@ -293,7 +294,12 @@
         f32 = functools.partial(jax.ShapeDtypeStruct, dtype=jnp.float32)
         state = call(
             functools.partial(attend_first_kernel, block, head_width),
-            [f32((block, known)), f32((8, known)), f32((8, known))],
+            [
+                f32((block, known)),
+                f32((8, known)),
+                f32((8, known)),
+                bf16((block // head_width, known, head_width)),
+            ],
             *slabs[:-1],
             scratch=[pltpu.VMEM((known, known), jnp.float32)],
             flops=55 * known * known * block,

time: 62.2 us -> 59 us (0.949)
  waiting for transfers between devices: 27.2 us -> 24.3 us
    ppermute x18, waiting for transfers between devices: 27.2 us -> 24.3 us  [move(): return lax.ppermute(data, AXES, pairs)]
where the time goes in v5:
time: 59 us; the launch traced here: 58.9 us
  starting transfers between devices  24.9 us (42%)
  waiting for transfers between devices  24.3 us (41%)
  Pallas kernels  8.9 us (15%)
  between operations  0.74 us (1%)
    ppermute x18, starting transfers between devices, move(): return lax.ppermute(data, AXES, pairs)  24.9 us
    ppermute x18, waiting for transfers between devices, move(): return lax.ppermute(data, AXES, pairs)  24.3 us
    pallas_call x8, Pallas kernels, call(): pl.pallas_call(kernel, out_shape=out_shape, in_specs=[placed(space) for s...  8.9 us
  transfers between devices with their start and end apart: 18, of which 7 were waited for; matrix products, arithmetic and copies ran while one was open for 0% of the time, Pallas kernels for 11%

profile of v5, /device:TPU:0, one launch (start us, length us, event | category | flops | bytes accessed | tf_op | source)
XLA Modules:
  0.0 58.9 jit_solution(13468857051624879520)
XLA Ops:
  0.6 1.5 %pack.1 = (bf16[976,128]{1,0:T(8,128)(2,1)S(1)}, bf16[976,128]{1,0:T(8,128)(2,1)S(1)}, bf16[976,128]{1,0:T(8,128)(2,1)S(1)}, bf16[976,128]{1,0:T(8,128)(2,1)S(1)}, bf16[128,1280]{1,0:T(8,128)(2,1)S(1)}) custom-call(s32[1,128]{1,0:T(1,128)} %bitcast.1, bf16[128,1280]{1,0:T(8,128)(2,1)} %refs_1_.1, bf16[128,1280]{1,0:T(8,128)(2,1)} %refs_2_.1, ...), custom_call_target="tpu_custom_call" | custom-call | bytes 2621440 | tf_op jit(solution)/shard_map/pack/pallas_call | solution.py:39
  2.2 5.1 %collective-permute-start = (bf16[976,128]{1,0:T(8,128)(2,1)S(1)}, bf16[976,128]{1,0:T(8,128)(2,1)S(1)}, u32[]{:S(2)}, u32[]{:S(2)}) collective-permute-start(bf16[976,128]{1,0:T(8,128)(2,1)S(1)} %get-tuple-element.22), channel_id=1, source_target_pairs={{0,6},{1,7},{2,4},{3,5},{4,2},{5,3},{6,0},{7,1},{8,14},{9,15},{10,... | collective-permute-start | bytes 749576 | tf_op jit(solution)/shard_map/exchange_heads/ppermute | solution.py:256
  7.3 0.6 %collective-permute-start.2 = (bf16[976,128]{1,0:T(8,128)(2,1)S(1)}, bf16[976,128]{1,0:T(8,128)(2,1)S(1)}, u32[]{:S(2)}, u32[]{:S(2)}) collective-permute-start(bf16[976,128]{1,0:T(8,128)(2,1)S(1)} %get-tuple-element.24), channel_id=1, source_target_pairs={{0,4},{1,5},{2,6},{3,7},{4,0},{5,1},{6,2},{7,3},{8,12},{9,13},{10,... | collective-permute-start | bytes 749576 | tf_op jit(solution)/shard_map/exchange_heads/ppermute | solution.py:256
  7.9 2.6 %collective-permute-start.12 = (bf16[128,1280]{1,0:T(8,128)(2,1)S(1)}, bf16[128,1280]{1,0:T(8,128)(2,1)S(1)}, u32[]{:S(2)}, u32[]{:S(2)}) collective-permute-start(bf16[128,1280]{1,0:T(8,128)(2,1)S(1)} %get-tuple-element.35.refs_0_), channel_id=1, source_target_pairs={{0,24},{1,25},{2,26},{3,27},{4,28},{5,29},{6,30},{7,31},{8,16},{9,... | collective-permute-start | bytes 983048 | tf_op jit(solution)/shard_map/gather_cotangent/ppermute | solution.py:256
  10.5 0.5 collective-permute-start.11
  11.0 3.2 %collective-permute-done.refs_1_ = bf16[976,128]{1,0:T(8,128)(2,1)S(1)} collective-permute-done((bf16[976,128]{1,0:T(8,128)(2,1)S(1)}, bf16[976,128]{1,0:T(8,128)(2,1)S(1)}, u32[]{:S(2)}, u32[]{:S(2)}) %collective-permute-start) | collective-permute-done | bytes 249888 | tf_op jit(solution)/shard_map/exchange_heads/ppermute | solution.py:256
  14.2 1.7 %collective-permute-start.10 = (bf16[128,1280]{1,0:T(8,128)(2,1)S(1)}, bf16[128,1280]{1,0:T(8,128)(2,1)S(1)}, u32[]{:S(2)}, u32[]{:S(2)}) collective-permute-start(bf16[128,1280]{1,0:T(8,128)(2,1)S(1)} %get-tuple-element.35.refs_0_), channel_id=1, source_target_pairs={{0,8},{1,9},{2,10},{3,11},{4,12},{5,13},{6,14},{7,15},{8,0},{9,1},... | collective-permute-start | bytes 983048 | tf_op jit(solution)/shard_map/gather_cotangent/ppermute | solution.py:256
  15.9 3.9 %collective-permute-done.1.refs_2_ = bf16[976,128]{1,0:T(8,128)(2,1)S(1)} collective-permute-done((bf16[976,128]{1,0:T(8,128)(2,1)S(1)}, bf16[976,128]{1,0:T(8,128)(2,1)S(1)}, u32[]{:S(2)}, u32[]{:S(2)}) %collective-permute-start.1) | collective-permute-done | bytes 249888 | tf_op jit(solution)/shard_map/exchange_heads/ppermute | solution.py:256
  19.8 1.7 %attention.2 = (f32[320,384]{1,0:T(8,128)S(1)}, f32[8,384]{1,0:T(8,128)S(1)}, f32[8,384]{1,0:T(8,128)S(1)}, bf16[4,384,80]{2,1,0:T(8,128)(2,1)S(1)}) custom-call(bf16[976,128]{1,0:T(8,128)(2,1)S(1)} %get-tuple-element.21.refs_0_, bf16[976,128]{1,0:T(8,128)(2,1)S(1)} %collective-permute-done.refs_1_, bf16[976,128]{1,0:T(8,128)(2,1)S(1)} %collective-permute-done.1.refs_2_), custom_call_target="tpu_custom_call" | custom-call | flops 2595225600 | bytes 1310720 | tf_op jit(solution)/shard_map/attention/pallas_call | solution.py:39
  21.5 7.0 %collective-permute-done.2.refs_3_ = bf16[976,128]{1,0:T(8,128)(2,1)S(1)} collective-permute-done((bf16[976,128]{1,0:T(8,128)(2,1)S(1)}, bf16[976,128]{1,0:T(8,128)(2,1)S(1)}, u32[]{:S(2)}, u32[]{:S(2)}) %collective-permute-start.2) | collective-permute-done | bytes 249888 | tf_op jit(solution)/shard_map/exchange_heads/ppermute | solution.py:256
  28.5 2.1 %attention.3 = (bf16[320,128]{1,0:T(8,128)(2,1)S(1)}, bf16[320,128]{1,0:T(8,128)(2,1)S(1)}, bf16[320,128]{1,0:T(8,128)(2,1)S(1)}, bf16[320,128]{1,0:T(8,128)(2,1)S(1)}) custom-call(bf16[976,128]{1,0:T(8,128)(2,1)S(1)} %get-tuple-element.21.refs_0_, bf16[976,128]{1,0:T(8,128)(2,1)S(1)} %collective-permute-done.refs_1_, ...), custom_call_target="tpu_custom_call" | custom-call | flops 2018508800 | bytes 1310720 | tf_op jit(solution)/shard_map/attention/pallas_call | solution.py:39
  30.7 0.6 collective-permute-start.3
  31.3 3.9 %collective-permute-start.5 = (bf16[320,128]{1,0:T(8,128)(2,1)S(1)}, bf16[320,128]{1,0:T(8,128)(2,1)S(1)}, u32[]{:S(2)}, u32[]{:S(2)}) collective-permute-start(bf16[320,128]{1,0:T(8,128)(2,1)S(1)} %get-tuple-element.30), channel_id=1, source_target_pairs={{0,30},{1,31},{2,28},{3,29},{4,26},{5,27},{6,24},{7,25},{8,22},{9,... | collective-permute-start | bytes 245768 | tf_op jit(solution)/shard_map/send_to_owner/ppermute | solution.py:256
  35.2 0.0 collective-permute-done.12.refs_3_
  35.2 0.9 %collective-permute-start.7 = (bf16[320,128]{1,0:T(8,128)(2,1)S(1)}, bf16[320,128]{1,0:T(8,128)(2,1)S(1)}, u32[]{:S(2)}, u32[]{:S(2)}) collective-permute-start(bf16[320,128]{1,0:T(8,128)(2,1)S(1)} %get-tuple-element.31), channel_id=1, source_target_pairs={{0,10},{1,11},{2,8},{3,9},{4,14},{5,15},{6,12},{7,13},{8,2},{9,3},... | collective-permute-start | bytes 245768 | tf_op jit(solution)/shard_map/send_to_owner/ppermute | solution.py:256
  36.0 0.0 collective-permute-done.11.refs_2_
  36.0 0.4 swap_cotangent.1.refs_2_
  36.5 0.1 collective-permute-start.13
  36.6 3.4 %collective-permute-done.3.refs_0_ = bf16[320,128]{1,0:T(8,128)(2,1)S(1)} collective-permute-done((bf16[320,128]{1,0:T(8,128)(2,1)S(1)}, bf16[320,128]{1,0:T(8,128)(2,1)S(1)}, u32[]{:S(2)}, u32[]{:S(2)}) %collective-permute-start.3) | collective-permute-done | bytes 81952 | tf_op jit(solution)/shard_map/send_to_owner/ppermute | solution.py:256
  39.9 1.3 %collective-permute-done.7.refs_2_ = bf16[320,128]{1,0:T(8,128)(2,1)S(1)} collective-permute-done((bf16[320,128]{1,0:T(8,128)(2,1)S(1)}, bf16[320,128]{1,0:T(8,128)(2,1)S(1)}, u32[]{:S(2)}, u32[]{:S(2)}) %collective-permute-start.7) | collective-permute-done | bytes 81952 | tf_op jit(solution)/shard_map/send_to_owner/ppermute | solution.py:256
  41.3 0.1 collective-permute-start.9
  41.3 0.8 %collective-permute-start.4 = (bf16[320,128]{1,0:T(8,128)(2,1)S(1)}, bf16[320,128]{1,0:T(8,128)(2,1)S(1)}, u32[]{:S(2)}, u32[]{:S(2)}) collective-permute-start(bf16[320,128]{1,0:T(8,128)(2,1)S(1)} %collective-permute-done.3.refs_0_), channel_id=1, source_target_pairs={{0,16},{1,17},{2,18},{3,19},{4,20},{5,21},{6,22},{7,23},{8,24},{9,... | collective-permute-start | bytes 245768 | tf_op jit(solution)/shard_map/send_home/ppermute | solution.py:256
  42.1 1.5 %collective-permute-start.6 = (bf16[320,128]{1,0:T(8,128)(2,1)S(1)}, bf16[320,128]{1,0:T(8,128)(2,1)S(1)}, u32[]{:S(2)}, u32[]{:S(2)}) collective-permute-start(bf16[320,128]{1,0:T(8,128)(2,1)S(1)} %collective-permute-done.5.refs_1_), channel_id=1, source_target_pairs={{0,24},{1,25},{2,26},{3,27},{4,28},{5,29},{6,30},{7,31},{8,16},{9,... | collective-permute-start | bytes 245768 | tf_op jit(solution)/shard_map/send_home/ppermute | solution.py:256
  43.7 1.2 %collective-permute-start.8 = (bf16[320,128]{1,0:T(8,128)(2,1)S(1)}, bf16[320,128]{1,0:T(8,128)(2,1)S(1)}, u32[]{:S(2)}, u32[]{:S(2)}) collective-permute-start(bf16[320,128]{1,0:T(8,128)(2,1)S(1)} %collective-permute-done.7.refs_2_), channel_id=1, source_target_pairs={{0,8},{1,9},{2,10},{3,11},{4,12},{5,13},{6,14},{7,15},{8,0},{9,1},... | collective-permute-start | bytes 245768 | tf_op jit(solution)/shard_map/send_home/ppermute | solution.py:256
  44.9 0.9 %gradient.1 = (bf16[80,640]{1,0:T(8,128)(2,1)S(1)}, bf16[80,640]{1,0:T(8,128)(2,1)S(1)}, bf16[80,640]{1,0:T(8,128)(2,1)S(1)}, bf16[80,640]{1,0:T(8,128)(2,1)S(1)}) custom-call(bf16[4,160,128]{2,1,0:T(8,128)(2,1)S(1)} %get-tuple-element.33.refs_0_, bf16[4,160,128]{2,1,0:T(8,128)(2,1)S(1)} %collective-permute-done.9.refs_1_, ...), custom_call_target="tpu_custom_call" | custom-call | flops 419430400 | bytes 2621440 | tf_op jit(solution)/shard_map/gradient/pallas_call | solution.py:39
  45.8 2.1 %collective-permute-start.14 = (bf16[80,640]{1,0:T(8,128)(2,1)S(1)}, bf16[80,640]{1,0:T(8,128)(2,1)S(1)}, u32[]{:S(2)}, u32[]{:S(2)}) collective-permute-start(bf16[80,640]{1,0:T(8,128)(2,1)S(1)} %get-tuple-element.36), channel_id=1, source_target_pairs={{0,4},{1,5},{2,14},{3,15},{4,16},{5,17},{6,26},{7,27},{8,12},{9,13... | collective-permute-start | bytes 307208 | tf_op jit(solution)/shard_map/sum_gradient/ppermute | solution.py:256
  48.0 2.5 %collective-permute-start.15 = (bf16[80,640]{1,0:T(8,128)(2,1)S(1)}, bf16[80,640]{1,0:T(8,128)(2,1)S(1)}, u32[]{:S(2)}, u32[]{:S(2)}) collective-permute-start(bf16[80,640]{1,0:T(8,128)(2,1)S(1)} %get-tuple-element.37), channel_id=1, source_target_pairs={{0,6},{1,7},{2,12},{3,13},{4,18},{5,19},{6,24},{7,25},{8,14},{9,15... | collective-permute-start | bytes 307208 | tf_op jit(solution)/shard_map/sum_gradient/ppermute | solution.py:256
  50.5 0.7 %collective-permute-start.17 = (bf16[80,640]{1,0:T(8,128)(2,1)S(1)}, bf16[80,640]{1,0:T(8,128)(2,1)S(1)}, u32[]{:S(2)}, u32[]{:S(2)}) collective-permute-start(bf16[80,640]{1,0:T(8,128)(2,1)S(1)} %get-tuple-element.39), channel_id=1, source_target_pairs={{0,0},{1,1},{2,10},{3,11},{4,20},{5,21},{6,30},{7,31},{8,8},{9,9},... | collective-permute-start | bytes 307208 | tf_op jit(solution)/shard_map/sum_gradient/ppermute | solution.py:256
  51.2 1.4 %project.1 = bf16[128,1280]{1,0:T(8,128)(2,1)} custom-call(bf16[320,128]{1,0:T(8,128)(2,1)S(1)} %collective-permute-done.4.refs_0_, bf16[320,128]{1,0:T(8,128)(2,1)S(1)} %collective-permute-done.6.refs_1_, bf16[320,128]{1,0:T(8,128)(2,1)S(1)} %collective-permute-done.8.refs_2_, bf16[320,128]{1,0:T(8,128)(2,1)S(1)} %get-tuple-element.32.refs_3_, ...), custom_call_target="tpu_custom_call" | custom-call | flops 419430400 | bytes 3276800 | tf_op jit(solution)/shard_map/project/pallas_call | solution.py:39
  52.6 5.2 %collective-permute-done.14.refs_0_ = bf16[80,640]{1,0:T(8,128)(2,1)S(1)} collective-permute-done((bf16[80,640]{1,0:T(8,128)(2,1)S(1)}, bf16[80,640]{1,0:T(8,128)(2,1)S(1)}, u32[]{:S(2)}, u32[]{:S(2)}) %collective-permute-start.14) | collective-permute-done | bytes 102432 | tf_op jit(solution)/shard_map/sum_gradient/ppermute | solution.py:256
  57.8 0.3 collective-permute-done.15.refs_1_
  58.0 0.8 %add_gradient.1 = f32[160,320]{1,0:T(8,128)} custom-call(bf16[80,640]{1,0:T(8,128)(2,1)S(1)} %collective-permute-done.14.refs_0_, bf16[80,640]{1,0:T(8,128)(2,1)S(1)} %collective-permute-done.15.refs_1_, bf16[80,640]{1,0:T(8,128)(2,1)S(1)} %collective-permute-done.16.refs_2_, bf16[80,640]{1,0:T(8,128)(2,1)S(1)} %collective-permute-done.17.refs_3_), custom_call_target="tpu_custom_call" | custom-call | bytes 819200 | tf_op jit(solution)/shard_map/add_gradient/pallas_call | solution.py:39
  (16 shorter events, 0.1 us)
Async XLA Ops:
  2.2 12.1 %collective-permute-start = (bf16[976,128]{1,0:T(8,128)(2,1)S(1)}, bf16[976,128]{1,0:T(8,128)(2,1)S(1)}, u32[]{:S(2)}, u32[]{:S(2)}) collective-permute-start(bf16[976,128]{1,0:T(8,128)(2,1)S(1)} %get-tuple-element.22), channel_id=1, source_target_pairs={{0,6},{1,7},{2,4},{3,5},{4,2},{5,3},{6,0},{7,1},{8,14},{9,15},{10,... | collective-permute-start | bytes 749576 | tf_op jit(solution)/shard_map/exchange_heads/ppermute | solution.py:256
  7.3 12.5 %collective-permute-start.1 = (bf16[976,128]{1,0:T(8,128)(2,1)S(1)}, bf16[976,128]{1,0:T(8,128)(2,1)S(1)}, u32[]{:S(2)}, u32[]{:S(2)}) collective-permute-start(bf16[976,128]{1,0:T(8,128)(2,1)S(1)} %get-tuple-element.23), channel_id=1, source_target_pairs={{0,2},{1,3},{2,0},{3,1},{4,6},{5,7},{6,4},{7,5},{8,10},{9,11},{10,... | collective-permute-start | bytes 749576 | tf_op jit(solution)/shard_map/exchange_heads/ppermute | solution.py:256
  7.3 21.2 %collective-permute-start.2 = (bf16[976,128]{1,0:T(8,128)(2,1)S(1)}, bf16[976,128]{1,0:T(8,128)(2,1)S(1)}, u32[]{:S(2)}, u32[]{:S(2)}) collective-permute-start(bf16[976,128]{1,0:T(8,128)(2,1)S(1)} %get-tuple-element.24), channel_id=1, source_target_pairs={{0,4},{1,5},{2,6},{3,7},{4,0},{5,1},{6,2},{7,3},{8,12},{9,13},{10,... | collective-permute-start | bytes 749576 | tf_op jit(solution)/shard_map/exchange_heads/ppermute | solution.py:256
  7.9 27.3 %collective-permute-start.12 = (bf16[128,1280]{1,0:T(8,128)(2,1)S(1)}, bf16[128,1280]{1,0:T(8,128)(2,1)S(1)}, u32[]{:S(2)}, u32[]{:S(2)}) collective-permute-start(bf16[128,1280]{1,0:T(8,128)(2,1)S(1)} %get-tuple-element.35.refs_0_), channel_id=1, source_target_pairs={{0,24},{1,25},{2,26},{3,27},{4,28},{5,29},{6,30},{7,31},{8,16},{9,... | collective-permute-start | bytes 983048 | tf_op jit(solution)/shard_map/gather_cotangent/ppermute | solution.py:256
  10.5 25.5 %collective-permute-start.11 = (bf16[128,1280]{1,0:T(8,128)(2,1)S(1)}, bf16[128,1280]{1,0:T(8,128)(2,1)S(1)}, u32[]{:S(2)}, u32[]{:S(2)}) collective-permute-start(bf16[128,1280]{1,0:T(8,128)(2,1)S(1)} %get-tuple-element.35.refs_0_), channel_id=1, source_target_pairs={{0,16},{1,17},{2,18},{3,19},{4,20},{5,21},{6,22},{7,23},{8,24},{9,... | collective-permute-start | bytes 983048 | tf_op jit(solution)/shard_map/gather_cotangent/ppermute | solution.py:256
  14.2 21.8 %collective-permute-start.10 = (bf16[128,1280]{1,0:T(8,128)(2,1)S(1)}, bf16[128,1280]{1,0:T(8,128)(2,1)S(1)}, u32[]{:S(2)}, u32[]{:S(2)}) collective-permute-start(bf16[128,1280]{1,0:T(8,128)(2,1)S(1)} %get-tuple-element.35.refs_0_), channel_id=1, source_target_pairs={{0,8},{1,9},{2,10},{3,11},{4,12},{5,13},{6,14},{7,15},{8,0},{9,1},... | collective-permute-start | bytes 983048 | tf_op jit(solution)/shard_map/gather_cotangent/ppermute | solution.py:256
  30.7 9.3 %collective-permute-start.3 = (bf16[320,128]{1,0:T(8,128)(2,1)S(1)}, bf16[320,128]{1,0:T(8,128)(2,1)S(1)}, u32[]{:S(2)}, u32[]{:S(2)}) collective-permute-start(bf16[320,128]{1,0:T(8,128)(2,1)S(1)} %get-tuple-element.29), channel_id=1, source_target_pairs={{0,20},{1,21},{2,22},{3,23},{4,16},{5,17},{6,18},{7,19},{8,28},{9,... | collective-permute-start | bytes 245768 | tf_op jit(solution)/shard_map/send_to_owner/ppermute | solution.py:256
  31.3 8.7 %collective-permute-start.5 = (bf16[320,128]{1,0:T(8,128)(2,1)S(1)}, bf16[320,128]{1,0:T(8,128)(2,1)S(1)}, u32[]{:S(2)}, u32[]{:S(2)}) collective-permute-start(bf16[320,128]{1,0:T(8,128)(2,1)S(1)} %get-tuple-element.30), channel_id=1, source_target_pairs={{0,30},{1,31},{2,28},{3,29},{4,26},{5,27},{6,24},{7,25},{8,22},{9,... | collective-permute-start | bytes 245768 | tf_op jit(solution)/shard_map/send_to_owner/ppermute | solution.py:256
  35.2 6.0 %collective-permute-start.7 = (bf16[320,128]{1,0:T(8,128)(2,1)S(1)}, bf16[320,128]{1,0:T(8,128)(2,1)S(1)}, u32[]{:S(2)}, u32[]{:S(2)}) collective-permute-start(bf16[320,128]{1,0:T(8,128)(2,1)S(1)} %get-tuple-element.31), channel_id=1, source_target_pairs={{0,10},{1,11},{2,8},{3,9},{4,14},{5,15},{6,12},{7,13},{8,2},{9,3},... | collective-permute-start | bytes 245768 | tf_op jit(solution)/shard_map/send_to_owner/ppermute | solution.py:256
  36.5 8.4 %collective-permute-start.13 = (bf16[4,128,1280]{2,1,0:T(8,128)(2,1)S(1)}, bf16[4,128,1280]{2,1,0:T(8,128)(2,1)S(1)}, u32[]{:S(2)}, u32[]{:S(2)}) collective-permute-start(bf16[4,128,1280]{2,1,0:T(8,128)(2,1)S(1)} %swap_cotangent.1.refs_2_), channel_id=1, source_target_pairs={{0,1},{1,0},{2,3},{3,2},{4,5},{5,4},{6,7},{7,6},{8,9},{9,8},{10,11... | collective-permute-start | bytes 3932168 | tf_op jit(solution)/shard_map/gradient/ppermute | solution.py:256
  41.2 10.0 %copy-start = (bf16[1280,1280]{1,0:T(8,128)(2,1)S(1)}, bf16[1280,1280]{1,0:T(8,128)(2,1)}, u32[]{:S(2)}) copy-start(bf16[1280,1280]{1,0:T(8,128)(2,1)} %refs_5_.1) | copy-start | bytes 9830404
  41.3 3.6 %collective-permute-start.9 = (bf16[4,160,128]{2,1,0:T(8,128)(2,1)S(1)}, bf16[4,160,128]{2,1,0:T(8,128)(2,1)S(1)}, u32[]{:S(2)}, u32[]{:S(2)}) collective-permute-start(bf16[4,160,128]{2,1,0:T(8,128)(2,1)S(1)} %get-tuple-element.34), channel_id=1, source_target_pairs={{0,1},{1,0},{2,3},{3,2},{4,5},{5,4},{6,7},{7,6},{8,9},{9,8},{10,11... | collective-permute-start | bytes 491528 | tf_op jit(solution)/shard_map/send_to_owner/ppermute | solution.py:256
  41.3 9.2 %collective-permute-start.4 = (bf16[320,128]{1,0:T(8,128)(2,1)S(1)}, bf16[320,128]{1,0:T(8,128)(2,1)S(1)}, u32[]{:S(2)}, u32[]{:S(2)}) collective-permute-start(bf16[320,128]{1,0:T(8,128)(2,1)S(1)} %collective-permute-done.3.refs_0_), channel_id=1, source_target_pairs={{0,16},{1,17},{2,18},{3,19},{4,20},{5,21},{6,22},{7,23},{8,24},{9,... | collective-permute-start | bytes 245768 | tf_op jit(solution)/shard_map/send_home/ppermute | solution.py:256
  42.1 8.3 %collective-permute-start.6 = (bf16[320,128]{1,0:T(8,128)(2,1)S(1)}, bf16[320,128]{1,0:T(8,128)(2,1)S(1)}, u32[]{:S(2)}, u32[]{:S(2)}) collective-permute-start(bf16[320,128]{1,0:T(8,128)(2,1)S(1)} %collective-permute-done.5.refs_1_), channel_id=1, source_target_pairs={{0,24},{1,25},{2,26},{3,27},{4,28},{5,29},{6,30},{7,31},{8,16},{9,... | collective-permute-start | bytes 245768 | tf_op jit(solution)/shard_map/send_home/ppermute | solution.py:256
  43.7 7.5 %collective-permute-start.8 = (bf16[320,128]{1,0:T(8,128)(2,1)S(1)}, bf16[320,128]{1,0:T(8,128)(2,1)S(1)}, u32[]{:S(2)}, u32[]{:S(2)}) collective-permute-start(bf16[320,128]{1,0:T(8,128)(2,1)S(1)} %collective-permute-done.7.refs_2_), channel_id=1, source_target_pairs={{0,8},{1,9},{2,10},{3,11},{4,12},{5,13},{6,14},{7,15},{8,0},{9,1},... | collective-permute-start | bytes 245768 | tf_op jit(solution)/shard_map/send_home/ppermute | solution.py:256
  44.9 6.3 %copy-start.1 = (bf16[128,1280]{1,0:T(8,128)(2,1)S(1)}, bf16[128,1280]{1,0:T(8,128)(2,1)}, u32[]{:S(2)}) copy-start(bf16[128,1280]{1,0:T(8,128)(2,1)} %refs_4_.3) | copy-start | bytes 983044
  45.8 11.9 %collective-permute-start.14 = (bf16[80,640]{1,0:T(8,128)(2,1)S(1)}, bf16[80,640]{1,0:T(8,128)(2,1)S(1)}, u32[]{:S(2)}, u32[]{:S(2)}) collective-permute-start(bf16[80,640]{1,0:T(8,128)(2,1)S(1)} %get-tuple-element.36), channel_id=1, source_target_pairs={{0,4},{1,5},{2,14},{3,15},{4,16},{5,17},{6,26},{7,27},{8,12},{9,13... | collective-permute-start | bytes 307208 | tf_op jit(solution)/shard_map/sum_gradient/ppermute | solution.py:256
  48.0 10.1 %collective-permute-start.15 = (bf16[80,640]{1,0:T(8,128)(2,1)S(1)}, bf16[80,640]{1,0:T(8,128)(2,1)S(1)}, u32[]{:S(2)}, u32[]{:S(2)}) collective-permute-start(bf16[80,640]{1,0:T(8,128)(2,1)S(1)} %get-tuple-element.37), channel_id=1, source_target_pairs={{0,6},{1,7},{2,12},{3,13},{4,18},{5,19},{6,24},{7,25},{8,14},{9,15... | collective-permute-start | bytes 307208 | tf_op jit(solution)/shard_map/sum_gradient/ppermute | solution.py:256
  50.5 7.6 %collective-permute-start.16 = (bf16[80,640]{1,0:T(8,128)(2,1)S(1)}, bf16[80,640]{1,0:T(8,128)(2,1)S(1)}, u32[]{:S(2)}, u32[]{:S(2)}) collective-permute-start(bf16[80,640]{1,0:T(8,128)(2,1)S(1)} %get-tuple-element.38), channel_id=1, source_target_pairs={{0,2},{1,3},{2,8},{3,9},{4,22},{5,23},{6,28},{7,29},{8,10},{9,11},... | collective-permute-start | bytes 307208 | tf_op jit(solution)/shard_map/sum_gradient/ppermute | solution.py:256
  50.5 7.6 %collective-permute-start.17 = (bf16[80,640]{1,0:T(8,128)(2,1)S(1)}, bf16[80,640]{1,0:T(8,128)(2,1)S(1)}, u32[]{:S(2)}, u32[]{:S(2)}) collective-permute-start(bf16[80,640]{1,0:T(8,128)(2,1)S(1)} %get-tuple-element.39), channel_id=1, source_target_pairs={{0,0},{1,1},{2,10},{3,11},{4,20},{5,21},{6,30},{7,31},{8,8},{9,9},... | collective-permute-start | bytes 307208 | tf_op jit(solution)/shard_map/sum_gradient/ppermute | solution.py:256

commit v6 on v4

--- a/solution.py
+++ b/solution.py
@@ -12,9 +12,9 @@
 AXES = ("dp", "enc", "seq")
 ID_ROWS = 16
 ID_BASE = 64
-SENDS = (0, 3, 1, 2)
-RETURNS = (1, 3, 2, 0)
-SUMS = (1, 3, 2, 0)
+SENDS = (3, 0, 1, 2)
+RETURNS = (2, 3, 1, 0)
+SUMS = (2, 3, 1, 0)
 
 
 def call(
@@ -121,46 +121,53 @@
         )
 
 
-def attend_last_kernel(block, head_width, *refs):
-    count = len(SENDS)
-    slabs, (mixed, highest, total), outs = refs[:count], refs[count : count + 3], refs[count + 3 : -2]
-    old_bias, new_bias = refs[-2:]
-    *early, late = slabs
-    rows = late.shape[1]
-    *early_ids, late_id = identifiers(slabs, block)
-    set_bias(old_bias, [late_id], early_ids)
-    set_bias(new_bias, early_ids + [late_id], [late_id])
+def attend_more(early, late, state, bias, outs, first, head_width):
+    mixed, highest, total = state
+    block, rows = outs[0].shape
+    columns = slice(first, first + len(early) * rows)
+    set_bias(bias, identifiers([late], block), identifiers(early, block))
     factor = math.log2(math.e) / math.sqrt(head_width)
     for head in range(block // head_width):
         span = slice(head * head_width, (head + 1) * head_width)
-        query, key, value = (gather(early, which, block, head, head_width) for which in range(3))
-        new_query, new_key, new_value = (
-            gather([late], which, block, head, head_width) for which in range(3)
-        )
-        scores, top = weigh(new_key, query, old_bias[...])
-        before = highest[head : head + 1]
+        query = gather(early, 0, block, head, head_width)
+        key, value = (gather([late], which, block, head, head_width) for which in (1, 2))
+        scores, top = weigh(key, query, bias[...])
+        before = highest[head : head + 1, columns]
         top = jnp.maximum(top, before)
         weights = jnp.exp2((scores - top) * factor)
         shrink = jnp.exp2((before - top) * factor)
-        sums = total[head : head + 1] * shrink + jnp.sum(weights, axis=0, keepdims=True)
-        result = mixed[span] * shrink + jnp.dot(
-            new_value, weights.astype(jnp.bfloat16), preferred_element_type=jnp.float32
+        sums = total[head : head + 1, columns] * shrink
+        sums = sums + jnp.sum(weights, axis=0, keepdims=True)
+        result = mixed[span, columns] * shrink + jnp.dot(
+            value, weights.astype(jnp.bfloat16), preferred_element_type=jnp.float32
         )
         result = (result / sums).astype(jnp.bfloat16)
-        for index in range(count - 1):
-            out = outs[RETURNS.index(SENDS[index])]
+        for index, out in enumerate(outs):
             out[span] = result[:, index * rows : (index + 1) * rows]
-        scores, top = weigh(
-            jnp.concatenate([key, new_key], axis=1), new_query, new_bias[...]
-        )
+
+
+def attend_across_kernel(head_width, *refs):
+    count = len(SENDS)
+    slabs, state, (first, last, old_bias, bias) = refs[:count], refs[count:-4], refs[-4:]
+    block = last.shape[0]
+    ids = identifiers(slabs, block)
+    set_bias(bias, ids, ids[-1:])
+    factor = math.log2(math.e) / math.sqrt(head_width)
+    for head in range(block // head_width):
+        span = slice(head * head_width, (head + 1) * head_width)
+        query = gather(slabs[-1:], 0, block, head, head_width)
+        key, value = (gather(slabs, which, block, head, head_width) for which in (1, 2))
+        scores, top = weigh(key, query, bias[...])
         weights = jnp.exp2((scores - top) * factor)
         sums = jnp.sum(weights, axis=0, keepdims=True)
-        result = jnp.dot(
-            jnp.concatenate([value, new_value], axis=1),
-            weights.astype(jnp.bfloat16),
-            preferred_element_type=jnp.float32,
-        )
-        outs[RETURNS.index(SENDS[-1])][span] = (result / sums).astype(jnp.bfloat16)
+        result = jnp.dot(value, weights.astype(jnp.bfloat16), preferred_element_type=jnp.float32)
+        last[span] = (result / sums).astype(jnp.bfloat16)
+    attend_more(slabs[:1], slabs[-1], state, old_bias, [first], 0, head_width)
+
+
+def attend_rest_kernel(head_width, *refs):
+    early, late, state, outs, bias = refs[:2], refs[2], refs[3:6], refs[6:8], refs[8]
+    attend_more(early, late, state, bias, outs, late.shape[1], head_width)
 
 
 def stack_kernel(count, *refs):
@@ -299,15 +306,26 @@
             flops=55 * known * known * block,
             bytes_accessed=8 * group * block,
         )
-        pieces = call(
-            functools.partial(attend_last_kernel, block, head_width),
-            [bf16((block, rows))] * n_enc,
+        across = call(
+            functools.partial(attend_across_kernel, head_width),
+            [bf16((block, rows))] * 2,
             *slabs,
             *state,
-            scratch=[pltpu.VMEM((rows, known), jnp.float32), pltpu.VMEM((group, rows), jnp.float32)],
-            flops=55 * (group * group - known * known) * block,
+            scratch=[pltpu.VMEM((rows, rows), jnp.float32), pltpu.VMEM((group, rows), jnp.float32)],
+            flops=55 * rows * (rows + group) * block,
             bytes_accessed=8 * group * block,
         )
+        rest = call(
+            functools.partial(attend_rest_kernel, head_width),
+            [bf16((block, rows))] * 2,
+            *slabs[1:],
+            *state,
+            scratch=[pltpu.VMEM((rows, 2 * rows), jnp.float32)],
+            flops=55 * rows * 2 * rows * block,
+            bytes_accessed=8 * group * block,
+        )
+        pieces = dict(zip(SENDS, [across[0], *rest, across[1]]))
+        pieces = [pieces[hop] for hop in RETURNS]
     with jax.named_scope("send_to_owner"):
         pieces = [
             move(piece, lambda d, e, s, hop=hop: (d ^ hop, e ^ hop, s)) if hop else piece

time: 62.2 us -> 58.4 us (0.939)
  waiting for transfers between devices: 27.2 us -> 23.6 us
    ppermute x18, waiting for transfers between devices: 27.2 us -> 23.6 us  [move(): return lax.ppermute(data, AXES, pairs)]
    pallas_call x8 -> x9, Pallas kernels: 8.9 us -> 9.29 us  [call(): pl.pallas_call(kernel, out_shape=out_shape, in_specs=[placed(space) for s...]
  transfers between devices with their start and end apart: 18 -> 18, of which waited for: 7 -> 7; matrix products, arithmetic and copies ran while one was open for 0% -> 0% of each run, Pallas kernels for 11% -> 12%
where the time goes in v6:
time: 58.4 us; the launch traced here: 58.3 us
  starting transfers between devices  24.7 us (42%)
  waiting for transfers between devices  23.6 us (40%)
  Pallas kernels  9.29 us (16%)
  between operations  0.76 us (1%)
    ppermute x18, starting transfers between devices, move(): return lax.ppermute(data, AXES, pairs)  24.7 us
    ppermute x18, waiting for transfers between devices, move(): return lax.ppermute(data, AXES, pairs)  23.6 us
    pallas_call x9, Pallas kernels, call(): pl.pallas_call(kernel, out_shape=out_shape, in_specs=[placed(space) for s...  9.29 us
  transfers between devices with their start and end apart: 18, of which 7 were waited for; matrix products, arithmetic and copies ran while one was open for 0% of the time, Pallas kernels for 12%

profile of v6, /device:TPU:0, one launch (start us, length us, event | category | flops | bytes accessed | tf_op | source)
XLA Modules:
  0.0 58.3 jit_solution(17079584653436483883)
XLA Ops:
  0.6 1.5 %pack.1 = (bf16[976,128]{1,0:T(8,128)(2,1)S(1)}, bf16[976,128]{1,0:T(8,128)(2,1)S(1)}, bf16[976,128]{1,0:T(8,128)(2,1)S(1)}, bf16[976,128]{1,0:T(8,128)(2,1)S(1)}, bf16[128,1280]{1,0:T(8,128)(2,1)S(1)}) custom-call(s32[1,128]{1,0:T(1,128)} %bitcast.1, bf16[128,1280]{1,0:T(8,128)(2,1)} %refs_1_.1, bf16[128,1280]{1,0:T(8,128)(2,1)} %refs_2_.1, ...), custom_call_target="tpu_custom_call" | custom-call | bytes 2621440 | tf_op jit(solution)/shard_map/pack/pallas_call | solution.py:39
  2.2 5.1 %collective-permute-start = (bf16[976,128]{1,0:T(8,128)(2,1)S(1)}, bf16[976,128]{1,0:T(8,128)(2,1)S(1)}, u32[]{:S(2)}, u32[]{:S(2)}) collective-permute-start(bf16[976,128]{1,0:T(8,128)(2,1)S(1)} %get-tuple-element.20), channel_id=1, source_target_pairs={{0,6},{1,7},{2,4},{3,5},{4,2},{5,3},{6,0},{7,1},{8,14},{9,15},{10,... | collective-permute-start | bytes 749576 | tf_op jit(solution)/shard_map/exchange_heads/ppermute | solution.py:262
  7.3 0.6 %collective-permute-start.2 = (bf16[976,128]{1,0:T(8,128)(2,1)S(1)}, bf16[976,128]{1,0:T(8,128)(2,1)S(1)}, u32[]{:S(2)}, u32[]{:S(2)}) collective-permute-start(bf16[976,128]{1,0:T(8,128)(2,1)S(1)} %get-tuple-element.23), channel_id=1, source_target_pairs={{0,4},{1,5},{2,6},{3,7},{4,0},{5,1},{6,2},{7,3},{8,12},{9,13},{10,... | collective-permute-start | bytes 749576 | tf_op jit(solution)/shard_map/exchange_heads/ppermute | solution.py:262
  7.9 2.6 %collective-permute-start.12 = (bf16[128,1280]{1,0:T(8,128)(2,1)S(1)}, bf16[128,1280]{1,0:T(8,128)(2,1)S(1)}, u32[]{:S(2)}, u32[]{:S(2)}) collective-permute-start(bf16[128,1280]{1,0:T(8,128)(2,1)S(1)} %get-tuple-element.33.refs_0_), channel_id=1, source_target_pairs={{0,24},{1,25},{2,26},{3,27},{4,28},{5,29},{6,30},{7,31},{8,16},{9,... | collective-permute-start | bytes 983048 | tf_op jit(solution)/shard_map/gather_cotangent/ppermute | solution.py:262
  10.5 0.5 collective-permute-start.11
  11.0 3.2 %collective-permute-done.refs_0_ = bf16[976,128]{1,0:T(8,128)(2,1)S(1)} collective-permute-done((bf16[976,128]{1,0:T(8,128)(2,1)S(1)}, bf16[976,128]{1,0:T(8,128)(2,1)S(1)}, u32[]{:S(2)}, u32[]{:S(2)}) %collective-permute-start) | collective-permute-done | bytes 249888 | tf_op jit(solution)/shard_map/exchange_heads/ppermute | solution.py:262
  14.2 1.7 %collective-permute-start.10 = (bf16[128,1280]{1,0:T(8,128)(2,1)S(1)}, bf16[128,1280]{1,0:T(8,128)(2,1)S(1)}, u32[]{:S(2)}, u32[]{:S(2)}) collective-permute-start(bf16[128,1280]{1,0:T(8,128)(2,1)S(1)} %get-tuple-element.33.refs_0_), channel_id=1, source_target_pairs={{0,8},{1,9},{2,10},{3,11},{4,12},{5,13},{6,14},{7,15},{8,0},{9,1},... | collective-permute-start | bytes 983048 | tf_op jit(solution)/shard_map/gather_cotangent/ppermute | solution.py:262
  15.9 3.9 %collective-permute-done.1.refs_2_.refs_1_ = bf16[976,128]{1,0:T(8,128)(2,1)S(1)} collective-permute-done((bf16[976,128]{1,0:T(8,128)(2,1)S(1)}, bf16[976,128]{1,0:T(8,128)(2,1)S(1)}, u32[]{:S(2)}, u32[]{:S(2)}) %collective-permute-start.1) | collective-permute-done | bytes 249888 | tf_op jit(solution)/shard_map/exchange_heads/ppermute | solution.py:262
  19.8 1.7 %attention.3 = (f32[320,384]{1,0:T(8,128)S(1)}, f32[8,384]{1,0:T(8,128)S(1)}, f32[8,384]{1,0:T(8,128)S(1)}) custom-call(bf16[976,128]{1,0:T(8,128)(2,1)S(1)} %collective-permute-done.refs_0_, bf16[976,128]{1,0:T(8,128)(2,1)S(1)} %get-tuple-element.21.refs_1_.refs_0_, bf16[976,128]{1,0:T(8,128)(2,1)S(1)} %collective-permute-done.1.refs_2_.refs_1_), custom_call_target="tpu_custom_call" | custom-call | flops 2595225600 | bytes 1310720 | tf_op jit(solution)/shard_map/attention/pallas_call | solution.py:39
  21.5 7.1 %collective-permute-done.2.refs_3_.refs_2_ = bf16[976,128]{1,0:T(8,128)(2,1)S(1)} collective-permute-done((bf16[976,128]{1,0:T(8,128)(2,1)S(1)}, bf16[976,128]{1,0:T(8,128)(2,1)S(1)}, u32[]{:S(2)}, u32[]{:S(2)}) %collective-permute-start.2) | collective-permute-done | bytes 249888 | tf_op jit(solution)/shard_map/exchange_heads/ppermute | solution.py:262
  28.5 1.5 %attention.4 = (bf16[320,128]{1,0:T(8,128)(2,1)S(1)}, bf16[320,128]{1,0:T(8,128)(2,1)S(1)}) custom-call(bf16[976,128]{1,0:T(8,128)(2,1)S(1)} %collective-permute-done.refs_0_, bf16[976,128]{1,0:T(8,128)(2,1)S(1)} %get-tuple-element.21.refs_1_.refs_0_, bf16[976,128]{1,0:T(8,128)(2,1)S(1)} %collective-permute-done.1.refs_2_.refs_1_, ...), custom_call_target="tpu_custom_call" | custom-call | flops 1441792000 | bytes 1310720 | tf_op jit(solution)/shard_map/attention/pallas_call | solution.py:39
  30.0 0.6 collective-permute-start.3
  30.6 3.9 %collective-permute-start.5 = (bf16[320,128]{1,0:T(8,128)(2,1)S(1)}, bf16[320,128]{1,0:T(8,128)(2,1)S(1)}, u32[]{:S(2)}, u32[]{:S(2)}) collective-permute-start(bf16[320,128]{1,0:T(8,128)(2,1)S(1)} %get-tuple-element.28), channel_id=1, source_target_pairs={{0,30},{1,31},{2,28},{3,29},{4,26},{5,27},{6,24},{7,25},{8,22},{9,... | collective-permute-start | bytes 245768 | tf_op jit(solution)/shard_map/send_to_owner/ppermute | solution.py:262
  34.5 1.0 %attention.5 = (bf16[320,128]{1,0:T(8,128)(2,1)S(1)}, bf16[320,128]{1,0:T(8,128)(2,1)S(1)}) custom-call(bf16[976,128]{1,0:T(8,128)(2,1)S(1)} %get-tuple-element.21.refs_1_.refs_0_, bf16[976,128]{1,0:T(8,128)(2,1)S(1)} %collective-permute-done.1.refs_2_.refs_1_, bf16[976,128]{1,0:T(8,128)(2,1)S(1)} %collective-permute-done.2.refs_3_.refs_2_, ...), custom_call_target="tpu_custom_call" | custom-call | flops 576716800 | bytes 1310720 | tf_op jit(solution)/shard_map/attention/pallas_call | solution.py:39
  35.6 0.0 collective-permute-done.12.refs_3_
  35.6 0.9 %collective-permute-start.7 = (bf16[320,128]{1,0:T(8,128)(2,1)S(1)}, bf16[320,128]{1,0:T(8,128)(2,1)S(1)}, u32[]{:S(2)}, u32[]{:S(2)}) collective-permute-start(bf16[320,128]{1,0:T(8,128)(2,1)S(1)} %get-tuple-element.29), channel_id=1, source_target_pairs={{0,10},{1,11},{2,8},{3,9},{4,14},{5,15},{6,12},{7,13},{8,2},{9,3},... | collective-permute-start | bytes 245768 | tf_op jit(solution)/shard_map/send_to_owner/ppermute | solution.py:262
  36.5 0.4 swap_cotangent.1.refs_2_
  37.0 0.1 collective-permute-start.13
  37.0 2.4 %collective-permute-done.3.refs_0_ = bf16[320,128]{1,0:T(8,128)(2,1)S(1)} collective-permute-done((bf16[320,128]{1,0:T(8,128)(2,1)S(1)}, bf16[320,128]{1,0:T(8,128)(2,1)S(1)}, u32[]{:S(2)}, u32[]{:S(2)}) %collective-permute-start.3) | collective-permute-done | bytes 81952 | tf_op jit(solution)/shard_map/send_to_owner/ppermute | solution.py:262
  39.4 1.6 %collective-permute-done.7.refs_2_ = bf16[320,128]{1,0:T(8,128)(2,1)S(1)} collective-permute-done((bf16[320,128]{1,0:T(8,128)(2,1)S(1)}, bf16[320,128]{1,0:T(8,128)(2,1)S(1)}, u32[]{:S(2)}, u32[]{:S(2)}) %collective-permute-start.7) | collective-permute-done | bytes 81952 | tf_op jit(solution)/shard_map/send_to_owner/ppermute | solution.py:262
  41.0 0.1 collective-permute-start.9
  41.1 1.0 %collective-permute-start.4 = (bf16[320,128]{1,0:T(8,128)(2,1)S(1)}, bf16[320,128]{1,0:T(8,128)(2,1)S(1)}, u32[]{:S(2)}, u32[]{:S(2)}) collective-permute-start(bf16[320,128]{1,0:T(8,128)(2,1)S(1)} %collective-permute-done.3.refs_0_), channel_id=1, source_target_pairs={{0,16},{1,17},{2,18},{3,19},{4,20},{5,21},{6,22},{7,23},{8,24},{9,... | collective-permute-start | bytes 245768 | tf_op jit(solution)/shard_map/send_home/ppermute | solution.py:262
  42.1 1.1 %collective-permute-start.6 = (bf16[320,128]{1,0:T(8,128)(2,1)S(1)}, bf16[320,128]{1,0:T(8,128)(2,1)S(1)}, u32[]{:S(2)}, u32[]{:S(2)}) collective-permute-start(bf16[320,128]{1,0:T(8,128)(2,1)S(1)} %collective-permute-done.5.refs_1_), channel_id=1, source_target_pairs={{0,24},{1,25},{2,26},{3,27},{4,28},{5,29},{6,30},{7,31},{8,16},{9,... | collective-permute-start | bytes 245768 | tf_op jit(solution)/shard_map/send_home/ppermute | solution.py:262
  43.2 1.5 %collective-permute-start.8 = (bf16[320,128]{1,0:T(8,128)(2,1)S(1)}, bf16[320,128]{1,0:T(8,128)(2,1)S(1)}, u32[]{:S(2)}, u32[]{:S(2)}) collective-permute-start(bf16[320,128]{1,0:T(8,128)(2,1)S(1)} %collective-permute-done.7.refs_2_), channel_id=1, source_target_pairs={{0,8},{1,9},{2,10},{3,11},{4,12},{5,13},{6,14},{7,15},{8,0},{9,1},... | collective-permute-start | bytes 245768 | tf_op jit(solution)/shard_map/send_home/ppermute | solution.py:262
  44.7 0.9 %gradient.1 = (bf16[80,640]{1,0:T(8,128)(2,1)S(1)}, bf16[80,640]{1,0:T(8,128)(2,1)S(1)}, bf16[80,640]{1,0:T(8,128)(2,1)S(1)}, bf16[80,640]{1,0:T(8,128)(2,1)S(1)}) custom-call(bf16[4,160,128]{2,1,0:T(8,128)(2,1)S(1)} %get-tuple-element.31.refs_0_, bf16[4,160,128]{2,1,0:T(8,128)(2,1)S(1)} %collective-permute-done.9.refs_1_, ...), custom_call_target="tpu_custom_call" | custom-call | flops 419430400 | bytes 2621440 | tf_op jit(solution)/shard_map/gradient/pallas_call | solution.py:39
  45.6 2.1 %collective-permute-start.14 = (bf16[80,640]{1,0:T(8,128)(2,1)S(1)}, bf16[80,640]{1,0:T(8,128)(2,1)S(1)}, u32[]{:S(2)}, u32[]{:S(2)}) collective-permute-start(bf16[80,640]{1,0:T(8,128)(2,1)S(1)} %get-tuple-element.34), channel_id=1, source_target_pairs={{0,4},{1,5},{2,14},{3,15},{4,16},{5,17},{6,26},{7,27},{8,12},{9,13... | collective-permute-start | bytes 307208 | tf_op jit(solution)/shard_map/sum_gradient/ppermute | solution.py:262
  47.7 2.2 %collective-permute-start.15 = (bf16[80,640]{1,0:T(8,128)(2,1)S(1)}, bf16[80,640]{1,0:T(8,128)(2,1)S(1)}, u32[]{:S(2)}, u32[]{:S(2)}) collective-permute-start(bf16[80,640]{1,0:T(8,128)(2,1)S(1)} %get-tuple-element.35), channel_id=1, source_target_pairs={{0,6},{1,7},{2,12},{3,13},{4,18},{5,19},{6,24},{7,25},{8,14},{9,15... | collective-permute-start | bytes 307208 | tf_op jit(solution)/shard_map/sum_gradient/ppermute | solution.py:262
  49.9 0.7 %collective-permute-start.17 = (bf16[80,640]{1,0:T(8,128)(2,1)S(1)}, bf16[80,640]{1,0:T(8,128)(2,1)S(1)}, u32[]{:S(2)}, u32[]{:S(2)}) collective-permute-start(bf16[80,640]{1,0:T(8,128)(2,1)S(1)} %get-tuple-element.37), channel_id=1, source_target_pairs={{0,0},{1,1},{2,10},{3,11},{4,20},{5,21},{6,30},{7,31},{8,8},{9,9},... | collective-permute-start | bytes 307208 | tf_op jit(solution)/shard_map/sum_gradient/ppermute | solution.py:262
  50.6 1.4 %project.1 = bf16[128,1280]{1,0:T(8,128)(2,1)} custom-call(bf16[320,128]{1,0:T(8,128)(2,1)S(1)} %collective-permute-done.4.refs_0_, bf16[320,128]{1,0:T(8,128)(2,1)S(1)} %collective-permute-done.6.refs_1_, bf16[320,128]{1,0:T(8,128)(2,1)S(1)} %collective-permute-done.8.refs_2_, bf16[320,128]{1,0:T(8,128)(2,1)S(1)} %get-tuple-element.30.refs_3_, ...), custom_call_target="tpu_custom_call" | custom-call | flops 419430400 | bytes 3276800 | tf_op jit(solution)/shard_map/project/pallas_call | solution.py:39
  52.0 5.1 %collective-permute-done.14.refs_0_ = bf16[80,640]{1,0:T(8,128)(2,1)S(1)} collective-permute-done((bf16[80,640]{1,0:T(8,128)(2,1)S(1)}, bf16[80,640]{1,0:T(8,128)(2,1)S(1)}, u32[]{:S(2)}, u32[]{:S(2)}) %collective-permute-start.14) | collective-permute-done | bytes 102432 | tf_op jit(solution)/shard_map/sum_gradient/ppermute | solution.py:262
  57.1 0.4 collective-permute-done.16.refs_2_
  57.5 0.8 %add_gradient.1 = f32[160,320]{1,0:T(8,128)} custom-call(bf16[80,640]{1,0:T(8,128)(2,1)S(1)} %collective-permute-done.14.refs_0_, bf16[80,640]{1,0:T(8,128)(2,1)S(1)} %collective-permute-done.15.refs_1_, bf16[80,640]{1,0:T(8,128)(2,1)S(1)} %collective-permute-done.16.refs_2_, bf16[80,640]{1,0:T(8,128)(2,1)S(1)} %collective-permute-done.17.refs_3_), custom_call_target="tpu_custom_call" | custom-call | bytes 819200 | tf_op jit(solution)/shard_map/add_gradient/pallas_call | solution.py:39
  (17 shorter events, 0.1 us)
Async XLA Ops:
  2.2 12.1 %collective-permute-start = (bf16[976,128]{1,0:T(8,128)(2,1)S(1)}, bf16[976,128]{1,0:T(8,128)(2,1)S(1)}, u32[]{:S(2)}, u32[]{:S(2)}) collective-permute-start(bf16[976,128]{1,0:T(8,128)(2,1)S(1)} %get-tuple-element.20), channel_id=1, source_target_pairs={{0,6},{1,7},{2,4},{3,5},{4,2},{5,3},{6,0},{7,1},{8,14},{9,15},{10,... | collective-permute-start | bytes 749576 | tf_op jit(solution)/shard_map/exchange_heads/ppermute | solution.py:262
  7.3 12.5 %collective-permute-start.1 = (bf16[976,128]{1,0:T(8,128)(2,1)S(1)}, bf16[976,128]{1,0:T(8,128)(2,1)S(1)}, u32[]{:S(2)}, u32[]{:S(2)}) collective-permute-start(bf16[976,128]{1,0:T(8,128)(2,1)S(1)} %get-tuple-element.22), channel_id=1, source_target_pairs={{0,2},{1,3},{2,0},{3,1},{4,6},{5,7},{6,4},{7,5},{8,10},{9,11},{10,... | collective-permute-start | bytes 749576 | tf_op jit(solution)/shard_map/exchange_heads/ppermute | solution.py:262
  7.3 21.3 %collective-permute-start.2 = (bf16[976,128]{1,0:T(8,128)(2,1)S(1)}, bf16[976,128]{1,0:T(8,128)(2,1)S(1)}, u32[]{:S(2)}, u32[]{:S(2)}) collective-permute-start(bf16[976,128]{1,0:T(8,128)(2,1)S(1)} %get-tuple-element.23), channel_id=1, source_target_pairs={{0,4},{1,5},{2,6},{3,7},{4,0},{5,1},{6,2},{7,3},{8,12},{9,13},{10,... | collective-permute-start | bytes 749576 | tf_op jit(solution)/shard_map/exchange_heads/ppermute | solution.py:262
  7.9 27.7 %collective-permute-start.12 = (bf16[128,1280]{1,0:T(8,128)(2,1)S(1)}, bf16[128,1280]{1,0:T(8,128)(2,1)S(1)}, u32[]{:S(2)}, u32[]{:S(2)}) collective-permute-start(bf16[128,1280]{1,0:T(8,128)(2,1)S(1)} %get-tuple-element.33.refs_0_), channel_id=1, source_target_pairs={{0,24},{1,25},{2,26},{3,27},{4,28},{5,29},{6,30},{7,31},{8,16},{9,... | collective-permute-start | bytes 983048 | tf_op jit(solution)/shard_map/gather_cotangent/ppermute | solution.py:262
  10.5 26.0 %collective-permute-start.11 = (bf16[128,1280]{1,0:T(8,128)(2,1)S(1)}, bf16[128,1280]{1,0:T(8,128)(2,1)S(1)}, u32[]{:S(2)}, u32[]{:S(2)}) collective-permute-start(bf16[128,1280]{1,0:T(8,128)(2,1)S(1)} %get-tuple-element.33.refs_0_), channel_id=1, source_target_pairs={{0,16},{1,17},{2,18},{3,19},{4,20},{5,21},{6,22},{7,23},{8,24},{9,... | collective-permute-start | bytes 983048 | tf_op jit(solution)/shard_map/gather_cotangent/ppermute | solution.py:262
  14.2 22.3 %collective-permute-start.10 = (bf16[128,1280]{1,0:T(8,128)(2,1)S(1)}, bf16[128,1280]{1,0:T(8,128)(2,1)S(1)}, u32[]{:S(2)}, u32[]{:S(2)}) collective-permute-start(bf16[128,1280]{1,0:T(8,128)(2,1)S(1)} %get-tuple-element.33.refs_0_), channel_id=1, source_target_pairs={{0,8},{1,9},{2,10},{3,11},{4,12},{5,13},{6,14},{7,15},{8,0},{9,1},... | collective-permute-start | bytes 983048 | tf_op jit(solution)/shard_map/gather_cotangent/ppermute | solution.py:262
  30.0 9.4 %collective-permute-start.3 = (bf16[320,128]{1,0:T(8,128)(2,1)S(1)}, bf16[320,128]{1,0:T(8,128)(2,1)S(1)}, u32[]{:S(2)}, u32[]{:S(2)}) collective-permute-start(bf16[320,128]{1,0:T(8,128)(2,1)S(1)} %get-tuple-element.27), channel_id=1, source_target_pairs={{0,20},{1,21},{2,22},{3,23},{4,16},{5,17},{6,18},{7,19},{8,28},{9,... | collective-permute-start | bytes 245768 | tf_op jit(solution)/shard_map/send_to_owner/ppermute | solution.py:262
  30.6 8.8 %collective-permute-start.5 = (bf16[320,128]{1,0:T(8,128)(2,1)S(1)}, bf16[320,128]{1,0:T(8,128)(2,1)S(1)}, u32[]{:S(2)}, u32[]{:S(2)}) collective-permute-start(bf16[320,128]{1,0:T(8,128)(2,1)S(1)} %get-tuple-element.28), channel_id=1, source_target_pairs={{0,30},{1,31},{2,28},{3,29},{4,26},{5,27},{6,24},{7,25},{8,22},{9,... | collective-permute-start | bytes 245768 | tf_op jit(solution)/shard_map/send_to_owner/ppermute | solution.py:262
  35.6 5.4 %collective-permute-start.7 = (bf16[320,128]{1,0:T(8,128)(2,1)S(1)}, bf16[320,128]{1,0:T(8,128)(2,1)S(1)}, u32[]{:S(2)}, u32[]{:S(2)}) collective-permute-start(bf16[320,128]{1,0:T(8,128)(2,1)S(1)} %get-tuple-element.29), channel_id=1, source_target_pairs={{0,10},{1,11},{2,8},{3,9},{4,14},{5,15},{6,12},{7,13},{8,2},{9,3},... | collective-permute-start | bytes 245768 | tf_op jit(solution)/shard_map/send_to_owner/ppermute | solution.py:262
  37.0 7.7 %collective-permute-start.13 = (bf16[4,128,1280]{2,1,0:T(8,128)(2,1)S(1)}, bf16[4,128,1280]{2,1,0:T(8,128)(2,1)S(1)}, u32[]{:S(2)}, u32[]{:S(2)}) collective-permute-start(bf16[4,128,1280]{2,1,0:T(8,128)(2,1)S(1)} %swap_cotangent.1.refs_2_), channel_id=1, source_target_pairs={{0,1},{1,0},{2,3},{3,2},{4,5},{5,4},{6,7},{7,6},{8,9},{9,8},{10,11... | collective-permute-start | bytes 3932168 | tf_op jit(solution)/shard_map/gradient/ppermute | solution.py:262
  41.0 9.6 %copy-start = (bf16[1280,1280]{1,0:T(8,128)(2,1)S(1)}, bf16[1280,1280]{1,0:T(8,128)(2,1)}, u32[]{:S(2)}) copy-start(bf16[1280,1280]{1,0:T(8,128)(2,1)} %refs_5_.1) | copy-start | bytes 9830404
  41.0 3.6 %collective-permute-start.9 = (bf16[4,160,128]{2,1,0:T(8,128)(2,1)S(1)}, bf16[4,160,128]{2,1,0:T(8,128)(2,1)S(1)}, u32[]{:S(2)}, u32[]{:S(2)}) collective-permute-start(bf16[4,160,128]{2,1,0:T(8,128)(2,1)S(1)} %get-tuple-element.32), channel_id=1, source_target_pairs={{0,1},{1,0},{2,3},{3,2},{4,5},{5,4},{6,7},{7,6},{8,9},{9,8},{10,11... | collective-permute-start | bytes 491528 | tf_op jit(solution)/shard_map/send_to_owner/ppermute | solution.py:262
  41.1 8.8 %collective-permute-start.4 = (bf16[320,128]{1,0:T(8,128)(2,1)S(1)}, bf16[320,128]{1,0:T(8,128)(2,1)S(1)}, u32[]{:S(2)}, u32[]{:S(2)}) collective-permute-start(bf16[320,128]{1,0:T(8,128)(2,1)S(1)} %collective-permute-done.3.refs_0_), channel_id=1, source_target_pairs={{0,16},{1,17},{2,18},{3,19},{4,20},{5,21},{6,22},{7,23},{8,24},{9,... | collective-permute-start | bytes 245768 | tf_op jit(solution)/shard_map/send_home/ppermute | solution.py:262
  42.1 7.8 %collective-permute-start.6 = (bf16[320,128]{1,0:T(8,128)(2,1)S(1)}, bf16[320,128]{1,0:T(8,128)(2,1)S(1)}, u32[]{:S(2)}, u32[]{:S(2)}) collective-permute-start(bf16[320,128]{1,0:T(8,128)(2,1)S(1)} %collective-permute-done.5.refs_1_), channel_id=1, source_target_pairs={{0,24},{1,25},{2,26},{3,27},{4,28},{5,29},{6,30},{7,31},{8,16},{9,... | collective-permute-start | bytes 245768 | tf_op jit(solution)/shard_map/send_home/ppermute | solution.py:262
  43.2 7.4 %collective-permute-start.8 = (bf16[320,128]{1,0:T(8,128)(2,1)S(1)}, bf16[320,128]{1,0:T(8,128)(2,1)S(1)}, u32[]{:S(2)}, u32[]{:S(2)}) collective-permute-start(bf16[320,128]{1,0:T(8,128)(2,1)S(1)} %collective-permute-done.7.refs_2_), channel_id=1, source_target_pairs={{0,8},{1,9},{2,10},{3,11},{4,12},{5,13},{6,14},{7,15},{8,0},{9,1},... | collective-permute-start | bytes 245768 | tf_op jit(solution)/shard_map/send_home/ppermute | solution.py:262
  44.7 6.0 %copy-start.1 = (bf16[128,1280]{1,0:T(8,128)(2,1)S(1)}, bf16[128,1280]{1,0:T(8,128)(2,1)}, u32[]{:S(2)}) copy-start(bf16[128,1280]{1,0:T(8,128)(2,1)} %refs_4_.3) | copy-start | bytes 983044
  45.6 11.5 %collective-permute-start.14 = (bf16[80,640]{1,0:T(8,128)(2,1)S(1)}, bf16[80,640]{1,0:T(8,128)(2,1)S(1)}, u32[]{:S(2)}, u32[]{:S(2)}) collective-permute-start(bf16[80,640]{1,0:T(8,128)(2,1)S(1)} %get-tuple-element.34), channel_id=1, source_target_pairs={{0,4},{1,5},{2,14},{3,15},{4,16},{5,17},{6,26},{7,27},{8,12},{9,13... | collective-permute-start | bytes 307208 | tf_op jit(solution)/shard_map/sum_gradient/ppermute | solution.py:262
  47.7 9.4 %collective-permute-start.15 = (bf16[80,640]{1,0:T(8,128)(2,1)S(1)}, bf16[80,640]{1,0:T(8,128)(2,1)S(1)}, u32[]{:S(2)}, u32[]{:S(2)}) collective-permute-start(bf16[80,640]{1,0:T(8,128)(2,1)S(1)} %get-tuple-element.35), channel_id=1, source_target_pairs={{0,6},{1,7},{2,12},{3,13},{4,18},{5,19},{6,24},{7,25},{8,14},{9,15... | collective-permute-start | bytes 307208 | tf_op jit(solution)/shard_map/sum_gradient/ppermute | solution.py:262
  49.9 7.6 %collective-permute-start.16 = (bf16[80,640]{1,0:T(8,128)(2,1)S(1)}, bf16[80,640]{1,0:T(8,128)(2,1)S(1)}, u32[]{:S(2)}, u32[]{:S(2)}) collective-permute-start(bf16[80,640]{1,0:T(8,128)(2,1)S(1)} %get-tuple-element.36), channel_id=1, source_target_pairs={{0,2},{1,3},{2,8},{3,9},{4,22},{5,23},{6,28},{7,29},{8,10},{9,11},... | collective-permute-start | bytes 307208 | tf_op jit(solution)/shard_map/sum_gradient/ppermute | solution.py:262
  49.9 7.6 %collective-permute-start.17 = (bf16[80,640]{1,0:T(8,128)(2,1)S(1)}, bf16[80,640]{1,0:T(8,128)(2,1)S(1)}, u32[]{:S(2)}, u32[]{:S(2)}) collective-permute-start(bf16[80,640]{1,0:T(8,128)(2,1)S(1)} %get-tuple-element.37), channel_id=1, source_target_pairs={{0,0},{1,1},{2,10},{3,11},{4,20},{5,21},{6,30},{7,31},{8,8},{9,9},... | collective-permute-start | bytes 307208 | tf_op jit(solution)/shard_map/sum_gradient/ppermute | solution.py:262

commit v7 on v6

--- a/solution.py
+++ b/solution.py
@@ -15,6 +15,7 @@
 SENDS = (3, 0, 1, 2)
 RETURNS = (2, 3, 1, 0)
 SUMS = (2, 3, 1, 0)
+TURN = (0, 3, 2, 1)
 
 
 def call(
@@ -58,7 +59,7 @@
     ]
     for copy in copies:
         copy.start()
-    first = lax.axis_index("dp") ^ lax.axis_index("enc")
+    first = lax.axis_index("dp") ^ ((4 - lax.axis_index("enc")) & 3)
     copies[0].wait()
     ids = ids_held[...]
     row = lax.broadcasted_iota(jnp.int32, (ID_ROWS, ids.shape[1]), 0)
@@ -70,7 +71,7 @@
         copies[1 + which].wait()
         held[...] = arrived[which].T
         for hop, out in zip(SENDS, outs):
-            begin = pl.multiple_of((first ^ hop) * block, 16)
+            begin = pl.multiple_of((first ^ TURN[hop]) * block, 16)
             out[which * block : (which + 1) * block] = held[pl.ds(begin, block)]
     copies[4].wait()
 
@@ -165,9 +166,9 @@
     attend_more(slabs[:1], slabs[-1], state, old_bias, [first], 0, head_width)
 
 
-def attend_rest_kernel(head_width, *refs):
-    early, late, state, outs, bias = refs[:2], refs[2], refs[3:6], refs[6:8], refs[8]
-    attend_more(early, late, state, bias, outs, late.shape[1], head_width)
+def attend_one_kernel(head_width, first, early, late, *refs):
+    state, (out, bias) = refs[:3], refs[3:]
+    attend_more([early], late, state, bias, [out], first, head_width)
 
 
 def stack_kernel(count, *refs):
@@ -187,8 +188,8 @@
     s = lax.axis_index("seq")
     half = kept.shape[1]
     for hop, piece in zip(RETURNS, pieces):
-        kept[hop] = piece[pl.ds(pl.multiple_of(s * half, 16), half)]
-        given[hop] = piece[pl.ds(pl.multiple_of((1 - s) * half, 16), half)]
+        kept[TURN[hop]] = piece[pl.ds(pl.multiple_of(s * half, 16), half)]
+        given[TURN[hop]] = piece[pl.ds(pl.multiple_of((1 - s) * half, 16), half)]
 
 
 def gradient_kernel(count, *refs):
@@ -217,10 +218,10 @@
 
 def project_kernel(*refs):
     pieces, (residual, weight, out, attended) = refs[:-4], refs[-4:]
-    first = lax.axis_index("dp") ^ lax.axis_index("enc")
+    first = lax.axis_index("dp") ^ ((4 - lax.axis_index("enc")) & 3)
     block = pieces[0].shape[0]
     for hop, piece in zip(RETURNS, pieces):
-        attended[pl.ds(pl.multiple_of((first ^ hop) * block, 16), block)] = piece[...]
+        attended[pl.ds(pl.multiple_of((first ^ TURN[hop]) * block, 16), block)] = piece[...]
     projected = lax.dot_general(
         attended[...], weight[...], (((0,), (0,)), ((), ())), preferred_element_type=jnp.float32
     )
@@ -315,20 +316,24 @@
             flops=55 * rows * (rows + group) * block,
             bytes_accessed=8 * group * block,
         )
-        rest = call(
-            functools.partial(attend_rest_kernel, head_width),
-            [bf16((block, rows))] * 2,
-            *slabs[1:],
-            *state,
-            scratch=[pltpu.VMEM((rows, 2 * rows), jnp.float32)],
-            flops=55 * rows * 2 * rows * block,
-            bytes_accessed=8 * group * block,
-        )
+        rest = [
+            call(
+                functools.partial(attend_one_kernel, head_width, index * rows),
+                bf16((block, rows)),
+                slabs[index],
+                slabs[-1],
+                *state,
+                scratch=[pltpu.VMEM((rows, rows), jnp.float32)],
+                flops=55 * rows * rows * block,
+                bytes_accessed=8 * rows * block,
+            )
+            for index in (1, 2)
+        ]
         pieces = dict(zip(SENDS, [across[0], *rest, across[1]]))
         pieces = [pieces[hop] for hop in RETURNS]
     with jax.named_scope("send_to_owner"):
         pieces = [
-            move(piece, lambda d, e, s, hop=hop: (d ^ hop, e ^ hop, s)) if hop else piece
+            move(piece, lambda d, e, s, hop=hop: (d ^ TURN[hop], e ^ hop, s)) if hop else piece
             for hop, piece in zip(RETURNS, pieces)
         ]
         kept, given = call(
@@ -360,12 +365,12 @@
         )
     with jax.named_scope("sum_gradient"):
         partial = [
-            move(part, lambda d, e, s, hop=hop: (d ^ e, e ^ hop, s))
+            move(part, lambda d, e, s, hop=hop: (d ^ TURN[e], e ^ hop, s))
             for hop, part in zip(SUMS, partial)
         ]
     with jax.named_scope("send_home"):
         homes = [
-            move(piece, lambda d, e, s, hop=hop: (d ^ hop, e, s)) if hop else piece
+            move(piece, lambda d, e, s, hop=hop: (d ^ TURN[hop], e, s)) if hop else piece
             for hop, piece in zip(RETURNS, pieces)
         ]
     with jax.named_scope("project"):

time: 58.4 us -> 59.4 us (1.017)
  waiting for transfers between devices: 23.6 us -> 24.7 us
    ppermute x18, waiting for transfers between devices: 23.6 us -> 24.7 us  [move(): return lax.ppermute(data, AXES, pairs)]
    pallas_call x9 -> x10, Pallas kernels: 9.29 us -> 9.11 us  [call(): pl.pallas_call(kernel, out_shape=out_shape, in_specs=[placed(space) for s...]
  transfers between devices with their start and end apart: 18 -> 18, of which waited for: 7 -> 7; matrix products, arithmetic and copies ran while one was open for 0% -> 0% of each run, Pallas kernels for 12% -> 11%
where the time goes in v7:
time: 59.4 us; the launch traced here: 59.3 us
  starting transfers between devices  24.7 us (42%)
  waiting for transfers between devices  24.7 us (42%)
  Pallas kernels  9.11 us (15%)
  between operations  0.77 us (1%)
    ppermute x18, starting transfers between devices, move(): return lax.ppermute(data, AXES, pairs)  24.7 us
    ppermute x18, waiting for transfers between devices, move(): return lax.ppermute(data, AXES, pairs)  24.7 us
    pallas_call x10, Pallas kernels, call(): pl.pallas_call(kernel, out_shape=out_shape, in_specs=[placed(space) for s...  9.11 us
  transfers between devices with their start and end apart: 18, of which 7 were waited for; matrix products, arithmetic and copies ran while one was open for 0% of the time, Pallas kernels for 11%

profile of v7, /device:TPU:0, one launch (start us, length us, event | category | flops | bytes accessed | tf_op | source)
XLA Modules:
  0.0 59.3 jit_solution(8977209004686226412)
XLA Ops:
  0.6 1.5 %pack.1 = (bf16[976,128]{1,0:T(8,128)(2,1)S(1)}, bf16[976,128]{1,0:T(8,128)(2,1)S(1)}, bf16[976,128]{1,0:T(8,128)(2,1)S(1)}, bf16[976,128]{1,0:T(8,128)(2,1)S(1)}, bf16[128,1280]{1,0:T(8,128)(2,1)S(1)}) custom-call(s32[1,128]{1,0:T(1,128)} %bitcast.1, bf16[128,1280]{1,0:T(8,128)(2,1)} %refs_1_.1, bf16[128,1280]{1,0:T(8,128)(2,1)} %refs_2_.1, ...), custom_call_target="tpu_custom_call" | custom-call | bytes 2621440 | tf_op jit(solution)/shard_map/pack/pallas_call | solution.py:40
  2.2 5.1 %collective-permute-start = (bf16[976,128]{1,0:T(8,128)(2,1)S(1)}, bf16[976,128]{1,0:T(8,128)(2,1)S(1)}, u32[]{:S(2)}, u32[]{:S(2)}) collective-permute-start(bf16[976,128]{1,0:T(8,128)(2,1)S(1)} %get-tuple-element.18), channel_id=1, source_target_pairs={{0,6},{1,7},{2,4},{3,5},{4,2},{5,3},{6,0},{7,1},{8,14},{9,15},{10,... | collective-permute-start | bytes 749576 | tf_op jit(solution)/shard_map/exchange_heads/ppermute | solution.py:263
  7.3 0.6 %collective-permute-start.2 = (bf16[976,128]{1,0:T(8,128)(2,1)S(1)}, bf16[976,128]{1,0:T(8,128)(2,1)S(1)}, u32[]{:S(2)}, u32[]{:S(2)}) collective-permute-start(bf16[976,128]{1,0:T(8,128)(2,1)S(1)} %get-tuple-element.21), channel_id=1, source_target_pairs={{0,4},{1,5},{2,6},{3,7},{4,0},{5,1},{6,2},{7,3},{8,12},{9,13},{10,... | collective-permute-start | bytes 749576 | tf_op jit(solution)/shard_map/exchange_heads/ppermute | solution.py:263
  7.9 2.6 %collective-permute-start.12 = (bf16[128,1280]{1,0:T(8,128)(2,1)S(1)}, bf16[128,1280]{1,0:T(8,128)(2,1)S(1)}, u32[]{:S(2)}, u32[]{:S(2)}) collective-permute-start(bf16[128,1280]{1,0:T(8,128)(2,1)S(1)} %get-tuple-element.29.refs_0_), channel_id=1, source_target_pairs={{0,24},{1,25},{2,26},{3,27},{4,28},{5,29},{6,30},{7,31},{8,16},{9,... | collective-permute-start | bytes 983048 | tf_op jit(solution)/shard_map/gather_cotangent/ppermute | solution.py:263
  10.5 0.5 collective-permute-start.11
  11.0 3.2 %collective-permute-done.refs_0_ = bf16[976,128]{1,0:T(8,128)(2,1)S(1)} collective-permute-done((bf16[976,128]{1,0:T(8,128)(2,1)S(1)}, bf16[976,128]{1,0:T(8,128)(2,1)S(1)}, u32[]{:S(2)}, u32[]{:S(2)}) %collective-permute-start) | collective-permute-done | bytes 249888 | tf_op jit(solution)/shard_map/exchange_heads/ppermute | solution.py:263
  14.2 1.7 %collective-permute-start.10 = (bf16[128,1280]{1,0:T(8,128)(2,1)S(1)}, bf16[128,1280]{1,0:T(8,128)(2,1)S(1)}, u32[]{:S(2)}, u32[]{:S(2)}) collective-permute-start(bf16[128,1280]{1,0:T(8,128)(2,1)S(1)} %get-tuple-element.29.refs_0_), channel_id=1, source_target_pairs={{0,8},{1,9},{2,10},{3,11},{4,12},{5,13},{6,14},{7,15},{8,0},{9,1},... | collective-permute-start | bytes 983048 | tf_op jit(solution)/shard_map/gather_cotangent/ppermute | solution.py:263
  15.9 3.9 %collective-permute-done.1.refs_2_.early = bf16[976,128]{1,0:T(8,128)(2,1)S(1)} collective-permute-done((bf16[976,128]{1,0:T(8,128)(2,1)S(1)}, bf16[976,128]{1,0:T(8,128)(2,1)S(1)}, u32[]{:S(2)}, u32[]{:S(2)}) %collective-permute-start.1) | collective-permute-done | bytes 249888 | tf_op jit(solution)/shard_map/exchange_heads/ppermute | solution.py:263
  19.8 1.7 %attention.4 = (f32[320,384]{1,0:T(8,128)S(1)}, f32[8,384]{1,0:T(8,128)S(1)}, f32[8,384]{1,0:T(8,128)S(1)}) custom-call(bf16[976,128]{1,0:T(8,128)(2,1)S(1)} %collective-permute-done.refs_0_, bf16[976,128]{1,0:T(8,128)(2,1)S(1)} %get-tuple-element.19.refs_1_.early, bf16[976,128]{1,0:T(8,128)(2,1)S(1)} %collective-permute-done.1.refs_2_.early), custom_call_target="tpu_custom_call" | custom-call | flops 2595225600 | bytes 1310720 | tf_op jit(solution)/shard_map/attention/pallas_call | solution.py:40
  21.5 7.0 %collective-permute-done.2.refs_3_.late = bf16[976,128]{1,0:T(8,128)(2,1)S(1)} collective-permute-done((bf16[976,128]{1,0:T(8,128)(2,1)S(1)}, bf16[976,128]{1,0:T(8,128)(2,1)S(1)}, u32[]{:S(2)}, u32[]{:S(2)}) %collective-permute-start.2) | collective-permute-done | bytes 249888 | tf_op jit(solution)/shard_map/exchange_heads/ppermute | solution.py:263
  28.5 1.5 %attention.5 = (bf16[320,128]{1,0:T(8,128)(2,1)S(1)}, bf16[320,128]{1,0:T(8,128)(2,1)S(1)}) custom-call(bf16[976,128]{1,0:T(8,128)(2,1)S(1)} %collective-permute-done.refs_0_, bf16[976,128]{1,0:T(8,128)(2,1)S(1)} %get-tuple-element.19.refs_1_.early, bf16[976,128]{1,0:T(8,128)(2,1)S(1)} %collective-permute-done.1.refs_2_.early, ...), custom_call_target="tpu_custom_call" | custom-call | flops 1441792000 | bytes 1310720 | tf_op jit(solution)/shard_map/attention/pallas_call | solution.py:40
  30.0 0.6 collective-permute-start.3
  30.6 3.4 %collective-permute-start.5 = (bf16[320,128]{1,0:T(8,128)(2,1)S(1)}, bf16[320,128]{1,0:T(8,128)(2,1)S(1)}, u32[]{:S(2)}, u32[]{:S(2)}) collective-permute-start(bf16[320,128]{1,0:T(8,128)(2,1)S(1)} %get-tuple-element.26), channel_id=1, source_target_pairs={{0,14},{1,15},{2,12},{3,13},{4,10},{5,11},{6,8},{7,9},{8,6},{9,7},... | collective-permute-start | bytes 245768 | tf_op jit(solution)/shard_map/send_to_owner/ppermute | solution.py:263
  34.0 0.4 attention.6
  34.4 1.5 %collective-permute-start.7 = (bf16[320,128]{1,0:T(8,128)(2,1)S(1)}, bf16[320,128]{1,0:T(8,128)(2,1)S(1)}, u32[]{:S(2)}, u32[]{:S(2)}) collective-permute-start(bf16[320,128]{1,0:T(8,128)(2,1)S(1)} %attention.6), channel_id=1, source_target_pairs={{0,26},{1,27},{2,24},{3,25},{4,30},{5,31},{6,28},{7,29},{8,18},{9,... | collective-permute-start | bytes 245768 | tf_op jit(solution)/shard_map/send_to_owner/ppermute | solution.py:263
  35.9 0.4 attention.7.refs_3_
  36.3 0.5 swap_cotangent.1.refs_2_
  36.8 0.1 collective-permute-start.13
  36.9 2.6 %collective-permute-done.3.refs_0_ = bf16[320,128]{1,0:T(8,128)(2,1)S(1)} collective-permute-done((bf16[320,128]{1,0:T(8,128)(2,1)S(1)}, bf16[320,128]{1,0:T(8,128)(2,1)S(1)}, u32[]{:S(2)}, u32[]{:S(2)}) %collective-permute-start.3) | collective-permute-done | bytes 81952 | tf_op jit(solution)/shard_map/send_to_owner/ppermute | solution.py:263
  39.5 1.8 %collective-permute-done.7.refs_2_ = bf16[320,128]{1,0:T(8,128)(2,1)S(1)} collective-permute-done((bf16[320,128]{1,0:T(8,128)(2,1)S(1)}, bf16[320,128]{1,0:T(8,128)(2,1)S(1)}, u32[]{:S(2)}, u32[]{:S(2)}) %collective-permute-start.7) | collective-permute-done | bytes 81952 | tf_op jit(solution)/shard_map/send_to_owner/ppermute | solution.py:263
  41.4 1.0 %collective-permute-start.4 = (bf16[320,128]{1,0:T(8,128)(2,1)S(1)}, bf16[320,128]{1,0:T(8,128)(2,1)S(1)}, u32[]{:S(2)}, u32[]{:S(2)}) collective-permute-start(bf16[320,128]{1,0:T(8,128)(2,1)S(1)} %collective-permute-done.3.refs_0_), channel_id=1, source_target_pairs={{0,16},{1,17},{2,18},{3,19},{4,20},{5,21},{6,22},{7,23},{8,24},{9,... | collective-permute-start | bytes 245768 | tf_op jit(solution)/shard_map/send_home/ppermute | solution.py:263
  42.4 0.6 %collective-permute-start.6 = (bf16[320,128]{1,0:T(8,128)(2,1)S(1)}, bf16[320,128]{1,0:T(8,128)(2,1)S(1)}, u32[]{:S(2)}, u32[]{:S(2)}) collective-permute-start(bf16[320,128]{1,0:T(8,128)(2,1)S(1)} %collective-permute-done.5.refs_1_), channel_id=1, source_target_pairs={{0,8},{1,9},{2,10},{3,11},{4,12},{5,13},{6,14},{7,15},{8,0},{9,1},... | collective-permute-start | bytes 245768 | tf_op jit(solution)/shard_map/send_home/ppermute | solution.py:263
  43.0 1.9 %collective-permute-start.8 = (bf16[320,128]{1,0:T(8,128)(2,1)S(1)}, bf16[320,128]{1,0:T(8,128)(2,1)S(1)}, u32[]{:S(2)}, u32[]{:S(2)}) collective-permute-start(bf16[320,128]{1,0:T(8,128)(2,1)S(1)} %collective-permute-done.7.refs_2_), channel_id=1, source_target_pairs={{0,24},{1,25},{2,26},{3,27},{4,28},{5,29},{6,30},{7,31},{8,16},{9,... | collective-permute-start | bytes 245768 | tf_op jit(solution)/shard_map/send_home/ppermute | solution.py:263
  44.9 0.9 %gradient.1 = (bf16[80,640]{1,0:T(8,128)(2,1)S(1)}, bf16[80,640]{1,0:T(8,128)(2,1)S(1)}, bf16[80,640]{1,0:T(8,128)(2,1)S(1)}, bf16[80,640]{1,0:T(8,128)(2,1)S(1)}) custom-call(bf16[4,160,128]{2,1,0:T(8,128)(2,1)S(1)} %get-tuple-element.27.refs_0_, bf16[4,160,128]{2,1,0:T(8,128)(2,1)S(1)} %collective-permute-done.9.refs_1_, ...), custom_call_target="tpu_custom_call" | custom-call | flops 419430400 | bytes 2621440 | tf_op jit(solution)/shard_map/gradient/pallas_call | solution.py:40
  45.9 2.0 %collective-permute-start.14 = (bf16[80,640]{1,0:T(8,128)(2,1)S(1)}, bf16[80,640]{1,0:T(8,128)(2,1)S(1)}, u32[]{:S(2)}, u32[]{:S(2)}) collective-permute-start(bf16[80,640]{1,0:T(8,128)(2,1)S(1)} %get-tuple-element.30), channel_id=1, source_target_pairs={{0,4},{1,5},{2,30},{3,31},{4,16},{5,17},{6,10},{7,11},{8,12},{9,13... | collective-permute-start | bytes 307208 | tf_op jit(solution)/shard_map/sum_gradient/ppermute | solution.py:263
  47.9 1.8 %collective-permute-start.15 = (bf16[80,640]{1,0:T(8,128)(2,1)S(1)}, bf16[80,640]{1,0:T(8,128)(2,1)S(1)}, u32[]{:S(2)}, u32[]{:S(2)}) collective-permute-start(bf16[80,640]{1,0:T(8,128)(2,1)S(1)} %get-tuple-element.31), channel_id=1, source_target_pairs={{0,6},{1,7},{2,28},{3,29},{4,18},{5,19},{6,8},{7,9},{8,14},{9,15},... | collective-permute-start | bytes 307208 | tf_op jit(solution)/shard_map/sum_gradient/ppermute | solution.py:263
  49.7 0.6 collective-permute-start.16
  50.3 0.7 %collective-permute-start.17 = (bf16[80,640]{1,0:T(8,128)(2,1)S(1)}, bf16[80,640]{1,0:T(8,128)(2,1)S(1)}, u32[]{:S(2)}, u32[]{:S(2)}) collective-permute-start(bf16[80,640]{1,0:T(8,128)(2,1)S(1)} %get-tuple-element.33), channel_id=1, source_target_pairs={{0,0},{1,1},{2,26},{3,27},{4,20},{5,21},{6,14},{7,15},{8,8},{9,9},... | collective-permute-start | bytes 307208 | tf_op jit(solution)/shard_map/sum_gradient/ppermute | solution.py:263
  51.0 1.4 %project.1 = bf16[128,1280]{1,0:T(8,128)(2,1)} custom-call(bf16[320,128]{1,0:T(8,128)(2,1)S(1)} %collective-permute-done.4.refs_0_, bf16[320,128]{1,0:T(8,128)(2,1)S(1)} %collective-permute-done.6.refs_1_, bf16[320,128]{1,0:T(8,128)(2,1)S(1)} %collective-permute-done.8.refs_2_, bf16[320,128]{1,0:T(8,128)(2,1)S(1)} %attention.7.refs_3_, ...), custom_call_target="tpu_custom_call" | custom-call | flops 419430400 | bytes 3276800 | tf_op jit(solution)/shard_map/project/pallas_call | solution.py:40
  52.4 4.5 %collective-permute-done.14.refs_0_ = bf16[80,640]{1,0:T(8,128)(2,1)S(1)} collective-permute-done((bf16[80,640]{1,0:T(8,128)(2,1)S(1)}, bf16[80,640]{1,0:T(8,128)(2,1)S(1)}, u32[]{:S(2)}, u32[]{:S(2)}) %collective-permute-start.14) | collective-permute-done | bytes 102432 | tf_op jit(solution)/shard_map/sum_gradient/ppermute | solution.py:263
  56.9 1.6 %collective-permute-done.16.refs_2_ = bf16[80,640]{1,0:T(8,128)(2,1)S(1)} collective-permute-done((bf16[80,640]{1,0:T(8,128)(2,1)S(1)}, bf16[80,640]{1,0:T(8,128)(2,1)S(1)}, u32[]{:S(2)}, u32[]{:S(2)}) %collective-permute-start.16) | collective-permute-done | bytes 102432 | tf_op jit(solution)/shard_map/sum_gradient/ppermute | solution.py:263
  58.5 0.8 %add_gradient.1 = f32[160,320]{1,0:T(8,128)} custom-call(bf16[80,640]{1,0:T(8,128)(2,1)S(1)} %collective-permute-done.14.refs_0_, bf16[80,640]{1,0:T(8,128)(2,1)S(1)} %collective-permute-done.15.refs_1_, bf16[80,640]{1,0:T(8,128)(2,1)S(1)} %collective-permute-done.16.refs_2_, bf16[80,640]{1,0:T(8,128)(2,1)S(1)} %collective-permute-done.17.refs_3_), custom_call_target="tpu_custom_call" | custom-call | bytes 819200 | tf_op jit(solution)/shard_map/add_gradient/pallas_call | solution.py:40
  (18 shorter events, 0.1 us)
Async XLA Ops:
  2.2 12.1 %collective-permute-start = (bf16[976,128]{1,0:T(8,128)(2,1)S(1)}, bf16[976,128]{1,0:T(8,128)(2,1)S(1)}, u32[]{:S(2)}, u32[]{:S(2)}) collective-permute-start(bf16[976,128]{1,0:T(8,128)(2,1)S(1)} %get-tuple-element.18), channel_id=1, source_target_pairs={{0,6},{1,7},{2,4},{3,5},{4,2},{5,3},{6,0},{7,1},{8,14},{9,15},{10,... | collective-permute-start | bytes 749576 | tf_op jit(solution)/shard_map/exchange_heads/ppermute | solution.py:263
  7.3 12.5 %collective-permute-start.1 = (bf16[976,128]{1,0:T(8,128)(2,1)S(1)}, bf16[976,128]{1,0:T(8,128)(2,1)S(1)}, u32[]{:S(2)}, u32[]{:S(2)}) collective-permute-start(bf16[976,128]{1,0:T(8,128)(2,1)S(1)} %get-tuple-element.20), channel_id=1, source_target_pairs={{0,2},{1,3},{2,0},{3,1},{4,6},{5,7},{6,4},{7,5},{8,10},{9,11},{10,... | collective-permute-start | bytes 749576 | tf_op jit(solution)/shard_map/exchange_heads/ppermute | solution.py:263
  7.3 21.3 %collective-permute-start.2 = (bf16[976,128]{1,0:T(8,128)(2,1)S(1)}, bf16[976,128]{1,0:T(8,128)(2,1)S(1)}, u32[]{:S(2)}, u32[]{:S(2)}) collective-permute-start(bf16[976,128]{1,0:T(8,128)(2,1)S(1)} %get-tuple-element.21), channel_id=1, source_target_pairs={{0,4},{1,5},{2,6},{3,7},{4,0},{5,1},{6,2},{7,3},{8,12},{9,13},{10,... | collective-permute-start | bytes 749576 | tf_op jit(solution)/shard_map/exchange_heads/ppermute | solution.py:263
  7.9 26.5 %collective-permute-start.12 = (bf16[128,1280]{1,0:T(8,128)(2,1)S(1)}, bf16[128,1280]{1,0:T(8,128)(2,1)S(1)}, u32[]{:S(2)}, u32[]{:S(2)}) collective-permute-start(bf16[128,1280]{1,0:T(8,128)(2,1)S(1)} %get-tuple-element.29.refs_0_), channel_id=1, source_target_pairs={{0,24},{1,25},{2,26},{3,27},{4,28},{5,29},{6,30},{7,31},{8,16},{9,... | collective-permute-start | bytes 983048 | tf_op jit(solution)/shard_map/gather_cotangent/ppermute | solution.py:263
  10.5 25.8 %collective-permute-start.11 = (bf16[128,1280]{1,0:T(8,128)(2,1)S(1)}, bf16[128,1280]{1,0:T(8,128)(2,1)S(1)}, u32[]{:S(2)}, u32[]{:S(2)}) collective-permute-start(bf16[128,1280]{1,0:T(8,128)(2,1)S(1)} %get-tuple-element.29.refs_0_), channel_id=1, source_target_pairs={{0,16},{1,17},{2,18},{3,19},{4,20},{5,21},{6,22},{7,23},{8,24},{9,... | collective-permute-start | bytes 983048 | tf_op jit(solution)/shard_map/gather_cotangent/ppermute | solution.py:263
  14.2 22.1 %collective-permute-start.10 = (bf16[128,1280]{1,0:T(8,128)(2,1)S(1)}, bf16[128,1280]{1,0:T(8,128)(2,1)S(1)}, u32[]{:S(2)}, u32[]{:S(2)}) collective-permute-start(bf16[128,1280]{1,0:T(8,128)(2,1)S(1)} %get-tuple-element.29.refs_0_), channel_id=1, source_target_pairs={{0,8},{1,9},{2,10},{3,11},{4,12},{5,13},{6,14},{7,15},{8,0},{9,1},... | collective-permute-start | bytes 983048 | tf_op jit(solution)/shard_map/gather_cotangent/ppermute | solution.py:263
  30.0 9.4 %collective-permute-start.3 = (bf16[320,128]{1,0:T(8,128)(2,1)S(1)}, bf16[320,128]{1,0:T(8,128)(2,1)S(1)}, u32[]{:S(2)}, u32[]{:S(2)}) collective-permute-start(bf16[320,128]{1,0:T(8,128)(2,1)S(1)} %get-tuple-element.25), channel_id=1, source_target_pairs={{0,20},{1,21},{2,22},{3,23},{4,16},{5,17},{6,18},{7,19},{8,28},{9,... | collective-permute-start | bytes 245768 | tf_op jit(solution)/shard_map/send_to_owner/ppermute | solution.py:263
  30.6 8.9 %collective-permute-start.5 = (bf16[320,128]{1,0:T(8,128)(2,1)S(1)}, bf16[320,128]{1,0:T(8,128)(2,1)S(1)}, u32[]{:S(2)}, u32[]{:S(2)}) collective-permute-start(bf16[320,128]{1,0:T(8,128)(2,1)S(1)} %get-tuple-element.26), channel_id=1, source_target_pairs={{0,14},{1,15},{2,12},{3,13},{4,10},{5,11},{6,8},{7,9},{8,6},{9,7},... | collective-permute-start | bytes 245768 | tf_op jit(solution)/shard_map/send_to_owner/ppermute | solution.py:263
  34.4 6.8 %collective-permute-start.7 = (bf16[320,128]{1,0:T(8,128)(2,1)S(1)}, bf16[320,128]{1,0:T(8,128)(2,1)S(1)}, u32[]{:S(2)}, u32[]{:S(2)}) collective-permute-start(bf16[320,128]{1,0:T(8,128)(2,1)S(1)} %attention.6), channel_id=1, source_target_pairs={{0,26},{1,27},{2,24},{3,25},{4,30},{5,31},{6,28},{7,29},{8,18},{9,... | collective-permute-start | bytes 245768 | tf_op jit(solution)/shard_map/send_to_owner/ppermute | solution.py:263
  36.8 8.1 %collective-permute-start.13 = (bf16[4,128,1280]{2,1,0:T(8,128)(2,1)S(1)}, bf16[4,128,1280]{2,1,0:T(8,128)(2,1)S(1)}, u32[]{:S(2)}, u32[]{:S(2)}) collective-permute-start(bf16[4,128,1280]{2,1,0:T(8,128)(2,1)S(1)} %swap_cotangent.1.refs_2_), channel_id=1, source_target_pairs={{0,1},{1,0},{2,3},{3,2},{4,5},{5,4},{6,7},{7,6},{8,9},{9,8},{10,11... | collective-permute-start | bytes 3932168 | tf_op jit(solution)/shard_map/gradient/ppermute | solution.py:263
  41.3 9.7 %copy-start = (bf16[1280,1280]{1,0:T(8,128)(2,1)S(1)}, bf16[1280,1280]{1,0:T(8,128)(2,1)}, u32[]{:S(2)}) copy-start(bf16[1280,1280]{1,0:T(8,128)(2,1)} %refs_5_.1) | copy-start | bytes 9830404
  41.3 3.6 %collective-permute-start.9 = (bf16[4,160,128]{2,1,0:T(8,128)(2,1)S(1)}, bf16[4,160,128]{2,1,0:T(8,128)(2,1)S(1)}, u32[]{:S(2)}, u32[]{:S(2)}) collective-permute-start(bf16[4,160,128]{2,1,0:T(8,128)(2,1)S(1)} %get-tuple-element.28), channel_id=1, source_target_pairs={{0,1},{1,0},{2,3},{3,2},{4,5},{5,4},{6,7},{7,6},{8,9},{9,8},{10,11... | collective-permute-start | bytes 491528 | tf_op jit(solution)/shard_map/send_to_owner/ppermute | solution.py:263
  41.4 8.3 %collective-permute-start.4 = (bf16[320,128]{1,0:T(8,128)(2,1)S(1)}, bf16[320,128]{1,0:T(8,128)(2,1)S(1)}, u32[]{:S(2)}, u32[]{:S(2)}) collective-permute-start(bf16[320,128]{1,0:T(8,128)(2,1)S(1)} %collective-permute-done.3.refs_0_), channel_id=1, source_target_pairs={{0,16},{1,17},{2,18},{3,19},{4,20},{5,21},{6,22},{7,23},{8,24},{9,... | collective-permute-start | bytes 245768 | tf_op jit(solution)/shard_map/send_home/ppermute | solution.py:263
  42.4 7.9 %collective-permute-start.6 = (bf16[320,128]{1,0:T(8,128)(2,1)S(1)}, bf16[320,128]{1,0:T(8,128)(2,1)S(1)}, u32[]{:S(2)}, u32[]{:S(2)}) collective-permute-start(bf16[320,128]{1,0:T(8,128)(2,1)S(1)} %collective-permute-done.5.refs_1_), channel_id=1, source_target_pairs={{0,8},{1,9},{2,10},{3,11},{4,12},{5,13},{6,14},{7,15},{8,0},{9,1},... | collective-permute-start | bytes 245768 | tf_op jit(solution)/shard_map/send_home/ppermute | solution.py:263
  43.0 7.9 %collective-permute-start.8 = (bf16[320,128]{1,0:T(8,128)(2,1)S(1)}, bf16[320,128]{1,0:T(8,128)(2,1)S(1)}, u32[]{:S(2)}, u32[]{:S(2)}) collective-permute-start(bf16[320,128]{1,0:T(8,128)(2,1)S(1)} %collective-permute-done.7.refs_2_), channel_id=1, source_target_pairs={{0,24},{1,25},{2,26},{3,27},{4,28},{5,29},{6,30},{7,31},{8,16},{9,... | collective-permute-start | bytes 245768 | tf_op jit(solution)/shard_map/send_home/ppermute | solution.py:263
  44.9 6.0 %copy-start.1 = (bf16[128,1280]{1,0:T(8,128)(2,1)S(1)}, bf16[128,1280]{1,0:T(8,128)(2,1)}, u32[]{:S(2)}) copy-start(bf16[128,1280]{1,0:T(8,128)(2,1)} %refs_4_.3) | copy-start | bytes 983044
  45.9 11.0 %collective-permute-start.14 = (bf16[80,640]{1,0:T(8,128)(2,1)S(1)}, bf16[80,640]{1,0:T(8,128)(2,1)S(1)}, u32[]{:S(2)}, u32[]{:S(2)}) collective-permute-start(bf16[80,640]{1,0:T(8,128)(2,1)S(1)} %get-tuple-element.30), channel_id=1, source_target_pairs={{0,4},{1,5},{2,30},{3,31},{4,16},{5,17},{6,10},{7,11},{8,12},{9,13... | collective-permute-start | bytes 307208 | tf_op jit(solution)/shard_map/sum_gradient/ppermute | solution.py:263
  47.9 9.0 %collective-permute-start.15 = (bf16[80,640]{1,0:T(8,128)(2,1)S(1)}, bf16[80,640]{1,0:T(8,128)(2,1)S(1)}, u32[]{:S(2)}, u32[]{:S(2)}) collective-permute-start(bf16[80,640]{1,0:T(8,128)(2,1)S(1)} %get-tuple-element.31), channel_id=1, source_target_pairs={{0,6},{1,7},{2,28},{3,29},{4,18},{5,19},{6,8},{7,9},{8,14},{9,15},... | collective-permute-start | bytes 307208 | tf_op jit(solution)/shard_map/sum_gradient/ppermute | solution.py:263
  49.7 8.7 %collective-permute-start.16 = (bf16[80,640]{1,0:T(8,128)(2,1)S(1)}, bf16[80,640]{1,0:T(8,128)(2,1)S(1)}, u32[]{:S(2)}, u32[]{:S(2)}) collective-permute-start(bf16[80,640]{1,0:T(8,128)(2,1)S(1)} %get-tuple-element.32), channel_id=1, source_target_pairs={{0,2},{1,3},{2,24},{3,25},{4,22},{5,23},{6,12},{7,13},{8,10},{9,11... | collective-permute-start | bytes 307208 | tf_op jit(solution)/shard_map/sum_gradient/ppermute | solution.py:263
  50.3 8.2 %collective-permute-start.17 = (bf16[80,640]{1,0:T(8,128)(2,1)S(1)}, bf16[80,640]{1,0:T(8,128)(2,1)S(1)}, u32[]{:S(2)}, u32[]{:S(2)}) collective-permute-start(bf16[80,640]{1,0:T(8,128)(2,1)S(1)} %get-tuple-element.33), channel_id=1, source_target_pairs={{0,0},{1,1},{2,26},{3,27},{4,20},{5,21},{6,14},{7,15},{8,8},{9,9},... | collective-permute-start | bytes 307208 | tf_op jit(solution)/shard_map/sum_gradient/ppermute | solution.py:263

commit v8 on v7

--- a/solution.py
+++ b/solution.py
@@ -15,7 +15,6 @@
 SENDS = (3, 0, 1, 2)
 RETURNS = (2, 3, 1, 0)
 SUMS = (2, 3, 1, 0)
-TURN = (0, 3, 2, 1)
 
 
 def call(
@@ -59,7 +58,7 @@
     ]
     for copy in copies:
         copy.start()
-    first = lax.axis_index("dp") ^ ((4 - lax.axis_index("enc")) & 3)
+    first = lax.axis_index("dp") ^ lax.axis_index("enc")
     copies[0].wait()
     ids = ids_held[...]
     row = lax.broadcasted_iota(jnp.int32, (ID_ROWS, ids.shape[1]), 0)
@@ -71,7 +70,7 @@
         copies[1 + which].wait()
         held[...] = arrived[which].T
         for hop, out in zip(SENDS, outs):
-            begin = pl.multiple_of((first ^ TURN[hop]) * block, 16)
+            begin = pl.multiple_of((first ^ hop) * block, 16)
             out[which * block : (which + 1) * block] = held[pl.ds(begin, block)]
     copies[4].wait()
 
@@ -188,8 +187,8 @@
     s = lax.axis_index("seq")
     half = kept.shape[1]
     for hop, piece in zip(RETURNS, pieces):
-        kept[TURN[hop]] = piece[pl.ds(pl.multiple_of(s * half, 16), half)]
-        given[TURN[hop]] = piece[pl.ds(pl.multiple_of((1 - s) * half, 16), half)]
+        kept[hop] = piece[pl.ds(pl.multiple_of(s * half, 16), half)]
+        given[hop] = piece[pl.ds(pl.multiple_of((1 - s) * half, 16), half)]
 
 
 def gradient_kernel(count, *refs):
@@ -218,10 +217,10 @@
 
 def project_kernel(*refs):
     pieces, (residual, weight, out, attended) = refs[:-4], refs[-4:]
-    first = lax.axis_index("dp") ^ ((4 - lax.axis_index("enc")) & 3)
+    first = lax.axis_index("dp") ^ lax.axis_index("enc")
     block = pieces[0].shape[0]
     for hop, piece in zip(RETURNS, pieces):
-        attended[pl.ds(pl.multiple_of((first ^ TURN[hop]) * block, 16), block)] = piece[...]
+        attended[pl.ds(pl.multiple_of((first ^ hop) * block, 16), block)] = piece[...]
     projected = lax.dot_general(
         attended[...], weight[...], (((0,), (0,)), ((), ())), preferred_element_type=jnp.float32
     )
@@ -333,7 +332,7 @@
         pieces = [pieces[hop] for hop in RETURNS]
     with jax.named_scope("send_to_owner"):
         pieces = [
-            move(piece, lambda d, e, s, hop=hop: (d ^ TURN[hop], e ^ hop, s)) if hop else piece
+            move(piece, lambda d, e, s, hop=hop: (d ^ hop, e ^ hop, s)) if hop else piece
             for hop, piece in zip(RETURNS, pieces)
         ]
         kept, given = call(
@@ -365,12 +364,12 @@
         )
     with jax.named_scope("sum_gradient"):
         partial = [
-            move(part, lambda d, e, s, hop=hop: (d ^ TURN[e], e ^ hop, s))
+            move(part, lambda d, e, s, hop=hop: (d ^ e, e ^ hop, s))
             for hop, part in zip(SUMS, partial)
         ]
     with jax.named_scope("send_home"):
         homes = [
-            move(piece, lambda d, e, s, hop=hop: (d ^ TURN[hop], e, s)) if hop else piece
+            move(piece, lambda d, e, s, hop=hop: (d ^ hop, e, s)) if hop else piece
             for hop, piece in zip(RETURNS, pieces)
         ]
     with jax.named_scope("project"):

time: 59.4 us -> 58.4 us (0.983)
  waiting for transfers between devices: 24.7 us -> 23.5 us
    ppermute x18, waiting for transfers between devices: 24.7 us -> 23.5 us  [move(): return lax.ppermute(data, AXES, pairs)]
  transfers between devices with their start and end apart: 18 -> 18, of which waited for: 7 -> 7; matrix products, arithmetic and copies ran while one was open for 0% -> 0% of each run, Pallas kernels for 11% -> 12%
where the time goes in v8:
time: 58.4 us; the launch traced here: 58.3 us
  starting transfers between devices  24.9 us (43%)
  waiting for transfers between devices  23.5 us (40%)
  Pallas kernels  9.12 us (16%)
  between operations  0.77 us (1%)
    ppermute x18, starting transfers between devices, move(): return lax.ppermute(data, AXES, pairs)  24.9 us
    ppermute x18, waiting for transfers between devices, move(): return lax.ppermute(data, AXES, pairs)  23.5 us
    pallas_call x10, Pallas kernels, call(): pl.pallas_call(kernel, out_shape=out_shape, in_specs=[placed(space) for s...  9.12 us
  transfers between devices with their start and end apart: 18, of which 7 were waited for; matrix products, arithmetic and copies ran while one was open for 0% of the time, Pallas kernels for 12%

profile of v8, /device:TPU:0, one launch (start us, length us, event | category | flops | bytes accessed | tf_op | source)
XLA Modules:
  0.0 58.3 jit_solution(3104992062730731469)
XLA Ops:
  0.6 1.5 %pack.1 = (bf16[976,128]{1,0:T(8,128)(2,1)S(1)}, bf16[976,128]{1,0:T(8,128)(2,1)S(1)}, bf16[976,128]{1,0:T(8,128)(2,1)S(1)}, bf16[976,128]{1,0:T(8,128)(2,1)S(1)}, bf16[128,1280]{1,0:T(8,128)(2,1)S(1)}) custom-call(s32[1,128]{1,0:T(1,128)} %bitcast.1, bf16[128,1280]{1,0:T(8,128)(2,1)} %refs_1_.1, bf16[128,1280]{1,0:T(8,128)(2,1)} %refs_2_.1, ...), custom_call_target="tpu_custom_call" | custom-call | bytes 2621440 | tf_op jit(solution)/shard_map/pack/pallas_call | solution.py:39
  2.2 5.1 %collective-permute-start = (bf16[976,128]{1,0:T(8,128)(2,1)S(1)}, bf16[976,128]{1,0:T(8,128)(2,1)S(1)}, u32[]{:S(2)}, u32[]{:S(2)}) collective-permute-start(bf16[976,128]{1,0:T(8,128)(2,1)S(1)} %get-tuple-element.18), channel_id=1, source_target_pairs={{0,6},{1,7},{2,4},{3,5},{4,2},{5,3},{6,0},{7,1},{8,14},{9,15},{10,... | collective-permute-start | bytes 749576 | tf_op jit(solution)/shard_map/exchange_heads/ppermute | solution.py:262
  7.3 0.6 %collective-permute-start.2 = (bf16[976,128]{1,0:T(8,128)(2,1)S(1)}, bf16[976,128]{1,0:T(8,128)(2,1)S(1)}, u32[]{:S(2)}, u32[]{:S(2)}) collective-permute-start(bf16[976,128]{1,0:T(8,128)(2,1)S(1)} %get-tuple-element.21), channel_id=1, source_target_pairs={{0,4},{1,5},{2,6},{3,7},{4,0},{5,1},{6,2},{7,3},{8,12},{9,13},{10,... | collective-permute-start | bytes 749576 | tf_op jit(solution)/shard_map/exchange_heads/ppermute | solution.py:262
  7.9 2.6 %collective-permute-start.12 = (bf16[128,1280]{1,0:T(8,128)(2,1)S(1)}, bf16[128,1280]{1,0:T(8,128)(2,1)S(1)}, u32[]{:S(2)}, u32[]{:S(2)}) collective-permute-start(bf16[128,1280]{1,0:T(8,128)(2,1)S(1)} %get-tuple-element.29.refs_0_), channel_id=1, source_target_pairs={{0,24},{1,25},{2,26},{3,27},{4,28},{5,29},{6,30},{7,31},{8,16},{9,... | collective-permute-start | bytes 983048 | tf_op jit(solution)/shard_map/gather_cotangent/ppermute | solution.py:262
  10.5 0.5 collective-permute-start.11
  11.0 3.2 %collective-permute-done.refs_0_ = bf16[976,128]{1,0:T(8,128)(2,1)S(1)} collective-permute-done((bf16[976,128]{1,0:T(8,128)(2,1)S(1)}, bf16[976,128]{1,0:T(8,128)(2,1)S(1)}, u32[]{:S(2)}, u32[]{:S(2)}) %collective-permute-start) | collective-permute-done | bytes 249888 | tf_op jit(solution)/shard_map/exchange_heads/ppermute | solution.py:262
  14.2 1.7 %collective-permute-start.10 = (bf16[128,1280]{1,0:T(8,128)(2,1)S(1)}, bf16[128,1280]{1,0:T(8,128)(2,1)S(1)}, u32[]{:S(2)}, u32[]{:S(2)}) collective-permute-start(bf16[128,1280]{1,0:T(8,128)(2,1)S(1)} %get-tuple-element.29.refs_0_), channel_id=1, source_target_pairs={{0,8},{1,9},{2,10},{3,11},{4,12},{5,13},{6,14},{7,15},{8,0},{9,1},... | collective-permute-start | bytes 983048 | tf_op jit(solution)/shard_map/gather_cotangent/ppermute | solution.py:262
  15.9 3.9 %collective-permute-done.1.refs_2_.early = bf16[976,128]{1,0:T(8,128)(2,1)S(1)} collective-permute-done((bf16[976,128]{1,0:T(8,128)(2,1)S(1)}, bf16[976,128]{1,0:T(8,128)(2,1)S(1)}, u32[]{:S(2)}, u32[]{:S(2)}) %collective-permute-start.1) | collective-permute-done | bytes 249888 | tf_op jit(solution)/shard_map/exchange_heads/ppermute | solution.py:262
  19.8 1.7 %attention.4 = (f32[320,384]{1,0:T(8,128)S(1)}, f32[8,384]{1,0:T(8,128)S(1)}, f32[8,384]{1,0:T(8,128)S(1)}) custom-call(bf16[976,128]{1,0:T(8,128)(2,1)S(1)} %collective-permute-done.refs_0_, bf16[976,128]{1,0:T(8,128)(2,1)S(1)} %get-tuple-element.19.refs_1_.early, bf16[976,128]{1,0:T(8,128)(2,1)S(1)} %collective-permute-done.1.refs_2_.early), custom_call_target="tpu_custom_call" | custom-call | flops 2595225600 | bytes 1310720 | tf_op jit(solution)/shard_map/attention/pallas_call | solution.py:39
  21.5 7.0 %collective-permute-done.2.refs_3_.late = bf16[976,128]{1,0:T(8,128)(2,1)S(1)} collective-permute-done((bf16[976,128]{1,0:T(8,128)(2,1)S(1)}, bf16[976,128]{1,0:T(8,128)(2,1)S(1)}, u32[]{:S(2)}, u32[]{:S(2)}) %collective-permute-start.2) | collective-permute-done | bytes 249888 | tf_op jit(solution)/shard_map/exchange_heads/ppermute | solution.py:262
  28.5 1.5 %attention.5 = (bf16[320,128]{1,0:T(8,128)(2,1)S(1)}, bf16[320,128]{1,0:T(8,128)(2,1)S(1)}) custom-call(bf16[976,128]{1,0:T(8,128)(2,1)S(1)} %collective-permute-done.refs_0_, bf16[976,128]{1,0:T(8,128)(2,1)S(1)} %get-tuple-element.19.refs_1_.early, bf16[976,128]{1,0:T(8,128)(2,1)S(1)} %collective-permute-done.1.refs_2_.early, ...), custom_call_target="tpu_custom_call" | custom-call | flops 1441792000 | bytes 1310720 | tf_op jit(solution)/shard_map/attention/pallas_call | solution.py:39
  30.0 0.6 collective-permute-start.3
  30.6 3.9 %collective-permute-start.5 = (bf16[320,128]{1,0:T(8,128)(2,1)S(1)}, bf16[320,128]{1,0:T(8,128)(2,1)S(1)}, u32[]{:S(2)}, u32[]{:S(2)}) collective-permute-start(bf16[320,128]{1,0:T(8,128)(2,1)S(1)} %get-tuple-element.26), channel_id=1, source_target_pairs={{0,30},{1,31},{2,28},{3,29},{4,26},{5,27},{6,24},{7,25},{8,22},{9,... | collective-permute-start | bytes 245768 | tf_op jit(solution)/shard_map/send_to_owner/ppermute | solution.py:262
  34.5 0.4 attention.6
  35.0 0.9 %collective-permute-start.7 = (bf16[320,128]{1,0:T(8,128)(2,1)S(1)}, bf16[320,128]{1,0:T(8,128)(2,1)S(1)}, u32[]{:S(2)}, u32[]{:S(2)}) collective-permute-start(bf16[320,128]{1,0:T(8,128)(2,1)S(1)} %attention.6), channel_id=1, source_target_pairs={{0,10},{1,11},{2,8},{3,9},{4,14},{5,15},{6,12},{7,13},{8,2},{9,3},... | collective-permute-start | bytes 245768 | tf_op jit(solution)/shard_map/send_to_owner/ppermute | solution.py:262
  35.9 0.4 attention.7.refs_3_
  36.3 0.5 swap_cotangent.1.refs_2_
  36.8 0.1 collective-permute-start.13
  36.9 2.5 %collective-permute-done.3.refs_0_ = bf16[320,128]{1,0:T(8,128)(2,1)S(1)} collective-permute-done((bf16[320,128]{1,0:T(8,128)(2,1)S(1)}, bf16[320,128]{1,0:T(8,128)(2,1)S(1)}, u32[]{:S(2)}, u32[]{:S(2)}) %collective-permute-start.3) | collective-permute-done | bytes 81952 | tf_op jit(solution)/shard_map/send_to_owner/ppermute | solution.py:262
  39.4 1.4 %collective-permute-done.7.refs_2_ = bf16[320,128]{1,0:T(8,128)(2,1)S(1)} collective-permute-done((bf16[320,128]{1,0:T(8,128)(2,1)S(1)}, bf16[320,128]{1,0:T(8,128)(2,1)S(1)}, u32[]{:S(2)}, u32[]{:S(2)}) %collective-permute-start.7) | collective-permute-done | bytes 81952 | tf_op jit(solution)/shard_map/send_to_owner/ppermute | solution.py:262
  40.8 0.1 collective-permute-start.9
  40.9 0.9 %collective-permute-start.4 = (bf16[320,128]{1,0:T(8,128)(2,1)S(1)}, bf16[320,128]{1,0:T(8,128)(2,1)S(1)}, u32[]{:S(2)}, u32[]{:S(2)}) collective-permute-start(bf16[320,128]{1,0:T(8,128)(2,1)S(1)} %collective-permute-done.3.refs_0_), channel_id=1, source_target_pairs={{0,16},{1,17},{2,18},{3,19},{4,20},{5,21},{6,22},{7,23},{8,24},{9,... | collective-permute-start | bytes 245768 | tf_op jit(solution)/shard_map/send_home/ppermute | solution.py:262
  41.8 1.2 %collective-permute-start.6 = (bf16[320,128]{1,0:T(8,128)(2,1)S(1)}, bf16[320,128]{1,0:T(8,128)(2,1)S(1)}, u32[]{:S(2)}, u32[]{:S(2)}) collective-permute-start(bf16[320,128]{1,0:T(8,128)(2,1)S(1)} %collective-permute-done.5.refs_1_), channel_id=1, source_target_pairs={{0,24},{1,25},{2,26},{3,27},{4,28},{5,29},{6,30},{7,31},{8,16},{9,... | collective-permute-start | bytes 245768 | tf_op jit(solution)/shard_map/send_home/ppermute | solution.py:262
  43.0 1.5 %collective-permute-start.8 = (bf16[320,128]{1,0:T(8,128)(2,1)S(1)}, bf16[320,128]{1,0:T(8,128)(2,1)S(1)}, u32[]{:S(2)}, u32[]{:S(2)}) collective-permute-start(bf16[320,128]{1,0:T(8,128)(2,1)S(1)} %collective-permute-done.7.refs_2_), channel_id=1, source_target_pairs={{0,8},{1,9},{2,10},{3,11},{4,12},{5,13},{6,14},{7,15},{8,0},{9,1},... | collective-permute-start | bytes 245768 | tf_op jit(solution)/shard_map/send_home/ppermute | solution.py:262
  44.5 0.9 %gradient.1 = (bf16[80,640]{1,0:T(8,128)(2,1)S(1)}, bf16[80,640]{1,0:T(8,128)(2,1)S(1)}, bf16[80,640]{1,0:T(8,128)(2,1)S(1)}, bf16[80,640]{1,0:T(8,128)(2,1)S(1)}) custom-call(bf16[4,160,128]{2,1,0:T(8,128)(2,1)S(1)} %get-tuple-element.27.refs_0_, bf16[4,160,128]{2,1,0:T(8,128)(2,1)S(1)} %collective-permute-done.9.refs_1_, ...), custom_call_target="tpu_custom_call" | custom-call | flops 419430400 | bytes 2621440 | tf_op jit(solution)/shard_map/gradient/pallas_call | solution.py:39
  45.4 2.3 %collective-permute-start.14 = (bf16[80,640]{1,0:T(8,128)(2,1)S(1)}, bf16[80,640]{1,0:T(8,128)(2,1)S(1)}, u32[]{:S(2)}, u32[]{:S(2)}) collective-permute-start(bf16[80,640]{1,0:T(8,128)(2,1)S(1)} %get-tuple-element.30), channel_id=1, source_target_pairs={{0,4},{1,5},{2,14},{3,15},{4,16},{5,17},{6,26},{7,27},{8,12},{9,13... | collective-permute-start | bytes 307208 | tf_op jit(solution)/shard_map/sum_gradient/ppermute | solution.py:262
  47.7 2.3 %collective-permute-start.15 = (bf16[80,640]{1,0:T(8,128)(2,1)S(1)}, bf16[80,640]{1,0:T(8,128)(2,1)S(1)}, u32[]{:S(2)}, u32[]{:S(2)}) collective-permute-start(bf16[80,640]{1,0:T(8,128)(2,1)S(1)} %get-tuple-element.31), channel_id=1, source_target_pairs={{0,6},{1,7},{2,12},{3,13},{4,18},{5,19},{6,24},{7,25},{8,14},{9,15... | collective-permute-start | bytes 307208 | tf_op jit(solution)/shard_map/sum_gradient/ppermute | solution.py:262
  50.0 0.7 %collective-permute-start.17 = (bf16[80,640]{1,0:T(8,128)(2,1)S(1)}, bf16[80,640]{1,0:T(8,128)(2,1)S(1)}, u32[]{:S(2)}, u32[]{:S(2)}) collective-permute-start(bf16[80,640]{1,0:T(8,128)(2,1)S(1)} %get-tuple-element.33), channel_id=1, source_target_pairs={{0,0},{1,1},{2,10},{3,11},{4,20},{5,21},{6,30},{7,31},{8,8},{9,9},... | collective-permute-start | bytes 307208 | tf_op jit(solution)/shard_map/sum_gradient/ppermute | solution.py:262
  50.7 1.4 %project.1 = bf16[128,1280]{1,0:T(8,128)(2,1)} custom-call(bf16[320,128]{1,0:T(8,128)(2,1)S(1)} %collective-permute-done.4.refs_0_, bf16[320,128]{1,0:T(8,128)(2,1)S(1)} %collective-permute-done.6.refs_1_, bf16[320,128]{1,0:T(8,128)(2,1)S(1)} %collective-permute-done.8.refs_2_, bf16[320,128]{1,0:T(8,128)(2,1)S(1)} %attention.7.refs_3_, ...), custom_call_target="tpu_custom_call" | custom-call | flops 419430400 | bytes 3276800 | tf_op jit(solution)/shard_map/project/pallas_call | solution.py:39
  52.1 5.0 %collective-permute-done.14.refs_0_ = bf16[80,640]{1,0:T(8,128)(2,1)S(1)} collective-permute-done((bf16[80,640]{1,0:T(8,128)(2,1)S(1)}, bf16[80,640]{1,0:T(8,128)(2,1)S(1)}, u32[]{:S(2)}, u32[]{:S(2)}) %collective-permute-start.14) | collective-permute-done | bytes 102432 | tf_op jit(solution)/shard_map/sum_gradient/ppermute | solution.py:262
  57.1 0.3 collective-permute-done.16.refs_2_
  57.5 0.8 %add_gradient.1 = f32[160,320]{1,0:T(8,128)} custom-call(bf16[80,640]{1,0:T(8,128)(2,1)S(1)} %collective-permute-done.14.refs_0_, bf16[80,640]{1,0:T(8,128)(2,1)S(1)} %collective-permute-done.15.refs_1_, bf16[80,640]{1,0:T(8,128)(2,1)S(1)} %collective-permute-done.16.refs_2_, bf16[80,640]{1,0:T(8,128)(2,1)S(1)} %collective-permute-done.17.refs_3_), custom_call_target="tpu_custom_call" | custom-call | bytes 819200 | tf_op jit(solution)/shard_map/add_gradient/pallas_call | solution.py:39
  (18 shorter events, 0.1 us)
Async XLA Ops:
  2.2 12.1 %collective-permute-start = (bf16[976,128]{1,0:T(8,128)(2,1)S(1)}, bf16[976,128]{1,0:T(8,128)(2,1)S(1)}, u32[]{:S(2)}, u32[]{:S(2)}) collective-permute-start(bf16[976,128]{1,0:T(8,128)(2,1)S(1)} %get-tuple-element.18), channel_id=1, source_target_pairs={{0,6},{1,7},{2,4},{3,5},{4,2},{5,3},{6,0},{7,1},{8,14},{9,15},{10,... | collective-permute-start | bytes 749576 | tf_op jit(solution)/shard_map/exchange_heads/ppermute | solution.py:262
  7.3 12.5 %collective-permute-start.1 = (bf16[976,128]{1,0:T(8,128)(2,1)S(1)}, bf16[976,128]{1,0:T(8,128)(2,1)S(1)}, u32[]{:S(2)}, u32[]{:S(2)}) collective-permute-start(bf16[976,128]{1,0:T(8,128)(2,1)S(1)} %get-tuple-element.20), channel_id=1, source_target_pairs={{0,2},{1,3},{2,0},{3,1},{4,6},{5,7},{6,4},{7,5},{8,10},{9,11},{10,... | collective-permute-start | bytes 749576 | tf_op jit(solution)/shard_map/exchange_heads/ppermute | solution.py:262
  7.3 21.3 %collective-permute-start.2 = (bf16[976,128]{1,0:T(8,128)(2,1)S(1)}, bf16[976,128]{1,0:T(8,128)(2,1)S(1)}, u32[]{:S(2)}, u32[]{:S(2)}) collective-permute-start(bf16[976,128]{1,0:T(8,128)(2,1)S(1)} %get-tuple-element.21), channel_id=1, source_target_pairs={{0,4},{1,5},{2,6},{3,7},{4,0},{5,1},{6,2},{7,3},{8,12},{9,13},{10,... | collective-permute-start | bytes 749576 | tf_op jit(solution)/shard_map/exchange_heads/ppermute | solution.py:262
  7.9 27.0 %collective-permute-start.12 = (bf16[128,1280]{1,0:T(8,128)(2,1)S(1)}, bf16[128,1280]{1,0:T(8,128)(2,1)S(1)}, u32[]{:S(2)}, u32[]{:S(2)}) collective-permute-start(bf16[128,1280]{1,0:T(8,128)(2,1)S(1)} %get-tuple-element.29.refs_0_), channel_id=1, source_target_pairs={{0,24},{1,25},{2,26},{3,27},{4,28},{5,29},{6,30},{7,31},{8,16},{9,... | collective-permute-start | bytes 983048 | tf_op jit(solution)/shard_map/gather_cotangent/ppermute | solution.py:262
  10.5 25.8 %collective-permute-start.11 = (bf16[128,1280]{1,0:T(8,128)(2,1)S(1)}, bf16[128,1280]{1,0:T(8,128)(2,1)S(1)}, u32[]{:S(2)}, u32[]{:S(2)}) collective-permute-start(bf16[128,1280]{1,0:T(8,128)(2,1)S(1)} %get-tuple-element.29.refs_0_), channel_id=1, source_target_pairs={{0,16},{1,17},{2,18},{3,19},{4,20},{5,21},{6,22},{7,23},{8,24},{9,... | collective-permute-start | bytes 983048 | tf_op jit(solution)/shard_map/gather_cotangent/ppermute | solution.py:262
  14.2 22.1 %collective-permute-start.10 = (bf16[128,1280]{1,0:T(8,128)(2,1)S(1)}, bf16[128,1280]{1,0:T(8,128)(2,1)S(1)}, u32[]{:S(2)}, u32[]{:S(2)}) collective-permute-start(bf16[128,1280]{1,0:T(8,128)(2,1)S(1)} %get-tuple-element.29.refs_0_), channel_id=1, source_target_pairs={{0,8},{1,9},{2,10},{3,11},{4,12},{5,13},{6,14},{7,15},{8,0},{9,1},... | collective-permute-start | bytes 983048 | tf_op jit(solution)/shard_map/gather_cotangent/ppermute | solution.py:262
  30.0 9.4 %collective-permute-start.3 = (bf16[320,128]{1,0:T(8,128)(2,1)S(1)}, bf16[320,128]{1,0:T(8,128)(2,1)S(1)}, u32[]{:S(2)}, u32[]{:S(2)}) collective-permute-start(bf16[320,128]{1,0:T(8,128)(2,1)S(1)} %get-tuple-element.25), channel_id=1, source_target_pairs={{0,20},{1,21},{2,22},{3,23},{4,16},{5,17},{6,18},{7,19},{8,28},{9,... | collective-permute-start | bytes 245768 | tf_op jit(solution)/shard_map/send_to_owner/ppermute | solution.py:262
  30.6 8.8 %collective-permute-start.5 = (bf16[320,128]{1,0:T(8,128)(2,1)S(1)}, bf16[320,128]{1,0:T(8,128)(2,1)S(1)}, u32[]{:S(2)}, u32[]{:S(2)}) collective-permute-start(bf16[320,128]{1,0:T(8,128)(2,1)S(1)} %get-tuple-element.26), channel_id=1, source_target_pairs={{0,30},{1,31},{2,28},{3,29},{4,26},{5,27},{6,24},{7,25},{8,22},{9,... | collective-permute-start | bytes 245768 | tf_op jit(solution)/shard_map/send_to_owner/ppermute | solution.py:262
  35.0 5.9 %collective-permute-start.7 = (bf16[320,128]{1,0:T(8,128)(2,1)S(1)}, bf16[320,128]{1,0:T(8,128)(2,1)S(1)}, u32[]{:S(2)}, u32[]{:S(2)}) collective-permute-start(bf16[320,128]{1,0:T(8,128)(2,1)S(1)} %attention.6), channel_id=1, source_target_pairs={{0,10},{1,11},{2,8},{3,9},{4,14},{5,15},{6,12},{7,13},{8,2},{9,3},... | collective-permute-start | bytes 245768 | tf_op jit(solution)/shard_map/send_to_owner/ppermute | solution.py:262
  36.8 7.7 %collective-permute-start.13 = (bf16[4,128,1280]{2,1,0:T(8,128)(2,1)S(1)}, bf16[4,128,1280]{2,1,0:T(8,128)(2,1)S(1)}, u32[]{:S(2)}, u32[]{:S(2)}) collective-permute-start(bf16[4,128,1280]{2,1,0:T(8,128)(2,1)S(1)} %swap_cotangent.1.refs_2_), channel_id=1, source_target_pairs={{0,1},{1,0},{2,3},{3,2},{4,5},{5,4},{6,7},{7,6},{8,9},{9,8},{10,11... | collective-permute-start | bytes 3932168 | tf_op jit(solution)/shard_map/gradient/ppermute | solution.py:262
  40.8 9.9 %copy-start = (bf16[1280,1280]{1,0:T(8,128)(2,1)S(1)}, bf16[1280,1280]{1,0:T(8,128)(2,1)}, u32[]{:S(2)}) copy-start(bf16[1280,1280]{1,0:T(8,128)(2,1)} %refs_5_.1) | copy-start | bytes 9830404
  40.8 3.6 %collective-permute-start.9 = (bf16[4,160,128]{2,1,0:T(8,128)(2,1)S(1)}, bf16[4,160,128]{2,1,0:T(8,128)(2,1)S(1)}, u32[]{:S(2)}, u32[]{:S(2)}) collective-permute-start(bf16[4,160,128]{2,1,0:T(8,128)(2,1)S(1)} %get-tuple-element.28), channel_id=1, source_target_pairs={{0,1},{1,0},{2,3},{3,2},{4,5},{5,4},{6,7},{7,6},{8,9},{9,8},{10,11... | collective-permute-start | bytes 491528 | tf_op jit(solution)/shard_map/send_to_owner/ppermute | solution.py:262
  40.9 9.1 %collective-permute-start.4 = (bf16[320,128]{1,0:T(8,128)(2,1)S(1)}, bf16[320,128]{1,0:T(8,128)(2,1)S(1)}, u32[]{:S(2)}, u32[]{:S(2)}) collective-permute-start(bf16[320,128]{1,0:T(8,128)(2,1)S(1)} %collective-permute-done.3.refs_0_), channel_id=1, source_target_pairs={{0,16},{1,17},{2,18},{3,19},{4,20},{5,21},{6,22},{7,23},{8,24},{9,... | collective-permute-start | bytes 245768 | tf_op jit(solution)/shard_map/send_home/ppermute | solution.py:262
  41.8 8.2 %collective-permute-start.6 = (bf16[320,128]{1,0:T(8,128)(2,1)S(1)}, bf16[320,128]{1,0:T(8,128)(2,1)S(1)}, u32[]{:S(2)}, u32[]{:S(2)}) collective-permute-start(bf16[320,128]{1,0:T(8,128)(2,1)S(1)} %collective-permute-done.5.refs_1_), channel_id=1, source_target_pairs={{0,24},{1,25},{2,26},{3,27},{4,28},{5,29},{6,30},{7,31},{8,16},{9,... | collective-permute-start | bytes 245768 | tf_op jit(solution)/shard_map/send_home/ppermute | solution.py:262
  43.0 7.7 %collective-permute-start.8 = (bf16[320,128]{1,0:T(8,128)(2,1)S(1)}, bf16[320,128]{1,0:T(8,128)(2,1)S(1)}, u32[]{:S(2)}, u32[]{:S(2)}) collective-permute-start(bf16[320,128]{1,0:T(8,128)(2,1)S(1)} %collective-permute-done.7.refs_2_), channel_id=1, source_target_pairs={{0,8},{1,9},{2,10},{3,11},{4,12},{5,13},{6,14},{7,15},{8,0},{9,1},... | collective-permute-start | bytes 245768 | tf_op jit(solution)/shard_map/send_home/ppermute | solution.py:262
  44.5 6.2 %copy-start.1 = (bf16[128,1280]{1,0:T(8,128)(2,1)S(1)}, bf16[128,1280]{1,0:T(8,128)(2,1)}, u32[]{:S(2)}) copy-start(bf16[128,1280]{1,0:T(8,128)(2,1)} %refs_4_.3) | copy-start | bytes 983044
  45.4 11.7 %collective-permute-start.14 = (bf16[80,640]{1,0:T(8,128)(2,1)S(1)}, bf16[80,640]{1,0:T(8,128)(2,1)S(1)}, u32[]{:S(2)}, u32[]{:S(2)}) collective-permute-start(bf16[80,640]{1,0:T(8,128)(2,1)S(1)} %get-tuple-element.30), channel_id=1, source_target_pairs={{0,4},{1,5},{2,14},{3,15},{4,16},{5,17},{6,26},{7,27},{8,12},{9,13... | collective-permute-start | bytes 307208 | tf_op jit(solution)/shard_map/sum_gradient/ppermute | solution.py:262
  47.7 9.5 %collective-permute-start.15 = (bf16[80,640]{1,0:T(8,128)(2,1)S(1)}, bf16[80,640]{1,0:T(8,128)(2,1)S(1)}, u32[]{:S(2)}, u32[]{:S(2)}) collective-permute-start(bf16[80,640]{1,0:T(8,128)(2,1)S(1)} %get-tuple-element.31), channel_id=1, source_target_pairs={{0,6},{1,7},{2,12},{3,13},{4,18},{5,19},{6,24},{7,25},{8,14},{9,15... | collective-permute-start | bytes 307208 | tf_op jit(solution)/shard_map/sum_gradient/ppermute | solution.py:262
  50.0 7.5 %collective-permute-start.16 = (bf16[80,640]{1,0:T(8,128)(2,1)S(1)}, bf16[80,640]{1,0:T(8,128)(2,1)S(1)}, u32[]{:S(2)}, u32[]{:S(2)}) collective-permute-start(bf16[80,640]{1,0:T(8,128)(2,1)S(1)} %get-tuple-element.32), channel_id=1, source_target_pairs={{0,2},{1,3},{2,8},{3,9},{4,22},{5,23},{6,28},{7,29},{8,10},{9,11},... | collective-permute-start | bytes 307208 | tf_op jit(solution)/shard_map/sum_gradient/ppermute | solution.py:262
  50.0 7.5 %collective-permute-start.17 = (bf16[80,640]{1,0:T(8,128)(2,1)S(1)}, bf16[80,640]{1,0:T(8,128)(2,1)S(1)}, u32[]{:S(2)}, u32[]{:S(2)}) collective-permute-start(bf16[80,640]{1,0:T(8,128)(2,1)S(1)} %get-tuple-element.33), channel_id=1, source_target_pairs={{0,0},{1,1},{2,10},{3,11},{4,20},{5,21},{6,30},{7,31},{8,8},{9,9},... | collective-permute-start | bytes 307208 | tf_op jit(solution)/shard_map/sum_gradient/ppermute | solution.py:262

commit v9 on v6

--- a/solution.py
+++ b/solution.py
@@ -13,8 +13,8 @@
 ID_ROWS = 16
 ID_BASE = 64
 SENDS = (3, 0, 1, 2)
-RETURNS = (2, 3, 1, 0)
-SUMS = (2, 3, 1, 0)
+RETURNS = (2, 3, 0, 1)
+SUMS = (2, 3, 1)
 
 
 def call(
@@ -183,16 +183,23 @@
 
 
 def halve_kernel(*refs):
-    pieces, (kept, given) = refs[:-2], refs[-2:]
-    s = lax.axis_index("seq")
+    count = len(RETURNS)
+    pieces, homes, (kept, given) = refs[:count], refs[count : 2 * count], refs[2 * count :]
+    e, s = lax.axis_index("enc"), lax.axis_index("seq")
     half = kept.shape[1]
     for hop, piece in zip(RETURNS, pieces):
-        kept[hop] = piece[pl.ds(pl.multiple_of(s * half, 16), half)]
-        given[hop] = piece[pl.ds(pl.multiple_of((1 - s) * half, 16), half)]
+        kept[e ^ hop] = piece[pl.ds(pl.multiple_of(s * half, 16), half)]
+        given[e ^ hop] = piece[pl.ds(pl.multiple_of((1 - s) * half, 16), half)]
+    for hop, piece in zip(RETURNS, pieces):
+        for step, home in enumerate(homes):
+
+            @pl.when(e ^ hop == step)
+            def _():
+                home[...] = piece[...]
 
 
 def gradient_kernel(count, *refs):
-    kept, given, same, others, *outs = refs
+    kept, given, same, others, own, *outs = refs
     e = lax.axis_index("enc")
     features, rows = [], []
     for step in range(count):
@@ -208,6 +215,10 @@
         block = total[:, target * width : (target + 1) * width]
         folded = jnp.concatenate([block[:short], block[short:]], axis=1).astype(jnp.bfloat16)
 
+        @pl.when(e == target)
+        def _():
+            own[...] = block
+
         for index, out in enumerate(outs):
 
             @pl.when(e ^ target == SUMS[index])
@@ -217,24 +228,24 @@
 
 def project_kernel(*refs):
     pieces, (residual, weight, out, attended) = refs[:-4], refs[-4:]
-    first = lax.axis_index("dp") ^ lax.axis_index("enc")
+    d = lax.axis_index("dp")
     block = pieces[0].shape[0]
-    for hop, piece in zip(RETURNS, pieces):
-        attended[pl.ds(pl.multiple_of((first ^ hop) * block, 16), block)] = piece[...]
+    for step, piece in enumerate(pieces):
+        attended[pl.ds(pl.multiple_of((d ^ step) * block, 16), block)] = piece[...]
     projected = lax.dot_general(
         attended[...], weight[...], (((0,), (0,)), ((), ())), preferred_element_type=jnp.float32
     )
     out[...] = (residual[...].astype(jnp.float32) + projected).astype(jnp.bfloat16)
 
 
-def add_kernel(*refs):
-    partial, out = refs[:-1], refs[-1]
-    total = partial[0][...].astype(jnp.float32)
-    for ref in partial[1:]:
+def add_kernel(own, *refs):
+    out, width = refs[-1], own.shape[1]
+    total = refs[0][...].astype(jnp.float32)
+    for ref in refs[1:-1]:
         total = total + ref[...].astype(jnp.float32)
-    short, width = total.shape[0], out.shape[1]
-    out[:short] = total[:, :width]
-    out[short:] = total[:, width:]
+    short = total.shape[0]
+    out[:short] = own[:short] + total[:, :width]
+    out[short:] = own[short:] + total[:, width:]
 
 
 def exchange_body(
@@ -328,12 +339,12 @@
         pieces = [pieces[hop] for hop in RETURNS]
     with jax.named_scope("send_to_owner"):
         pieces = [
-            move(piece, lambda d, e, s, hop=hop: (d ^ hop, e ^ hop, s)) if hop else piece
+            move(piece, lambda d, e, s, hop=hop: (d ^ e, e ^ hop, s))
             for hop, piece in zip(RETURNS, pieces)
         ]
-        kept, given = call(
+        *homes, kept, given = call(
             halve_kernel,
-            [bf16((n_dp, half, rows))] * 2,
+            [bf16((block, rows))] * n_dp + [bf16((n_dp, half, rows))] * 2,
             *pieces,
             flops=400 * group * group * half,
         )
@@ -348,9 +359,10 @@
             bytes_accessed=4 * n_dp * rows * width,
         )
     with jax.named_scope("gradient"):
-        partial = call(
+        mine, *partial = call(
             functools.partial(gradient_kernel, n_enc),
-            [bf16((half // 2, 2 * block))] * n_enc,
+            [jax.ShapeDtypeStruct((half, block), jnp.float32)]
+            + [bf16((half // 2, 2 * block))] * (n_enc - 1),
             kept,
             given,
             stacked,
@@ -359,14 +371,10 @@
             bytes_accessed=2 * n_dp * n_seq * rows * width,
         )
     with jax.named_scope("sum_gradient"):
-        partial = [
-            move(part, lambda d, e, s, hop=hop: (d ^ e, e ^ hop, s))
-            for hop, part in zip(SUMS, partial)
-        ]
+        partial = along_enc(partial, SUMS)
     with jax.named_scope("send_home"):
-        homes = [
-            move(piece, lambda d, e, s, hop=hop: (d ^ hop, e, s)) if hop else piece
-            for hop, piece in zip(RETURNS, pieces)
+        homes[1:] = [
+            move(homes[k], lambda d, e, s, k=k: (d ^ k, e, s)) for k in range(1, n_dp)
         ]
     with jax.named_scope("project"):
         layer_out = call(
@@ -376,13 +384,14 @@
             residual,
             out_weight,
             scratch=[pltpu.VMEM((width, rows), jnp.bfloat16)],
-            flops=2 * rows * width * width,
+            flops=1 * rows * width * width,
             bytes_accessed=2 * width * width,
         )
     with jax.named_scope("add_gradient"):
         grad_weight = call(
             add_kernel,
             jax.ShapeDtypeStruct((half, block), jnp.float32),
+            mine,
             *partial,
             bytes_accessed=4 * half * block * 4,
         )

time: 58.4 us -> 58.8 us (level)
  starting transfers between devices: 24.7 us -> 26 us
  waiting for transfers between devices: 23.6 us -> 22.4 us
    ppermute x18, starting transfers between devices: 24.7 us -> 26 us  [move(): return lax.ppermute(data, AXES, pairs)]
    ppermute x18, waiting for transfers between devices: 23.6 us -> 22.4 us  [move(): return lax.ppermute(data, AXES, pairs)]
  transfers between devices with their start and end apart: 18 -> 18, of which waited for: 7 -> 8; matrix products, arithmetic and copies ran while one was open for 0% -> 0% of each run, Pallas kernels for 12% -> 12%
where the time goes in v9:
time: 58.8 us; the launch traced here: 58.6 us
  starting transfers between devices  26 us (44%)
  waiting for transfers between devices  22.4 us (38%)
  Pallas kernels  9.43 us (16%)
  between operations  0.75 us (1%)
    ppermute x18, starting transfers between devices, move(): return lax.ppermute(data, AXES, pairs)  26 us
    ppermute x18, waiting for transfers between devices, move(): return lax.ppermute(data, AXES, pairs)  22.4 us
    pallas_call x9, Pallas kernels, call(): pl.pallas_call(kernel, out_shape=out_shape, in_specs=[placed(space) for s...  9.43 us
  transfers between devices with their start and end apart: 18, of which 8 were waited for; matrix products, arithmetic and copies ran while one was open for 0% of the time, Pallas kernels for 12%

profile of v9, /device:TPU:0, one launch (start us, length us, event | category | flops | bytes accessed | tf_op | source)
XLA Modules:
  0.0 58.6 jit_solution(10766857190992355920)
XLA Ops:
  0.6 1.5 %pack.1 = (bf16[976,128]{1,0:T(8,128)(2,1)S(1)}, bf16[976,128]{1,0:T(8,128)(2,1)S(1)}, bf16[976,128]{1,0:T(8,128)(2,1)S(1)}, bf16[976,128]{1,0:T(8,128)(2,1)S(1)}, bf16[128,1280]{1,0:T(8,128)(2,1)S(1)}) custom-call(s32[1,128]{1,0:T(1,128)} %bitcast.1, bf16[128,1280]{1,0:T(8,128)(2,1)} %refs_1_.1, bf16[128,1280]{1,0:T(8,128)(2,1)} %refs_2_.1, ...), custom_call_target="tpu_custom_call" | custom-call | bytes 2621440 | tf_op jit(solution)/shard_map/pack/pallas_call | solution.py:39
  2.2 5.1 %collective-permute-start = (bf16[976,128]{1,0:T(8,128)(2,1)S(1)}, bf16[976,128]{1,0:T(8,128)(2,1)S(1)}, u32[]{:S(2)}, u32[]{:S(2)}) collective-permute-start(bf16[976,128]{1,0:T(8,128)(2,1)S(1)} %get-tuple-element.24), channel_id=1, source_target_pairs={{0,6},{1,7},{2,4},{3,5},{4,2},{5,3},{6,0},{7,1},{8,14},{9,15},{10,... | collective-permute-start | bytes 749576 | tf_op jit(solution)/shard_map/exchange_heads/ppermute | solution.py:273
  7.3 0.6 %collective-permute-start.2 = (bf16[976,128]{1,0:T(8,128)(2,1)S(1)}, bf16[976,128]{1,0:T(8,128)(2,1)S(1)}, u32[]{:S(2)}, u32[]{:S(2)}) collective-permute-start(bf16[976,128]{1,0:T(8,128)(2,1)S(1)} %get-tuple-element.27), channel_id=1, source_target_pairs={{0,4},{1,5},{2,6},{3,7},{4,0},{5,1},{6,2},{7,3},{8,12},{9,13},{10,... | collective-permute-start | bytes 749576 | tf_op jit(solution)/shard_map/exchange_heads/ppermute | solution.py:273
  7.9 2.6 %collective-permute-start.13 = (bf16[128,1280]{1,0:T(8,128)(2,1)S(1)}, bf16[128,1280]{1,0:T(8,128)(2,1)S(1)}, u32[]{:S(2)}, u32[]{:S(2)}) collective-permute-start(bf16[128,1280]{1,0:T(8,128)(2,1)S(1)} %get-tuple-element.41.refs_0_), channel_id=1, source_target_pairs={{0,24},{1,25},{2,26},{3,27},{4,28},{5,29},{6,30},{7,31},{8,16},{9,... | collective-permute-start | bytes 983048 | tf_op jit(solution)/shard_map/gather_cotangent/ppermute | solution.py:273
  10.5 0.5 collective-permute-start.12
  11.0 3.2 %collective-permute-done.refs_0_ = bf16[976,128]{1,0:T(8,128)(2,1)S(1)} collective-permute-done((bf16[976,128]{1,0:T(8,128)(2,1)S(1)}, bf16[976,128]{1,0:T(8,128)(2,1)S(1)}, u32[]{:S(2)}, u32[]{:S(2)}) %collective-permute-start) | collective-permute-done | bytes 249888 | tf_op jit(solution)/shard_map/exchange_heads/ppermute | solution.py:273
  14.2 1.7 %collective-permute-start.11 = (bf16[128,1280]{1,0:T(8,128)(2,1)S(1)}, bf16[128,1280]{1,0:T(8,128)(2,1)S(1)}, u32[]{:S(2)}, u32[]{:S(2)}) collective-permute-start(bf16[128,1280]{1,0:T(8,128)(2,1)S(1)} %get-tuple-element.41.refs_0_), channel_id=1, source_target_pairs={{0,8},{1,9},{2,10},{3,11},{4,12},{5,13},{6,14},{7,15},{8,0},{9,1},... | collective-permute-start | bytes 983048 | tf_op jit(solution)/shard_map/gather_cotangent/ppermute | solution.py:273
  15.9 3.9 %collective-permute-done.1.refs_2_.refs_1_ = bf16[976,128]{1,0:T(8,128)(2,1)S(1)} collective-permute-done((bf16[976,128]{1,0:T(8,128)(2,1)S(1)}, bf16[976,128]{1,0:T(8,128)(2,1)S(1)}, u32[]{:S(2)}, u32[]{:S(2)}) %collective-permute-start.1) | collective-permute-done | bytes 249888 | tf_op jit(solution)/shard_map/exchange_heads/ppermute | solution.py:273
  19.8 1.7 %attention.3 = (f32[320,384]{1,0:T(8,128)S(1)}, f32[8,384]{1,0:T(8,128)S(1)}, f32[8,384]{1,0:T(8,128)S(1)}) custom-call(bf16[976,128]{1,0:T(8,128)(2,1)S(1)} %collective-permute-done.refs_0_, bf16[976,128]{1,0:T(8,128)(2,1)S(1)} %get-tuple-element.25.refs_1_.refs_0_, bf16[976,128]{1,0:T(8,128)(2,1)S(1)} %collective-permute-done.1.refs_2_.refs_1_), custom_call_target="tpu_custom_call" | custom-call | flops 2595225600 | bytes 1310720 | tf_op jit(solution)/shard_map/attention/pallas_call | solution.py:39
  21.5 7.1 %collective-permute-done.2.refs_3_.refs_2_ = bf16[976,128]{1,0:T(8,128)(2,1)S(1)} collective-permute-done((bf16[976,128]{1,0:T(8,128)(2,1)S(1)}, bf16[976,128]{1,0:T(8,128)(2,1)S(1)}, u32[]{:S(2)}, u32[]{:S(2)}) %collective-permute-start.2) | collective-permute-done | bytes 249888 | tf_op jit(solution)/shard_map/exchange_heads/ppermute | solution.py:273
  28.5 1.5 %attention.4 = (bf16[320,128]{1,0:T(8,128)(2,1)S(1)}, bf16[320,128]{1,0:T(8,128)(2,1)S(1)}) custom-call(bf16[976,128]{1,0:T(8,128)(2,1)S(1)} %collective-permute-done.refs_0_, bf16[976,128]{1,0:T(8,128)(2,1)S(1)} %get-tuple-element.25.refs_1_.refs_0_, bf16[976,128]{1,0:T(8,128)(2,1)S(1)} %collective-permute-done.1.refs_2_.refs_1_, ...), custom_call_target="tpu_custom_call" | custom-call | flops 1441792000 | bytes 1310720 | tf_op jit(solution)/shard_map/attention/pallas_call | solution.py:39
  30.1 3.9 %collective-permute-start.4 = (bf16[320,128]{1,0:T(8,128)(2,1)S(1)}, bf16[320,128]{1,0:T(8,128)(2,1)S(1)}, u32[]{:S(2)}, u32[]{:S(2)}) collective-permute-start(bf16[320,128]{1,0:T(8,128)(2,1)S(1)} %get-tuple-element.32), channel_id=1, source_target_pairs={{0,6},{1,7},{2,12},{3,13},{4,18},{5,19},{6,24},{7,25},{8,14},{9,15... | collective-permute-start | bytes 245768 | tf_op jit(solution)/shard_map/send_to_owner/ppermute | solution.py:273
  34.0 1.0 %attention.5 = (bf16[320,128]{1,0:T(8,128)(2,1)S(1)}, bf16[320,128]{1,0:T(8,128)(2,1)S(1)}) custom-call(bf16[976,128]{1,0:T(8,128)(2,1)S(1)} %get-tuple-element.25.refs_1_.refs_0_, bf16[976,128]{1,0:T(8,128)(2,1)S(1)} %collective-permute-done.1.refs_2_.refs_1_, bf16[976,128]{1,0:T(8,128)(2,1)S(1)} %collective-permute-done.2.refs_3_.refs_2_, ...), custom_call_target="tpu_custom_call" | custom-call | flops 576716800 | bytes 1310720 | tf_op jit(solution)/shard_map/attention/pallas_call | solution.py:39
  35.0 0.7 %collective-permute-start.5 = (bf16[320,128]{1,0:T(8,128)(2,1)S(1)}, bf16[320,128]{1,0:T(8,128)(2,1)S(1)}, u32[]{:S(2)}, u32[]{:S(2)}) collective-permute-start(bf16[320,128]{1,0:T(8,128)(2,1)S(1)} %get-tuple-element.33), channel_id=1, source_target_pairs={{0,0},{1,1},{2,10},{3,11},{4,20},{5,21},{6,30},{7,31},{8,8},{9,9},... | collective-permute-start | bytes 245768 | tf_op jit(solution)/shard_map/send_to_owner/ppermute | solution.py:273
  35.7 3.3 %collective-permute-start.6 = (bf16[320,128]{1,0:T(8,128)(2,1)S(1)}, bf16[320,128]{1,0:T(8,128)(2,1)S(1)}, u32[]{:S(2)}, u32[]{:S(2)}) collective-permute-start(bf16[320,128]{1,0:T(8,128)(2,1)S(1)} %get-tuple-element.34), channel_id=1, source_target_pairs={{0,2},{1,3},{2,8},{3,9},{4,22},{5,23},{6,28},{7,29},{8,10},{9,11},... | collective-permute-start | bytes 245768 | tf_op jit(solution)/shard_map/send_to_owner/ppermute | solution.py:273
  39.0 0.4 swap_cotangent.1.refs_2_
  39.5 0.1 collective-permute-start.14
  39.6 0.2 collective-permute-done.3.refs_0_
  39.7 2.6 %collective-permute-done.6.refs_3_ = bf16[320,128]{1,0:T(8,128)(2,1)S(1)} collective-permute-done((bf16[320,128]{1,0:T(8,128)(2,1)S(1)}, bf16[320,128]{1,0:T(8,128)(2,1)S(1)}, u32[]{:S(2)}, u32[]{:S(2)}) %collective-permute-start.6) | collective-permute-done | bytes 81952 | tf_op jit(solution)/shard_map/send_to_owner/ppermute | solution.py:273
  42.4 0.1 send_to_owner.1
  42.5 0.1 collective-permute-start.10
  42.6 0.6 %collective-permute-start.7 = (bf16[320,128]{1,0:T(8,128)(2,1)S(1)}, bf16[320,128]{1,0:T(8,128)(2,1)S(1)}, u32[]{:S(2)}, u32[]{:S(2)}) collective-permute-start(bf16[320,128]{1,0:T(8,128)(2,1)S(1)} %get-tuple-element.36), channel_id=1, source_target_pairs={{0,8},{1,9},{2,10},{3,11},{4,12},{5,13},{6,14},{7,15},{8,0},{9,1},... | collective-permute-start | bytes 245768 | tf_op jit(solution)/shard_map/send_home/ppermute | solution.py:273
  43.2 0.8 %collective-permute-done.10.refs_1_ = bf16[4,160,128]{2,1,0:T(8,128)(2,1)S(1)} collective-permute-done((bf16[4,160,128]{2,1,0:T(8,128)(2,1)S(1)}, bf16[4,160,128]{2,1,0:T(8,128)(2,1)S(1)}, u32[]{:S(2)}, u32[]{:S(2)}) %collective-permute-start.10) | collective-permute-done | bytes 163872 | tf_op jit(solution)/shard_map/send_to_owner/ppermute | solution.py:273
  43.9 1.0 %gradient.1 = (f32[160,320]{1,0:T(8,128)S(1)}, bf16[80,640]{1,0:T(8,128)(2,1)S(1)}, bf16[80,640]{1,0:T(8,128)(2,1)S(1)}, bf16[80,640]{1,0:T(8,128)(2,1)S(1)}) custom-call(bf16[4,160,128]{2,1,0:T(8,128)(2,1)S(1)} %get-tuple-element.39.refs_0_, bf16[4,160,128]{2,1,0:T(8,128)(2,1)S(1)} %collective-permute-done.10.refs_1_, ...), custom_call_target="tpu_custom_call" | custom-call | flops 419430400 | bytes 2621440 | tf_op jit(solution)/shard_map/gradient/pallas_call | solution.py:39
  44.9 3.9 %collective-permute-start.15 = (bf16[80,640]{1,0:T(8,128)(2,1)S(1)}, bf16[80,640]{1,0:T(8,128)(2,1)S(1)}, u32[]{:S(2)}, u32[]{:S(2)}) collective-permute-start(bf16[80,640]{1,0:T(8,128)(2,1)S(1)} %get-tuple-element.43), channel_id=1, source_target_pairs={{0,4},{1,5},{2,6},{3,7},{4,0},{5,1},{6,2},{7,3},{8,12},{9,13},{10,... | collective-permute-start | bytes 307208 | tf_op jit(solution)/shard_map/sum_gradient/ppermute | solution.py:273
  48.9 0.6 %collective-permute-start.17 = (bf16[80,640]{1,0:T(8,128)(2,1)S(1)}, bf16[80,640]{1,0:T(8,128)(2,1)S(1)}, u32[]{:S(2)}, u32[]{:S(2)}) collective-permute-start(bf16[80,640]{1,0:T(8,128)(2,1)S(1)} %get-tuple-element.45), channel_id=1, source_target_pairs={{0,2},{1,3},{2,0},{3,1},{4,6},{5,7},{6,4},{7,5},{8,10},{9,11},{10,... | collective-permute-start | bytes 307208 | tf_op jit(solution)/shard_map/sum_gradient/ppermute | solution.py:273
  49.5 1.5 %collective-permute-start.8 = (bf16[320,128]{1,0:T(8,128)(2,1)S(1)}, bf16[320,128]{1,0:T(8,128)(2,1)S(1)}, u32[]{:S(2)}, u32[]{:S(2)}) collective-permute-start(bf16[320,128]{1,0:T(8,128)(2,1)S(1)} %get-tuple-element.37), channel_id=1, source_target_pairs={{0,16},{1,17},{2,18},{3,19},{4,20},{5,21},{6,22},{7,23},{8,24},{9,... | collective-permute-start | bytes 245768 | tf_op jit(solution)/shard_map/send_home/ppermute | solution.py:273
  51.0 0.7 %collective-permute-start.9 = (bf16[320,128]{1,0:T(8,128)(2,1)S(1)}, bf16[320,128]{1,0:T(8,128)(2,1)S(1)}, u32[]{:S(2)}, u32[]{:S(2)}) collective-permute-start(bf16[320,128]{1,0:T(8,128)(2,1)S(1)} %get-tuple-element.38), channel_id=1, source_target_pairs={{0,24},{1,25},{2,26},{3,27},{4,28},{5,29},{6,30},{7,31},{8,16},{9,... | collective-permute-start | bytes 245768 | tf_op jit(solution)/shard_map/send_home/ppermute | solution.py:273
  51.7 3.1 %collective-permute-done.8.refs_2_ = bf16[320,128]{1,0:T(8,128)(2,1)S(1)} collective-permute-done((bf16[320,128]{1,0:T(8,128)(2,1)S(1)}, bf16[320,128]{1,0:T(8,128)(2,1)S(1)}, u32[]{:S(2)}, u32[]{:S(2)}) %collective-permute-start.8) | collective-permute-done | bytes 81952 | tf_op jit(solution)/shard_map/send_home/ppermute | solution.py:273
  54.8 1.5 %collective-permute-done.9.refs_3_ = bf16[320,128]{1,0:T(8,128)(2,1)S(1)} collective-permute-done((bf16[320,128]{1,0:T(8,128)(2,1)S(1)}, bf16[320,128]{1,0:T(8,128)(2,1)S(1)}, u32[]{:S(2)}, u32[]{:S(2)}) %collective-permute-start.9) | collective-permute-done | bytes 81952 | tf_op jit(solution)/shard_map/send_home/ppermute | solution.py:273
  56.4 1.4 %project.1 = bf16[128,1280]{1,0:T(8,128)(2,1)} custom-call(bf16[320,128]{1,0:T(8,128)(2,1)S(1)} %get-tuple-element.35.refs_0_, bf16[320,128]{1,0:T(8,128)(2,1)S(1)} %collective-permute-done.7.refs_1_, bf16[320,128]{1,0:T(8,128)(2,1)S(1)} %collective-permute-done.8.refs_2_, bf16[320,128]{1,0:T(8,128)(2,1)S(1)} %collective-permute-done.9.refs_3_, ...), custom_call_target="tpu_custom_call" | custom-call | flops 209715200 | bytes 3276800 | tf_op jit(solution)/shard_map/project/pallas_call | solution.py:39
  57.8 0.8 %add_gradient.1 = f32[160,320]{1,0:T(8,128)} custom-call(f32[160,320]{1,0:T(8,128)S(1)} %get-tuple-element.42.own, bf16[80,640]{1,0:T(8,128)(2,1)S(1)} %collective-permute-done.15.refs_0_, bf16[80,640]{1,0:T(8,128)(2,1)S(1)} %collective-permute-done.16.refs_1_, bf16[80,640]{1,0:T(8,128)(2,1)S(1)} %collective-permute-done.17.refs_2_), custom_call_target="tpu_custom_call" | custom-call | bytes 819200 | tf_op jit(solution)/shard_map/add_gradient/pallas_call | solution.py:39
  (17 shorter events, 0.1 us)
Async XLA Ops:
  2.2 12.1 %collective-permute-start = (bf16[976,128]{1,0:T(8,128)(2,1)S(1)}, bf16[976,128]{1,0:T(8,128)(2,1)S(1)}, u32[]{:S(2)}, u32[]{:S(2)}) collective-permute-start(bf16[976,128]{1,0:T(8,128)(2,1)S(1)} %get-tuple-element.24), channel_id=1, source_target_pairs={{0,6},{1,7},{2,4},{3,5},{4,2},{5,3},{6,0},{7,1},{8,14},{9,15},{10,... | collective-permute-start | bytes 749576 | tf_op jit(solution)/shard_map/exchange_heads/ppermute | solution.py:273
  7.3 12.5 %collective-permute-start.1 = (bf16[976,128]{1,0:T(8,128)(2,1)S(1)}, bf16[976,128]{1,0:T(8,128)(2,1)S(1)}, u32[]{:S(2)}, u32[]{:S(2)}) collective-permute-start(bf16[976,128]{1,0:T(8,128)(2,1)S(1)} %get-tuple-element.26), channel_id=1, source_target_pairs={{0,2},{1,3},{2,0},{3,1},{4,6},{5,7},{6,4},{7,5},{8,10},{9,11},{10,... | collective-permute-start | bytes 749576 | tf_op jit(solution)/shard_map/exchange_heads/ppermute | solution.py:273
  7.3 21.3 %collective-permute-start.2 = (bf16[976,128]{1,0:T(8,128)(2,1)S(1)}, bf16[976,128]{1,0:T(8,128)(2,1)S(1)}, u32[]{:S(2)}, u32[]{:S(2)}) collective-permute-start(bf16[976,128]{1,0:T(8,128)(2,1)S(1)} %get-tuple-element.27), channel_id=1, source_target_pairs={{0,4},{1,5},{2,6},{3,7},{4,0},{5,1},{6,2},{7,3},{8,12},{9,13},{10,... | collective-permute-start | bytes 749576 | tf_op jit(solution)/shard_map/exchange_heads/ppermute | solution.py:273
  7.9 27.1 %collective-permute-start.13 = (bf16[128,1280]{1,0:T(8,128)(2,1)S(1)}, bf16[128,1280]{1,0:T(8,128)(2,1)S(1)}, u32[]{:S(2)}, u32[]{:S(2)}) collective-permute-start(bf16[128,1280]{1,0:T(8,128)(2,1)S(1)} %get-tuple-element.41.refs_0_), channel_id=1, source_target_pairs={{0,24},{1,25},{2,26},{3,27},{4,28},{5,29},{6,30},{7,31},{8,16},{9,... | collective-permute-start | bytes 983048 | tf_op jit(solution)/shard_map/gather_cotangent/ppermute | solution.py:273
  10.5 25.2 %collective-permute-start.12 = (bf16[128,1280]{1,0:T(8,128)(2,1)S(1)}, bf16[128,1280]{1,0:T(8,128)(2,1)S(1)}, u32[]{:S(2)}, u32[]{:S(2)}) collective-permute-start(bf16[128,1280]{1,0:T(8,128)(2,1)S(1)} %get-tuple-element.41.refs_0_), channel_id=1, source_target_pairs={{0,16},{1,17},{2,18},{3,19},{4,20},{5,21},{6,22},{7,23},{8,24},{9,... | collective-permute-start | bytes 983048 | tf_op jit(solution)/shard_map/gather_cotangent/ppermute | solution.py:273
  14.2 24.8 %collective-permute-start.11 = (bf16[128,1280]{1,0:T(8,128)(2,1)S(1)}, bf16[128,1280]{1,0:T(8,128)(2,1)S(1)}, u32[]{:S(2)}, u32[]{:S(2)}) collective-permute-start(bf16[128,1280]{1,0:T(8,128)(2,1)S(1)} %get-tuple-element.41.refs_0_), channel_id=1, source_target_pairs={{0,8},{1,9},{2,10},{3,11},{4,12},{5,13},{6,14},{7,15},{8,0},{9,1},... | collective-permute-start | bytes 983048 | tf_op jit(solution)/shard_map/gather_cotangent/ppermute | solution.py:273
  30.0 9.7 %collective-permute-start.3 = (bf16[320,128]{1,0:T(8,128)(2,1)S(1)}, bf16[320,128]{1,0:T(8,128)(2,1)S(1)}, u32[]{:S(2)}, u32[]{:S(2)}) collective-permute-start(bf16[320,128]{1,0:T(8,128)(2,1)S(1)} %get-tuple-element.31), channel_id=1, source_target_pairs={{0,4},{1,5},{2,14},{3,15},{4,16},{5,17},{6,26},{7,27},{8,12},{9,13... | collective-permute-start | bytes 245768 | tf_op jit(solution)/shard_map/send_to_owner/ppermute | solution.py:273
  30.1 9.6 %collective-permute-start.4 = (bf16[320,128]{1,0:T(8,128)(2,1)S(1)}, bf16[320,128]{1,0:T(8,128)(2,1)S(1)}, u32[]{:S(2)}, u32[]{:S(2)}) collective-permute-start(bf16[320,128]{1,0:T(8,128)(2,1)S(1)} %get-tuple-element.32), channel_id=1, source_target_pairs={{0,6},{1,7},{2,12},{3,13},{4,18},{5,19},{6,24},{7,25},{8,14},{9,15... | collective-permute-start | bytes 245768 | tf_op jit(solution)/shard_map/send_to_owner/ppermute | solution.py:273
  35.0 4.7 %collective-permute-start.5 = (bf16[320,128]{1,0:T(8,128)(2,1)S(1)}, bf16[320,128]{1,0:T(8,128)(2,1)S(1)}, u32[]{:S(2)}, u32[]{:S(2)}) collective-permute-start(bf16[320,128]{1,0:T(8,128)(2,1)S(1)} %get-tuple-element.33), channel_id=1, source_target_pairs={{0,0},{1,1},{2,10},{3,11},{4,20},{5,21},{6,30},{7,31},{8,8},{9,9},... | collective-permute-start | bytes 245768 | tf_op jit(solution)/shard_map/send_to_owner/ppermute | solution.py:273
  35.7 6.6 %collective-permute-start.6 = (bf16[320,128]{1,0:T(8,128)(2,1)S(1)}, bf16[320,128]{1,0:T(8,128)(2,1)S(1)}, u32[]{:S(2)}, u32[]{:S(2)}) collective-permute-start(bf16[320,128]{1,0:T(8,128)(2,1)S(1)} %get-tuple-element.34), channel_id=1, source_target_pairs={{0,2},{1,3},{2,8},{3,9},{4,22},{5,23},{6,28},{7,29},{8,10},{9,11},... | collective-permute-start | bytes 245768 | tf_op jit(solution)/shard_map/send_to_owner/ppermute | solution.py:273
  39.5 4.5 %collective-permute-start.14 = (bf16[4,128,1280]{2,1,0:T(8,128)(2,1)S(1)}, bf16[4,128,1280]{2,1,0:T(8,128)(2,1)S(1)}, u32[]{:S(2)}, u32[]{:S(2)}) collective-permute-start(bf16[4,128,1280]{2,1,0:T(8,128)(2,1)S(1)} %swap_cotangent.1.refs_2_), channel_id=1, source_target_pairs={{0,1},{1,0},{2,3},{3,2},{4,5},{5,4},{6,7},{7,6},{8,9},{9,8},{10,11... | collective-permute-start | bytes 3932168 | tf_op jit(solution)/shard_map/gradient/ppermute | solution.py:273
  42.4 14.0 %copy-start = (bf16[1280,1280]{1,0:T(8,128)(2,1)S(1)}, bf16[1280,1280]{1,0:T(8,128)(2,1)}, u32[]{:S(2)}) copy-start(bf16[1280,1280]{1,0:T(8,128)(2,1)} %refs_5_.1) | copy-start | bytes 9830404
  42.5 1.5 %collective-permute-start.10 = (bf16[4,160,128]{2,1,0:T(8,128)(2,1)S(1)}, bf16[4,160,128]{2,1,0:T(8,128)(2,1)S(1)}, u32[]{:S(2)}, u32[]{:S(2)}) collective-permute-start(bf16[4,160,128]{2,1,0:T(8,128)(2,1)S(1)} %get-tuple-element.40), channel_id=1, source_target_pairs={{0,1},{1,0},{2,3},{3,2},{4,5},{5,4},{6,7},{7,6},{8,9},{9,8},{10,11... | collective-permute-start | bytes 491528 | tf_op jit(solution)/shard_map/send_to_owner/ppermute | solution.py:273
  42.6 8.5 %collective-permute-start.7 = (bf16[320,128]{1,0:T(8,128)(2,1)S(1)}, bf16[320,128]{1,0:T(8,128)(2,1)S(1)}, u32[]{:S(2)}, u32[]{:S(2)}) collective-permute-start(bf16[320,128]{1,0:T(8,128)(2,1)S(1)} %get-tuple-element.36), channel_id=1, source_target_pairs={{0,8},{1,9},{2,10},{3,11},{4,12},{5,13},{6,14},{7,15},{8,0},{9,1},... | collective-permute-start | bytes 245768 | tf_op jit(solution)/shard_map/send_home/ppermute | solution.py:273
  43.9 12.4 %copy-start.1 = (bf16[128,1280]{1,0:T(8,128)(2,1)S(1)}, bf16[128,1280]{1,0:T(8,128)(2,1)}, u32[]{:S(2)}) copy-start(bf16[128,1280]{1,0:T(8,128)(2,1)} %refs_4_.3) | copy-start | bytes 983044
  44.9 12.9 %collective-permute-start.15 = (bf16[80,640]{1,0:T(8,128)(2,1)S(1)}, bf16[80,640]{1,0:T(8,128)(2,1)S(1)}, u32[]{:S(2)}, u32[]{:S(2)}) collective-permute-start(bf16[80,640]{1,0:T(8,128)(2,1)S(1)} %get-tuple-element.43), channel_id=1, source_target_pairs={{0,4},{1,5},{2,6},{3,7},{4,0},{5,1},{6,2},{7,3},{8,12},{9,13},{10,... | collective-permute-start | bytes 307208 | tf_op jit(solution)/shard_map/sum_gradient/ppermute | solution.py:273
  48.9 8.9 %collective-permute-start.16 = (bf16[80,640]{1,0:T(8,128)(2,1)S(1)}, bf16[80,640]{1,0:T(8,128)(2,1)S(1)}, u32[]{:S(2)}, u32[]{:S(2)}) collective-permute-start(bf16[80,640]{1,0:T(8,128)(2,1)S(1)} %get-tuple-element.44), channel_id=1, source_target_pairs={{0,6},{1,7},{2,4},{3,5},{4,2},{5,3},{6,0},{7,1},{8,14},{9,15},{10,... | collective-permute-start | bytes 307208 | tf_op jit(solution)/shard_map/sum_gradient/ppermute | solution.py:273
  48.9 8.9 %collective-permute-start.17 = (bf16[80,640]{1,0:T(8,128)(2,1)S(1)}, bf16[80,640]{1,0:T(8,128)(2,1)S(1)}, u32[]{:S(2)}, u32[]{:S(2)}) collective-permute-start(bf16[80,640]{1,0:T(8,128)(2,1)S(1)} %get-tuple-element.45), channel_id=1, source_target_pairs={{0,2},{1,3},{2,0},{3,1},{4,6},{5,7},{6,4},{7,5},{8,10},{9,11},{10,... | collective-permute-start | bytes 307208 | tf_op jit(solution)/shard_map/sum_gradient/ppermute | solution.py:273
  49.5 5.3 %collective-permute-start.8 = (bf16[320,128]{1,0:T(8,128)(2,1)S(1)}, bf16[320,128]{1,0:T(8,128)(2,1)S(1)}, u32[]{:S(2)}, u32[]{:S(2)}) collective-permute-start(bf16[320,128]{1,0:T(8,128)(2,1)S(1)} %get-tuple-element.37), channel_id=1, source_target_pairs={{0,16},{1,17},{2,18},{3,19},{4,20},{5,21},{6,22},{7,23},{8,24},{9,... | collective-permute-start | bytes 245768 | tf_op jit(solution)/shard_map/send_home/ppermute | solution.py:273
  51.0 5.3 %collective-permute-start.9 = (bf16[320,128]{1,0:T(8,128)(2,1)S(1)}, bf16[320,128]{1,0:T(8,128)(2,1)S(1)}, u32[]{:S(2)}, u32[]{:S(2)}) collective-permute-start(bf16[320,128]{1,0:T(8,128)(2,1)S(1)} %get-tuple-element.38), channel_id=1, source_target_pairs={{0,24},{1,25},{2,26},{3,27},{4,28},{5,29},{6,30},{7,31},{8,16},{9,... | collective-permute-start | bytes 245768 | tf_op jit(solution)/shard_map/send_home/ppermute | solution.py:273

commit v10 on v6

--- a/solution.py
+++ b/solution.py
@@ -227,11 +227,13 @@
     out[...] = (residual[...].astype(jnp.float32) + projected).astype(jnp.bfloat16)
 
 
-def add_kernel(*refs):
+def add_kernel(kept, *refs):
     partial, out = refs[:-1], refs[-1]
-    total = partial[0][...].astype(jnp.float32)
-    for ref in partial[1:]:
-        total = total + ref[...].astype(jnp.float32)
+    stays = lax.axis_index("enc") == 0
+    total = jnp.where(stays, kept[...], partial[SUMS.index(0)][...]).astype(jnp.float32)
+    for hop, ref in zip(SUMS, partial):
+        if hop:
+            total = total + ref[...].astype(jnp.float32)
     short, width = total.shape[0], out.shape[1]
     out[:short] = total[:, :width]
     out[short:] = total[:, width:]
@@ -256,9 +258,10 @@
             for e in range(n_enc):
                 for s in range(n_seq):
                     to_d, to_e, to_s = partner(d, e, s)
-                    pairs.append(
-                        ((d * n_enc + e) * n_seq + s, (to_d * n_enc + to_e) * n_seq + to_s)
-                    )
+                    source = (d * n_enc + e) * n_seq + s
+                    target = (to_d * n_enc + to_e) * n_seq + to_s
+                    if source != target:
+                        pairs.append((source, target))
         return lax.ppermute(data, AXES, pairs)
 
     def along_enc(pieces, hops):
@@ -359,6 +362,7 @@
             bytes_accessed=2 * n_dp * n_seq * rows * width,
         )
     with jax.named_scope("sum_gradient"):
+        kept = partial[SUMS.index(0)]
         partial = [
             move(part, lambda d, e, s, hop=hop: (d ^ e, e ^ hop, s))
             for hop, part in zip(SUMS, partial)
@@ -383,6 +387,7 @@
         grad_weight = call(
             add_kernel,
             jax.ShapeDtypeStruct((half, block), jnp.float32),
+            kept,
             *partial,
             bytes_accessed=4 * half * block * 4,
         )

time: 58.4 us -> 58.5 us (level)
  no operation moved by 1% of the time
where the time goes in v10:
time: 58.5 us; the launch traced here: 58.3 us
  starting transfers between devices  24.7 us (42%)
  waiting for transfers between devices  23.6 us (40%)
  Pallas kernels  9.33 us (16%)
  between operations  0.76 us (1%)
    ppermute x18, starting transfers between devices, move(): return lax.ppermute(data, AXES, pairs)  24.7 us
    ppermute x18, waiting for transfers between devices, move(): return lax.ppermute(data, AXES, pairs)  23.6 us
    pallas_call x9, Pallas kernels, call(): pl.pallas_call(kernel, out_shape=out_shape, in_specs=[placed(space) for s...  9.33 us
  transfers between devices with their start and end apart: 18, of which 7 were waited for; matrix products, arithmetic and copies ran while one was open for 0% of the time, Pallas kernels for 12%

profile of v10, /device:TPU:0, one launch (start us, length us, event | category | flops | bytes accessed | tf_op | source)
XLA Modules:
  0.0 58.3 jit_solution(13802983067872011597)
XLA Ops:
  0.6 1.5 %pack.1 = (bf16[976,128]{1,0:T(8,128)(2,1)S(1)}, bf16[976,128]{1,0:T(8,128)(2,1)S(1)}, bf16[976,128]{1,0:T(8,128)(2,1)S(1)}, bf16[976,128]{1,0:T(8,128)(2,1)S(1)}, bf16[128,1280]{1,0:T(8,128)(2,1)S(1)}) custom-call(s32[1,128]{1,0:T(1,128)} %bitcast.1, bf16[128,1280]{1,0:T(8,128)(2,1)} %refs_1_.1, bf16[128,1280]{1,0:T(8,128)(2,1)} %refs_2_.1, ...), custom_call_target="tpu_custom_call" | custom-call | bytes 2621440 | tf_op jit(solution)/shard_map/pack/pallas_call | solution.py:39
  2.2 5.1 %collective-permute-start = (bf16[976,128]{1,0:T(8,128)(2,1)S(1)}, bf16[976,128]{1,0:T(8,128)(2,1)S(1)}, u32[]{:S(2)}, u32[]{:S(2)}) collective-permute-start(bf16[976,128]{1,0:T(8,128)(2,1)S(1)} %get-tuple-element.20), channel_id=1, source_target_pairs={{0,6},{1,7},{2,4},{3,5},{4,2},{5,3},{6,0},{7,1},{8,14},{9,15},{10,... | collective-permute-start | bytes 749576 | tf_op jit(solution)/shard_map/exchange_heads/ppermute | solution.py:265
  7.3 0.0 collective-permute-start.1
  7.3 0.6 %collective-permute-start.2 = (bf16[976,128]{1,0:T(8,128)(2,1)S(1)}, bf16[976,128]{1,0:T(8,128)(2,1)S(1)}, u32[]{:S(2)}, u32[]{:S(2)}) collective-permute-start(bf16[976,128]{1,0:T(8,128)(2,1)S(1)} %get-tuple-element.23), channel_id=1, source_target_pairs={{0,4},{1,5},{2,6},{3,7},{4,0},{5,1},{6,2},{7,3},{8,12},{9,13},{10,... | collective-permute-start | bytes 749576 | tf_op jit(solution)/shard_map/exchange_heads/ppermute | solution.py:265
  7.9 2.6 %collective-permute-start.12 = (bf16[128,1280]{1,0:T(8,128)(2,1)S(1)}, bf16[128,1280]{1,0:T(8,128)(2,1)S(1)}, u32[]{:S(2)}, u32[]{:S(2)}) collective-permute-start(bf16[128,1280]{1,0:T(8,128)(2,1)S(1)} %get-tuple-element.33.refs_0_), channel_id=1, source_target_pairs={{0,24},{1,25},{2,26},{3,27},{4,28},{5,29},{6,30},{7,31},{8,16},{9,... | collective-permute-start | bytes 983048 | tf_op jit(solution)/shard_map/gather_cotangent/ppermute | solution.py:265
  10.5 0.5 collective-permute-start.11
  11.0 3.2 %collective-permute-done.refs_0_ = bf16[976,128]{1,0:T(8,128)(2,1)S(1)} collective-permute-done((bf16[976,128]{1,0:T(8,128)(2,1)S(1)}, bf16[976,128]{1,0:T(8,128)(2,1)S(1)}, u32[]{:S(2)}, u32[]{:S(2)}) %collective-permute-start) | collective-permute-done | bytes 249888 | tf_op jit(solution)/shard_map/exchange_heads/ppermute | solution.py:265
  14.2 1.7 %collective-permute-start.10 = (bf16[128,1280]{1,0:T(8,128)(2,1)S(1)}, bf16[128,1280]{1,0:T(8,128)(2,1)S(1)}, u32[]{:S(2)}, u32[]{:S(2)}) collective-permute-start(bf16[128,1280]{1,0:T(8,128)(2,1)S(1)} %get-tuple-element.33.refs_0_), channel_id=1, source_target_pairs={{0,8},{1,9},{2,10},{3,11},{4,12},{5,13},{6,14},{7,15},{8,0},{9,1},... | collective-permute-start | bytes 983048 | tf_op jit(solution)/shard_map/gather_cotangent/ppermute | solution.py:265
  15.9 3.9 %collective-permute-done.1.refs_2_.refs_1_ = bf16[976,128]{1,0:T(8,128)(2,1)S(1)} collective-permute-done((bf16[976,128]{1,0:T(8,128)(2,1)S(1)}, bf16[976,128]{1,0:T(8,128)(2,1)S(1)}, u32[]{:S(2)}, u32[]{:S(2)}) %collective-permute-start.1) | collective-permute-done | bytes 249888 | tf_op jit(solution)/shard_map/exchange_heads/ppermute | solution.py:265
  19.8 1.7 %attention.3 = (f32[320,384]{1,0:T(8,128)S(1)}, f32[8,384]{1,0:T(8,128)S(1)}, f32[8,384]{1,0:T(8,128)S(1)}) custom-call(bf16[976,128]{1,0:T(8,128)(2,1)S(1)} %collective-permute-done.refs_0_, bf16[976,128]{1,0:T(8,128)(2,1)S(1)} %get-tuple-element.21.refs_1_.refs_0_, bf16[976,128]{1,0:T(8,128)(2,1)S(1)} %collective-permute-done.1.refs_2_.refs_1_), custom_call_target="tpu_custom_call" | custom-call | flops 2595225600 | bytes 1310720 | tf_op jit(solution)/shard_map/attention/pallas_call | solution.py:39
  21.5 7.1 %collective-permute-done.2.refs_3_.refs_2_ = bf16[976,128]{1,0:T(8,128)(2,1)S(1)} collective-permute-done((bf16[976,128]{1,0:T(8,128)(2,1)S(1)}, bf16[976,128]{1,0:T(8,128)(2,1)S(1)}, u32[]{:S(2)}, u32[]{:S(2)}) %collective-permute-start.2) | collective-permute-done | bytes 249888 | tf_op jit(solution)/shard_map/exchange_heads/ppermute | solution.py:265
  28.5 1.5 %attention.4 = (bf16[320,128]{1,0:T(8,128)(2,1)S(1)}, bf16[320,128]{1,0:T(8,128)(2,1)S(1)}) custom-call(bf16[976,128]{1,0:T(8,128)(2,1)S(1)} %collective-permute-done.refs_0_, bf16[976,128]{1,0:T(8,128)(2,1)S(1)} %get-tuple-element.21.refs_1_.refs_0_, bf16[976,128]{1,0:T(8,128)(2,1)S(1)} %collective-permute-done.1.refs_2_.refs_1_, ...), custom_call_target="tpu_custom_call" | custom-call | flops 1441792000 | bytes 1310720 | tf_op jit(solution)/shard_map/attention/pallas_call | solution.py:39
  30.0 0.6 collective-permute-start.3
  30.6 3.9 %collective-permute-start.5 = (bf16[320,128]{1,0:T(8,128)(2,1)S(1)}, bf16[320,128]{1,0:T(8,128)(2,1)S(1)}, u32[]{:S(2)}, u32[]{:S(2)}) collective-permute-start(bf16[320,128]{1,0:T(8,128)(2,1)S(1)} %get-tuple-element.28), channel_id=1, source_target_pairs={{0,30},{1,31},{2,28},{3,29},{4,26},{5,27},{6,24},{7,25},{8,22},{9,... | collective-permute-start | bytes 245768 | tf_op jit(solution)/shard_map/send_to_owner/ppermute | solution.py:265
  34.5 1.0 %attention.5 = (bf16[320,128]{1,0:T(8,128)(2,1)S(1)}, bf16[320,128]{1,0:T(8,128)(2,1)S(1)}) custom-call(bf16[976,128]{1,0:T(8,128)(2,1)S(1)} %get-tuple-element.21.refs_1_.refs_0_, bf16[976,128]{1,0:T(8,128)(2,1)S(1)} %collective-permute-done.1.refs_2_.refs_1_, bf16[976,128]{1,0:T(8,128)(2,1)S(1)} %collective-permute-done.2.refs_3_.refs_2_, ...), custom_call_target="tpu_custom_call" | custom-call | flops 576716800 | bytes 1310720 | tf_op jit(solution)/shard_map/attention/pallas_call | solution.py:39
  35.6 0.9 %collective-permute-start.7 = (bf16[320,128]{1,0:T(8,128)(2,1)S(1)}, bf16[320,128]{1,0:T(8,128)(2,1)S(1)}, u32[]{:S(2)}, u32[]{:S(2)}) collective-permute-start(bf16[320,128]{1,0:T(8,128)(2,1)S(1)} %get-tuple-element.29), channel_id=1, source_target_pairs={{0,10},{1,11},{2,8},{3,9},{4,14},{5,15},{6,12},{7,13},{8,2},{9,3},... | collective-permute-start | bytes 245768 | tf_op jit(solution)/shard_map/send_to_owner/ppermute | solution.py:265
  36.5 0.4 swap_cotangent.1.refs_2_
  37.0 0.1 collective-permute-start.13
  37.0 2.4 %collective-permute-done.3.refs_0_ = bf16[320,128]{1,0:T(8,128)(2,1)S(1)} collective-permute-done((bf16[320,128]{1,0:T(8,128)(2,1)S(1)}, bf16[320,128]{1,0:T(8,128)(2,1)S(1)}, u32[]{:S(2)}, u32[]{:S(2)}) %collective-permute-start.3) | collective-permute-done | bytes 81952 | tf_op jit(solution)/shard_map/send_to_owner/ppermute | solution.py:265
  39.4 1.6 %collective-permute-done.7.refs_2_ = bf16[320,128]{1,0:T(8,128)(2,1)S(1)} collective-permute-done((bf16[320,128]{1,0:T(8,128)(2,1)S(1)}, bf16[320,128]{1,0:T(8,128)(2,1)S(1)}, u32[]{:S(2)}, u32[]{:S(2)}) %collective-permute-start.7) | collective-permute-done | bytes 81952 | tf_op jit(solution)/shard_map/send_to_owner/ppermute | solution.py:265
  41.0 0.1 collective-permute-start.9
  41.1 1.0 %collective-permute-start.4 = (bf16[320,128]{1,0:T(8,128)(2,1)S(1)}, bf16[320,128]{1,0:T(8,128)(2,1)S(1)}, u32[]{:S(2)}, u32[]{:S(2)}) collective-permute-start(bf16[320,128]{1,0:T(8,128)(2,1)S(1)} %collective-permute-done.3.refs_0_), channel_id=1, source_target_pairs={{0,16},{1,17},{2,18},{3,19},{4,20},{5,21},{6,22},{7,23},{8,24},{9,... | collective-permute-start | bytes 245768 | tf_op jit(solution)/shard_map/send_home/ppermute | solution.py:265
  42.1 1.1 %collective-permute-start.6 = (bf16[320,128]{1,0:T(8,128)(2,1)S(1)}, bf16[320,128]{1,0:T(8,128)(2,1)S(1)}, u32[]{:S(2)}, u32[]{:S(2)}) collective-permute-start(bf16[320,128]{1,0:T(8,128)(2,1)S(1)} %collective-permute-done.5.refs_1_), channel_id=1, source_target_pairs={{0,24},{1,25},{2,26},{3,27},{4,28},{5,29},{6,30},{7,31},{8,16},{9,... | collective-permute-start | bytes 245768 | tf_op jit(solution)/shard_map/send_home/ppermute | solution.py:265
  43.2 1.5 %collective-permute-start.8 = (bf16[320,128]{1,0:T(8,128)(2,1)S(1)}, bf16[320,128]{1,0:T(8,128)(2,1)S(1)}, u32[]{:S(2)}, u32[]{:S(2)}) collective-permute-start(bf16[320,128]{1,0:T(8,128)(2,1)S(1)} %collective-permute-done.7.refs_2_), channel_id=1, source_target_pairs={{0,8},{1,9},{2,10},{3,11},{4,12},{5,13},{6,14},{7,15},{8,0},{9,1},... | collective-permute-start | bytes 245768 | tf_op jit(solution)/shard_map/send_home/ppermute | solution.py:265
  44.7 0.9 %gradient.1 = (bf16[80,640]{1,0:T(8,128)(2,1)S(1)}, bf16[80,640]{1,0:T(8,128)(2,1)S(1)}, bf16[80,640]{1,0:T(8,128)(2,1)S(1)}, bf16[80,640]{1,0:T(8,128)(2,1)S(1)}) custom-call(bf16[4,160,128]{2,1,0:T(8,128)(2,1)S(1)} %get-tuple-element.31.refs_0_, bf16[4,160,128]{2,1,0:T(8,128)(2,1)S(1)} %collective-permute-done.9.refs_1_, ...), custom_call_target="tpu_custom_call" | custom-call | flops 419430400 | bytes 2621440 | tf_op jit(solution)/shard_map/gradient/pallas_call | solution.py:39
  45.6 2.1 %collective-permute-start.14 = (bf16[80,640]{1,0:T(8,128)(2,1)S(1)}, bf16[80,640]{1,0:T(8,128)(2,1)S(1)}, u32[]{:S(2)}, u32[]{:S(2)}) collective-permute-start(bf16[80,640]{1,0:T(8,128)(2,1)S(1)} %get-tuple-element.35), channel_id=1, source_target_pairs={{0,4},{1,5},{2,14},{3,15},{4,16},{5,17},{6,26},{7,27},{8,12},{9,13... | collective-permute-start | bytes 307208 | tf_op jit(solution)/shard_map/sum_gradient/ppermute | solution.py:265
  47.7 2.2 %collective-permute-start.15 = (bf16[80,640]{1,0:T(8,128)(2,1)S(1)}, bf16[80,640]{1,0:T(8,128)(2,1)S(1)}, u32[]{:S(2)}, u32[]{:S(2)}) collective-permute-start(bf16[80,640]{1,0:T(8,128)(2,1)S(1)} %get-tuple-element.36), channel_id=1, source_target_pairs={{0,6},{1,7},{2,12},{3,13},{4,18},{5,19},{6,24},{7,25},{8,14},{9,15... | collective-permute-start | bytes 307208 | tf_op jit(solution)/shard_map/sum_gradient/ppermute | solution.py:265
  49.9 0.7 %collective-permute-start.17 = (bf16[80,640]{1,0:T(8,128)(2,1)S(1)}, bf16[80,640]{1,0:T(8,128)(2,1)S(1)}, u32[]{:S(2)}, u32[]{:S(2)}) collective-permute-start(bf16[80,640]{1,0:T(8,128)(2,1)S(1)} %get-tuple-element.34.kept), channel_id=1, source_target_pairs={{2,10},{3,11},{4,20},{5,21},{6,30},{7,31},{10,2},{11,3},{12,28},{1... | collective-permute-start | bytes 307208 | tf_op jit(solution)/shard_map/sum_gradient/ppermute | solution.py:265
  50.6 1.4 %project.1 = bf16[128,1280]{1,0:T(8,128)(2,1)} custom-call(bf16[320,128]{1,0:T(8,128)(2,1)S(1)} %collective-permute-done.4.refs_0_, bf16[320,128]{1,0:T(8,128)(2,1)S(1)} %collective-permute-done.6.refs_1_, bf16[320,128]{1,0:T(8,128)(2,1)S(1)} %collective-permute-done.8.refs_2_, bf16[320,128]{1,0:T(8,128)(2,1)S(1)} %get-tuple-element.30.refs_3_, ...), custom_call_target="tpu_custom_call" | custom-call | flops 419430400 | bytes 3276800 | tf_op jit(solution)/shard_map/project/pallas_call | solution.py:39
  52.0 5.1 %collective-permute-done.14.refs_0_ = bf16[80,640]{1,0:T(8,128)(2,1)S(1)} collective-permute-done((bf16[80,640]{1,0:T(8,128)(2,1)S(1)}, bf16[80,640]{1,0:T(8,128)(2,1)S(1)}, u32[]{:S(2)}, u32[]{:S(2)}) %collective-permute-start.14) | collective-permute-done | bytes 102432 | tf_op jit(solution)/shard_map/sum_gradient/ppermute | solution.py:265
  57.1 0.4 collective-permute-done.16.refs_2_
  57.5 0.8 %add_gradient.1 = f32[160,320]{1,0:T(8,128)} custom-call(bf16[80,640]{1,0:T(8,128)(2,1)S(1)} %get-tuple-element.34.kept, bf16[80,640]{1,0:T(8,128)(2,1)S(1)} %collective-permute-done.14.refs_0_, bf16[80,640]{1,0:T(8,128)(2,1)S(1)} %collective-permute-done.15.refs_1_, bf16[80,640]{1,0:T(8,128)(2,1)S(1)} %collective-permute-done.16.refs_2_, ...), custom_call_target="tpu_custom_call" | custom-call | bytes 819200 | tf_op jit(solution)/shard_map/add_gradient/pallas_call | solution.py:39
  (17 shorter events, 0.1 us)
Async XLA Ops:
  2.2 12.1 %collective-permute-start = (bf16[976,128]{1,0:T(8,128)(2,1)S(1)}, bf16[976,128]{1,0:T(8,128)(2,1)S(1)}, u32[]{:S(2)}, u32[]{:S(2)}) collective-permute-start(bf16[976,128]{1,0:T(8,128)(2,1)S(1)} %get-tuple-element.20), channel_id=1, source_target_pairs={{0,6},{1,7},{2,4},{3,5},{4,2},{5,3},{6,0},{7,1},{8,14},{9,15},{10,... | collective-permute-start | bytes 749576 | tf_op jit(solution)/shard_map/exchange_heads/ppermute | solution.py:265
  7.3 12.5 %collective-permute-start.1 = (bf16[976,128]{1,0:T(8,128)(2,1)S(1)}, bf16[976,128]{1,0:T(8,128)(2,1)S(1)}, u32[]{:S(2)}, u32[]{:S(2)}) collective-permute-start(bf16[976,128]{1,0:T(8,128)(2,1)S(1)} %get-tuple-element.22), channel_id=1, source_target_pairs={{0,2},{1,3},{2,0},{3,1},{4,6},{5,7},{6,4},{7,5},{8,10},{9,11},{10,... | collective-permute-start | bytes 749576 | tf_op jit(solution)/shard_map/exchange_heads/ppermute | solution.py:265
  7.3 21.3 %collective-permute-start.2 = (bf16[976,128]{1,0:T(8,128)(2,1)S(1)}, bf16[976,128]{1,0:T(8,128)(2,1)S(1)}, u32[]{:S(2)}, u32[]{:S(2)}) collective-permute-start(bf16[976,128]{1,0:T(8,128)(2,1)S(1)} %get-tuple-element.23), channel_id=1, source_target_pairs={{0,4},{1,5},{2,6},{3,7},{4,0},{5,1},{6,2},{7,3},{8,12},{9,13},{10,... | collective-permute-start | bytes 749576 | tf_op jit(solution)/shard_map/exchange_heads/ppermute | solution.py:265
  7.9 27.7 %collective-permute-start.12 = (bf16[128,1280]{1,0:T(8,128)(2,1)S(1)}, bf16[128,1280]{1,0:T(8,128)(2,1)S(1)}, u32[]{:S(2)}, u32[]{:S(2)}) collective-permute-start(bf16[128,1280]{1,0:T(8,128)(2,1)S(1)} %get-tuple-element.33.refs_0_), channel_id=1, source_target_pairs={{0,24},{1,25},{2,26},{3,27},{4,28},{5,29},{6,30},{7,31},{8,16},{9,... | collective-permute-start | bytes 983048 | tf_op jit(solution)/shard_map/gather_cotangent/ppermute | solution.py:265
  10.5 26.0 %collective-permute-start.11 = (bf16[128,1280]{1,0:T(8,128)(2,1)S(1)}, bf16[128,1280]{1,0:T(8,128)(2,1)S(1)}, u32[]{:S(2)}, u32[]{:S(2)}) collective-permute-start(bf16[128,1280]{1,0:T(8,128)(2,1)S(1)} %get-tuple-element.33.refs_0_), channel_id=1, source_target_pairs={{0,16},{1,17},{2,18},{3,19},{4,20},{5,21},{6,22},{7,23},{8,24},{9,... | collective-permute-start | bytes 983048 | tf_op jit(solution)/shard_map/gather_cotangent/ppermute | solution.py:265
  14.2 22.3 %collective-permute-start.10 = (bf16[128,1280]{1,0:T(8,128)(2,1)S(1)}, bf16[128,1280]{1,0:T(8,128)(2,1)S(1)}, u32[]{:S(2)}, u32[]{:S(2)}) collective-permute-start(bf16[128,1280]{1,0:T(8,128)(2,1)S(1)} %get-tuple-element.33.refs_0_), channel_id=1, source_target_pairs={{0,8},{1,9},{2,10},{3,11},{4,12},{5,13},{6,14},{7,15},{8,0},{9,1},... | collective-permute-start | bytes 983048 | tf_op jit(solution)/shard_map/gather_cotangent/ppermute | solution.py:265
  30.0 9.4 %collective-permute-start.3 = (bf16[320,128]{1,0:T(8,128)(2,1)S(1)}, bf16[320,128]{1,0:T(8,128)(2,1)S(1)}, u32[]{:S(2)}, u32[]{:S(2)}) collective-permute-start(bf16[320,128]{1,0:T(8,128)(2,1)S(1)} %get-tuple-element.27), channel_id=1, source_target_pairs={{0,20},{1,21},{2,22},{3,23},{4,16},{5,17},{6,18},{7,19},{8,28},{9,... | collective-permute-start | bytes 245768 | tf_op jit(solution)/shard_map/send_to_owner/ppermute | solution.py:265
  30.6 8.8 %collective-permute-start.5 = (bf16[320,128]{1,0:T(8,128)(2,1)S(1)}, bf16[320,128]{1,0:T(8,128)(2,1)S(1)}, u32[]{:S(2)}, u32[]{:S(2)}) collective-permute-start(bf16[320,128]{1,0:T(8,128)(2,1)S(1)} %get-tuple-element.28), channel_id=1, source_target_pairs={{0,30},{1,31},{2,28},{3,29},{4,26},{5,27},{6,24},{7,25},{8,22},{9,... | collective-permute-start | bytes 245768 | tf_op jit(solution)/shard_map/send_to_owner/ppermute | solution.py:265
  35.6 5.4 %collective-permute-start.7 = (bf16[320,128]{1,0:T(8,128)(2,1)S(1)}, bf16[320,128]{1,0:T(8,128)(2,1)S(1)}, u32[]{:S(2)}, u32[]{:S(2)}) collective-permute-start(bf16[320,128]{1,0:T(8,128)(2,1)S(1)} %get-tuple-element.29), channel_id=1, source_target_pairs={{0,10},{1,11},{2,8},{3,9},{4,14},{5,15},{6,12},{7,13},{8,2},{9,3},... | collective-permute-start | bytes 245768 | tf_op jit(solution)/shard_map/send_to_owner/ppermute | solution.py:265
  37.0 7.7 %collective-permute-start.13 = (bf16[4,128,1280]{2,1,0:T(8,128)(2,1)S(1)}, bf16[4,128,1280]{2,1,0:T(8,128)(2,1)S(1)}, u32[]{:S(2)}, u32[]{:S(2)}) collective-permute-start(bf16[4,128,1280]{2,1,0:T(8,128)(2,1)S(1)} %swap_cotangent.1.refs_2_), channel_id=1, source_target_pairs={{0,1},{1,0},{2,3},{3,2},{4,5},{5,4},{6,7},{7,6},{8,9},{9,8},{10,11... | collective-permute-start | bytes 3932168 | tf_op jit(solution)/shard_map/gradient/ppermute | solution.py:265
  41.0 9.6 %copy-start = (bf16[1280,1280]{1,0:T(8,128)(2,1)S(1)}, bf16[1280,1280]{1,0:T(8,128)(2,1)}, u32[]{:S(2)}) copy-start(bf16[1280,1280]{1,0:T(8,128)(2,1)} %refs_5_.1) | copy-start | bytes 9830404
  41.0 3.6 %collective-permute-start.9 = (bf16[4,160,128]{2,1,0:T(8,128)(2,1)S(1)}, bf16[4,160,128]{2,1,0:T(8,128)(2,1)S(1)}, u32[]{:S(2)}, u32[]{:S(2)}) collective-permute-start(bf16[4,160,128]{2,1,0:T(8,128)(2,1)S(1)} %get-tuple-element.32), channel_id=1, source_target_pairs={{0,1},{1,0},{2,3},{3,2},{4,5},{5,4},{6,7},{7,6},{8,9},{9,8},{10,11... | collective-permute-start | bytes 491528 | tf_op jit(solution)/shard_map/send_to_owner/ppermute | solution.py:265
  41.1 8.8 %collective-permute-start.4 = (bf16[320,128]{1,0:T(8,128)(2,1)S(1)}, bf16[320,128]{1,0:T(8,128)(2,1)S(1)}, u32[]{:S(2)}, u32[]{:S(2)}) collective-permute-start(bf16[320,128]{1,0:T(8,128)(2,1)S(1)} %collective-permute-done.3.refs_0_), channel_id=1, source_target_pairs={{0,16},{1,17},{2,18},{3,19},{4,20},{5,21},{6,22},{7,23},{8,24},{9,... | collective-permute-start | bytes 245768 | tf_op jit(solution)/shard_map/send_home/ppermute | solution.py:265
  42.1 7.8 %collective-permute-start.6 = (bf16[320,128]{1,0:T(8,128)(2,1)S(1)}, bf16[320,128]{1,0:T(8,128)(2,1)S(1)}, u32[]{:S(2)}, u32[]{:S(2)}) collective-permute-start(bf16[320,128]{1,0:T(8,128)(2,1)S(1)} %collective-permute-done.5.refs_1_), channel_id=1, source_target_pairs={{0,24},{1,25},{2,26},{3,27},{4,28},{5,29},{6,30},{7,31},{8,16},{9,... | collective-permute-start | bytes 245768 | tf_op jit(solution)/shard_map/send_home/ppermute | solution.py:265
  43.2 7.4 %collective-permute-start.8 = (bf16[320,128]{1,0:T(8,128)(2,1)S(1)}, bf16[320,128]{1,0:T(8,128)(2,1)S(1)}, u32[]{:S(2)}, u32[]{:S(2)}) collective-permute-start(bf16[320,128]{1,0:T(8,128)(2,1)S(1)} %collective-permute-done.7.refs_2_), channel_id=1, source_target_pairs={{0,8},{1,9},{2,10},{3,11},{4,12},{5,13},{6,14},{7,15},{8,0},{9,1},... | collective-permute-start | bytes 245768 | tf_op jit(solution)/shard_map/send_home/ppermute | solution.py:265
  44.7 6.0 %copy-start.1 = (bf16[128,1280]{1,0:T(8,128)(2,1)S(1)}, bf16[128,1280]{1,0:T(8,128)(2,1)}, u32[]{:S(2)}) copy-start(bf16[128,1280]{1,0:T(8,128)(2,1)} %refs_4_.3) | copy-start | bytes 983044
  45.6 11.5 %collective-permute-start.14 = (bf16[80,640]{1,0:T(8,128)(2,1)S(1)}, bf16[80,640]{1,0:T(8,128)(2,1)S(1)}, u32[]{:S(2)}, u32[]{:S(2)}) collective-permute-start(bf16[80,640]{1,0:T(8,128)(2,1)S(1)} %get-tuple-element.35), channel_id=1, source_target_pairs={{0,4},{1,5},{2,14},{3,15},{4,16},{5,17},{6,26},{7,27},{8,12},{9,13... | collective-permute-start | bytes 307208 | tf_op jit(solution)/shard_map/sum_gradient/ppermute | solution.py:265
  47.7 9.4 %collective-permute-start.15 = (bf16[80,640]{1,0:T(8,128)(2,1)S(1)}, bf16[80,640]{1,0:T(8,128)(2,1)S(1)}, u32[]{:S(2)}, u32[]{:S(2)}) collective-permute-start(bf16[80,640]{1,0:T(8,128)(2,1)S(1)} %get-tuple-element.36), channel_id=1, source_target_pairs={{0,6},{1,7},{2,12},{3,13},{4,18},{5,19},{6,24},{7,25},{8,14},{9,15... | collective-permute-start | bytes 307208 | tf_op jit(solution)/shard_map/sum_gradient/ppermute | solution.py:265
  49.9 7.6 %collective-permute-start.16 = (bf16[80,640]{1,0:T(8,128)(2,1)S(1)}, bf16[80,640]{1,0:T(8,128)(2,1)S(1)}, u32[]{:S(2)}, u32[]{:S(2)}) collective-permute-start(bf16[80,640]{1,0:T(8,128)(2,1)S(1)} %get-tuple-element.37), channel_id=1, source_target_pairs={{0,2},{1,3},{2,8},{3,9},{4,22},{5,23},{6,28},{7,29},{8,10},{9,11},... | collective-permute-start | bytes 307208 | tf_op jit(solution)/shard_map/sum_gradient/ppermute | solution.py:265
  49.9 7.6 %collective-permute-start.17 = (bf16[80,640]{1,0:T(8,128)(2,1)S(1)}, bf16[80,640]{1,0:T(8,128)(2,1)S(1)}, u32[]{:S(2)}, u32[]{:S(2)}) collective-permute-start(bf16[80,640]{1,0:T(8,128)(2,1)S(1)} %get-tuple-element.34.kept), channel_id=1, source_target_pairs={{2,10},{3,11},{4,20},{5,21},{6,30},{7,31},{10,2},{11,3},{12,28},{1... | collective-permute-start | bytes 307208 | tf_op jit(solution)/shard_map/sum_gradient/ppermute | solution.py:265

commit v11 on v10

--- a/solution.py
+++ b/solution.py
@@ -14,7 +14,7 @@
 ID_BASE = 64
 SENDS = (3, 0, 1, 2)
 RETURNS = (2, 3, 1, 0)
-SUMS = (2, 3, 1, 0)
+SUMS = (2, 3, 0, 1)
 
 
 def call(

time: 58.5 us -> 58.5 us (level)
  no operation moved by 1% of the time
where the time goes in v11:
time: 58.5 us; the launch traced here: 58.3 us
  starting transfers between devices  24.7 us (42%)
  waiting for transfers between devices  23.6 us (40%)
  Pallas kernels  9.33 us (16%)
  between operations  0.76 us (1%)
    ppermute x18, starting transfers between devices, move(): return lax.ppermute(data, AXES, pairs)  24.7 us
    ppermute x18, waiting for transfers between devices, move(): return lax.ppermute(data, AXES, pairs)  23.6 us
    pallas_call x9, Pallas kernels, call(): pl.pallas_call(kernel, out_shape=out_shape, in_specs=[placed(space) for s...  9.33 us
  transfers between devices with their start and end apart: 18, of which 7 were waited for; matrix products, arithmetic and copies ran while one was open for 0% of the time, Pallas kernels for 12%

profile of v11, /device:TPU:0, one launch (start us, length us, event | category | flops | bytes accessed | tf_op | source)
XLA Modules:
  0.0 58.3 jit_solution(10059661039784026790)
XLA Ops:
  0.6 1.5 %pack.1 = (bf16[976,128]{1,0:T(8,128)(2,1)S(1)}, bf16[976,128]{1,0:T(8,128)(2,1)S(1)}, bf16[976,128]{1,0:T(8,128)(2,1)S(1)}, bf16[976,128]{1,0:T(8,128)(2,1)S(1)}, bf16[128,1280]{1,0:T(8,128)(2,1)S(1)}) custom-call(s32[1,128]{1,0:T(1,128)} %bitcast.1, bf16[128,1280]{1,0:T(8,128)(2,1)} %refs_1_.1, bf16[128,1280]{1,0:T(8,128)(2,1)} %refs_2_.1, ...), custom_call_target="tpu_custom_call" | custom-call | bytes 2621440 | tf_op jit(solution)/shard_map/pack/pallas_call | solution.py:39
  2.2 5.1 %collective-permute-start = (bf16[976,128]{1,0:T(8,128)(2,1)S(1)}, bf16[976,128]{1,0:T(8,128)(2,1)S(1)}, u32[]{:S(2)}, u32[]{:S(2)}) collective-permute-start(bf16[976,128]{1,0:T(8,128)(2,1)S(1)} %get-tuple-element.20), channel_id=1, source_target_pairs={{0,6},{1,7},{2,4},{3,5},{4,2},{5,3},{6,0},{7,1},{8,14},{9,15},{10,... | collective-permute-start | bytes 749576 | tf_op jit(solution)/shard_map/exchange_heads/ppermute | solution.py:265
  7.3 0.6 %collective-permute-start.2 = (bf16[976,128]{1,0:T(8,128)(2,1)S(1)}, bf16[976,128]{1,0:T(8,128)(2,1)S(1)}, u32[]{:S(2)}, u32[]{:S(2)}) collective-permute-start(bf16[976,128]{1,0:T(8,128)(2,1)S(1)} %get-tuple-element.23), channel_id=1, source_target_pairs={{0,4},{1,5},{2,6},{3,7},{4,0},{5,1},{6,2},{7,3},{8,12},{9,13},{10,... | collective-permute-start | bytes 749576 | tf_op jit(solution)/shard_map/exchange_heads/ppermute | solution.py:265
  7.9 2.6 %collective-permute-start.12 = (bf16[128,1280]{1,0:T(8,128)(2,1)S(1)}, bf16[128,1280]{1,0:T(8,128)(2,1)S(1)}, u32[]{:S(2)}, u32[]{:S(2)}) collective-permute-start(bf16[128,1280]{1,0:T(8,128)(2,1)S(1)} %get-tuple-element.33.refs_0_), channel_id=1, source_target_pairs={{0,24},{1,25},{2,26},{3,27},{4,28},{5,29},{6,30},{7,31},{8,16},{9,... | collective-permute-start | bytes 983048 | tf_op jit(solution)/shard_map/gather_cotangent/ppermute | solution.py:265
  10.5 0.5 collective-permute-start.11
  11.0 3.2 %collective-permute-done.refs_0_ = bf16[976,128]{1,0:T(8,128)(2,1)S(1)} collective-permute-done((bf16[976,128]{1,0:T(8,128)(2,1)S(1)}, bf16[976,128]{1,0:T(8,128)(2,1)S(1)}, u32[]{:S(2)}, u32[]{:S(2)}) %collective-permute-start) | collective-permute-done | bytes 249888 | tf_op jit(solution)/shard_map/exchange_heads/ppermute | solution.py:265
  14.2 1.7 %collective-permute-start.10 = (bf16[128,1280]{1,0:T(8,128)(2,1)S(1)}, bf16[128,1280]{1,0:T(8,128)(2,1)S(1)}, u32[]{:S(2)}, u32[]{:S(2)}) collective-permute-start(bf16[128,1280]{1,0:T(8,128)(2,1)S(1)} %get-tuple-element.33.refs_0_), channel_id=1, source_target_pairs={{0,8},{1,9},{2,10},{3,11},{4,12},{5,13},{6,14},{7,15},{8,0},{9,1},... | collective-permute-start | bytes 983048 | tf_op jit(solution)/shard_map/gather_cotangent/ppermute | solution.py:265
  15.9 3.9 %collective-permute-done.1.refs_2_.refs_1_ = bf16[976,128]{1,0:T(8,128)(2,1)S(1)} collective-permute-done((bf16[976,128]{1,0:T(8,128)(2,1)S(1)}, bf16[976,128]{1,0:T(8,128)(2,1)S(1)}, u32[]{:S(2)}, u32[]{:S(2)}) %collective-permute-start.1) | collective-permute-done | bytes 249888 | tf_op jit(solution)/shard_map/exchange_heads/ppermute | solution.py:265
  19.8 1.7 %attention.3 = (f32[320,384]{1,0:T(8,128)S(1)}, f32[8,384]{1,0:T(8,128)S(1)}, f32[8,384]{1,0:T(8,128)S(1)}) custom-call(bf16[976,128]{1,0:T(8,128)(2,1)S(1)} %collective-permute-done.refs_0_, bf16[976,128]{1,0:T(8,128)(2,1)S(1)} %get-tuple-element.21.refs_1_.refs_0_, bf16[976,128]{1,0:T(8,128)(2,1)S(1)} %collective-permute-done.1.refs_2_.refs_1_), custom_call_target="tpu_custom_call" | custom-call | flops 2595225600 | bytes 1310720 | tf_op jit(solution)/shard_map/attention/pallas_call | solution.py:39
  21.5 7.1 %collective-permute-done.2.refs_3_.refs_2_ = bf16[976,128]{1,0:T(8,128)(2,1)S(1)} collective-permute-done((bf16[976,128]{1,0:T(8,128)(2,1)S(1)}, bf16[976,128]{1,0:T(8,128)(2,1)S(1)}, u32[]{:S(2)}, u32[]{:S(2)}) %collective-permute-start.2) | collective-permute-done | bytes 249888 | tf_op jit(solution)/shard_map/exchange_heads/ppermute | solution.py:265
  28.5 1.5 %attention.4 = (bf16[320,128]{1,0:T(8,128)(2,1)S(1)}, bf16[320,128]{1,0:T(8,128)(2,1)S(1)}) custom-call(bf16[976,128]{1,0:T(8,128)(2,1)S(1)} %collective-permute-done.refs_0_, bf16[976,128]{1,0:T(8,128)(2,1)S(1)} %get-tuple-element.21.refs_1_.refs_0_, bf16[976,128]{1,0:T(8,128)(2,1)S(1)} %collective-permute-done.1.refs_2_.refs_1_, ...), custom_call_target="tpu_custom_call" | custom-call | flops 1441792000 | bytes 1310720 | tf_op jit(solution)/shard_map/attention/pallas_call | solution.py:39
  30.0 0.6 collective-permute-start.3
  30.6 3.9 %collective-permute-start.5 = (bf16[320,128]{1,0:T(8,128)(2,1)S(1)}, bf16[320,128]{1,0:T(8,128)(2,1)S(1)}, u32[]{:S(2)}, u32[]{:S(2)}) collective-permute-start(bf16[320,128]{1,0:T(8,128)(2,1)S(1)} %get-tuple-element.28), channel_id=1, source_target_pairs={{0,30},{1,31},{2,28},{3,29},{4,26},{5,27},{6,24},{7,25},{8,22},{9,... | collective-permute-start | bytes 245768 | tf_op jit(solution)/shard_map/send_to_owner/ppermute | solution.py:265
  34.5 1.0 %attention.5 = (bf16[320,128]{1,0:T(8,128)(2,1)S(1)}, bf16[320,128]{1,0:T(8,128)(2,1)S(1)}) custom-call(bf16[976,128]{1,0:T(8,128)(2,1)S(1)} %get-tuple-element.21.refs_1_.refs_0_, bf16[976,128]{1,0:T(8,128)(2,1)S(1)} %collective-permute-done.1.refs_2_.refs_1_, bf16[976,128]{1,0:T(8,128)(2,1)S(1)} %collective-permute-done.2.refs_3_.refs_2_, ...), custom_call_target="tpu_custom_call" | custom-call | flops 576716800 | bytes 1310720 | tf_op jit(solution)/shard_map/attention/pallas_call | solution.py:39
  35.6 0.0 collective-permute-done.12.refs_3_
  35.6 0.9 %collective-permute-start.7 = (bf16[320,128]{1,0:T(8,128)(2,1)S(1)}, bf16[320,128]{1,0:T(8,128)(2,1)S(1)}, u32[]{:S(2)}, u32[]{:S(2)}) collective-permute-start(bf16[320,128]{1,0:T(8,128)(2,1)S(1)} %get-tuple-element.29), channel_id=1, source_target_pairs={{0,10},{1,11},{2,8},{3,9},{4,14},{5,15},{6,12},{7,13},{8,2},{9,3},... | collective-permute-start | bytes 245768 | tf_op jit(solution)/shard_map/send_to_owner/ppermute | solution.py:265
  36.5 0.4 swap_cotangent.1.refs_2_
  37.0 0.1 collective-permute-start.13
  37.0 2.4 %collective-permute-done.3.refs_0_ = bf16[320,128]{1,0:T(8,128)(2,1)S(1)} collective-permute-done((bf16[320,128]{1,0:T(8,128)(2,1)S(1)}, bf16[320,128]{1,0:T(8,128)(2,1)S(1)}, u32[]{:S(2)}, u32[]{:S(2)}) %collective-permute-start.3) | collective-permute-done | bytes 81952 | tf_op jit(solution)/shard_map/send_to_owner/ppermute | solution.py:265
  39.4 1.6 %collective-permute-done.7.refs_2_ = bf16[320,128]{1,0:T(8,128)(2,1)S(1)} collective-permute-done((bf16[320,128]{1,0:T(8,128)(2,1)S(1)}, bf16[320,128]{1,0:T(8,128)(2,1)S(1)}, u32[]{:S(2)}, u32[]{:S(2)}) %collective-permute-start.7) | collective-permute-done | bytes 81952 | tf_op jit(solution)/shard_map/send_to_owner/ppermute | solution.py:265
  41.0 0.1 collective-permute-start.9
  41.1 1.0 %collective-permute-start.4 = (bf16[320,128]{1,0:T(8,128)(2,1)S(1)}, bf16[320,128]{1,0:T(8,128)(2,1)S(1)}, u32[]{:S(2)}, u32[]{:S(2)}) collective-permute-start(bf16[320,128]{1,0:T(8,128)(2,1)S(1)} %collective-permute-done.3.refs_0_), channel_id=1, source_target_pairs={{0,16},{1,17},{2,18},{3,19},{4,20},{5,21},{6,22},{7,23},{8,24},{9,... | collective-permute-start | bytes 245768 | tf_op jit(solution)/shard_map/send_home/ppermute | solution.py:265
  42.1 1.1 %collective-permute-start.6 = (bf16[320,128]{1,0:T(8,128)(2,1)S(1)}, bf16[320,128]{1,0:T(8,128)(2,1)S(1)}, u32[]{:S(2)}, u32[]{:S(2)}) collective-permute-start(bf16[320,128]{1,0:T(8,128)(2,1)S(1)} %collective-permute-done.5.refs_1_), channel_id=1, source_target_pairs={{0,24},{1,25},{2,26},{3,27},{4,28},{5,29},{6,30},{7,31},{8,16},{9,... | collective-permute-start | bytes 245768 | tf_op jit(solution)/shard_map/send_home/ppermute | solution.py:265
  43.2 1.5 %collective-permute-start.8 = (bf16[320,128]{1,0:T(8,128)(2,1)S(1)}, bf16[320,128]{1,0:T(8,128)(2,1)S(1)}, u32[]{:S(2)}, u32[]{:S(2)}) collective-permute-start(bf16[320,128]{1,0:T(8,128)(2,1)S(1)} %collective-permute-done.7.refs_2_), channel_id=1, source_target_pairs={{0,8},{1,9},{2,10},{3,11},{4,12},{5,13},{6,14},{7,15},{8,0},{9,1},... | collective-permute-start | bytes 245768 | tf_op jit(solution)/shard_map/send_home/ppermute | solution.py:265
  44.7 0.9 %gradient.1 = (bf16[80,640]{1,0:T(8,128)(2,1)S(1)}, bf16[80,640]{1,0:T(8,128)(2,1)S(1)}, bf16[80,640]{1,0:T(8,128)(2,1)S(1)}, bf16[80,640]{1,0:T(8,128)(2,1)S(1)}) custom-call(bf16[4,160,128]{2,1,0:T(8,128)(2,1)S(1)} %get-tuple-element.31.refs_0_, bf16[4,160,128]{2,1,0:T(8,128)(2,1)S(1)} %collective-permute-done.9.refs_1_, ...), custom_call_target="tpu_custom_call" | custom-call | flops 419430400 | bytes 2621440 | tf_op jit(solution)/shard_map/gradient/pallas_call | solution.py:39
  45.6 2.1 %collective-permute-start.14 = (bf16[80,640]{1,0:T(8,128)(2,1)S(1)}, bf16[80,640]{1,0:T(8,128)(2,1)S(1)}, u32[]{:S(2)}, u32[]{:S(2)}) collective-permute-start(bf16[80,640]{1,0:T(8,128)(2,1)S(1)} %get-tuple-element.35), channel_id=1, source_target_pairs={{0,4},{1,5},{2,14},{3,15},{4,16},{5,17},{6,26},{7,27},{8,12},{9,13... | collective-permute-start | bytes 307208 | tf_op jit(solution)/shard_map/sum_gradient/ppermute | solution.py:265
  47.7 2.2 %collective-permute-start.15 = (bf16[80,640]{1,0:T(8,128)(2,1)S(1)}, bf16[80,640]{1,0:T(8,128)(2,1)S(1)}, u32[]{:S(2)}, u32[]{:S(2)}) collective-permute-start(bf16[80,640]{1,0:T(8,128)(2,1)S(1)} %get-tuple-element.36), channel_id=1, source_target_pairs={{0,6},{1,7},{2,12},{3,13},{4,18},{5,19},{6,24},{7,25},{8,14},{9,15... | collective-permute-start | bytes 307208 | tf_op jit(solution)/shard_map/sum_gradient/ppermute | solution.py:265
  49.9 0.7 %collective-permute-start.16 = (bf16[80,640]{1,0:T(8,128)(2,1)S(1)}, bf16[80,640]{1,0:T(8,128)(2,1)S(1)}, u32[]{:S(2)}, u32[]{:S(2)}) collective-permute-start(bf16[80,640]{1,0:T(8,128)(2,1)S(1)} %get-tuple-element.34.kept), channel_id=1, source_target_pairs={{2,10},{3,11},{4,20},{5,21},{6,30},{7,31},{10,2},{11,3},{12,28},{1... | collective-permute-start | bytes 307208 | tf_op jit(solution)/shard_map/sum_gradient/ppermute | solution.py:265
  50.6 1.4 %project.1 = bf16[128,1280]{1,0:T(8,128)(2,1)} custom-call(bf16[320,128]{1,0:T(8,128)(2,1)S(1)} %collective-permute-done.4.refs_0_, bf16[320,128]{1,0:T(8,128)(2,1)S(1)} %collective-permute-done.6.refs_1_, bf16[320,128]{1,0:T(8,128)(2,1)S(1)} %collective-permute-done.8.refs_2_, bf16[320,128]{1,0:T(8,128)(2,1)S(1)} %get-tuple-element.30.refs_3_, ...), custom_call_target="tpu_custom_call" | custom-call | flops 419430400 | bytes 3276800 | tf_op jit(solution)/shard_map/project/pallas_call | solution.py:39
  52.0 5.1 %collective-permute-done.14.refs_0_ = bf16[80,640]{1,0:T(8,128)(2,1)S(1)} collective-permute-done((bf16[80,640]{1,0:T(8,128)(2,1)S(1)}, bf16[80,640]{1,0:T(8,128)(2,1)S(1)}, u32[]{:S(2)}, u32[]{:S(2)}) %collective-permute-start.14) | collective-permute-done | bytes 102432 | tf_op jit(solution)/shard_map/sum_gradient/ppermute | solution.py:265
  57.1 0.4 collective-permute-done.17.refs_3_
  57.5 0.8 %add_gradient.1 = f32[160,320]{1,0:T(8,128)} custom-call(bf16[80,640]{1,0:T(8,128)(2,1)S(1)} %get-tuple-element.34.kept, bf16[80,640]{1,0:T(8,128)(2,1)S(1)} %collective-permute-done.14.refs_0_, bf16[80,640]{1,0:T(8,128)(2,1)S(1)} %collective-permute-done.15.refs_1_, bf16[80,640]{1,0:T(8,128)(2,1)S(1)} %collective-permute-done.16.refs_2_, ...), custom_call_target="tpu_custom_call" | custom-call | bytes 819200 | tf_op jit(solution)/shard_map/add_gradient/pallas_call | solution.py:39
  (17 shorter events, 0.1 us)
Async XLA Ops:
  2.2 12.1 %collective-permute-start = (bf16[976,128]{1,0:T(8,128)(2,1)S(1)}, bf16[976,128]{1,0:T(8,128)(2,1)S(1)}, u32[]{:S(2)}, u32[]{:S(2)}) collective-permute-start(bf16[976,128]{1,0:T(8,128)(2,1)S(1)} %get-tuple-element.20), channel_id=1, source_target_pairs={{0,6},{1,7},{2,4},{3,5},{4,2},{5,3},{6,0},{7,1},{8,14},{9,15},{10,... | collective-permute-start | bytes 749576 | tf_op jit(solution)/shard_map/exchange_heads/ppermute | solution.py:265
  7.3 12.5 %collective-permute-start.1 = (bf16[976,128]{1,0:T(8,128)(2,1)S(1)}, bf16[976,128]{1,0:T(8,128)(2,1)S(1)}, u32[]{:S(2)}, u32[]{:S(2)}) collective-permute-start(bf16[976,128]{1,0:T(8,128)(2,1)S(1)} %get-tuple-element.22), channel_id=1, source_target_pairs={{0,2},{1,3},{2,0},{3,1},{4,6},{5,7},{6,4},{7,5},{8,10},{9,11},{10,... | collective-permute-start | bytes 749576 | tf_op jit(solution)/shard_map/exchange_heads/ppermute | solution.py:265
  7.3 21.3 %collective-permute-start.2 = (bf16[976,128]{1,0:T(8,128)(2,1)S(1)}, bf16[976,128]{1,0:T(8,128)(2,1)S(1)}, u32[]{:S(2)}, u32[]{:S(2)}) collective-permute-start(bf16[976,128]{1,0:T(8,128)(2,1)S(1)} %get-tuple-element.23), channel_id=1, source_target_pairs={{0,4},{1,5},{2,6},{3,7},{4,0},{5,1},{6,2},{7,3},{8,12},{9,13},{10,... | collective-permute-start | bytes 749576 | tf_op jit(solution)/shard_map/exchange_heads/ppermute | solution.py:265
  7.9 27.7 %collective-permute-start.12 = (bf16[128,1280]{1,0:T(8,128)(2,1)S(1)}, bf16[128,1280]{1,0:T(8,128)(2,1)S(1)}, u32[]{:S(2)}, u32[]{:S(2)}) collective-permute-start(bf16[128,1280]{1,0:T(8,128)(2,1)S(1)} %get-tuple-element.33.refs_0_), channel_id=1, source_target_pairs={{0,24},{1,25},{2,26},{3,27},{4,28},{5,29},{6,30},{7,31},{8,16},{9,... | collective-permute-start | bytes 983048 | tf_op jit(solution)/shard_map/gather_cotangent/ppermute | solution.py:265
  10.5 26.0 %collective-permute-start.11 = (bf16[128,1280]{1,0:T(8,128)(2,1)S(1)}, bf16[128,1280]{1,0:T(8,128)(2,1)S(1)}, u32[]{:S(2)}, u32[]{:S(2)}) collective-permute-start(bf16[128,1280]{1,0:T(8,128)(2,1)S(1)} %get-tuple-element.33.refs_0_), channel_id=1, source_target_pairs={{0,16},{1,17},{2,18},{3,19},{4,20},{5,21},{6,22},{7,23},{8,24},{9,... | collective-permute-start | bytes 983048 | tf_op jit(solution)/shard_map/gather_cotangent/ppermute | solution.py:265
  14.2 22.3 %collective-permute-start.10 = (bf16[128,1280]{1,0:T(8,128)(2,1)S(1)}, bf16[128,1280]{1,0:T(8,128)(2,1)S(1)}, u32[]{:S(2)}, u32[]{:S(2)}) collective-permute-start(bf16[128,1280]{1,0:T(8,128)(2,1)S(1)} %get-tuple-element.33.refs_0_), channel_id=1, source_target_pairs={{0,8},{1,9},{2,10},{3,11},{4,12},{5,13},{6,14},{7,15},{8,0},{9,1},... | collective-permute-start | bytes 983048 | tf_op jit(solution)/shard_map/gather_cotangent/ppermute | solution.py:265
  30.0 9.4 %collective-permute-start.3 = (bf16[320,128]{1,0:T(8,128)(2,1)S(1)}, bf16[320,128]{1,0:T(8,128)(2,1)S(1)}, u32[]{:S(2)}, u32[]{:S(2)}) collective-permute-start(bf16[320,128]{1,0:T(8,128)(2,1)S(1)} %get-tuple-element.27), channel_id=1, source_target_pairs={{0,20},{1,21},{2,22},{3,23},{4,16},{5,17},{6,18},{7,19},{8,28},{9,... | collective-permute-start | bytes 245768 | tf_op jit(solution)/shard_map/send_to_owner/ppermute | solution.py:265
  30.6 8.8 %collective-permute-start.5 = (bf16[320,128]{1,0:T(8,128)(2,1)S(1)}, bf16[320,128]{1,0:T(8,128)(2,1)S(1)}, u32[]{:S(2)}, u32[]{:S(2)}) collective-permute-start(bf16[320,128]{1,0:T(8,128)(2,1)S(1)} %get-tuple-element.28), channel_id=1, source_target_pairs={{0,30},{1,31},{2,28},{3,29},{4,26},{5,27},{6,24},{7,25},{8,22},{9,... | collective-permute-start | bytes 245768 | tf_op jit(solution)/shard_map/send_to_owner/ppermute | solution.py:265
  35.6 5.4 %collective-permute-start.7 = (bf16[320,128]{1,0:T(8,128)(2,1)S(1)}, bf16[320,128]{1,0:T(8,128)(2,1)S(1)}, u32[]{:S(2)}, u32[]{:S(2)}) collective-permute-start(bf16[320,128]{1,0:T(8,128)(2,1)S(1)} %get-tuple-element.29), channel_id=1, source_target_pairs={{0,10},{1,11},{2,8},{3,9},{4,14},{5,15},{6,12},{7,13},{8,2},{9,3},... | collective-permute-start | bytes 245768 | tf_op jit(solution)/shard_map/send_to_owner/ppermute | solution.py:265
  37.0 7.7 %collective-permute-start.13 = (bf16[4,128,1280]{2,1,0:T(8,128)(2,1)S(1)}, bf16[4,128,1280]{2,1,0:T(8,128)(2,1)S(1)}, u32[]{:S(2)}, u32[]{:S(2)}) collective-permute-start(bf16[4,128,1280]{2,1,0:T(8,128)(2,1)S(1)} %swap_cotangent.1.refs_2_), channel_id=1, source_target_pairs={{0,1},{1,0},{2,3},{3,2},{4,5},{5,4},{6,7},{7,6},{8,9},{9,8},{10,11... | collective-permute-start | bytes 3932168 | tf_op jit(solution)/shard_map/gradient/ppermute | solution.py:265
  41.0 9.6 %copy-start = (bf16[1280,1280]{1,0:T(8,128)(2,1)S(1)}, bf16[1280,1280]{1,0:T(8,128)(2,1)}, u32[]{:S(2)}) copy-start(bf16[1280,1280]{1,0:T(8,128)(2,1)} %refs_5_.1) | copy-start | bytes 9830404
  41.0 3.6 %collective-permute-start.9 = (bf16[4,160,128]{2,1,0:T(8,128)(2,1)S(1)}, bf16[4,160,128]{2,1,0:T(8,128)(2,1)S(1)}, u32[]{:S(2)}, u32[]{:S(2)}) collective-permute-start(bf16[4,160,128]{2,1,0:T(8,128)(2,1)S(1)} %get-tuple-element.32), channel_id=1, source_target_pairs={{0,1},{1,0},{2,3},{3,2},{4,5},{5,4},{6,7},{7,6},{8,9},{9,8},{10,11... | collective-permute-start | bytes 491528 | tf_op jit(solution)/shard_map/send_to_owner/ppermute | solution.py:265
  41.1 8.8 %collective-permute-start.4 = (bf16[320,128]{1,0:T(8,128)(2,1)S(1)}, bf16[320,128]{1,0:T(8,128)(2,1)S(1)}, u32[]{:S(2)}, u32[]{:S(2)}) collective-permute-start(bf16[320,128]{1,0:T(8,128)(2,1)S(1)} %collective-permute-done.3.refs_0_), channel_id=1, source_target_pairs={{0,16},{1,17},{2,18},{3,19},{4,20},{5,21},{6,22},{7,23},{8,24},{9,... | collective-permute-start | bytes 245768 | tf_op jit(solution)/shard_map/send_home/ppermute | solution.py:265
  42.1 7.8 %collective-permute-start.6 = (bf16[320,128]{1,0:T(8,128)(2,1)S(1)}, bf16[320,128]{1,0:T(8,128)(2,1)S(1)}, u32[]{:S(2)}, u32[]{:S(2)}) collective-permute-start(bf16[320,128]{1,0:T(8,128)(2,1)S(1)} %collective-permute-done.5.refs_1_), channel_id=1, source_target_pairs={{0,24},{1,25},{2,26},{3,27},{4,28},{5,29},{6,30},{7,31},{8,16},{9,... | collective-permute-start | bytes 245768 | tf_op jit(solution)/shard_map/send_home/ppermute | solution.py:265
  43.2 7.4 %collective-permute-start.8 = (bf16[320,128]{1,0:T(8,128)(2,1)S(1)}, bf16[320,128]{1,0:T(8,128)(2,1)S(1)}, u32[]{:S(2)}, u32[]{:S(2)}) collective-permute-start(bf16[320,128]{1,0:T(8,128)(2,1)S(1)} %collective-permute-done.7.refs_2_), channel_id=1, source_target_pairs={{0,8},{1,9},{2,10},{3,11},{4,12},{5,13},{6,14},{7,15},{8,0},{9,1},... | collective-permute-start | bytes 245768 | tf_op jit(solution)/shard_map/send_home/ppermute | solution.py:265
  44.7 6.0 %copy-start.1 = (bf16[128,1280]{1,0:T(8,128)(2,1)S(1)}, bf16[128,1280]{1,0:T(8,128)(2,1)}, u32[]{:S(2)}) copy-start(bf16[128,1280]{1,0:T(8,128)(2,1)} %refs_4_.3) | copy-start | bytes 983044
  45.6 11.5 %collective-permute-start.14 = (bf16[80,640]{1,0:T(8,128)(2,1)S(1)}, bf16[80,640]{1,0:T(8,128)(2,1)S(1)}, u32[]{:S(2)}, u32[]{:S(2)}) collective-permute-start(bf16[80,640]{1,0:T(8,128)(2,1)S(1)} %get-tuple-element.35), channel_id=1, source_target_pairs={{0,4},{1,5},{2,14},{3,15},{4,16},{5,17},{6,26},{7,27},{8,12},{9,13... | collective-permute-start | bytes 307208 | tf_op jit(solution)/shard_map/sum_gradient/ppermute | solution.py:265
  47.7 9.4 %collective-permute-start.15 = (bf16[80,640]{1,0:T(8,128)(2,1)S(1)}, bf16[80,640]{1,0:T(8,128)(2,1)S(1)}, u32[]{:S(2)}, u32[]{:S(2)}) collective-permute-start(bf16[80,640]{1,0:T(8,128)(2,1)S(1)} %get-tuple-element.36), channel_id=1, source_target_pairs={{0,6},{1,7},{2,12},{3,13},{4,18},{5,19},{6,24},{7,25},{8,14},{9,15... | collective-permute-start | bytes 307208 | tf_op jit(solution)/shard_map/sum_gradient/ppermute | solution.py:265
  49.9 7.6 %collective-permute-start.17 = (bf16[80,640]{1,0:T(8,128)(2,1)S(1)}, bf16[80,640]{1,0:T(8,128)(2,1)S(1)}, u32[]{:S(2)}, u32[]{:S(2)}) collective-permute-start(bf16[80,640]{1,0:T(8,128)(2,1)S(1)} %get-tuple-element.37), channel_id=1, source_target_pairs={{0,2},{1,3},{2,8},{3,9},{4,22},{5,23},{6,28},{7,29},{8,10},{9,11},... | collective-permute-start | bytes 307208 | tf_op jit(solution)/shard_map/sum_gradient/ppermute | solution.py:265
  49.9 7.6 %collective-permute-start.16 = (bf16[80,640]{1,0:T(8,128)(2,1)S(1)}, bf16[80,640]{1,0:T(8,128)(2,1)S(1)}, u32[]{:S(2)}, u32[]{:S(2)}) collective-permute-start(bf16[80,640]{1,0:T(8,128)(2,1)S(1)} %get-tuple-element.34.kept), channel_id=1, source_target_pairs={{2,10},{3,11},{4,20},{5,21},{6,30},{7,31},{10,2},{11,3},{12,28},{1... | collective-permute-start | bytes 307208 | tf_op jit(solution)/shard_map/sum_gradient/ppermute | solution.py:265

commit v12 on v6

--- a/solution.py
+++ b/solution.py
@@ -12,6 +12,7 @@
 AXES = ("dp", "enc", "seq")
 ID_ROWS = 16
 ID_BASE = 64
+VMEM_LIMIT = 16 * 1024 * 1024
 SENDS = (3, 0, 1, 2)
 RETURNS = (2, 3, 1, 0)
 SUMS = (2, 3, 1, 0)
@@ -23,7 +24,6 @@
     *args,
     spaces=None,
     scratch=(),
-    limit=16,
     flops=0,
     bytes_accessed=0,
 ):
@@ -42,7 +42,7 @@
         in_specs=[placed(space) for space in spaces],
         out_specs=[placed(pltpu.VMEM)] * len(out_shape) if many else placed(pltpu.VMEM),
         scratch_shapes=list(scratch),
-        compiler_params=pltpu.CompilerParams(vmem_limit_bytes=limit * 1024 * 1024),
+        compiler_params=pltpu.CompilerParams(vmem_limit_bytes=VMEM_LIMIT),
         cost_estimate=pl.CostEstimate(
             flops=flops, bytes_accessed=bytes_accessed, transcendentals=0
         ),
@@ -170,8 +170,8 @@
     attend_more(early, late, state, bias, outs, late.shape[1], head_width)
 
 
-def stack_kernel(count, *refs):
-    sources, out, sems = refs[:count], refs[-2], refs[-1]
+def stack_kernel(*refs):
+    sources, (out, sems) = refs[:-2], refs[-2:]
     copies = [
         pltpu.make_async_copy(source, out.at[index], sems.at[index])
         for index, source in enumerate(sources)
@@ -340,10 +340,9 @@
         given = along_seq(given)
     with jax.named_scope("swap_cotangent"):
         stacked = call(
-            functools.partial(stack_kernel, n_dp),
+            stack_kernel,
             bf16((n_dp, rows, width)),
             *same,
-            spaces=[pltpu.VMEM] * n_dp + [pl.ANY] * 0,
             scratch=[pltpu.SemaphoreType.DMA((n_dp,))],
             bytes_accessed=4 * n_dp * rows * width,
         )

time: 58.4 us -> 58.4 us (level)
  no operation moved by 1% of the time
where the time goes in v12:
time: 58.4 us; the launch traced here: 58.3 us
  starting transfers between devices  24.7 us (42%)
  waiting for transfers between devices  23.6 us (40%)
  Pallas kernels  9.29 us (16%)
  between operations  0.76 us (1%)
    ppermute x18, starting transfers between devices, move(): return lax.ppermute(data, AXES, pairs)  24.7 us
    ppermute x18, waiting for transfers between devices, move(): return lax.ppermute(data, AXES, pairs)  23.6 us
    pallas_call x9, Pallas kernels, call(): pl.pallas_call(kernel, out_shape=out_shape, in_specs=[placed(space) for s...  9.29 us
  transfers between devices with their start and end apart: 18, of which 7 were waited for; matrix products, arithmetic and copies ran while one was open for 0% of the time, Pallas kernels for 12%

profile of v12, /device:TPU:0, one launch (start us, length us, event | category | flops | bytes accessed | tf_op | source)
XLA Modules:
  0.0 58.3 jit_solution(17079584653436483883)
XLA Ops:
  0.6 1.5 %pack.1 = (bf16[976,128]{1,0:T(8,128)(2,1)S(1)}, bf16[976,128]{1,0:T(8,128)(2,1)S(1)}, bf16[976,128]{1,0:T(8,128)(2,1)S(1)}, bf16[976,128]{1,0:T(8,128)(2,1)S(1)}, bf16[128,1280]{1,0:T(8,128)(2,1)S(1)}) custom-call(s32[1,128]{1,0:T(1,128)} %bitcast.1, bf16[128,1280]{1,0:T(8,128)(2,1)} %refs_1_.1, bf16[128,1280]{1,0:T(8,128)(2,1)} %refs_2_.1, ...), custom_call_target="tpu_custom_call" | custom-call | bytes 2621440 | tf_op jit(solution)/shard_map/pack/pallas_call | solution.py:39
  2.2 5.1 %collective-permute-start = (bf16[976,128]{1,0:T(8,128)(2,1)S(1)}, bf16[976,128]{1,0:T(8,128)(2,1)S(1)}, u32[]{:S(2)}, u32[]{:S(2)}) collective-permute-start(bf16[976,128]{1,0:T(8,128)(2,1)S(1)} %get-tuple-element.20), channel_id=1, source_target_pairs={{0,6},{1,7},{2,4},{3,5},{4,2},{5,3},{6,0},{7,1},{8,14},{9,15},{10,... | collective-permute-start | bytes 749576 | tf_op jit(solution)/shard_map/exchange_heads/ppermute | solution.py:262
  7.3 0.6 %collective-permute-start.2 = (bf16[976,128]{1,0:T(8,128)(2,1)S(1)}, bf16[976,128]{1,0:T(8,128)(2,1)S(1)}, u32[]{:S(2)}, u32[]{:S(2)}) collective-permute-start(bf16[976,128]{1,0:T(8,128)(2,1)S(1)} %get-tuple-element.23), channel_id=1, source_target_pairs={{0,4},{1,5},{2,6},{3,7},{4,0},{5,1},{6,2},{7,3},{8,12},{9,13},{10,... | collective-permute-start | bytes 749576 | tf_op jit(solution)/shard_map/exchange_heads/ppermute | solution.py:262
  7.9 2.6 %collective-permute-start.12 = (bf16[128,1280]{1,0:T(8,128)(2,1)S(1)}, bf16[128,1280]{1,0:T(8,128)(2,1)S(1)}, u32[]{:S(2)}, u32[]{:S(2)}) collective-permute-start(bf16[128,1280]{1,0:T(8,128)(2,1)S(1)} %get-tuple-element.33.refs_0_), channel_id=1, source_target_pairs={{0,24},{1,25},{2,26},{3,27},{4,28},{5,29},{6,30},{7,31},{8,16},{9,... | collective-permute-start | bytes 983048 | tf_op jit(solution)/shard_map/gather_cotangent/ppermute | solution.py:262
  10.5 0.5 collective-permute-start.11
  11.0 3.2 %collective-permute-done.refs_0_ = bf16[976,128]{1,0:T(8,128)(2,1)S(1)} collective-permute-done((bf16[976,128]{1,0:T(8,128)(2,1)S(1)}, bf16[976,128]{1,0:T(8,128)(2,1)S(1)}, u32[]{:S(2)}, u32[]{:S(2)}) %collective-permute-start) | collective-permute-done | bytes 249888 | tf_op jit(solution)/shard_map/exchange_heads/ppermute | solution.py:262
  14.2 1.7 %collective-permute-start.10 = (bf16[128,1280]{1,0:T(8,128)(2,1)S(1)}, bf16[128,1280]{1,0:T(8,128)(2,1)S(1)}, u32[]{:S(2)}, u32[]{:S(2)}) collective-permute-start(bf16[128,1280]{1,0:T(8,128)(2,1)S(1)} %get-tuple-element.33.refs_0_), channel_id=1, source_target_pairs={{0,8},{1,9},{2,10},{3,11},{4,12},{5,13},{6,14},{7,15},{8,0},{9,1},... | collective-permute-start | bytes 983048 | tf_op jit(solution)/shard_map/gather_cotangent/ppermute | solution.py:262
  15.9 3.9 %collective-permute-done.1.refs_2_.refs_1_ = bf16[976,128]{1,0:T(8,128)(2,1)S(1)} collective-permute-done((bf16[976,128]{1,0:T(8,128)(2,1)S(1)}, bf16[976,128]{1,0:T(8,128)(2,1)S(1)}, u32[]{:S(2)}, u32[]{:S(2)}) %collective-permute-start.1) | collective-permute-done | bytes 249888 | tf_op jit(solution)/shard_map/exchange_heads/ppermute | solution.py:262
  19.8 1.7 %attention.3 = (f32[320,384]{1,0:T(8,128)S(1)}, f32[8,384]{1,0:T(8,128)S(1)}, f32[8,384]{1,0:T(8,128)S(1)}) custom-call(bf16[976,128]{1,0:T(8,128)(2,1)S(1)} %collective-permute-done.refs_0_, bf16[976,128]{1,0:T(8,128)(2,1)S(1)} %get-tuple-element.21.refs_1_.refs_0_, bf16[976,128]{1,0:T(8,128)(2,1)S(1)} %collective-permute-done.1.refs_2_.refs_1_), custom_call_target="tpu_custom_call" | custom-call | flops 2595225600 | bytes 1310720 | tf_op jit(solution)/shard_map/attention/pallas_call | solution.py:39
  21.5 7.1 %collective-permute-done.2.refs_3_.refs_2_ = bf16[976,128]{1,0:T(8,128)(2,1)S(1)} collective-permute-done((bf16[976,128]{1,0:T(8,128)(2,1)S(1)}, bf16[976,128]{1,0:T(8,128)(2,1)S(1)}, u32[]{:S(2)}, u32[]{:S(2)}) %collective-permute-start.2) | collective-permute-done | bytes 249888 | tf_op jit(solution)/shard_map/exchange_heads/ppermute | solution.py:262
  28.5 1.5 %attention.4 = (bf16[320,128]{1,0:T(8,128)(2,1)S(1)}, bf16[320,128]{1,0:T(8,128)(2,1)S(1)}) custom-call(bf16[976,128]{1,0:T(8,128)(2,1)S(1)} %collective-permute-done.refs_0_, bf16[976,128]{1,0:T(8,128)(2,1)S(1)} %get-tuple-element.21.refs_1_.refs_0_, bf16[976,128]{1,0:T(8,128)(2,1)S(1)} %collective-permute-done.1.refs_2_.refs_1_, ...), custom_call_target="tpu_custom_call" | custom-call | flops 1441792000 | bytes 1310720 | tf_op jit(solution)/shard_map/attention/pallas_call | solution.py:39
  30.0 0.6 collective-permute-start.3
  30.6 3.9 %collective-permute-start.5 = (bf16[320,128]{1,0:T(8,128)(2,1)S(1)}, bf16[320,128]{1,0:T(8,128)(2,1)S(1)}, u32[]{:S(2)}, u32[]{:S(2)}) collective-permute-start(bf16[320,128]{1,0:T(8,128)(2,1)S(1)} %get-tuple-element.28), channel_id=1, source_target_pairs={{0,30},{1,31},{2,28},{3,29},{4,26},{5,27},{6,24},{7,25},{8,22},{9,... | collective-permute-start | bytes 245768 | tf_op jit(solution)/shard_map/send_to_owner/ppermute | solution.py:262
  34.5 1.0 %attention.5 = (bf16[320,128]{1,0:T(8,128)(2,1)S(1)}, bf16[320,128]{1,0:T(8,128)(2,1)S(1)}) custom-call(bf16[976,128]{1,0:T(8,128)(2,1)S(1)} %get-tuple-element.21.refs_1_.refs_0_, bf16[976,128]{1,0:T(8,128)(2,1)S(1)} %collective-permute-done.1.refs_2_.refs_1_, bf16[976,128]{1,0:T(8,128)(2,1)S(1)} %collective-permute-done.2.refs_3_.refs_2_, ...), custom_call_target="tpu_custom_call" | custom-call | flops 576716800 | bytes 1310720 | tf_op jit(solution)/shard_map/attention/pallas_call | solution.py:39
  35.6 0.0 collective-permute-done.12.refs_3_
  35.6 0.9 %collective-permute-start.7 = (bf16[320,128]{1,0:T(8,128)(2,1)S(1)}, bf16[320,128]{1,0:T(8,128)(2,1)S(1)}, u32[]{:S(2)}, u32[]{:S(2)}) collective-permute-start(bf16[320,128]{1,0:T(8,128)(2,1)S(1)} %get-tuple-element.29), channel_id=1, source_target_pairs={{0,10},{1,11},{2,8},{3,9},{4,14},{5,15},{6,12},{7,13},{8,2},{9,3},... | collective-permute-start | bytes 245768 | tf_op jit(solution)/shard_map/send_to_owner/ppermute | solution.py:262
  36.5 0.4 swap_cotangent.1.refs_2_
  37.0 0.1 collective-permute-start.13
  37.0 2.4 %collective-permute-done.3.refs_0_ = bf16[320,128]{1,0:T(8,128)(2,1)S(1)} collective-permute-done((bf16[320,128]{1,0:T(8,128)(2,1)S(1)}, bf16[320,128]{1,0:T(8,128)(2,1)S(1)}, u32[]{:S(2)}, u32[]{:S(2)}) %collective-permute-start.3) | collective-permute-done | bytes 81952 | tf_op jit(solution)/shard_map/send_to_owner/ppermute | solution.py:262
  39.4 1.6 %collective-permute-done.7.refs_2_ = bf16[320,128]{1,0:T(8,128)(2,1)S(1)} collective-permute-done((bf16[320,128]{1,0:T(8,128)(2,1)S(1)}, bf16[320,128]{1,0:T(8,128)(2,1)S(1)}, u32[]{:S(2)}, u32[]{:S(2)}) %collective-permute-start.7) | collective-permute-done | bytes 81952 | tf_op jit(solution)/shard_map/send_to_owner/ppermute | solution.py:262
  41.0 0.1 collective-permute-start.9
  41.1 1.0 %collective-permute-start.4 = (bf16[320,128]{1,0:T(8,128)(2,1)S(1)}, bf16[320,128]{1,0:T(8,128)(2,1)S(1)}, u32[]{:S(2)}, u32[]{:S(2)}) collective-permute-start(bf16[320,128]{1,0:T(8,128)(2,1)S(1)} %collective-permute-done.3.refs_0_), channel_id=1, source_target_pairs={{0,16},{1,17},{2,18},{3,19},{4,20},{5,21},{6,22},{7,23},{8,24},{9,... | collective-permute-start | bytes 245768 | tf_op jit(solution)/shard_map/send_home/ppermute | solution.py:262
  42.1 1.1 %collective-permute-start.6 = (bf16[320,128]{1,0:T(8,128)(2,1)S(1)}, bf16[320,128]{1,0:T(8,128)(2,1)S(1)}, u32[]{:S(2)}, u32[]{:S(2)}) collective-permute-start(bf16[320,128]{1,0:T(8,128)(2,1)S(1)} %collective-permute-done.5.refs_1_), channel_id=1, source_target_pairs={{0,24},{1,25},{2,26},{3,27},{4,28},{5,29},{6,30},{7,31},{8,16},{9,... | collective-permute-start | bytes 245768 | tf_op jit(solution)/shard_map/send_home/ppermute | solution.py:262
  43.2 1.5 %collective-permute-start.8 = (bf16[320,128]{1,0:T(8,128)(2,1)S(1)}, bf16[320,128]{1,0:T(8,128)(2,1)S(1)}, u32[]{:S(2)}, u32[]{:S(2)}) collective-permute-start(bf16[320,128]{1,0:T(8,128)(2,1)S(1)} %collective-permute-done.7.refs_2_), channel_id=1, source_target_pairs={{0,8},{1,9},{2,10},{3,11},{4,12},{5,13},{6,14},{7,15},{8,0},{9,1},... | collective-permute-start | bytes 245768 | tf_op jit(solution)/shard_map/send_home/ppermute | solution.py:262
  44.7 0.9 %gradient.1 = (bf16[80,640]{1,0:T(8,128)(2,1)S(1)}, bf16[80,640]{1,0:T(8,128)(2,1)S(1)}, bf16[80,640]{1,0:T(8,128)(2,1)S(1)}, bf16[80,640]{1,0:T(8,128)(2,1)S(1)}) custom-call(bf16[4,160,128]{2,1,0:T(8,128)(2,1)S(1)} %get-tuple-element.31.refs_0_, bf16[4,160,128]{2,1,0:T(8,128)(2,1)S(1)} %collective-permute-done.9.refs_1_, ...), custom_call_target="tpu_custom_call" | custom-call | flops 419430400 | bytes 2621440 | tf_op jit(solution)/shard_map/gradient/pallas_call | solution.py:39
  45.6 2.1 %collective-permute-start.14 = (bf16[80,640]{1,0:T(8,128)(2,1)S(1)}, bf16[80,640]{1,0:T(8,128)(2,1)S(1)}, u32[]{:S(2)}, u32[]{:S(2)}) collective-permute-start(bf16[80,640]{1,0:T(8,128)(2,1)S(1)} %get-tuple-element.34), channel_id=1, source_target_pairs={{0,4},{1,5},{2,14},{3,15},{4,16},{5,17},{6,26},{7,27},{8,12},{9,13... | collective-permute-start | bytes 307208 | tf_op jit(solution)/shard_map/sum_gradient/ppermute | solution.py:262
  47.7 2.2 %collective-permute-start.15 = (bf16[80,640]{1,0:T(8,128)(2,1)S(1)}, bf16[80,640]{1,0:T(8,128)(2,1)S(1)}, u32[]{:S(2)}, u32[]{:S(2)}) collective-permute-start(bf16[80,640]{1,0:T(8,128)(2,1)S(1)} %get-tuple-element.35), channel_id=1, source_target_pairs={{0,6},{1,7},{2,12},{3,13},{4,18},{5,19},{6,24},{7,25},{8,14},{9,15... | collective-permute-start | bytes 307208 | tf_op jit(solution)/shard_map/sum_gradient/ppermute | solution.py:262
  49.9 0.7 %collective-permute-start.17 = (bf16[80,640]{1,0:T(8,128)(2,1)S(1)}, bf16[80,640]{1,0:T(8,128)(2,1)S(1)}, u32[]{:S(2)}, u32[]{:S(2)}) collective-permute-start(bf16[80,640]{1,0:T(8,128)(2,1)S(1)} %get-tuple-element.37), channel_id=1, source_target_pairs={{0,0},{1,1},{2,10},{3,11},{4,20},{5,21},{6,30},{7,31},{8,8},{9,9},... | collective-permute-start | bytes 307208 | tf_op jit(solution)/shard_map/sum_gradient/ppermute | solution.py:262
  50.6 1.4 %project.1 = bf16[128,1280]{1,0:T(8,128)(2,1)} custom-call(bf16[320,128]{1,0:T(8,128)(2,1)S(1)} %collective-permute-done.4.refs_0_, bf16[320,128]{1,0:T(8,128)(2,1)S(1)} %collective-permute-done.6.refs_1_, bf16[320,128]{1,0:T(8,128)(2,1)S(1)} %collective-permute-done.8.refs_2_, bf16[320,128]{1,0:T(8,128)(2,1)S(1)} %get-tuple-element.30.refs_3_, ...), custom_call_target="tpu_custom_call" | custom-call | flops 419430400 | bytes 3276800 | tf_op jit(solution)/shard_map/project/pallas_call | solution.py:39
  52.0 5.1 %collective-permute-done.14.refs_0_ = bf16[80,640]{1,0:T(8,128)(2,1)S(1)} collective-permute-done((bf16[80,640]{1,0:T(8,128)(2,1)S(1)}, bf16[80,640]{1,0:T(8,128)(2,1)S(1)}, u32[]{:S(2)}, u32[]{:S(2)}) %collective-permute-start.14) | collective-permute-done | bytes 102432 | tf_op jit(solution)/shard_map/sum_gradient/ppermute | solution.py:262
  57.1 0.4 collective-permute-done.16.refs_2_
  57.5 0.8 %add_gradient.1 = f32[160,320]{1,0:T(8,128)} custom-call(bf16[80,640]{1,0:T(8,128)(2,1)S(1)} %collective-permute-done.14.refs_0_, bf16[80,640]{1,0:T(8,128)(2,1)S(1)} %collective-permute-done.15.refs_1_, bf16[80,640]{1,0:T(8,128)(2,1)S(1)} %collective-permute-done.16.refs_2_, bf16[80,640]{1,0:T(8,128)(2,1)S(1)} %collective-permute-done.17.refs_3_), custom_call_target="tpu_custom_call" | custom-call | bytes 819200 | tf_op jit(solution)/shard_map/add_gradient/pallas_call | solution.py:39
  (17 shorter events, 0.1 us)
Async XLA Ops:
  2.2 12.1 %collective-permute-start = (bf16[976,128]{1,0:T(8,128)(2,1)S(1)}, bf16[976,128]{1,0:T(8,128)(2,1)S(1)}, u32[]{:S(2)}, u32[]{:S(2)}) collective-permute-start(bf16[976,128]{1,0:T(8,128)(2,1)S(1)} %get-tuple-element.20), channel_id=1, source_target_pairs={{0,6},{1,7},{2,4},{3,5},{4,2},{5,3},{6,0},{7,1},{8,14},{9,15},{10,... | collective-permute-start | bytes 749576 | tf_op jit(solution)/shard_map/exchange_heads/ppermute | solution.py:262
  7.3 12.5 %collective-permute-start.1 = (bf16[976,128]{1,0:T(8,128)(2,1)S(1)}, bf16[976,128]{1,0:T(8,128)(2,1)S(1)}, u32[]{:S(2)}, u32[]{:S(2)}) collective-permute-start(bf16[976,128]{1,0:T(8,128)(2,1)S(1)} %get-tuple-element.22), channel_id=1, source_target_pairs={{0,2},{1,3},{2,0},{3,1},{4,6},{5,7},{6,4},{7,5},{8,10},{9,11},{10,... | collective-permute-start | bytes 749576 | tf_op jit(solution)/shard_map/exchange_heads/ppermute | solution.py:262
  7.3 21.3 %collective-permute-start.2 = (bf16[976,128]{1,0:T(8,128)(2,1)S(1)}, bf16[976,128]{1,0:T(8,128)(2,1)S(1)}, u32[]{:S(2)}, u32[]{:S(2)}) collective-permute-start(bf16[976,128]{1,0:T(8,128)(2,1)S(1)} %get-tuple-element.23), channel_id=1, source_target_pairs={{0,4},{1,5},{2,6},{3,7},{4,0},{5,1},{6,2},{7,3},{8,12},{9,13},{10,... | collective-permute-start | bytes 749576 | tf_op jit(solution)/shard_map/exchange_heads/ppermute | solution.py:262
  7.9 27.7 %collective-permute-start.12 = (bf16[128,1280]{1,0:T(8,128)(2,1)S(1)}, bf16[128,1280]{1,0:T(8,128)(2,1)S(1)}, u32[]{:S(2)}, u32[]{:S(2)}) collective-permute-start(bf16[128,1280]{1,0:T(8,128)(2,1)S(1)} %get-tuple-element.33.refs_0_), channel_id=1, source_target_pairs={{0,24},{1,25},{2,26},{3,27},{4,28},{5,29},{6,30},{7,31},{8,16},{9,... | collective-permute-start | bytes 983048 | tf_op jit(solution)/shard_map/gather_cotangent/ppermute | solution.py:262
  10.5 26.0 %collective-permute-start.11 = (bf16[128,1280]{1,0:T(8,128)(2,1)S(1)}, bf16[128,1280]{1,0:T(8,128)(2,1)S(1)}, u32[]{:S(2)}, u32[]{:S(2)}) collective-permute-start(bf16[128,1280]{1,0:T(8,128)(2,1)S(1)} %get-tuple-element.33.refs_0_), channel_id=1, source_target_pairs={{0,16},{1,17},{2,18},{3,19},{4,20},{5,21},{6,22},{7,23},{8,24},{9,... | collective-permute-start | bytes 983048 | tf_op jit(solution)/shard_map/gather_cotangent/ppermute | solution.py:262
  14.2 22.3 %collective-permute-start.10 = (bf16[128,1280]{1,0:T(8,128)(2,1)S(1)}, bf16[128,1280]{1,0:T(8,128)(2,1)S(1)}, u32[]{:S(2)}, u32[]{:S(2)}) collective-permute-start(bf16[128,1280]{1,0:T(8,128)(2,1)S(1)} %get-tuple-element.33.refs_0_), channel_id=1, source_target_pairs={{0,8},{1,9},{2,10},{3,11},{4,12},{5,13},{6,14},{7,15},{8,0},{9,1},... | collective-permute-start | bytes 983048 | tf_op jit(solution)/shard_map/gather_cotangent/ppermute | solution.py:262
  30.0 9.4 %collective-permute-start.3 = (bf16[320,128]{1,0:T(8,128)(2,1)S(1)}, bf16[320,128]{1,0:T(8,128)(2,1)S(1)}, u32[]{:S(2)}, u32[]{:S(2)}) collective-permute-start(bf16[320,128]{1,0:T(8,128)(2,1)S(1)} %get-tuple-element.27), channel_id=1, source_target_pairs={{0,20},{1,21},{2,22},{3,23},{4,16},{5,17},{6,18},{7,19},{8,28},{9,... | collective-permute-start | bytes 245768 | tf_op jit(solution)/shard_map/send_to_owner/ppermute | solution.py:262
  30.6 8.8 %collective-permute-start.5 = (bf16[320,128]{1,0:T(8,128)(2,1)S(1)}, bf16[320,128]{1,0:T(8,128)(2,1)S(1)}, u32[]{:S(2)}, u32[]{:S(2)}) collective-permute-start(bf16[320,128]{1,0:T(8,128)(2,1)S(1)} %get-tuple-element.28), channel_id=1, source_target_pairs={{0,30},{1,31},{2,28},{3,29},{4,26},{5,27},{6,24},{7,25},{8,22},{9,... | collective-permute-start | bytes 245768 | tf_op jit(solution)/shard_map/send_to_owner/ppermute | solution.py:262
  35.6 5.4 %collective-permute-start.7 = (bf16[320,128]{1,0:T(8,128)(2,1)S(1)}, bf16[320,128]{1,0:T(8,128)(2,1)S(1)}, u32[]{:S(2)}, u32[]{:S(2)}) collective-permute-start(bf16[320,128]{1,0:T(8,128)(2,1)S(1)} %get-tuple-element.29), channel_id=1, source_target_pairs={{0,10},{1,11},{2,8},{3,9},{4,14},{5,15},{6,12},{7,13},{8,2},{9,3},... | collective-permute-start | bytes 245768 | tf_op jit(solution)/shard_map/send_to_owner/ppermute | solution.py:262
  37.0 7.7 %collective-permute-start.13 = (bf16[4,128,1280]{2,1,0:T(8,128)(2,1)S(1)}, bf16[4,128,1280]{2,1,0:T(8,128)(2,1)S(1)}, u32[]{:S(2)}, u32[]{:S(2)}) collective-permute-start(bf16[4,128,1280]{2,1,0:T(8,128)(2,1)S(1)} %swap_cotangent.1.refs_2_), channel_id=1, source_target_pairs={{0,1},{1,0},{2,3},{3,2},{4,5},{5,4},{6,7},{7,6},{8,9},{9,8},{10,11... | collective-permute-start | bytes 3932168 | tf_op jit(solution)/shard_map/gradient/ppermute | solution.py:262
  41.0 9.6 %copy-start = (bf16[1280,1280]{1,0:T(8,128)(2,1)S(1)}, bf16[1280,1280]{1,0:T(8,128)(2,1)}, u32[]{:S(2)}) copy-start(bf16[1280,1280]{1,0:T(8,128)(2,1)} %refs_5_.1) | copy-start | bytes 9830404
  41.0 3.6 %collective-permute-start.9 = (bf16[4,160,128]{2,1,0:T(8,128)(2,1)S(1)}, bf16[4,160,128]{2,1,0:T(8,128)(2,1)S(1)}, u32[]{:S(2)}, u32[]{:S(2)}) collective-permute-start(bf16[4,160,128]{2,1,0:T(8,128)(2,1)S(1)} %get-tuple-element.32), channel_id=1, source_target_pairs={{0,1},{1,0},{2,3},{3,2},{4,5},{5,4},{6,7},{7,6},{8,9},{9,8},{10,11... | collective-permute-start | bytes 491528 | tf_op jit(solution)/shard_map/send_to_owner/ppermute | solution.py:262
  41.1 8.8 %collective-permute-start.4 = (bf16[320,128]{1,0:T(8,128)(2,1)S(1)}, bf16[320,128]{1,0:T(8,128)(2,1)S(1)}, u32[]{:S(2)}, u32[]{:S(2)}) collective-permute-start(bf16[320,128]{1,0:T(8,128)(2,1)S(1)} %collective-permute-done.3.refs_0_), channel_id=1, source_target_pairs={{0,16},{1,17},{2,18},{3,19},{4,20},{5,21},{6,22},{7,23},{8,24},{9,... | collective-permute-start | bytes 245768 | tf_op jit(solution)/shard_map/send_home/ppermute | solution.py:262
  42.1 7.8 %collective-permute-start.6 = (bf16[320,128]{1,0:T(8,128)(2,1)S(1)}, bf16[320,128]{1,0:T(8,128)(2,1)S(1)}, u32[]{:S(2)}, u32[]{:S(2)}) collective-permute-start(bf16[320,128]{1,0:T(8,128)(2,1)S(1)} %collective-permute-done.5.refs_1_), channel_id=1, source_target_pairs={{0,24},{1,25},{2,26},{3,27},{4,28},{5,29},{6,30},{7,31},{8,16},{9,... | collective-permute-start | bytes 245768 | tf_op jit(solution)/shard_map/send_home/ppermute | solution.py:262
  43.2 7.4 %collective-permute-start.8 = (bf16[320,128]{1,0:T(8,128)(2,1)S(1)}, bf16[320,128]{1,0:T(8,128)(2,1)S(1)}, u32[]{:S(2)}, u32[]{:S(2)}) collective-permute-start(bf16[320,128]{1,0:T(8,128)(2,1)S(1)} %collective-permute-done.7.refs_2_), channel_id=1, source_target_pairs={{0,8},{1,9},{2,10},{3,11},{4,12},{5,13},{6,14},{7,15},{8,0},{9,1},... | collective-permute-start | bytes 245768 | tf_op jit(solution)/shard_map/send_home/ppermute | solution.py:262
  44.7 6.0 %copy-start.1 = (bf16[128,1280]{1,0:T(8,128)(2,1)S(1)}, bf16[128,1280]{1,0:T(8,128)(2,1)}, u32[]{:S(2)}) copy-start(bf16[128,1280]{1,0:T(8,128)(2,1)} %refs_4_.3) | copy-start | bytes 983044
  45.6 11.5 %collective-permute-start.14 = (bf16[80,640]{1,0:T(8,128)(2,1)S(1)}, bf16[80,640]{1,0:T(8,128)(2,1)S(1)}, u32[]{:S(2)}, u32[]{:S(2)}) collective-permute-start(bf16[80,640]{1,0:T(8,128)(2,1)S(1)} %get-tuple-element.34), channel_id=1, source_target_pairs={{0,4},{1,5},{2,14},{3,15},{4,16},{5,17},{6,26},{7,27},{8,12},{9,13... | collective-permute-start | bytes 307208 | tf_op jit(solution)/shard_map/sum_gradient/ppermute | solution.py:262
  47.7 9.4 %collective-permute-start.15 = (bf16[80,640]{1,0:T(8,128)(2,1)S(1)}, bf16[80,640]{1,0:T(8,128)(2,1)S(1)}, u32[]{:S(2)}, u32[]{:S(2)}) collective-permute-start(bf16[80,640]{1,0:T(8,128)(2,1)S(1)} %get-tuple-element.35), channel_id=1, source_target_pairs={{0,6},{1,7},{2,12},{3,13},{4,18},{5,19},{6,24},{7,25},{8,14},{9,15... | collective-permute-start | bytes 307208 | tf_op jit(solution)/shard_map/sum_gradient/ppermute | solution.py:262
  49.9 7.6 %collective-permute-start.16 = (bf16[80,640]{1,0:T(8,128)(2,1)S(1)}, bf16[80,640]{1,0:T(8,128)(2,1)S(1)}, u32[]{:S(2)}, u32[]{:S(2)}) collective-permute-start(bf16[80,640]{1,0:T(8,128)(2,1)S(1)} %get-tuple-element.36), channel_id=1, source_target_pairs={{0,2},{1,3},{2,8},{3,9},{4,22},{5,23},{6,28},{7,29},{8,10},{9,11},... | collective-permute-start | bytes 307208 | tf_op jit(solution)/shard_map/sum_gradient/ppermute | solution.py:262
  49.9 7.6 %collective-permute-start.17 = (bf16[80,640]{1,0:T(8,128)(2,1)S(1)}, bf16[80,640]{1,0:T(8,128)(2,1)S(1)}, u32[]{:S(2)}, u32[]{:S(2)}) collective-permute-start(bf16[80,640]{1,0:T(8,128)(2,1)S(1)} %get-tuple-element.37), channel_id=1, source_target_pairs={{0,0},{1,1},{2,10},{3,11},{4,20},{5,21},{6,30},{7,31},{8,8},{9,9},... | collective-permute-start | bytes 307208 | tf_op jit(solution)/shard_map/sum_gradient/ppermute | solution.py:262

commit v13 on v9

--- a/solution.py
+++ b/solution.py
@@ -13,7 +13,7 @@
 ID_ROWS = 16
 ID_BASE = 64
 SENDS = (3, 0, 1, 2)
-RETURNS = (2, 3, 0, 1)
+RETURNS = (2, 3, 1, 0)
 SUMS = (2, 3, 1)
 
 
@@ -226,26 +226,39 @@
                 out[...] = folded
 
 
-def project_kernel(*refs):
-    pieces, (residual, weight, out, attended) = refs[:-4], refs[-4:]
+def project(pieces, steps, weight, attended):
     d = lax.axis_index("dp")
     block = pieces[0].shape[0]
-    for step, piece in enumerate(pieces):
-        attended[pl.ds(pl.multiple_of((d ^ step) * block, 16), block)] = piece[...]
-    projected = lax.dot_general(
-        attended[...], weight[...], (((0,), (0,)), ((), ())), preferred_element_type=jnp.float32
-    )
-    out[...] = (residual[...].astype(jnp.float32) + projected).astype(jnp.bfloat16)
-
-
-def add_kernel(own, *refs):
-    out, width = refs[-1], own.shape[1]
-    total = refs[0][...].astype(jnp.float32)
-    for ref in refs[1:-1]:
+    rows = []
+    for index, (step, piece) in enumerate(zip(steps, pieces)):
+        attended[index * block : (index + 1) * block] = piece[...]
+        rows.append(weight[pl.ds(pl.multiple_of((d ^ step) * block, 16), block)])
+    return lax.dot_general(
+        attended[...],
+        jnp.concatenate(rows, axis=0),
+        (((0,), (0,)), ((), ())),
+        preferred_element_type=jnp.float32,
+    )
+
+
+def project_kernel(residual, weight, *refs):
+    pieces, (out, attended) = refs[:-2], refs[-2:]
+    out[...] = residual[...].astype(jnp.float32) + project(
+        pieces, range(len(pieces)), weight, attended
+    )
+
+
+def finish_kernel(count, early, *refs):
+    partial, mine, pieces = refs[: count - 1], refs[count - 1], refs[count : 2 * count - early]
+    projected, weight, out, grad, attended = refs[2 * count - early :]
+    total = partial[0][...].astype(jnp.float32)
+    for ref in partial[1:]:
         total = total + ref[...].astype(jnp.float32)
-    short = total.shape[0]
-    out[:short] = own[:short] + total[:, :width]
-    out[short:] = own[short:] + total[:, width:]
+    short, width = total.shape[0], mine.shape[1]
+    grad[:short] = mine[:short] + total[:, :width]
+    grad[short:] = mine[short:] + total[:, width:]
+    projected = projected[...] + project(pieces, range(early, count), weight, attended)
+    out[...] = projected.astype(jnp.bfloat16)
 
 
 def exchange_body(
@@ -376,24 +389,30 @@
         homes[1:] = [
             move(homes[k], lambda d, e, s, k=k: (d ^ k, e, s)) for k in range(1, n_dp)
         ]
+    early = 2
     with jax.named_scope("project"):
-        layer_out = call(
+        projected = call(
             project_kernel,
-            bf16((rows, width)),
-            *homes,
+            jax.ShapeDtypeStruct((rows, width), jnp.float32),
             residual,
             out_weight,
-            scratch=[pltpu.VMEM((width, rows), jnp.bfloat16)],
-            flops=1 * rows * width * width,
-            bytes_accessed=2 * width * width,
-        )
-    with jax.named_scope("add_gradient"):
-        grad_weight = call(
-            add_kernel,
-            jax.ShapeDtypeStruct((half, block), jnp.float32),
+            *homes[:early],
+            scratch=[pltpu.VMEM((early * block, rows), jnp.bfloat16)],
+            flops=2 * rows * early * block * width,
+            bytes_accessed=2 * early * block * width,
+        )
+    with jax.named_scope("finish"):
+        layer_out, grad_weight = call(
+            functools.partial(finish_kernel, n_dp, early),
+            [bf16((rows, width)), jax.ShapeDtypeStruct((half, block), jnp.float32)],
+            *partial,
             mine,
-            *partial,
-            bytes_accessed=4 * half * block * 4,
+            *homes[early:],
+            projected,
+            out_weight,
+            scratch=[pltpu.VMEM(((n_dp - early) * block, rows), jnp.bfloat16)],
+            flops=2 * rows * (n_dp - early) * block * width,
+            bytes_accessed=2 * (n_dp - early) * block * width,
         )
     return (layer_out, grad_weight)
 

time: 58.8 us -> 57.9 us (0.985)
  waiting for transfers between devices: 22.4 us -> 20.1 us
  starting transfers between devices: 26 us -> 27.9 us
    ppermute x18, waiting for transfers between devices: 22.4 us -> 20.1 us  [move(): return lax.ppermute(data, AXES, pairs)]
    ppermute x18, starting transfers between devices: 26 us -> 27.9 us  [move(): return lax.ppermute(data, AXES, pairs)]
  transfers between devices with their start and end apart: 18 -> 18, of which waited for: 8 -> 8; matrix products, arithmetic and copies ran while one was open for 0% -> 0% of each run, Pallas kernels for 12% -> 11%
where the time goes in v13:
time: 57.9 us; the launch traced here: 57.7 us
  starting transfers between devices  27.9 us (48%)
  waiting for transfers between devices  20.1 us (35%)
  Pallas kernels  8.95 us (15%)
  between operations  0.76 us (1%)
    ppermute x18, starting transfers between devices, move(): return lax.ppermute(data, AXES, pairs)  27.9 us
    ppermute x18, waiting for transfers between devices, move(): return lax.ppermute(data, AXES, pairs)  20.1 us
    pallas_call x9, Pallas kernels, call(): pl.pallas_call(kernel, out_shape=out_shape, in_specs=[placed(space) for s...  8.95 us
  transfers between devices with their start and end apart: 18, of which 8 were waited for; matrix products, arithmetic and copies ran while one was open for 0% of the time, Pallas kernels for 11%

profile of v13, /device:TPU:0, one launch (start us, length us, event | category | flops | bytes accessed | tf_op | source)
XLA Modules:
  0.0 57.7 jit_solution(5309003491027944886)
XLA Ops:
  0.6 1.5 %pack.1 = (bf16[976,128]{1,0:T(8,128)(2,1)S(1)}, bf16[976,128]{1,0:T(8,128)(2,1)S(1)}, bf16[976,128]{1,0:T(8,128)(2,1)S(1)}, bf16[976,128]{1,0:T(8,128)(2,1)S(1)}, bf16[128,1280]{1,0:T(8,128)(2,1)S(1)}) custom-call(s32[1,128]{1,0:T(1,128)} %bitcast.1, bf16[128,1280]{1,0:T(8,128)(2,1)} %refs_1_.1, bf16[128,1280]{1,0:T(8,128)(2,1)} %refs_2_.1, ...), custom_call_target="tpu_custom_call" | custom-call | bytes 2621440 | tf_op jit(solution)/shard_map/pack/pallas_call | solution.py:39
  2.2 5.1 %collective-permute-start = (bf16[976,128]{1,0:T(8,128)(2,1)S(1)}, bf16[976,128]{1,0:T(8,128)(2,1)S(1)}, u32[]{:S(2)}, u32[]{:S(2)}) collective-permute-start(bf16[976,128]{1,0:T(8,128)(2,1)S(1)} %get-tuple-element.24), channel_id=1, source_target_pairs={{0,6},{1,7},{2,4},{3,5},{4,2},{5,3},{6,0},{7,1},{8,14},{9,15},{10,... | collective-permute-start | bytes 749576 | tf_op jit(solution)/shard_map/exchange_heads/ppermute | solution.py:286
  7.3 0.6 %collective-permute-start.2 = (bf16[976,128]{1,0:T(8,128)(2,1)S(1)}, bf16[976,128]{1,0:T(8,128)(2,1)S(1)}, u32[]{:S(2)}, u32[]{:S(2)}) collective-permute-start(bf16[976,128]{1,0:T(8,128)(2,1)S(1)} %get-tuple-element.27), channel_id=1, source_target_pairs={{0,4},{1,5},{2,6},{3,7},{4,0},{5,1},{6,2},{7,3},{8,12},{9,13},{10,... | collective-permute-start | bytes 749576 | tf_op jit(solution)/shard_map/exchange_heads/ppermute | solution.py:286
  7.9 1.6 %collective-permute-start.8 = (bf16[128,1280]{1,0:T(8,128)(2,1)S(1)}, bf16[128,1280]{1,0:T(8,128)(2,1)S(1)}, u32[]{:S(2)}, u32[]{:S(2)}) collective-permute-start(bf16[128,1280]{1,0:T(8,128)(2,1)S(1)} %get-tuple-element.37.refs_0_), channel_id=1, source_target_pairs={{0,8},{1,9},{2,10},{3,11},{4,12},{5,13},{6,14},{7,15},{8,0},{9,1},... | collective-permute-start | bytes 983048 | tf_op jit(solution)/shard_map/gather_cotangent/ppermute | solution.py:286
  9.6 1.5 %collective-permute-start.9 = (bf16[128,1280]{1,0:T(8,128)(2,1)S(1)}, bf16[128,1280]{1,0:T(8,128)(2,1)S(1)}, u32[]{:S(2)}, u32[]{:S(2)}) collective-permute-start(bf16[128,1280]{1,0:T(8,128)(2,1)S(1)} %get-tuple-element.37.refs_0_), channel_id=1, source_target_pairs={{0,16},{1,17},{2,18},{3,19},{4,20},{5,21},{6,22},{7,23},{8,24},{9,... | collective-permute-start | bytes 983048 | tf_op jit(solution)/shard_map/gather_cotangent/ppermute | solution.py:286
  11.1 3.2 %collective-permute-done.refs_0_ = bf16[976,128]{1,0:T(8,128)(2,1)S(1)} collective-permute-done((bf16[976,128]{1,0:T(8,128)(2,1)S(1)}, bf16[976,128]{1,0:T(8,128)(2,1)S(1)}, u32[]{:S(2)}, u32[]{:S(2)}) %collective-permute-start) | collective-permute-done | bytes 249888 | tf_op jit(solution)/shard_map/exchange_heads/ppermute | solution.py:286
  14.2 2.6 %collective-permute-start.10 = (bf16[128,1280]{1,0:T(8,128)(2,1)S(1)}, bf16[128,1280]{1,0:T(8,128)(2,1)S(1)}, u32[]{:S(2)}, u32[]{:S(2)}) collective-permute-start(bf16[128,1280]{1,0:T(8,128)(2,1)S(1)} %get-tuple-element.37.refs_0_), channel_id=1, source_target_pairs={{0,24},{1,25},{2,26},{3,27},{4,28},{5,29},{6,30},{7,31},{8,16},{9,... | collective-permute-start | bytes 983048 | tf_op jit(solution)/shard_map/gather_cotangent/ppermute | solution.py:286
  16.9 2.9 %collective-permute-done.1.refs_2_.refs_1_ = bf16[976,128]{1,0:T(8,128)(2,1)S(1)} collective-permute-done((bf16[976,128]{1,0:T(8,128)(2,1)S(1)}, bf16[976,128]{1,0:T(8,128)(2,1)S(1)}, u32[]{:S(2)}, u32[]{:S(2)}) %collective-permute-start.1) | collective-permute-done | bytes 249888 | tf_op jit(solution)/shard_map/exchange_heads/ppermute | solution.py:286
  19.8 1.7 %attention.3 = (f32[320,384]{1,0:T(8,128)S(1)}, f32[8,384]{1,0:T(8,128)S(1)}, f32[8,384]{1,0:T(8,128)S(1)}) custom-call(bf16[976,128]{1,0:T(8,128)(2,1)S(1)} %collective-permute-done.refs_0_, bf16[976,128]{1,0:T(8,128)(2,1)S(1)} %get-tuple-element.25.refs_1_.refs_0_, bf16[976,128]{1,0:T(8,128)(2,1)S(1)} %collective-permute-done.1.refs_2_.refs_1_), custom_call_target="tpu_custom_call" | custom-call | flops 2595225600 | bytes 1310720 | tf_op jit(solution)/shard_map/attention/pallas_call | solution.py:39
  21.5 7.1 %collective-permute-done.2.refs_3_.refs_2_ = bf16[976,128]{1,0:T(8,128)(2,1)S(1)} collective-permute-done((bf16[976,128]{1,0:T(8,128)(2,1)S(1)}, bf16[976,128]{1,0:T(8,128)(2,1)S(1)}, u32[]{:S(2)}, u32[]{:S(2)}) %collective-permute-start.2) | collective-permute-done | bytes 249888 | tf_op jit(solution)/shard_map/exchange_heads/ppermute | solution.py:286
  28.5 1.5 %attention.4 = (bf16[320,128]{1,0:T(8,128)(2,1)S(1)}, bf16[320,128]{1,0:T(8,128)(2,1)S(1)}) custom-call(bf16[976,128]{1,0:T(8,128)(2,1)S(1)} %collective-permute-done.refs_0_, bf16[976,128]{1,0:T(8,128)(2,1)S(1)} %get-tuple-element.25.refs_1_.refs_0_, bf16[976,128]{1,0:T(8,128)(2,1)S(1)} %collective-permute-done.1.refs_2_.refs_1_, ...), custom_call_target="tpu_custom_call" | custom-call | flops 1441792000 | bytes 1310720 | tf_op jit(solution)/shard_map/attention/pallas_call | solution.py:39
  30.1 3.9 %collective-permute-start.4 = (bf16[320,128]{1,0:T(8,128)(2,1)S(1)}, bf16[320,128]{1,0:T(8,128)(2,1)S(1)}, u32[]{:S(2)}, u32[]{:S(2)}) collective-permute-start(bf16[320,128]{1,0:T(8,128)(2,1)S(1)} %get-tuple-element.32), channel_id=1, source_target_pairs={{0,6},{1,7},{2,12},{3,13},{4,18},{5,19},{6,24},{7,25},{8,14},{9,15... | collective-permute-start | bytes 245768 | tf_op jit(solution)/shard_map/send_to_owner/ppermute | solution.py:286
  34.0 1.0 %attention.5 = (bf16[320,128]{1,0:T(8,128)(2,1)S(1)}, bf16[320,128]{1,0:T(8,128)(2,1)S(1)}) custom-call(bf16[976,128]{1,0:T(8,128)(2,1)S(1)} %get-tuple-element.25.refs_1_.refs_0_, bf16[976,128]{1,0:T(8,128)(2,1)S(1)} %collective-permute-done.1.refs_2_.refs_1_, bf16[976,128]{1,0:T(8,128)(2,1)S(1)} %collective-permute-done.2.refs_3_.refs_2_, ...), custom_call_target="tpu_custom_call" | custom-call | flops 576716800 | bytes 1310720 | tf_op jit(solution)/shard_map/attention/pallas_call | solution.py:39
  35.0 1.5 %collective-permute-start.5 = (bf16[320,128]{1,0:T(8,128)(2,1)S(1)}, bf16[320,128]{1,0:T(8,128)(2,1)S(1)}, u32[]{:S(2)}, u32[]{:S(2)}) collective-permute-start(bf16[320,128]{1,0:T(8,128)(2,1)S(1)} %get-tuple-element.33), channel_id=1, source_target_pairs={{0,2},{1,3},{2,8},{3,9},{4,22},{5,23},{6,28},{7,29},{8,10},{9,11},... | collective-permute-start | bytes 245768 | tf_op jit(solution)/shard_map/send_to_owner/ppermute | solution.py:286
  36.6 0.7 %collective-permute-start.6 = (bf16[320,128]{1,0:T(8,128)(2,1)S(1)}, bf16[320,128]{1,0:T(8,128)(2,1)S(1)}, u32[]{:S(2)}, u32[]{:S(2)}) collective-permute-start(bf16[320,128]{1,0:T(8,128)(2,1)S(1)} %get-tuple-element.34), channel_id=1, source_target_pairs={{0,0},{1,1},{2,10},{3,11},{4,20},{5,21},{6,30},{7,31},{8,8},{9,9},... | collective-permute-start | bytes 245768 | tf_op jit(solution)/shard_map/send_to_owner/ppermute | solution.py:286
  37.2 0.5 swap_cotangent.1.refs_2_
  37.7 0.1 collective-permute-start.11
  37.8 2.0 %collective-permute-done.3.refs_0_ = bf16[320,128]{1,0:T(8,128)(2,1)S(1)} collective-permute-done((bf16[320,128]{1,0:T(8,128)(2,1)S(1)}, bf16[320,128]{1,0:T(8,128)(2,1)S(1)}, u32[]{:S(2)}, u32[]{:S(2)}) %collective-permute-start.3) | collective-permute-done | bytes 81952 | tf_op jit(solution)/shard_map/send_to_owner/ppermute | solution.py:286
  39.7 1.0 %collective-permute-done.5.refs_2_ = bf16[320,128]{1,0:T(8,128)(2,1)S(1)} collective-permute-done((bf16[320,128]{1,0:T(8,128)(2,1)S(1)}, bf16[320,128]{1,0:T(8,128)(2,1)S(1)}, u32[]{:S(2)}, u32[]{:S(2)}) %collective-permute-start.5) | collective-permute-done | bytes 81952 | tf_op jit(solution)/shard_map/send_to_owner/ppermute | solution.py:286
  40.7 0.1 send_to_owner.1
  40.9 1.0 %collective-permute-start.17 = (bf16[320,128]{1,0:T(8,128)(2,1)S(1)}, bf16[320,128]{1,0:T(8,128)(2,1)S(1)}, u32[]{:S(2)}, u32[]{:S(2)}) collective-permute-start(bf16[320,128]{1,0:T(8,128)(2,1)S(1)} %get-tuple-element.45), channel_id=1, source_target_pairs={{0,8},{1,9},{2,10},{3,11},{4,12},{5,13},{6,14},{7,15},{8,0},{9,1},... | collective-permute-start | bytes 245768 | tf_op jit(solution)/shard_map/send_home/ppermute | solution.py:286
  41.9 0.4 collective-permute-done.7.refs_1_
  42.3 0.9 %gradient.1 = (f32[160,320]{1,0:T(8,128)S(1)}, bf16[80,640]{1,0:T(8,128)(2,1)S(1)}, bf16[80,640]{1,0:T(8,128)(2,1)S(1)}, bf16[80,640]{1,0:T(8,128)(2,1)S(1)}) custom-call(bf16[4,160,128]{2,1,0:T(8,128)(2,1)S(1)} %get-tuple-element.35.refs_0_, bf16[4,160,128]{2,1,0:T(8,128)(2,1)S(1)} %collective-permute-done.7.refs_1_, ...), custom_call_target="tpu_custom_call" | custom-call | flops 419430400 | bytes 2621440 | tf_op jit(solution)/shard_map/gradient/pallas_call | solution.py:39
  43.2 4.1 %collective-permute-start.12 = (bf16[80,640]{1,0:T(8,128)(2,1)S(1)}, bf16[80,640]{1,0:T(8,128)(2,1)S(1)}, u32[]{:S(2)}, u32[]{:S(2)}) collective-permute-start(bf16[80,640]{1,0:T(8,128)(2,1)S(1)} %get-tuple-element.38), channel_id=1, source_target_pairs={{0,4},{1,5},{2,6},{3,7},{4,0},{5,1},{6,2},{7,3},{8,12},{9,13},{10,... | collective-permute-start | bytes 307208 | tf_op jit(solution)/shard_map/sum_gradient/ppermute | solution.py:286
  47.3 1.8 %collective-permute-start.13 = (bf16[80,640]{1,0:T(8,128)(2,1)S(1)}, bf16[80,640]{1,0:T(8,128)(2,1)S(1)}, u32[]{:S(2)}, u32[]{:S(2)}) collective-permute-start(bf16[80,640]{1,0:T(8,128)(2,1)S(1)} %get-tuple-element.39), channel_id=1, source_target_pairs={{0,6},{1,7},{2,4},{3,5},{4,2},{5,3},{6,0},{7,1},{8,14},{9,15},{10,... | collective-permute-start | bytes 307208 | tf_op jit(solution)/shard_map/sum_gradient/ppermute | solution.py:286
  49.1 0.5 collective-permute-start.14
  49.6 1.5 %collective-permute-start.15 = (bf16[320,128]{1,0:T(8,128)(2,1)S(1)}, bf16[320,128]{1,0:T(8,128)(2,1)S(1)}, u32[]{:S(2)}, u32[]{:S(2)}) collective-permute-start(bf16[320,128]{1,0:T(8,128)(2,1)S(1)} %get-tuple-element.42), channel_id=1, source_target_pairs={{0,16},{1,17},{2,18},{3,19},{4,20},{5,21},{6,22},{7,23},{8,24},{9,... | collective-permute-start | bytes 245768 | tf_op jit(solution)/shard_map/send_home/ppermute | solution.py:286
  51.1 1.3 %collective-permute-start.16 = (bf16[320,128]{1,0:T(8,128)(2,1)S(1)}, bf16[320,128]{1,0:T(8,128)(2,1)S(1)}, u32[]{:S(2)}, u32[]{:S(2)}) collective-permute-start(bf16[320,128]{1,0:T(8,128)(2,1)S(1)} %get-tuple-element.43), channel_id=1, source_target_pairs={{0,24},{1,25},{2,26},{3,27},{4,28},{5,29},{6,30},{7,31},{8,16},{9,... | collective-permute-start | bytes 245768 | tf_op jit(solution)/shard_map/send_home/ppermute | solution.py:286
  52.4 0.5 project.1.refs_6_
  52.9 1.2 %collective-permute-done.15.refs_4_ = bf16[320,128]{1,0:T(8,128)(2,1)S(1)} collective-permute-done((bf16[320,128]{1,0:T(8,128)(2,1)S(1)}, bf16[320,128]{1,0:T(8,128)(2,1)S(1)}, u32[]{:S(2)}, u32[]{:S(2)}) %collective-permute-start.15) | collective-permute-done | bytes 81952 | tf_op jit(solution)/shard_map/send_home/ppermute | solution.py:286
  54.1 2.4 %collective-permute-done.16.refs_5_ = bf16[320,128]{1,0:T(8,128)(2,1)S(1)} collective-permute-done((bf16[320,128]{1,0:T(8,128)(2,1)S(1)}, bf16[320,128]{1,0:T(8,128)(2,1)S(1)}, u32[]{:S(2)}, u32[]{:S(2)}) %collective-permute-start.16) | collective-permute-done | bytes 81952 | tf_op jit(solution)/shard_map/send_home/ppermute | solution.py:286
  56.5 1.2 %finish.1 = (bf16[128,1280]{1,0:T(8,128)(2,1)}, f32[160,320]{1,0:T(8,128)}) custom-call(bf16[80,640]{1,0:T(8,128)(2,1)S(1)} %collective-permute-done.12.refs_0_, bf16[80,640]{1,0:T(8,128)(2,1)S(1)} %collective-permute-done.13.refs_1_, bf16[80,640]{1,0:T(8,128)(2,1)S(1)} %collective-permute-done.14.refs_2_, f32[160,320]{1,0:T(8,128)S(1)} %get-tuple-element.41.refs_3_, ...), custom_call_target="tpu_custom_call" | custom-call | flops 209715200 | bytes 1638400 | tf_op jit(solution)/shard_map/finish/pallas_call | solution.py:39
  (17 shorter events, 0.2 us)
Async XLA Ops:
  2.2 12.1 %collective-permute-start = (bf16[976,128]{1,0:T(8,128)(2,1)S(1)}, bf16[976,128]{1,0:T(8,128)(2,1)S(1)}, u32[]{:S(2)}, u32[]{:S(2)}) collective-permute-start(bf16[976,128]{1,0:T(8,128)(2,1)S(1)} %get-tuple-element.24), channel_id=1, source_target_pairs={{0,6},{1,7},{2,4},{3,5},{4,2},{5,3},{6,0},{7,1},{8,14},{9,15},{10,... | collective-permute-start | bytes 749576 | tf_op jit(solution)/shard_map/exchange_heads/ppermute | solution.py:286
  7.3 12.5 %collective-permute-start.1 = (bf16[976,128]{1,0:T(8,128)(2,1)S(1)}, bf16[976,128]{1,0:T(8,128)(2,1)S(1)}, u32[]{:S(2)}, u32[]{:S(2)}) collective-permute-start(bf16[976,128]{1,0:T(8,128)(2,1)S(1)} %get-tuple-element.26), channel_id=1, source_target_pairs={{0,2},{1,3},{2,0},{3,1},{4,6},{5,7},{6,4},{7,5},{8,10},{9,11},{10,... | collective-permute-start | bytes 749576 | tf_op jit(solution)/shard_map/exchange_heads/ppermute | solution.py:286
  7.3 21.3 %collective-permute-start.2 = (bf16[976,128]{1,0:T(8,128)(2,1)S(1)}, bf16[976,128]{1,0:T(8,128)(2,1)S(1)}, u32[]{:S(2)}, u32[]{:S(2)}) collective-permute-start(bf16[976,128]{1,0:T(8,128)(2,1)S(1)} %get-tuple-element.27), channel_id=1, source_target_pairs={{0,4},{1,5},{2,6},{3,7},{4,0},{5,1},{6,2},{7,3},{8,12},{9,13},{10,... | collective-permute-start | bytes 749576 | tf_op jit(solution)/shard_map/exchange_heads/ppermute | solution.py:286
  7.9 27.1 %collective-permute-start.8 = (bf16[128,1280]{1,0:T(8,128)(2,1)S(1)}, bf16[128,1280]{1,0:T(8,128)(2,1)S(1)}, u32[]{:S(2)}, u32[]{:S(2)}) collective-permute-start(bf16[128,1280]{1,0:T(8,128)(2,1)S(1)} %get-tuple-element.37.refs_0_), channel_id=1, source_target_pairs={{0,8},{1,9},{2,10},{3,11},{4,12},{5,13},{6,14},{7,15},{8,0},{9,1},... | collective-permute-start | bytes 983048 | tf_op jit(solution)/shard_map/gather_cotangent/ppermute | solution.py:286
  9.6 27.0 %collective-permute-start.9 = (bf16[128,1280]{1,0:T(8,128)(2,1)S(1)}, bf16[128,1280]{1,0:T(8,128)(2,1)S(1)}, u32[]{:S(2)}, u32[]{:S(2)}) collective-permute-start(bf16[128,1280]{1,0:T(8,128)(2,1)S(1)} %get-tuple-element.37.refs_0_), channel_id=1, source_target_pairs={{0,16},{1,17},{2,18},{3,19},{4,20},{5,21},{6,22},{7,23},{8,24},{9,... | collective-permute-start | bytes 983048 | tf_op jit(solution)/shard_map/gather_cotangent/ppermute | solution.py:286
  14.2 23.0 %collective-permute-start.10 = (bf16[128,1280]{1,0:T(8,128)(2,1)S(1)}, bf16[128,1280]{1,0:T(8,128)(2,1)S(1)}, u32[]{:S(2)}, u32[]{:S(2)}) collective-permute-start(bf16[128,1280]{1,0:T(8,128)(2,1)S(1)} %get-tuple-element.37.refs_0_), channel_id=1, source_target_pairs={{0,24},{1,25},{2,26},{3,27},{4,28},{5,29},{6,30},{7,31},{8,16},{9,... | collective-permute-start | bytes 983048 | tf_op jit(solution)/shard_map/gather_cotangent/ppermute | solution.py:286
  30.0 9.7 %collective-permute-start.3 = (bf16[320,128]{1,0:T(8,128)(2,1)S(1)}, bf16[320,128]{1,0:T(8,128)(2,1)S(1)}, u32[]{:S(2)}, u32[]{:S(2)}) collective-permute-start(bf16[320,128]{1,0:T(8,128)(2,1)S(1)} %get-tuple-element.31), channel_id=1, source_target_pairs={{0,4},{1,5},{2,14},{3,15},{4,16},{5,17},{6,26},{7,27},{8,12},{9,13... | collective-permute-start | bytes 245768 | tf_op jit(solution)/shard_map/send_to_owner/ppermute | solution.py:286
  30.1 9.6 %collective-permute-start.4 = (bf16[320,128]{1,0:T(8,128)(2,1)S(1)}, bf16[320,128]{1,0:T(8,128)(2,1)S(1)}, u32[]{:S(2)}, u32[]{:S(2)}) collective-permute-start(bf16[320,128]{1,0:T(8,128)(2,1)S(1)} %get-tuple-element.32), channel_id=1, source_target_pairs={{0,6},{1,7},{2,12},{3,13},{4,18},{5,19},{6,24},{7,25},{8,14},{9,15... | collective-permute-start | bytes 245768 | tf_op jit(solution)/shard_map/send_to_owner/ppermute | solution.py:286
  35.0 5.7 %collective-permute-start.5 = (bf16[320,128]{1,0:T(8,128)(2,1)S(1)}, bf16[320,128]{1,0:T(8,128)(2,1)S(1)}, u32[]{:S(2)}, u32[]{:S(2)}) collective-permute-start(bf16[320,128]{1,0:T(8,128)(2,1)S(1)} %get-tuple-element.33), channel_id=1, source_target_pairs={{0,2},{1,3},{2,8},{3,9},{4,22},{5,23},{6,28},{7,29},{8,10},{9,11},... | collective-permute-start | bytes 245768 | tf_op jit(solution)/shard_map/send_to_owner/ppermute | solution.py:286
  36.6 4.1 %collective-permute-start.6 = (bf16[320,128]{1,0:T(8,128)(2,1)S(1)}, bf16[320,128]{1,0:T(8,128)(2,1)S(1)}, u32[]{:S(2)}, u32[]{:S(2)}) collective-permute-start(bf16[320,128]{1,0:T(8,128)(2,1)S(1)} %get-tuple-element.34), channel_id=1, source_target_pairs={{0,0},{1,1},{2,10},{3,11},{4,20},{5,21},{6,30},{7,31},{8,8},{9,9},... | collective-permute-start | bytes 245768 | tf_op jit(solution)/shard_map/send_to_owner/ppermute | solution.py:286
  37.7 4.6 %collective-permute-start.11 = (bf16[4,128,1280]{2,1,0:T(8,128)(2,1)S(1)}, bf16[4,128,1280]{2,1,0:T(8,128)(2,1)S(1)}, u32[]{:S(2)}, u32[]{:S(2)}) collective-permute-start(bf16[4,128,1280]{2,1,0:T(8,128)(2,1)S(1)} %swap_cotangent.1.refs_2_), channel_id=1, source_target_pairs={{0,1},{1,0},{2,3},{3,2},{4,5},{5,4},{6,7},{7,6},{8,9},{9,8},{10,11... | collective-permute-start | bytes 3932168 | tf_op jit(solution)/shard_map/gradient/ppermute | solution.py:286
  40.7 11.7 %copy-start = (bf16[1280,1280]{1,0:T(8,128)(2,1)S(1)}, bf16[1280,1280]{1,0:T(8,128)(2,1)}, u32[]{:S(2)}) copy-start(bf16[1280,1280]{1,0:T(8,128)(2,1)} %refs_7_.1) | copy-start | bytes 9830404
  40.8 1.5 %collective-permute-start.7 = (bf16[4,160,128]{2,1,0:T(8,128)(2,1)S(1)}, bf16[4,160,128]{2,1,0:T(8,128)(2,1)S(1)}, u32[]{:S(2)}, u32[]{:S(2)}) collective-permute-start(bf16[4,160,128]{2,1,0:T(8,128)(2,1)S(1)} %get-tuple-element.36), channel_id=1, source_target_pairs={{0,1},{1,0},{2,3},{3,2},{4,5},{5,4},{6,7},{7,6},{8,9},{9,8},{10,11... | collective-permute-start | bytes 491528 | tf_op jit(solution)/shard_map/send_to_owner/ppermute | solution.py:286
  40.9 10.3 %collective-permute-start.17 = (bf16[320,128]{1,0:T(8,128)(2,1)S(1)}, bf16[320,128]{1,0:T(8,128)(2,1)S(1)}, u32[]{:S(2)}, u32[]{:S(2)}) collective-permute-start(bf16[320,128]{1,0:T(8,128)(2,1)S(1)} %get-tuple-element.45), channel_id=1, source_target_pairs={{0,8},{1,9},{2,10},{3,11},{4,12},{5,13},{6,14},{7,15},{8,0},{9,1},... | collective-permute-start | bytes 245768 | tf_op jit(solution)/shard_map/send_home/ppermute | solution.py:286
  42.3 10.1 %copy-start.1 = (bf16[128,1280]{1,0:T(8,128)(2,1)S(1)}, bf16[128,1280]{1,0:T(8,128)(2,1)}, u32[]{:S(2)}) copy-start(bf16[128,1280]{1,0:T(8,128)(2,1)} %residual.1) | copy-start | bytes 983044
  43.2 13.2 %collective-permute-start.12 = (bf16[80,640]{1,0:T(8,128)(2,1)S(1)}, bf16[80,640]{1,0:T(8,128)(2,1)S(1)}, u32[]{:S(2)}, u32[]{:S(2)}) collective-permute-start(bf16[80,640]{1,0:T(8,128)(2,1)S(1)} %get-tuple-element.38), channel_id=1, source_target_pairs={{0,4},{1,5},{2,6},{3,7},{4,0},{5,1},{6,2},{7,3},{8,12},{9,13},{10,... | collective-permute-start | bytes 307208 | tf_op jit(solution)/shard_map/sum_gradient/ppermute | solution.py:286
  47.3 9.2 %collective-permute-start.13 = (bf16[80,640]{1,0:T(8,128)(2,1)S(1)}, bf16[80,640]{1,0:T(8,128)(2,1)S(1)}, u32[]{:S(2)}, u32[]{:S(2)}) collective-permute-start(bf16[80,640]{1,0:T(8,128)(2,1)S(1)} %get-tuple-element.39), channel_id=1, source_target_pairs={{0,6},{1,7},{2,4},{3,5},{4,2},{5,3},{6,0},{7,1},{8,14},{9,15},{10,... | collective-permute-start | bytes 307208 | tf_op jit(solution)/shard_map/sum_gradient/ppermute | solution.py:286
  49.1 7.4 %collective-permute-start.14 = (bf16[80,640]{1,0:T(8,128)(2,1)S(1)}, bf16[80,640]{1,0:T(8,128)(2,1)S(1)}, u32[]{:S(2)}, u32[]{:S(2)}) collective-permute-start(bf16[80,640]{1,0:T(8,128)(2,1)S(1)} %get-tuple-element.40), channel_id=1, source_target_pairs={{0,2},{1,3},{2,0},{3,1},{4,6},{5,7},{6,4},{7,5},{8,10},{9,11},{10,... | collective-permute-start | bytes 307208 | tf_op jit(solution)/shard_map/sum_gradient/ppermute | solution.py:286
  49.6 4.5 %collective-permute-start.15 = (bf16[320,128]{1,0:T(8,128)(2,1)S(1)}, bf16[320,128]{1,0:T(8,128)(2,1)S(1)}, u32[]{:S(2)}, u32[]{:S(2)}) collective-permute-start(bf16[320,128]{1,0:T(8,128)(2,1)S(1)} %get-tuple-element.42), channel_id=1, source_target_pairs={{0,16},{1,17},{2,18},{3,19},{4,20},{5,21},{6,22},{7,23},{8,24},{9,... | collective-permute-start | bytes 245768 | tf_op jit(solution)/shard_map/send_home/ppermute | solution.py:286
  51.1 5.3 %collective-permute-start.16 = (bf16[320,128]{1,0:T(8,128)(2,1)S(1)}, bf16[320,128]{1,0:T(8,128)(2,1)S(1)}, u32[]{:S(2)}, u32[]{:S(2)}) collective-permute-start(bf16[320,128]{1,0:T(8,128)(2,1)S(1)} %get-tuple-element.43), channel_id=1, source_target_pairs={{0,24},{1,25},{2,26},{3,27},{4,28},{5,29},{6,30},{7,31},{8,16},{9,... | collective-permute-start | bytes 245768 | tf_op jit(solution)/shard_map/send_home/ppermute | solution.py:286

commit v14 on v13

--- a/solution.py
+++ b/solution.py
@@ -389,7 +389,7 @@
         homes[1:] = [
             move(homes[k], lambda d, e, s, k=k: (d ^ k, e, s)) for k in range(1, n_dp)
         ]
-    early = 2
+    early = 3
     with jax.named_scope("project"):
         projected = call(
             project_kernel,

time: 57.9 us -> 58.5 us (1.010)
  waiting for transfers between devices: 20.1 us -> 20.8 us
    ppermute x18, waiting for transfers between devices: 20.1 us -> 20.8 us  [move(): return lax.ppermute(data, AXES, pairs)]
  transfers between devices with their start and end apart: 18 -> 18, of which waited for: 8 -> 7; matrix products, arithmetic and copies ran while one was open for 0% -> 0% of each run, Pallas kernels for 11% -> 11%
where the time goes in v14:
time: 58.5 us; the launch traced here: 58.3 us
  starting transfers between devices  27.8 us (48%)
  waiting for transfers between devices  20.8 us (36%)
  Pallas kernels  8.95 us (15%)
  between operations  0.76 us (1%)
    ppermute x18, starting transfers between devices, move(): return lax.ppermute(data, AXES, pairs)  27.8 us
    ppermute x18, waiting for transfers between devices, move(): return lax.ppermute(data, AXES, pairs)  20.8 us
    pallas_call x9, Pallas kernels, call(): pl.pallas_call(kernel, out_shape=out_shape, in_specs=[placed(space) for s...  8.95 us
  transfers between devices with their start and end apart: 18, of which 7 were waited for; matrix products, arithmetic and copies ran while one was open for 0% of the time, Pallas kernels for 11%

profile of v14, /device:TPU:0, one launch (start us, length us, event | category | flops | bytes accessed | tf_op | source)
XLA Modules:
  0.0 58.3 jit_solution(13832638177811683894)
XLA Ops:
  0.6 1.5 %pack.1 = (bf16[976,128]{1,0:T(8,128)(2,1)S(1)}, bf16[976,128]{1,0:T(8,128)(2,1)S(1)}, bf16[976,128]{1,0:T(8,128)(2,1)S(1)}, bf16[976,128]{1,0:T(8,128)(2,1)S(1)}, bf16[128,1280]{1,0:T(8,128)(2,1)S(1)}) custom-call(s32[1,128]{1,0:T(1,128)} %bitcast.1, bf16[128,1280]{1,0:T(8,128)(2,1)} %refs_1_.1, bf16[128,1280]{1,0:T(8,128)(2,1)} %refs_2_.1, ...), custom_call_target="tpu_custom_call" | custom-call | bytes 2621440 | tf_op jit(solution)/shard_map/pack/pallas_call | solution.py:39
  2.2 5.1 %collective-permute-start = (bf16[976,128]{1,0:T(8,128)(2,1)S(1)}, bf16[976,128]{1,0:T(8,128)(2,1)S(1)}, u32[]{:S(2)}, u32[]{:S(2)}) collective-permute-start(bf16[976,128]{1,0:T(8,128)(2,1)S(1)} %get-tuple-element.24), channel_id=1, source_target_pairs={{0,6},{1,7},{2,4},{3,5},{4,2},{5,3},{6,0},{7,1},{8,14},{9,15},{10,... | collective-permute-start | bytes 749576 | tf_op jit(solution)/shard_map/exchange_heads/ppermute | solution.py:286
  7.3 0.6 %collective-permute-start.2 = (bf16[976,128]{1,0:T(8,128)(2,1)S(1)}, bf16[976,128]{1,0:T(8,128)(2,1)S(1)}, u32[]{:S(2)}, u32[]{:S(2)}) collective-permute-start(bf16[976,128]{1,0:T(8,128)(2,1)S(1)} %get-tuple-element.27), channel_id=1, source_target_pairs={{0,4},{1,5},{2,6},{3,7},{4,0},{5,1},{6,2},{7,3},{8,12},{9,13},{10,... | collective-permute-start | bytes 749576 | tf_op jit(solution)/shard_map/exchange_heads/ppermute | solution.py:286
  7.9 1.6 %collective-permute-start.8 = (bf16[128,1280]{1,0:T(8,128)(2,1)S(1)}, bf16[128,1280]{1,0:T(8,128)(2,1)S(1)}, u32[]{:S(2)}, u32[]{:S(2)}) collective-permute-start(bf16[128,1280]{1,0:T(8,128)(2,1)S(1)} %get-tuple-element.37.refs_0_), channel_id=1, source_target_pairs={{0,8},{1,9},{2,10},{3,11},{4,12},{5,13},{6,14},{7,15},{8,0},{9,1},... | collective-permute-start | bytes 983048 | tf_op jit(solution)/shard_map/gather_cotangent/ppermute | solution.py:286
  9.6 1.5 %collective-permute-start.9 = (bf16[128,1280]{1,0:T(8,128)(2,1)S(1)}, bf16[128,1280]{1,0:T(8,128)(2,1)S(1)}, u32[]{:S(2)}, u32[]{:S(2)}) collective-permute-start(bf16[128,1280]{1,0:T(8,128)(2,1)S(1)} %get-tuple-element.37.refs_0_), channel_id=1, source_target_pairs={{0,16},{1,17},{2,18},{3,19},{4,20},{5,21},{6,22},{7,23},{8,24},{9,... | collective-permute-start | bytes 983048 | tf_op jit(solution)/shard_map/gather_cotangent/ppermute | solution.py:286
  11.1 3.2 %collective-permute-done.refs_0_ = bf16[976,128]{1,0:T(8,128)(2,1)S(1)} collective-permute-done((bf16[976,128]{1,0:T(8,128)(2,1)S(1)}, bf16[976,128]{1,0:T(8,128)(2,1)S(1)}, u32[]{:S(2)}, u32[]{:S(2)}) %collective-permute-start) | collective-permute-done | bytes 249888 | tf_op jit(solution)/shard_map/exchange_heads/ppermute | solution.py:286
  14.2 2.6 %collective-permute-start.10 = (bf16[128,1280]{1,0:T(8,128)(2,1)S(1)}, bf16[128,1280]{1,0:T(8,128)(2,1)S(1)}, u32[]{:S(2)}, u32[]{:S(2)}) collective-permute-start(bf16[128,1280]{1,0:T(8,128)(2,1)S(1)} %get-tuple-element.37.refs_0_), channel_id=1, source_target_pairs={{0,24},{1,25},{2,26},{3,27},{4,28},{5,29},{6,30},{7,31},{8,16},{9,... | collective-permute-start | bytes 983048 | tf_op jit(solution)/shard_map/gather_cotangent/ppermute | solution.py:286
  16.9 2.9 %collective-permute-done.1.refs_2_.refs_1_ = bf16[976,128]{1,0:T(8,128)(2,1)S(1)} collective-permute-done((bf16[976,128]{1,0:T(8,128)(2,1)S(1)}, bf16[976,128]{1,0:T(8,128)(2,1)S(1)}, u32[]{:S(2)}, u32[]{:S(2)}) %collective-permute-start.1) | collective-permute-done | bytes 249888 | tf_op jit(solution)/shard_map/exchange_heads/ppermute | solution.py:286
  19.8 1.7 %attention.3 = (f32[320,384]{1,0:T(8,128)S(1)}, f32[8,384]{1,0:T(8,128)S(1)}, f32[8,384]{1,0:T(8,128)S(1)}) custom-call(bf16[976,128]{1,0:T(8,128)(2,1)S(1)} %collective-permute-done.refs_0_, bf16[976,128]{1,0:T(8,128)(2,1)S(1)} %get-tuple-element.25.refs_1_.refs_0_, bf16[976,128]{1,0:T(8,128)(2,1)S(1)} %collective-permute-done.1.refs_2_.refs_1_), custom_call_target="tpu_custom_call" | custom-call | flops 2595225600 | bytes 1310720 | tf_op jit(solution)/shard_map/attention/pallas_call | solution.py:39
  21.5 7.1 %collective-permute-done.2.refs_3_.refs_2_ = bf16[976,128]{1,0:T(8,128)(2,1)S(1)} collective-permute-done((bf16[976,128]{1,0:T(8,128)(2,1)S(1)}, bf16[976,128]{1,0:T(8,128)(2,1)S(1)}, u32[]{:S(2)}, u32[]{:S(2)}) %collective-permute-start.2) | collective-permute-done | bytes 249888 | tf_op jit(solution)/shard_map/exchange_heads/ppermute | solution.py:286
  28.5 1.5 %attention.4 = (bf16[320,128]{1,0:T(8,128)(2,1)S(1)}, bf16[320,128]{1,0:T(8,128)(2,1)S(1)}) custom-call(bf16[976,128]{1,0:T(8,128)(2,1)S(1)} %collective-permute-done.refs_0_, bf16[976,128]{1,0:T(8,128)(2,1)S(1)} %get-tuple-element.25.refs_1_.refs_0_, bf16[976,128]{1,0:T(8,128)(2,1)S(1)} %collective-permute-done.1.refs_2_.refs_1_, ...), custom_call_target="tpu_custom_call" | custom-call | flops 1441792000 | bytes 1310720 | tf_op jit(solution)/shard_map/attention/pallas_call | solution.py:39
  30.1 3.9 %collective-permute-start.4 = (bf16[320,128]{1,0:T(8,128)(2,1)S(1)}, bf16[320,128]{1,0:T(8,128)(2,1)S(1)}, u32[]{:S(2)}, u32[]{:S(2)}) collective-permute-start(bf16[320,128]{1,0:T(8,128)(2,1)S(1)} %get-tuple-element.32), channel_id=1, source_target_pairs={{0,6},{1,7},{2,12},{3,13},{4,18},{5,19},{6,24},{7,25},{8,14},{9,15... | collective-permute-start | bytes 245768 | tf_op jit(solution)/shard_map/send_to_owner/ppermute | solution.py:286
  34.0 1.0 %attention.5 = (bf16[320,128]{1,0:T(8,128)(2,1)S(1)}, bf16[320,128]{1,0:T(8,128)(2,1)S(1)}) custom-call(bf16[976,128]{1,0:T(8,128)(2,1)S(1)} %get-tuple-element.25.refs_1_.refs_0_, bf16[976,128]{1,0:T(8,128)(2,1)S(1)} %collective-permute-done.1.refs_2_.refs_1_, bf16[976,128]{1,0:T(8,128)(2,1)S(1)} %collective-permute-done.2.refs_3_.refs_2_, ...), custom_call_target="tpu_custom_call" | custom-call | flops 576716800 | bytes 1310720 | tf_op jit(solution)/shard_map/attention/pallas_call | solution.py:39
  35.0 1.5 %collective-permute-start.5 = (bf16[320,128]{1,0:T(8,128)(2,1)S(1)}, bf16[320,128]{1,0:T(8,128)(2,1)S(1)}, u32[]{:S(2)}, u32[]{:S(2)}) collective-permute-start(bf16[320,128]{1,0:T(8,128)(2,1)S(1)} %get-tuple-element.33), channel_id=1, source_target_pairs={{0,2},{1,3},{2,8},{3,9},{4,22},{5,23},{6,28},{7,29},{8,10},{9,11},... | collective-permute-start | bytes 245768 | tf_op jit(solution)/shard_map/send_to_owner/ppermute | solution.py:286
  36.6 0.7 %collective-permute-start.6 = (bf16[320,128]{1,0:T(8,128)(2,1)S(1)}, bf16[320,128]{1,0:T(8,128)(2,1)S(1)}, u32[]{:S(2)}, u32[]{:S(2)}) collective-permute-start(bf16[320,128]{1,0:T(8,128)(2,1)S(1)} %get-tuple-element.34), channel_id=1, source_target_pairs={{0,0},{1,1},{2,10},{3,11},{4,20},{5,21},{6,30},{7,31},{8,8},{9,9},... | collective-permute-start | bytes 245768 | tf_op jit(solution)/shard_map/send_to_owner/ppermute | solution.py:286
  37.2 0.5 swap_cotangent.1.refs_2_
  37.7 0.1 collective-permute-start.11
  37.8 2.0 %collective-permute-done.3.refs_0_ = bf16[320,128]{1,0:T(8,128)(2,1)S(1)} collective-permute-done((bf16[320,128]{1,0:T(8,128)(2,1)S(1)}, bf16[320,128]{1,0:T(8,128)(2,1)S(1)}, u32[]{:S(2)}, u32[]{:S(2)}) %collective-permute-start.3) | collective-permute-done | bytes 81952 | tf_op jit(solution)/shard_map/send_to_owner/ppermute | solution.py:286
  39.7 1.0 %collective-permute-done.5.refs_2_ = bf16[320,128]{1,0:T(8,128)(2,1)S(1)} collective-permute-done((bf16[320,128]{1,0:T(8,128)(2,1)S(1)}, bf16[320,128]{1,0:T(8,128)(2,1)S(1)}, u32[]{:S(2)}, u32[]{:S(2)}) %collective-permute-start.5) | collective-permute-done | bytes 81952 | tf_op jit(solution)/shard_map/send_to_owner/ppermute | solution.py:286
  40.7 0.1 send_to_owner.1
  40.8 0.1 collective-permute-start.7
  40.9 1.0 %collective-permute-start.16 = (bf16[320,128]{1,0:T(8,128)(2,1)S(1)}, bf16[320,128]{1,0:T(8,128)(2,1)S(1)}, u32[]{:S(2)}, u32[]{:S(2)}) collective-permute-start(bf16[320,128]{1,0:T(8,128)(2,1)S(1)} %get-tuple-element.44), channel_id=1, source_target_pairs={{0,8},{1,9},{2,10},{3,11},{4,12},{5,13},{6,14},{7,15},{8,0},{9,1},... | collective-permute-start | bytes 245768 | tf_op jit(solution)/shard_map/send_home/ppermute | solution.py:286
  41.9 1.0 %collective-permute-start.17 = (bf16[320,128]{1,0:T(8,128)(2,1)S(1)}, bf16[320,128]{1,0:T(8,128)(2,1)S(1)}, u32[]{:S(2)}, u32[]{:S(2)}) collective-permute-start(bf16[320,128]{1,0:T(8,128)(2,1)S(1)} %get-tuple-element.45), channel_id=1, source_target_pairs={{0,16},{1,17},{2,18},{3,19},{4,20},{5,21},{6,22},{7,23},{8,24},{9,... | collective-permute-start | bytes 245768 | tf_op jit(solution)/shard_map/send_home/ppermute | solution.py:286
  42.8 1.0 %gradient.1 = (f32[160,320]{1,0:T(8,128)S(1)}, bf16[80,640]{1,0:T(8,128)(2,1)S(1)}, bf16[80,640]{1,0:T(8,128)(2,1)S(1)}, bf16[80,640]{1,0:T(8,128)(2,1)S(1)}) custom-call(bf16[4,160,128]{2,1,0:T(8,128)(2,1)S(1)} %get-tuple-element.35.refs_0_, bf16[4,160,128]{2,1,0:T(8,128)(2,1)S(1)} %collective-permute-done.7.refs_1_, ...), custom_call_target="tpu_custom_call" | custom-call | flops 419430400 | bytes 2621440 | tf_op jit(solution)/shard_map/gradient/pallas_call | solution.py:39
  43.8 3.5 %collective-permute-start.12 = (bf16[80,640]{1,0:T(8,128)(2,1)S(1)}, bf16[80,640]{1,0:T(8,128)(2,1)S(1)}, u32[]{:S(2)}, u32[]{:S(2)}) collective-permute-start(bf16[80,640]{1,0:T(8,128)(2,1)S(1)} %get-tuple-element.38), channel_id=1, source_target_pairs={{0,4},{1,5},{2,6},{3,7},{4,0},{5,1},{6,2},{7,3},{8,12},{9,13},{10,... | collective-permute-start | bytes 307208 | tf_op jit(solution)/shard_map/sum_gradient/ppermute | solution.py:286
  47.3 3.4 %collective-permute-start.13 = (bf16[80,640]{1,0:T(8,128)(2,1)S(1)}, bf16[80,640]{1,0:T(8,128)(2,1)S(1)}, u32[]{:S(2)}, u32[]{:S(2)}) collective-permute-start(bf16[80,640]{1,0:T(8,128)(2,1)S(1)} %get-tuple-element.39), channel_id=1, source_target_pairs={{0,6},{1,7},{2,4},{3,5},{4,2},{5,3},{6,0},{7,1},{8,14},{9,15},{10,... | collective-permute-start | bytes 307208 | tf_op jit(solution)/shard_map/sum_gradient/ppermute | solution.py:286
  50.6 0.5 collective-permute-start.14
  51.1 0.7 %collective-permute-start.15 = (bf16[320,128]{1,0:T(8,128)(2,1)S(1)}, bf16[320,128]{1,0:T(8,128)(2,1)S(1)}, u32[]{:S(2)}, u32[]{:S(2)}) collective-permute-start(bf16[320,128]{1,0:T(8,128)(2,1)S(1)} %get-tuple-element.42), channel_id=1, source_target_pairs={{0,24},{1,25},{2,26},{3,27},{4,28},{5,29},{6,30},{7,31},{8,16},{9,... | collective-permute-start | bytes 245768 | tf_op jit(solution)/shard_map/send_home/ppermute | solution.py:286
  51.9 0.6 %project.1.refs_5_ = f32[128,1280]{1,0:T(8,128)S(1)} custom-call(bf16[128,1280]{1,0:T(8,128)(2,1)S(1)} %copy-done.1, bf16[1280,1280]{1,0:T(8,128)(2,1)S(1)} %copy-done, bf16[320,128]{1,0:T(8,128)(2,1)S(1)} %get-tuple-element.43.refs_0_, bf16[320,128]{1,0:T(8,128)(2,1)S(1)} %collective-permute-done.16.refs_1_, ...), custom_call_target="tpu_custom_call" | custom-call | flops 314572800 | bytes 2457600 | tf_op jit(solution)/shard_map/project/pallas_call | solution.py:39
  52.5 4.0 %collective-permute-done.15.refs_4_ = bf16[320,128]{1,0:T(8,128)(2,1)S(1)} collective-permute-done((bf16[320,128]{1,0:T(8,128)(2,1)S(1)}, bf16[320,128]{1,0:T(8,128)(2,1)S(1)}, u32[]{:S(2)}, u32[]{:S(2)}) %collective-permute-start.15) | collective-permute-done | bytes 81952 | tf_op jit(solution)/shard_map/send_home/ppermute | solution.py:286
  56.5 0.7 %collective-permute-done.14.refs_2_ = bf16[80,640]{1,0:T(8,128)(2,1)S(1)} collective-permute-done((bf16[80,640]{1,0:T(8,128)(2,1)S(1)}, bf16[80,640]{1,0:T(8,128)(2,1)S(1)}, u32[]{:S(2)}, u32[]{:S(2)}) %collective-permute-start.14) | collective-permute-done | bytes 102432 | tf_op jit(solution)/shard_map/sum_gradient/ppermute | solution.py:286
  57.2 1.1 %finish.1 = (bf16[128,1280]{1,0:T(8,128)(2,1)}, f32[160,320]{1,0:T(8,128)}) custom-call(bf16[80,640]{1,0:T(8,128)(2,1)S(1)} %collective-permute-done.12.refs_0_, bf16[80,640]{1,0:T(8,128)(2,1)S(1)} %collective-permute-done.13.refs_1_, bf16[80,640]{1,0:T(8,128)(2,1)S(1)} %collective-permute-done.14.refs_2_, f32[160,320]{1,0:T(8,128)S(1)} %get-tuple-element.41.refs_3_, ...), custom_call_target="tpu_custom_call" | custom-call | flops 104857600 | bytes 819200 | tf_op jit(solution)/shard_map/finish/pallas_call | solution.py:39
  (17 shorter events, 0.1 us)
Async XLA Ops:
  2.2 12.1 %collective-permute-start = (bf16[976,128]{1,0:T(8,128)(2,1)S(1)}, bf16[976,128]{1,0:T(8,128)(2,1)S(1)}, u32[]{:S(2)}, u32[]{:S(2)}) collective-permute-start(bf16[976,128]{1,0:T(8,128)(2,1)S(1)} %get-tuple-element.24), channel_id=1, source_target_pairs={{0,6},{1,7},{2,4},{3,5},{4,2},{5,3},{6,0},{7,1},{8,14},{9,15},{10,... | collective-permute-start | bytes 749576 | tf_op jit(solution)/shard_map/exchange_heads/ppermute | solution.py:286
  7.3 12.5 %collective-permute-start.1 = (bf16[976,128]{1,0:T(8,128)(2,1)S(1)}, bf16[976,128]{1,0:T(8,128)(2,1)S(1)}, u32[]{:S(2)}, u32[]{:S(2)}) collective-permute-start(bf16[976,128]{1,0:T(8,128)(2,1)S(1)} %get-tuple-element.26), channel_id=1, source_target_pairs={{0,2},{1,3},{2,0},{3,1},{4,6},{5,7},{6,4},{7,5},{8,10},{9,11},{10,... | collective-permute-start | bytes 749576 | tf_op jit(solution)/shard_map/exchange_heads/ppermute | solution.py:286
  7.3 21.3 %collective-permute-start.2 = (bf16[976,128]{1,0:T(8,128)(2,1)S(1)}, bf16[976,128]{1,0:T(8,128)(2,1)S(1)}, u32[]{:S(2)}, u32[]{:S(2)}) collective-permute-start(bf16[976,128]{1,0:T(8,128)(2,1)S(1)} %get-tuple-element.27), channel_id=1, source_target_pairs={{0,4},{1,5},{2,6},{3,7},{4,0},{5,1},{6,2},{7,3},{8,12},{9,13},{10,... | collective-permute-start | bytes 749576 | tf_op jit(solution)/shard_map/exchange_heads/ppermute | solution.py:286
  7.9 27.1 %collective-permute-start.8 = (bf16[128,1280]{1,0:T(8,128)(2,1)S(1)}, bf16[128,1280]{1,0:T(8,128)(2,1)S(1)}, u32[]{:S(2)}, u32[]{:S(2)}) collective-permute-start(bf16[128,1280]{1,0:T(8,128)(2,1)S(1)} %get-tuple-element.37.refs_0_), channel_id=1, source_target_pairs={{0,8},{1,9},{2,10},{3,11},{4,12},{5,13},{6,14},{7,15},{8,0},{9,1},... | collective-permute-start | bytes 983048 | tf_op jit(solution)/shard_map/gather_cotangent/ppermute | solution.py:286
  9.6 27.0 %collective-permute-start.9 = (bf16[128,1280]{1,0:T(8,128)(2,1)S(1)}, bf16[128,1280]{1,0:T(8,128)(2,1)S(1)}, u32[]{:S(2)}, u32[]{:S(2)}) collective-permute-start(bf16[128,1280]{1,0:T(8,128)(2,1)S(1)} %get-tuple-element.37.refs_0_), channel_id=1, source_target_pairs={{0,16},{1,17},{2,18},{3,19},{4,20},{5,21},{6,22},{7,23},{8,24},{9,... | collective-permute-start | bytes 983048 | tf_op jit(solution)/shard_map/gather_cotangent/ppermute | solution.py:286
  14.2 23.0 %collective-permute-start.10 = (bf16[128,1280]{1,0:T(8,128)(2,1)S(1)}, bf16[128,1280]{1,0:T(8,128)(2,1)S(1)}, u32[]{:S(2)}, u32[]{:S(2)}) collective-permute-start(bf16[128,1280]{1,0:T(8,128)(2,1)S(1)} %get-tuple-element.37.refs_0_), channel_id=1, source_target_pairs={{0,24},{1,25},{2,26},{3,27},{4,28},{5,29},{6,30},{7,31},{8,16},{9,... | collective-permute-start | bytes 983048 | tf_op jit(solution)/shard_map/gather_cotangent/ppermute | solution.py:286
  30.0 9.7 %collective-permute-start.3 = (bf16[320,128]{1,0:T(8,128)(2,1)S(1)}, bf16[320,128]{1,0:T(8,128)(2,1)S(1)}, u32[]{:S(2)}, u32[]{:S(2)}) collective-permute-start(bf16[320,128]{1,0:T(8,128)(2,1)S(1)} %get-tuple-element.31), channel_id=1, source_target_pairs={{0,4},{1,5},{2,14},{3,15},{4,16},{5,17},{6,26},{7,27},{8,12},{9,13... | collective-permute-start | bytes 245768 | tf_op jit(solution)/shard_map/send_to_owner/ppermute | solution.py:286
  30.1 9.6 %collective-permute-start.4 = (bf16[320,128]{1,0:T(8,128)(2,1)S(1)}, bf16[320,128]{1,0:T(8,128)(2,1)S(1)}, u32[]{:S(2)}, u32[]{:S(2)}) collective-permute-start(bf16[320,128]{1,0:T(8,128)(2,1)S(1)} %get-tuple-element.32), channel_id=1, source_target_pairs={{0,6},{1,7},{2,12},{3,13},{4,18},{5,19},{6,24},{7,25},{8,14},{9,15... | collective-permute-start | bytes 245768 | tf_op jit(solution)/shard_map/send_to_owner/ppermute | solution.py:286
  35.0 5.7 %collective-permute-start.5 = (bf16[320,128]{1,0:T(8,128)(2,1)S(1)}, bf16[320,128]{1,0:T(8,128)(2,1)S(1)}, u32[]{:S(2)}, u32[]{:S(2)}) collective-permute-start(bf16[320,128]{1,0:T(8,128)(2,1)S(1)} %get-tuple-element.33), channel_id=1, source_target_pairs={{0,2},{1,3},{2,8},{3,9},{4,22},{5,23},{6,28},{7,29},{8,10},{9,11},... | collective-permute-start | bytes 245768 | tf_op jit(solution)/shard_map/send_to_owner/ppermute | solution.py:286
  36.6 4.1 %collective-permute-start.6 = (bf16[320,128]{1,0:T(8,128)(2,1)S(1)}, bf16[320,128]{1,0:T(8,128)(2,1)S(1)}, u32[]{:S(2)}, u32[]{:S(2)}) collective-permute-start(bf16[320,128]{1,0:T(8,128)(2,1)S(1)} %get-tuple-element.34), channel_id=1, source_target_pairs={{0,0},{1,1},{2,10},{3,11},{4,20},{5,21},{6,30},{7,31},{8,8},{9,9},... | collective-permute-start | bytes 245768 | tf_op jit(solution)/shard_map/send_to_owner/ppermute | solution.py:286
  37.7 5.1 %collective-permute-start.11 = (bf16[4,128,1280]{2,1,0:T(8,128)(2,1)S(1)}, bf16[4,128,1280]{2,1,0:T(8,128)(2,1)S(1)}, u32[]{:S(2)}, u32[]{:S(2)}) collective-permute-start(bf16[4,128,1280]{2,1,0:T(8,128)(2,1)S(1)} %swap_cotangent.1.refs_2_), channel_id=1, source_target_pairs={{0,1},{1,0},{2,3},{3,2},{4,5},{5,4},{6,7},{7,6},{8,9},{9,8},{10,11... | collective-permute-start | bytes 3932168 | tf_op jit(solution)/shard_map/gradient/ppermute | solution.py:286
  40.7 11.2 %copy-start = (bf16[1280,1280]{1,0:T(8,128)(2,1)S(1)}, bf16[1280,1280]{1,0:T(8,128)(2,1)}, u32[]{:S(2)}) copy-start(bf16[1280,1280]{1,0:T(8,128)(2,1)} %refs_6_.1) | copy-start | bytes 9830404
  40.8 2.0 %collective-permute-start.7 = (bf16[4,160,128]{2,1,0:T(8,128)(2,1)S(1)}, bf16[4,160,128]{2,1,0:T(8,128)(2,1)S(1)}, u32[]{:S(2)}, u32[]{:S(2)}) collective-permute-start(bf16[4,160,128]{2,1,0:T(8,128)(2,1)S(1)} %get-tuple-element.36), channel_id=1, source_target_pairs={{0,1},{1,0},{2,3},{3,2},{4,5},{5,4},{6,7},{7,6},{8,9},{9,8},{10,11... | collective-permute-start | bytes 491528 | tf_op jit(solution)/shard_map/send_to_owner/ppermute | solution.py:286
  40.9 10.3 %collective-permute-start.16 = (bf16[320,128]{1,0:T(8,128)(2,1)S(1)}, bf16[320,128]{1,0:T(8,128)(2,1)S(1)}, u32[]{:S(2)}, u32[]{:S(2)}) collective-permute-start(bf16[320,128]{1,0:T(8,128)(2,1)S(1)} %get-tuple-element.44), channel_id=1, source_target_pairs={{0,8},{1,9},{2,10},{3,11},{4,12},{5,13},{6,14},{7,15},{8,0},{9,1},... | collective-permute-start | bytes 245768 | tf_op jit(solution)/shard_map/send_home/ppermute | solution.py:286
  41.9 10.0 %collective-permute-start.17 = (bf16[320,128]{1,0:T(8,128)(2,1)S(1)}, bf16[320,128]{1,0:T(8,128)(2,1)S(1)}, u32[]{:S(2)}, u32[]{:S(2)}) collective-permute-start(bf16[320,128]{1,0:T(8,128)(2,1)S(1)} %get-tuple-element.45), channel_id=1, source_target_pairs={{0,16},{1,17},{2,18},{3,19},{4,20},{5,21},{6,22},{7,23},{8,24},{9,... | collective-permute-start | bytes 245768 | tf_op jit(solution)/shard_map/send_home/ppermute | solution.py:286
  42.8 9.1 %copy-start.1 = (bf16[128,1280]{1,0:T(8,128)(2,1)S(1)}, bf16[128,1280]{1,0:T(8,128)(2,1)}, u32[]{:S(2)}) copy-start(bf16[128,1280]{1,0:T(8,128)(2,1)} %residual.1) | copy-start | bytes 983044
  43.8 12.7 %collective-permute-start.12 = (bf16[80,640]{1,0:T(8,128)(2,1)S(1)}, bf16[80,640]{1,0:T(8,128)(2,1)S(1)}, u32[]{:S(2)}, u32[]{:S(2)}) collective-permute-start(bf16[80,640]{1,0:T(8,128)(2,1)S(1)} %get-tuple-element.38), channel_id=1, source_target_pairs={{0,4},{1,5},{2,6},{3,7},{4,0},{5,1},{6,2},{7,3},{8,12},{9,13},{10,... | collective-permute-start | bytes 307208 | tf_op jit(solution)/shard_map/sum_gradient/ppermute | solution.py:286
  47.3 9.2 %collective-permute-start.13 = (bf16[80,640]{1,0:T(8,128)(2,1)S(1)}, bf16[80,640]{1,0:T(8,128)(2,1)S(1)}, u32[]{:S(2)}, u32[]{:S(2)}) collective-permute-start(bf16[80,640]{1,0:T(8,128)(2,1)S(1)} %get-tuple-element.39), channel_id=1, source_target_pairs={{0,6},{1,7},{2,4},{3,5},{4,2},{5,3},{6,0},{7,1},{8,14},{9,15},{10,... | collective-permute-start | bytes 307208 | tf_op jit(solution)/shard_map/sum_gradient/ppermute | solution.py:286
  50.6 6.5 %collective-permute-start.14 = (bf16[80,640]{1,0:T(8,128)(2,1)S(1)}, bf16[80,640]{1,0:T(8,128)(2,1)S(1)}, u32[]{:S(2)}, u32[]{:S(2)}) collective-permute-start(bf16[80,640]{1,0:T(8,128)(2,1)S(1)} %get-tuple-element.40), channel_id=1, source_target_pairs={{0,2},{1,3},{2,0},{3,1},{4,6},{5,7},{6,4},{7,5},{8,10},{9,11},{10,... | collective-permute-start | bytes 307208 | tf_op jit(solution)/shard_map/sum_gradient/ppermute | solution.py:286
  51.1 5.3 %collective-permute-start.15 = (bf16[320,128]{1,0:T(8,128)(2,1)S(1)}, bf16[320,128]{1,0:T(8,128)(2,1)S(1)}, u32[]{:S(2)}, u32[]{:S(2)}) collective-permute-start(bf16[320,128]{1,0:T(8,128)(2,1)S(1)} %get-tuple-element.42), channel_id=1, source_target_pairs={{0,24},{1,25},{2,26},{3,27},{4,28},{5,29},{6,30},{7,31},{8,16},{9,... | collective-permute-start | bytes 245768 | tf_op jit(solution)/shard_map/send_home/ppermute | solution.py:286
